TPU v7x, 128 devices: a whole 4x4x4 slice. The times are simulated.
128 devices in a mesh: loop: 4 (over y_lo, core), wide: 32 (over y_hi, x, z).
Axes of the slice: x: 4, y: 4 (y_hi: 2, y_lo: 2; y = y_hi * 2 + y_lo), z: 4, core: 2. Of those that a mesh axis runs over, the one named last changes fastest.
Arguments:
- features: float32 [128, 65536], P(None, 'wide'), may hold values from -6 to 6
- weight: float32 [128, 128], replicated, may hold values from -0.5 to 0.5
- cotangent: float32 [128, 65536], P(None, 'wide'), may hold values from -6 to 6
- tiles: float32 [4, 32, 256, 128, 128], P('loop', 'wide'), may hold values from 0 to 0.001953125
- tile_rows: int32 [4, 32, 256], P('loop', 'wide'), may hold values from 0 to 15
- tile_cols: int32 [4, 32, 256], P('loop', 'wide'), may hold values from 0 to 127
- counts: int32 [4, 32], P('loop', 'wide'), may hold values from 64 to 256, as said below
Outputs:
- activated: float32 [128, 65536], P(None, 'wide')
- input_grad: float32 [128, 65536], P(None, 'wide')
- weight_grad: float32 [128, 128], replicated
Inputs may be any that keep to these rules, and one draw needn't show every extreme that they name: `counts`: each count is 256 / 4 times a power of two; one panel holds exactly 256 live tiles; slots at or past a panel's count are ignored.
All inputs are finite; a program needn't handle non-finite values.
Results may differ from a plain program's by a relative error of at most 0.0003.
Values sent between devices are 32-bit elements; how exact they have to be, the bound alone decides.
No kernel may reach another device: no remote copies, remote signals or barrier semaphores. Data moves between devices by JAX's collectives and lax.ppermute only.
A program may use at most 192 MiB of HBM per device.

v0:
```python
import math

import jax
import jax.numpy as jnp
from jax import lax
from jax.sharding import PartitionSpec as P

HI = lax.Precision.HIGHEST
MAX_BLOCK_SIZE = 64


def blocks_per_slot(entry_count, start_offset, slot_count, block_entry):
    return (jnp.clip(entry_count - start_offset, 0, slot_count) + block_entry - 1) // block_entry


def forward_part(group3, tile_collection, rows, cols, entry_count, start_offset, nrow):
    feats = group3.shape[0]
    width = group3.shape[2]
    slot_count = tile_collection.shape[0]
    block_entry = math.gcd(MAX_BLOCK_SIZE, slot_count)

    def forward_step(index, total):
        start = index * block_entry
        block_tiles = lax.dynamic_slice_in_dim(tile_collection, start, block_entry, 0)
        block_rows = lax.dynamic_slice_in_dim(rows, start, block_entry, 0)
        block_cols = lax.dynamic_slice_in_dim(cols, start, block_entry, 0)
        taken = jnp.take(group3, block_cols, axis=1)
        part = jnp.einsum("fbc,brc->bfr", taken, block_tiles, precision=HI)
        live = start_offset + start + jnp.arange(block_entry, dtype=jnp.int32) < entry_count
        onehot = (
            (block_rows[:, None] == jnp.arange(nrow, dtype=jnp.int32)[None, :]) & live[:, None]
        ).astype(jnp.float32)
        return total + jnp.einsum("bn,bfr->fnr", onehot, part, precision=HI)

    initial_carry = jnp.zeros((feats, nrow, width), jnp.float32)
    return lax.fori_loop(
        0,
        blocks_per_slot(entry_count, start_offset, slot_count, block_entry),
        forward_step,
        initial_carry,
    )


def backward_part(slope3, tile_collection, rows, cols, entry_count, start_offset, ngroup):
    feats = slope3.shape[0]
    width = slope3.shape[2]
    slot_count = tile_collection.shape[0]
    block_entry = math.gcd(MAX_BLOCK_SIZE, slot_count)

    def backward_step(index, total):
        start = index * block_entry
        block_tiles = lax.dynamic_slice_in_dim(tile_collection, start, block_entry, 0)
        block_rows = lax.dynamic_slice_in_dim(rows, start, block_entry, 0)
        block_cols = lax.dynamic_slice_in_dim(cols, start, block_entry, 0)
        taken = jnp.take(slope3, block_rows, axis=1)
        part = jnp.einsum("fbr,brc->bfc", taken, block_tiles, precision=HI)
        live = start_offset + start + jnp.arange(block_entry, dtype=jnp.int32) < entry_count
        onehot = (
            (block_cols[:, None] == jnp.arange(ngroup, dtype=jnp.int32)[None, :]) & live[:, None]
        ).astype(jnp.float32)
        return total + jnp.einsum("bn,bfc->fnc", onehot, part, precision=HI)

    initial_carry = jnp.zeros((feats, ngroup, width), jnp.float32)
    return lax.fori_loop(
        0,
        blocks_per_slot(entry_count, start_offset, slot_count, block_entry),
        backward_step,
        initial_carry,
    )


def per_device(features, weight, cotangent, tiles, tile_rows, tile_cols, counts):
    feats, shard_nodes = features.shape
    loops = lax.axis_size("loop")
    position = lax.axis_index("loop")
    quarter = shard_nodes // loops
    width = tiles.shape[-1]
    nrow = shard_nodes // width
    slots = tiles.shape[2]
    tile_collection = tiles.reshape(slots, width, width)
    rows = tile_rows.reshape(slots)
    cols = tile_cols.reshape(slots)
    count_vec = counts.reshape(1)
    entry_count = count_vec[0]
    projected = jnp.dot(weight.T, features, precision=HI, preferred_element_type=jnp.float32)
    own_cols = lax.dynamic_slice_in_dim(projected, position * quarter, quarter, 1)
    own_group = lax.all_gather(own_cols, "wide", axis=1, tiled=True)
    own3 = own_group.reshape(feats, -1, width)
    partial_value = forward_part(own3, tile_collection, rows, cols, entry_count, 0, nrow)
    ngroup = own3.shape[1]
    partial_value = partial_value.reshape(feats, shard_nodes)
    aggregated = lax.psum(partial_value, "loop")
    activated, pull = jax.vjp(jax.nn.gelu, aggregated)
    slope = pull(cotangent)[0]
    slope3 = slope.reshape(feats, nrow, width)
    own_back = backward_part(slope3, tile_collection, rows, cols, entry_count, 0, ngroup)
    grad_cols = lax.psum_scatter(
        own_back.reshape(feats, -1), "wide", scatter_dimension=1, tiled=True
    )
    feature_cols = lax.dynamic_slice_in_dim(features, position * quarter, quarter, 1)
    weight_term = jnp.dot(
        feature_cols, grad_cols.T, precision=HI, preferred_element_type=jnp.float32
    )
    weight_grad = lax.psum(weight_term, ("loop", "wide"))
    input_cols = jnp.dot(weight, grad_cols, precision=HI, preferred_element_type=jnp.float32)
    input_grad = lax.all_gather(input_cols, "loop", axis=1, tiled=True)
    return (activated, input_grad, weight_grad)


def solution(mesh):
    return jax.shard_map(
        per_device,
        mesh=mesh,
        in_specs=(
            P(None, "wide"),
            P(),
            P(None, "wide"),
            P("loop", "wide", None, None, None),
            P("loop", "wide", None),
            P("loop", "wide", None),
            P("loop", "wide"),
        ),
        out_specs=(P(None, "wide"), P(None, "wide"), P()),
        check_vma=False,
    )
```

profile of v0, /device:TPU:0, one launch (start us, length us, event | category | flops | bytes accessed | tf_op | source)
XLA Modules:
  0.0 746.2 jit_solution(2687843749686464451)
XLA Ops:
  11.8 106.1 %all-gather.3.cloned.1.call-done = f32[128,16384]{1,0:T(8,128)} async-done(((f32[128,512]{1,0:T(8,128)}), f32[128,16384]{1,0:T(8,128)}) %all-gather.3.cloned.1.call-update) | async-done | bytes 8388624 | tf_op jit(solution)/shard_map/all_gather | solution.py:87
  117.9 7.8 %copy_bitcast_fusion = f32[128,128,128]{2,0,1:T(8,128)} fusion(f32[128,16384]{1,0:T(8,128)} %all-gather.3.cloned.1.call-done), kind=kLoop, calls=%fused_computation.43 | loop fusion | bytes 16777216 | tf_op jit(solution)/shard_map/while | solution.py:36
  125.8 89.4 %while.20 = (s32[]{:T(128)}, f32[128,16,128]{2,1,0:T(8,128)S(1)}, s32[]{:T(128)}, s32[256]{0:T(256)S(1)}, f32[128,128,128]{2,0,1:T(8,128)}, /*index=5*/f32[256,1...) while((s32[]{:T(128)}, f32[128,16,128]{2,1,0:T(8,128)S(1)}, ...), condition=%wide.region_1.2_spmd, body=%wide.region_0.1_spmd.sunk | while | flops 1813253632 | bytes 27269304 | solution.py:36
  126.7 6.2 gather_fusion
  132.9 11.2 %fusion.70 = f32[64,128,128]{2,1,0:T(8,128)S(1)} fusion(f32[64,128,128]{2,1,0:T(8,128)} %gather_fusion, f32[256,128,128]{2,1,0:T(8,128)} %get-tuple-element.294, s32[]{:T(128)S(6)} %select_n.58, pred[64]{0:T(512)(128)(4,1)S(1)} %get-tuple-element.252), kind=kOutput, calls=%fused_computation.2.clone.1 | convolution fusion | flops 1611661312 | bytes 12582980 | tf_op jit(solution)/shard_map/while/body/fbc,brc->bfr/dot_general | solution.py:28
  149.0 6.2 gather_fusion
  155.2 11.2 %fusion.70 = f32[64,128,128]{2,1,0:T(8,128)S(1)} fusion(f32[64,128,128]{2,1,0:T(8,128)} %gather_fusion, f32[256,128,128]{2,1,0:T(8,128)} %get-tuple-element.294, s32[]{:T(128)S(6)} %select_n.58, pred[64]{0:T(512)(128)(4,1)S(1)} %get-tuple-element.252), kind=kOutput, calls=%fused_computation.2.clone.1 | convolution fusion | flops 1611661312 | bytes 12582980 | tf_op jit(solution)/shard_map/while/body/fbc,brc->bfr/dot_general | solution.py:28
  171.4 6.2 gather_fusion
  177.5 11.2 %fusion.70 = f32[64,128,128]{2,1,0:T(8,128)S(1)} fusion(f32[64,128,128]{2,1,0:T(8,128)} %gather_fusion, f32[256,128,128]{2,1,0:T(8,128)} %get-tuple-element.294, s32[]{:T(128)S(6)} %select_n.58, pred[64]{0:T(512)(128)(4,1)S(1)} %get-tuple-element.252), kind=kOutput, calls=%fused_computation.2.clone.1 | convolution fusion | flops 1611661312 | bytes 12582980 | tf_op jit(solution)/shard_map/while/body/fbc,brc->bfr/dot_general | solution.py:28
  199.9 11.2 %fusion.70 = f32[64,128,128]{2,1,0:T(8,128)S(1)} fusion(f32[64,128,128]{2,1,0:T(8,128)} %gather_fusion, f32[256,128,128]{2,1,0:T(8,128)} %get-tuple-element.294, s32[]{:T(128)S(6)} %select_n.58, pred[64]{0:T(512)(128)(4,1)S(1)} %get-tuple-element.252), kind=kOutput, calls=%fused_computation.2.clone.1 | convolution fusion | flops 1611661312 | bytes 12582980 | tf_op jit(solution)/shard_map/while/body/fbc,brc->bfr/dot_general | solution.py:28
  216.6 38.9 %all-reduce.3.cloned.1.call-done = f32[128,2048]{1,0:T(8,128)} async-done(((f32[128,2048]{1,0:T(8,128)}), f32[128,2048]{1,0:T(8,128)}) %all-reduce.3.cloned.1.call-update) | async-done | bytes 1048592 | tf_op jit(solution)/shard_map/psum | solution.py:92
  262.8 102.0 %while.21 = (s32[]{:T(128)}, f32[128,128,128]{1,2,0:T(8,128)}, s32[]{:T(128)}, s32[256]{0:T(256)S(1)}, f32[128,16,128]{2,0,1:T(8,128)S(1)}, /*index=5*/f32[256,1...) while((s32[]{:T(128)}, f32[128,128,128]{1,2,0:T(8,128)}, ...), condition=%wide.region_4.5_spmd, body=%wide.region_3.4_spmd.sunk | while | flops 3224389120 | bytes 109058288 | solution.py:64
  266.4 7.1 fusion.76
  273.5 11.6 %bitcast_add_fusion.2 = f32[128,128,128]{1,2,0:T(8,128)S(1)} fusion(f32[128,128,128]{1,2,0:T(8,128)S(1)} %copy-done.1, f32[64,128,128]{2,1,0:T(8,128)S(1)} %fusion.76, s32[64]{0:T(128)S(1)} %dynamic_slice.44, pred[64]{0:T(512)(128)(4,1)S(1)} %get-tuple-element.264), kind=kOutput, calls=%fused_computation.23.clone.1 | convolution fusion | flops 1612726272 | bytes 20971840 | tf_op jit(solution)/shard_map/while/body/bn,bfc->fnc/dot_general | solution.py:61
  291.9 7.1 fusion.76
  299.0 11.6 %bitcast_add_fusion.2 = f32[128,128,128]{1,2,0:T(8,128)S(1)} fusion(f32[128,128,128]{1,2,0:T(8,128)S(1)} %copy-done.1, f32[64,128,128]{2,1,0:T(8,128)S(1)} %fusion.76, s32[64]{0:T(128)S(1)} %dynamic_slice.44, pred[64]{0:T(512)(128)(4,1)S(1)} %get-tuple-element.264), kind=kOutput, calls=%fused_computation.23.clone.1 | convolution fusion | flops 1612726272 | bytes 20971840 | tf_op jit(solution)/shard_map/while/body/bn,bfc->fnc/dot_general | solution.py:61
  317.4 7.1 fusion.76
  324.5 11.6 %bitcast_add_fusion.2 = f32[128,128,128]{1,2,0:T(8,128)S(1)} fusion(f32[128,128,128]{1,2,0:T(8,128)S(1)} %copy-done.1, f32[64,128,128]{2,1,0:T(8,128)S(1)} %fusion.76, s32[64]{0:T(128)S(1)} %dynamic_slice.44, pred[64]{0:T(512)(128)(4,1)S(1)} %get-tuple-element.264), kind=kOutput, calls=%fused_computation.23.clone.1 | convolution fusion | flops 1612726272 | bytes 20971840 | tf_op jit(solution)/shard_map/while/body/bn,bfc->fnc/dot_general | solution.py:61
  342.9 7.1 fusion.76
  350.0 11.6 %bitcast_add_fusion.2 = f32[128,128,128]{1,2,0:T(8,128)S(1)} fusion(f32[128,128,128]{1,2,0:T(8,128)S(1)} %copy-done.1, f32[64,128,128]{2,1,0:T(8,128)S(1)} %fusion.76, s32[64]{0:T(128)S(1)} %dynamic_slice.44, pred[64]{0:T(512)(128)(4,1)S(1)} %get-tuple-element.264), kind=kOutput, calls=%fused_computation.23.clone.1 | convolution fusion | flops 1612726272 | bytes 20971840 | tf_op jit(solution)/shard_map/while/body/bn,bfc->fnc/dot_general | solution.py:61
  364.9 9.3 %copy.13 = f32[128,128,128]{0,2,1:T(8,128)} copy(f32[128,128,128]{1,2,0:T(8,128)} %get-tuple-element.90) | data formatting | bytes 16777216 | tf_op jit(solution)/shard_map/while | solution.py:64
  374.3 204.0 %reduce-scatter.2.cloned.1.call-done = f32[128,512]{0,1:T(8,128)} async-done(((f32[128,16384]{0,1:T(8,128)}), f32[128,512]{0,1:T(8,128)}) %reduce-scatter.2.cloned.1.call-update) | async-done | bytes 262160 | tf_op jit(solution)/shard_map/reduce_scatter | solution.py:97
  582.3 13.6 %all-gather.5.cloned.1.call-done = f32[128,2048]{0,1:T(8,128)} async-done(((f32[128,512]{0,1:T(8,128)}), f32[128,2048]{0,1:T(8,128)}) %all-gather.5.cloned.1.call-update) | async-done | bytes 1048592 | tf_op jit(solution)/shard_map/all_gather | solution.py:106
  598.4 139.7 %all-reduce.5.cloned.1.call-done = f32[128,128]{1,0:T(8,128)} async-done(((f32[128,128]{1,0:T(8,128)}), f32[128,128]{1,0:T(8,128)}) %all-reduce.5.cloned.1.call-update) | async-done | bytes 65552 | tf_op jit(solution)/shard_map/psum | solution.py:104
  (80 shorter events, 74.0 us)
Async XLA Ops:
  7.2 1.2 copy-start
  7.2 110.7 %all-gather.3.cloned.1.call-start = ((), (), s32[]{:S(2)}) async-start(), calls=%async_computation.1 | async-start | bytes 8650752 | tf_op jit(solution)/shard_map/all_gather | solution.py:87
  11.0 244.5 %all-reduce.3.cloned.1.call-start = ((), (), s32[]{:S(2)}) async-start(), calls=%async_computation.2 | async-start | bytes 2097152 | tf_op jit(solution)/shard_map/psum | solution.py:92
  11.8 114.0 %copy-start.5 = (s32[1,1,256]{2,1,0:T(1,128)S(1)}, s32[1,1,256]{2,1,0:T(1,128)}, u32[]{:S(2)}) copy-start(s32[1,1,256]{2,1,0:T(1,128)} %param.16) | copy-start | bytes 3076
  11.8 114.0 %copy-start.6 = (s32[1,1,256]{2,1,0:T(1,128)S(1)}, s32[1,1,256]{2,1,0:T(1,128)}, u32[]{:S(2)}) copy-start(s32[1,1,256]{2,1,0:T(1,128)} %param.15) | copy-start | bytes 3076
  125.8 129.7 %copy-start.3 = (f32[128,2048]{1,0:T(8,128)S(1)}, f32[128,2048]{1,0:T(8,128)}, u32[]{:S(2)}) copy-start(f32[128,2048]{1,0:T(8,128)} %param.13) | copy-start | bytes 3145732
  216.6 361.7 %reduce-scatter.2.cloned.1.call-start = ((), (), s32[]{:S(2)}) async-start(), calls=%async_computation.3 | async-start | bytes 8650752 | tf_op jit(solution)/shard_map/reduce_scatter | solution.py:97
  266.4 7.1 copy-start.1
  285.1 3.2 copy-start.2
  291.9 7.1 copy-start.1
  310.6 3.2 copy-start.2
  317.4 7.1 copy-start.1
  336.1 3.2 copy-start.2
  342.9 7.1 copy-start.1
  361.6 3.2 copy-start.2
  374.2 204.0 %copy-start.4 = (f32[128,128]{1,0:T(8,128)S(1)}, f32[128,128]{1,0:T(8,128)}, u32[]{:S(2)}) copy-start(f32[128,128]{1,0:T(8,128)} %param.12) | copy-start | bytes 196612
  374.2 221.7 %all-gather.5.cloned.1.call-start = ((), (), s32[]{:S(2)}) async-start(), calls=%async_computation.4 | async-start | bytes 1310720 | tf_op jit(solution)/shard_map/all_gather | solution.py:106
  580.3 157.9 %all-reduce.5.cloned.1.call-start = ((), (), s32[]{:S(2)}) async-start(), calls=%async_computation.5 | async-start | bytes 131072 | tf_op jit(solution)/shard_map/psum | solution.py:104
Sparse Core Ops, SparseCore 0:
  11.6 106.2 all-gather.2
  216.7 38.7 all-reduce.2
  374.4 203.8 reduce-scatter.1
  580.4 15.4 all-gather.4
  601.8 136.3 all-reduce.4
where the time goes:
time: 750 us; the launch traced here: 746 us
  waiting for transfers between devices  502 us (67%)
  matrix products  142 us (19%)
  local copies, waits for them, and re-layouts  78.1 us (10%)
  between operations  14.5 us (2%)
  other arithmetic  8.82 us (1%)
    reduce_scatter x1, waiting for transfers between devices, per_device(): lax.psum_scatter(own_back.reshape(feats, -1), 'wide', scatter_dimension=1...  204 us
    psum x1, waiting for transfers between devices, per_device(): weight_grad = lax.psum(weight_term, ('loop', 'wide'))  140 us
    all_gather x1, waiting for transfers between devices, per_device(): own_group = lax.all_gather(own_cols, 'wide', axis=1, tiled=True)  106 us
    dot_general x4, matrix products, backward_step(): return total + jnp.einsum('bn,bfc->fnc', onehot, part, precision=HI)  46.4 us
    dot_general x4, matrix products, forward_step(): part = jnp.einsum('fbc,brc->bfr', taken, block_tiles, precision=HI)  44.8 us
    psum x1, waiting for transfers between devices, per_device(): aggregated = lax.psum(partial_value, 'loop')  38.9 us
    dot_general x4, matrix products, backward_step(): part = jnp.einsum('fbr,brc->bfc', taken, block_tiles, precision=HI)  28.2 us
    gather x4, local copies, waits for them, and re-layouts, forward_step(): taken = jnp.take(group3, block_cols, axis=1)  24.6 us
  transfers between devices with their start and end apart: 5, of which 5 were waited for; matrix products, arithmetic and copies ran while one was open for 1% of the time, Pallas kernels for 0%

commit v1 on v0

v1 whole, which is shorter than its diff:
```python
import jax
import jax.numpy as jnp
from jax import lax
from jax.experimental import pallas as pl
from jax.experimental.pallas import tpu as pltpu
from jax.sharding import PartitionSpec as P

HI = lax.Precision.HIGHEST
AXES = ("loop", "wide")
SIDE = 4
TILE = 128
SLOTS = 256
CHUNK = 32
BUFFERS = 16
PER = 8
VMEM_BYTES = 56 * 1024 * 1024


def device_index(y, core, x, z):
    y, x, z = y % SIDE, x % SIDE, z % SIDE
    return (((y & 1) * 2 + core) * 2 + (y >> 1)) * 16 + x * SIDE + z


def permute(value, move):
    pairs = []
    for y in range(SIDE):
        for core in range(2):
            for x in range(SIDE):
                for z in range(SIDE):
                    pairs.append((device_index(y, core, x, z), device_index(*move(y, core, x, z))))
    return lax.ppermute(value, AXES, pairs)


def x_up(y, core, x, z):
    return (y, core, x + 1, z)


def x_down(y, core, x, z):
    return (y, core, x - 1, z)


def z_up(y, core, x, z):
    return (y, core, x, z + 1)


def z_down(y, core, x, z):
    return (y, core, x, z - 1)


def y_partner(y, core, x, z):
    return (3 - y, core, x, z)


def y_pair(y, core, x, z):
    return (y ^ 1, core, x, z)


def y_far(y, core, x, z):
    return (y + 2, core, x, z)


def core_swap(y, core, x, z):
    return (y, 1 - core, x, z)


def flip(y, core, x, z, axis, step):
    return (y, core, x ^ step, z) if axis == "x" else (y, core, x, z ^ step)


def ring_gather_near(value, up, down):
    one = permute(value, down)
    three = permute(value, up)
    two = permute(one, down)
    return [value, one, two, three]


def ring_gather_far(value, up, down):
    one = permute(value, down)
    three = permute(value, up)
    two = permute(three, up)
    return [value, one, two, three]


def ring_reduce_near(parts, up, down):
    moved = permute(parts[2], up)
    three = permute(parts[3], down)
    one = permute(parts[1] + moved, up)
    return parts[0] + one + three


def ring_reduce_far(parts, up, down):
    moved = permute(parts[2], down)
    one = permute(parts[1], up)
    three = permute(parts[3] + moved, down)
    return parts[0] + one + three


def split_high_low(value):
    high = value.astype(jnp.bfloat16)
    low = (value - high.astype(jnp.float32)).astype(jnp.bfloat16)
    return high, low


def tile_copy(tiles_ref, held, sems, chunk):
    part = pl.ds(chunk * CHUNK, CHUNK)
    return pltpu.make_async_copy(tiles_ref.at[part], held.at[part], sems.at[chunk])


def forward_kernel(count_ref, rows_ref, slots_ref, tiles_ref, *rest):
    buffers = rest[:BUFFERS]
    out_ref, held, group, pairs, tile_sems, group_sems = rest[BUFFERS:]
    count = count_ref[0]
    copies = []
    for index in range(BUFFERS):
        copy = pltpu.make_async_copy(
            buffers[index], group.at[pl.ds(index * PER, PER)], group_sems.at[index]
        )
        copy.start()
        copies.append(copy)
    for chunk in range(SLOTS // CHUNK):

        @pl.when(chunk * CHUNK < count)
        def _():
            tile_copy(tiles_ref, held, tile_sems, chunk).start()

    out_ref[...] = jnp.zeros_like(out_ref)
    for index in range(BUFFERS):
        copies[index].wait()

        @pl.loop(index * PER, (index + 1) * PER)
        def _(slot):
            high, low = split_high_low(group[slot])
            pairs[slot, :, :TILE] = high
            pairs[slot, :, TILE:] = low

    for chunk in range(SLOTS // CHUNK):

        @pl.when(chunk * CHUNK < count)
        def _():
            tile_copy(tiles_ref, held, tile_sems, chunk).wait()

            @pl.loop(chunk * CHUNK, (chunk + 1) * CHUNK, unroll=4)
            def _(t):
                high, low = split_high_low(held[t])
                right = pairs[slots_ref[t]]
                product = jnp.dot(
                    jnp.concatenate([high, low], axis=1),
                    jnp.concatenate([right, right], axis=0),
                    preferred_element_type=jnp.float32,
                )
                out_ref[rows_ref[t]] += product[:, :TILE] + product[:, TILE:]


def backward_kernel(count_ref, rows_ref, slots_ref, tiles_ref, slope_ref, *rest):
    buffers = rest[:BUFFERS]
    held, total, pairs, tile_sems, out_sems = rest[BUFFERS:]
    count = count_ref[0]
    for chunk in range(SLOTS // CHUNK):

        @pl.when(chunk * CHUNK < count)
        def _():
            tile_copy(tiles_ref, held, tile_sems, chunk).start()

    for row in range(pairs.shape[0]):
        high, low = split_high_low(slope_ref[:, row * TILE : (row + 1) * TILE])
        pairs[row, :, :TILE] = high
        pairs[row, :, TILE:] = low

    @pl.loop(0, BUFFERS * PER)
    def _(slot):
        total[slot] = jnp.zeros((TILE, TILE), jnp.float32)

    for chunk in range(SLOTS // CHUNK):

        @pl.when(chunk * CHUNK < count)
        def _():
            tile_copy(tiles_ref, held, tile_sems, chunk).wait()

            @pl.loop(chunk * CHUNK, (chunk + 1) * CHUNK, unroll=4)
            def _(t):
                high, low = split_high_low(held[t])
                right = jnp.concatenate([high, low], axis=1)
                product = jnp.dot(
                    pairs[rows_ref[t]],
                    jnp.concatenate([right, right], axis=0),
                    preferred_element_type=jnp.float32,
                )
                total[slots_ref[t]] += product[:, :TILE] + product[:, TILE:]

    copies = []
    for index in range(BUFFERS):
        copy = pltpu.make_async_copy(
            total.at[pl.ds(index * PER, PER)], buffers[index], out_sems.at[index]
        )
        copy.start()
        copies.append(copy)
    for copy in copies:
        copy.wait()


def smem():
    return pl.BlockSpec(memory_space=pltpu.SMEM)


def vmem():
    return pl.BlockSpec(memory_space=pltpu.VMEM)


def anywhere():
    return pl.BlockSpec(memory_space=pl.ANY)


def forward_part(count, rows, slots, tiles, buffers, nrow):
    return pl.pallas_call(
        forward_kernel,
        name="forward_tiles",
        out_shape=jax.ShapeDtypeStruct((nrow, TILE, TILE), jnp.float32),
        in_specs=[smem(), smem(), smem(), anywhere()] + [anywhere()] * BUFFERS,
        out_specs=vmem(),
        scratch_shapes=[
            pltpu.VMEM((SLOTS, TILE, TILE), jnp.float32),
            pltpu.VMEM((BUFFERS * PER, TILE, TILE), jnp.float32),
            pltpu.VMEM((BUFFERS * PER, TILE, 2 * TILE), jnp.bfloat16),
            pltpu.SemaphoreType.DMA((SLOTS // CHUNK,)),
            pltpu.SemaphoreType.DMA((BUFFERS,)),
        ],
        compiler_params=pltpu.CompilerParams(vmem_limit_bytes=VMEM_BYTES),
    )(count, rows, slots, tiles, *buffers)


def backward_part(count, rows, slots, tiles, slope):
    return pl.pallas_call(
        backward_kernel,
        name="backward_tiles",
        out_shape=[jax.ShapeDtypeStruct((PER, TILE, TILE), jnp.float32)] * BUFFERS,
        in_specs=[smem(), smem(), smem(), anywhere(), vmem()],
        out_specs=[anywhere()] * BUFFERS,
        scratch_shapes=[
            pltpu.VMEM((SLOTS, TILE, TILE), jnp.float32),
            pltpu.VMEM((BUFFERS * PER, TILE, TILE), jnp.float32),
            pltpu.VMEM((slope.shape[1] // TILE, TILE, 2 * TILE), jnp.bfloat16),
            pltpu.SemaphoreType.DMA((SLOTS // CHUNK,)),
            pltpu.SemaphoreType.DMA((BUFFERS,)),
        ],
        compiler_params=pltpu.CompilerParams(vmem_limit_bytes=VMEM_BYTES),
    )(count, rows, slots, tiles, slope)


def relative_slots(cols, wide):
    node_block = cols // 4
    part = cols % 4
    across = (node_block // 16) ^ (wide // 16)
    dx = (node_block // 4 - wide // 4) % 4
    dz = (node_block - wide) % 4
    first = (across * 4 + dz) * PER + dx * 2 + part
    second = (8 + across * 4 + dx) * PER + dz * 2 + part - 2
    return jnp.where(part < 2, first, second)


def gather_features(features, loop):
    feats, shard_nodes = features.shape
    split = features.reshape(feats, 4, 4, TILE)

    def quarter(index):
        piece = lax.dynamic_index_in_dim(split, index, 1, keepdims=False)
        return jnp.transpose(piece, (1, 2, 0))

    partner = permute(quarter(loop ^ 2), y_partner)
    own = quarter(loop)
    buffers = []
    halves = []
    for piece, gather in ((own, ring_gather_near), (partner, ring_gather_far)):
        row = gather(piece[:2], x_up, x_down)
        column = gather(piece[2:], z_up, z_down)
        halves.append((row, column, gather))
    for which in range(2):
        for row, column, gather in halves:
            if which == 0:
                buffers += gather(jnp.concatenate(row, axis=0), z_up, z_down)
            else:
                buffers += gather(jnp.concatenate(column, axis=0), x_up, x_down)
    return buffers


def scatter_terms(buffers):
    sums = []
    for across, reduce in ((0, ring_reduce_near), (1, ring_reduce_far)):
        row = reduce(buffers[across * 4 : across * 4 + 4], z_up, z_down)
        column = reduce(buffers[8 + across * 4 : 12 + across * 4], x_up, x_down)
        first = reduce([row[2 * i : 2 * i + 2] for i in range(4)], x_up, x_down)
        second = reduce([column[2 * i : 2 * i + 2] for i in range(4)], z_up, z_down)
        sums.append(jnp.concatenate([first, second], axis=0))
    return sums[0] + permute(sums[1], y_far)


def sum_over_loop(partial, loop):
    core = loop % 2
    half = partial.shape[0] // 2
    kept = lax.dynamic_slice_in_dim(partial, core * half, half, 0)
    given = lax.dynamic_slice_in_dim(partial, (1 - core) * half, half, 0)
    kept = kept + permute(given, core_swap)
    kept = kept + permute(kept, y_pair)
    other = permute(kept, core_swap)
    return jnp.where(
        core == 0,
        jnp.concatenate([kept, other], axis=0),
        jnp.concatenate([other, kept], axis=0),
    )


def sum_over_wide(value):
    for axis in ("x", "z"):
        for step in (1, 2):
            value = value + permute(value, lambda y, c, x, z: flip(y, c, x, z, axis, step))
    return value + permute(value, y_far)


def gather_loop(own, loop):
    low, core = loop // 2, loop % 2
    across = permute(own, y_pair)
    own_other = permute(own, core_swap)
    across_other = permute(across, core_swap)
    same = jnp.where(
        core == 0, jnp.stack([own, own_other]), jnp.stack([own_other, own])
    )
    far = jnp.where(
        core == 0, jnp.stack([across, across_other]), jnp.stack([across_other, across])
    )
    whole = jnp.where(low == 0, jnp.stack([same, far]), jnp.stack([far, same]))
    feats = own.shape[1]
    return jnp.transpose(whole.reshape(-1, feats, TILE), (1, 0, 2)).reshape(feats, -1)


def per_device(features, weight, cotangent, tiles, tile_rows, tile_cols, counts):
    feats, shard_nodes = features.shape
    loop = lax.axis_index("loop")
    wide = lax.axis_index("wide")
    nrow = shard_nodes // TILE
    tile_collection = tiles.reshape(SLOTS, TILE, TILE)
    rows = tile_rows.reshape(SLOTS)
    slots = relative_slots(tile_cols.reshape(SLOTS), wide)
    count = counts.reshape(1)

    buffers = gather_features(features, loop)
    partial = forward_part(count, rows, slots, tile_collection, buffers, nrow)
    gathered = sum_over_loop(partial, loop).reshape(shard_nodes, feats)
    aggregated = lax.dot_general(
        weight, gathered, (((0,), (1,)), ((), ())), precision=HI, preferred_element_type=jnp.float32
    )
    activated, pull = jax.vjp(jax.nn.gelu, aggregated)
    slope = pull(cotangent)[0]
    weight_term = lax.dot_general(
        gathered, slope, (((0,), (1,)), ((), ())), precision=HI, preferred_element_type=jnp.float32
    )
    weight_grad = sum_over_wide(weight_term)
    spread = jnp.dot(weight, slope, precision=HI, preferred_element_type=jnp.float32)
    terms = backward_part(count, rows, slots, tile_collection, spread)
    input_cols = scatter_terms(terms)
    input_grad = gather_loop(input_cols, loop)
    return (activated, input_grad, weight_grad)


def solution(mesh):
    return jax.shard_map(
        per_device,
        mesh=mesh,
        in_specs=(
            P(None, "wide"),
            P(),
            P(None, "wide"),
            P("loop", "wide", None, None, None),
            P("loop", "wide", None),
            P("loop", "wide", None),
            P("loop", "wide"),
        ),
        out_specs=(P(None, "wide"), P(None, "wide"), P()),
        check_vma=False,
    )
```

time: 750 us -> 251 us (0.33)
  waiting for transfers between devices: 502 us -> 106 us
  matrix products: 142 us -> 5.42 us
  starting transfers between devices: 0.2 us -> 97.9 us
  local copies, waits for them, and re-layouts: 78.1 us -> 5.55 us
  Pallas kernels: 0 us -> 20.8 us
  between operations: 14.5 us -> 1.93 us
    reduce_scatter x1 -> x0, waiting for transfers between devices: 204 us -> none  [per_device(): lax.psum_scatter(own_back.reshape(feats, -1), 'wide', scatter_dimension=1...]
    psum x2 -> x0, waiting for transfers between devices: 179 us -> none  [the longest x1 140 us: per_device(): weight_grad = lax.psum(weight_term, ('loop', 'wide'))]
    dot_general x19 -> x3, matrix products: 142 us -> 5.42 us  [the longest x1 2.05 us: per_device(): jnp.dot(weight, slope, precision=HI, preferred_element_type=jnp.float32)]
    all_gather x2 -> x0, waiting for transfers between devices: 120 us -> none  [the longest x1 106 us: per_device(): own_group = lax.all_gather(own_cols, 'wide', axis=1, tiled=True)]
    ppermute x0 -> x61, waiting for transfers between devices: none -> 106 us  [permute(): return lax.ppermute(value, AXES, pairs)]
    ppermute x0 -> x61, starting transfers between devices: none -> 97.9 us  [permute(): return lax.ppermute(value, AXES, pairs)]
    gather x8 -> x0, local copies, waits for them, and re-layouts: 35.7 us -> none  [the longest x4 24.6 us: forward_step(): taken = jnp.take(group3, block_cols, axis=1)]
    while x18 -> x0, local copies, waits for them, and re-layouts: 30.1 us -> none
  transfers between devices with their start and end apart: 5 -> 61, of which waited for: 5 -> 26; matrix products, arithmetic and copies ran while one was open for 1% -> 6% of each run, Pallas kernels for 0% -> 0%
where the time goes in v1:
time: 251 us; the launch traced here: 250 us
  waiting for transfers between devices  106 us (42%)
  starting transfers between devices  97.9 us (39%)
  Pallas kernels  20.8 us (8%)
  other arithmetic  12.6 us (5%)
  local copies, waits for them, and re-layouts  5.55 us (2%)
  matrix products  5.42 us (2%)
    ppermute x61, waiting for transfers between devices, permute(): return lax.ppermute(value, AXES, pairs)  106 us
    ppermute x61, starting transfers between devices, permute(): return lax.ppermute(value, AXES, pairs)  97.9 us
    pallas_call x1, Pallas kernels, forward_part(): pl.pallas_call(forward_kernel, name='forward_tiles', out_shape=jax.ShapeD...  10.5 us
    pallas_call x1, Pallas kernels, backward_part(): pl.pallas_call(backward_kernel, name='backward_tiles', out_shape=[jax.Sha...  10.3 us
  transfers between devices with their start and end apart: 61, of which 26 were waited for; matrix products, arithmetic and copies ran while one was open for 6% of the time, Pallas kernels for 0%

profile of v1, /device:TPU:0, one launch (start us, length us, event | category | flops | bytes accessed | tf_op | source)
XLA Modules:
  0.0 249.7 jit_solution(7379327600985525585)
XLA Ops:
  8.2 4.0 %collective-permute-start.13 = (f32[2,128,128]{2,1,0:T(8,128)S(1)}, f32[2,128,128]{2,1,0:T(8,128)S(1)}, u32[]{:S(2)}, u32[]{:S(2)}) collective-permute-start(f32[2,128,128]{2,1,0:T(8,128)S(1)} %get-tuple-element.52), channel_id=1, source_target_pairs={{0,3},{1,0},{2,1},{3,2},{4,7},{5,4},{6,5},{7,6},{8,11},{9,8},{10,9... | collective-permute-start | bytes 393224 | tf_op jit(solution)/shard_map/ppermute | solution.py:31
  12.3 3.2 %collective-permute-start.1 = (f32[2,128,128]{2,1,0:T(8,128)S(1)}, f32[2,128,128]{2,1,0:T(8,128)S(1)}, u32[]{:S(2)}, u32[]{:S(2)}) collective-permute-start(f32[2,128,128]{2,1,0:T(8,128)S(1)} %collective-permute-done), channel_id=1, source_target_pairs={{0,12},{1,13},{2,14},{3,15},{4,0},{5,1},{6,2},{7,3},{8,4},{9,5},{1... | collective-permute-start | bytes 393224 | tf_op jit(solution)/shard_map/ppermute | solution.py:31
  28.4 7.3 %collective-permute-done.20 = f32[2,128,128]{2,1,0:T(8,128)S(1)} collective-permute-done((f32[2,128,128]{2,1,0:T(8,128)S(1)}, f32[2,128,128]{2,1,0:T(8,128)S(1)}, u32[]{:S(2)}, u32[]{:S(2)}) %collective-permute-start.20) | collective-permute-done | bytes 131104 | tf_op jit(solution)/shard_map/ppermute | solution.py:31
  46.1 7.9 %collective-permute-done.18.rest_11_ = f32[8,128,128]{2,1,0:T(8,128)S(1)} collective-permute-done((f32[8,128,128]{2,1,0:T(8,128)S(1)}, f32[8,128,128]{2,1,0:T(8,128)S(1)}, u32[]{:S(2)}, u32[]{:S(2)}) %collective-permute-start.18) | collective-permute-done | bytes 524320 | tf_op jit(solution)/shard_map/ppermute | solution.py:31
  58.0 3.8 %collective-permute-done.23.rest_15_ = f32[8,128,128]{2,1,0:T(8,128)} collective-permute-done((f32[8,128,128]{2,1,0:T(8,128)S(1)}, f32[8,128,128]{2,1,0:T(8,128)}, u32[]{:S(2)}, u32[]{:S(2)}) %collective-permute-start.23) | collective-permute-done | bytes 524320 | tf_op jit(solution)/shard_map/ppermute | solution.py:31
  63.9 4.6 %collective-permute-done.22.rest_13_ = f32[8,128,128]{2,1,0:T(8,128)} collective-permute-done((f32[8,128,128]{2,1,0:T(8,128)S(1)}, f32[8,128,128]{2,1,0:T(8,128)}, u32[]{:S(2)}, u32[]{:S(2)}) %collective-permute-start.22) | collective-permute-done | bytes 524320 | tf_op jit(solution)/shard_map/ppermute | solution.py:31
  68.4 5.6 %collective-permute-done.17.rest_10_ = f32[8,128,128]{2,1,0:T(8,128)} collective-permute-done((f32[8,128,128]{2,1,0:T(8,128)}, f32[8,128,128]{2,1,0:T(8,128)}, u32[]{:S(2)}, u32[]{:S(2)}) %collective-permute-start.17) | collective-permute-done | bytes 524320 | tf_op jit(solution)/shard_map/ppermute | solution.py:31
  74.1 10.5 %forward_tiles.1 = f32[16,128,128]{2,1,0:T(8,128)} custom-call(s32[1]{0:T(128)} %bitcast.35.count_ref, s32[256]{0:T(256)} %bitcast.48, s32[256]{0:T(256)} %compare_select_fusion.4.slots_ref, f32[256,128,128]{2,1,0:T(8,128)} %bitcast.37, f32[8,128,128]{2,1,0:T(8,128)} %copy-done.1, f32[8,128,128]{2,1,0:T(8,128)} %collective-permute-done.3.rest_1_, ...), custom_call_target="tpu_custom_call" | custom-call | tf_op jit(solution)/shard_map/forward_tiles/pallas_call | solution.py:214
  89.3 14.2 %collective-permute-done.26 = f32[8,128,128]{2,1,0:T(8,128)S(1)} collective-permute-done((f32[8,128,128]{2,1,0:T(8,128)S(1)}, f32[8,128,128]{2,1,0:T(8,128)S(1)}, u32[]{:S(2)}, u32[]{:S(2)}) %collective-permute-start.26) | collective-permute-done | bytes 524320 | tf_op jit(solution)/shard_map/ppermute | solution.py:31
  109.2 10.3 %backward_tiles.1 = (f32[8,128,128]{2,1,0:T(8,128)}, f32[8,128,128]{2,1,0:T(8,128)}, f32[8,128,128]{2,1,0:T(8,128)}, f32[8,128,128]{2,1,0:T(8,128)}, f32[8,128,1...) custom-call(s32[1]{0:T(128)} %bitcast.36.count_ref, ...), custom_call_target="tpu_custom_call" | custom-call | tf_op jit(solution)/shard_map/backward_tiles/pallas_call | solution.py:232
  119.5 10.6 %collective-permute-start.28 = (f32[8,128,128]{2,1,0:T(8,128)}, f32[8,128,128]{2,1,0:T(8,128)S(1)}, u32[]{:S(2)}, u32[]{:S(2)}) collective-permute-start(f32[8,128,128]{2,1,0:T(8,128)} %get-tuple-element.21), channel_id=1, source_target_pairs={{0,1},{1,2},{2,3},{3,0},{4,5},{5,6},{6,7},{7,4},{8,9},{9,10},{10,1... | collective-permute-start | bytes 1572872 | tf_op jit(solution)/shard_map/ppermute | solution.py:31
  130.1 17.2 %collective-permute-start.41 = (f32[8,128,128]{2,1,0:T(8,128)}, f32[8,128,128]{2,1,0:T(8,128)S(1)}, u32[]{:S(2)}, u32[]{:S(2)}) collective-permute-start(f32[8,128,128]{2,1,0:T(8,128)} %get-tuple-element.30), channel_id=1, source_target_pairs={{0,3},{1,0},{2,1},{3,2},{4,7},{5,4},{6,5},{7,6},{8,11},{9,8},{10,9... | collective-permute-start | bytes 1572872 | tf_op jit(solution)/shard_map/ppermute | solution.py:31
  147.3 3.6 %collective-permute-start.47 = (f32[8,128,128]{2,1,0:T(8,128)}, f32[8,128,128]{2,1,0:T(8,128)S(1)}, u32[]{:S(2)}, u32[]{:S(2)}) collective-permute-start(f32[8,128,128]{2,1,0:T(8,128)} %get-tuple-element.34), channel_id=1, source_target_pairs={{0,12},{1,13},{2,14},{3,15},{4,0},{5,1},{6,2},{7,3},{8,4},{9,5},{1... | collective-permute-start | bytes 1572872 | tf_op jit(solution)/shard_map/ppermute | solution.py:31
  152.4 7.2 %collective-permute-done.28 = f32[8,128,128]{2,1,0:T(8,128)S(1)} collective-permute-done((f32[8,128,128]{2,1,0:T(8,128)}, f32[8,128,128]{2,1,0:T(8,128)S(1)}, u32[]{:S(2)}, u32[]{:S(2)}) %collective-permute-start.28) | collective-permute-done | bytes 524320 | tf_op jit(solution)/shard_map/ppermute | solution.py:31
  167.0 3.3 %collective-permute-done.30 = f32[8,128,128]{2,1,0:T(8,128)S(1)} collective-permute-done((f32[8,128,128]{2,1,0:T(8,128)}, f32[8,128,128]{2,1,0:T(8,128)S(1)}, u32[]{:S(2)}, u32[]{:S(2)}) %collective-permute-start.30) | collective-permute-done | bytes 524320 | tf_op jit(solution)/shard_map/ppermute | solution.py:31
  171.3 5.5 %collective-permute-done.29 = f32[8,128,128]{2,1,0:T(8,128)S(1)} collective-permute-done((f32[8,128,128]{2,1,0:T(8,128)S(1)}, f32[8,128,128]{2,1,0:T(8,128)S(1)}, u32[]{:S(2)}, u32[]{:S(2)}) %collective-permute-start.29) | collective-permute-done | bytes 524320 | tf_op jit(solution)/shard_map/ppermute | solution.py:31
  181.7 4.9 %collective-permute-done.40 = f32[8,128,128]{2,1,0:T(8,128)S(1)} collective-permute-done((f32[8,128,128]{2,1,0:T(8,128)}, f32[8,128,128]{2,1,0:T(8,128)S(1)}, u32[]{:S(2)}, u32[]{:S(2)}) %collective-permute-start.40) | collective-permute-done | bytes 524320 | tf_op jit(solution)/shard_map/ppermute | solution.py:31
  197.0 3.3 %collective-permute-start.33 = (f32[2,128,128]{2,1,0:T(8,128)S(1)}, f32[2,128,128]{2,1,0:T(8,128)S(1)}, u32[]{:S(2)}, u32[]{:S(2)}) collective-permute-start(f32[2,128,128]{2,1,0:T(8,128)S(1)} %get-tuple-element.43), channel_id=1, source_target_pairs={{0,12},{1,13},{2,14},{3,15},{4,0},{5,1},{6,2},{7,3},{8,4},{9,5},{1... | collective-permute-start | bytes 393224 | tf_op jit(solution)/shard_map/ppermute | solution.py:31
  200.5 4.8 %collective-permute-done.45 = f32[2,128,128]{2,1,0:T(8,128)S(1)} collective-permute-done((f32[2,128,128]{2,1,0:T(8,128)S(1)}, f32[2,128,128]{2,1,0:T(8,128)S(1)}, u32[]{:S(2)}, u32[]{:S(2)}) %collective-permute-start.45) | collective-permute-done | bytes 131104 | tf_op jit(solution)/shard_map/ppermute | solution.py:31
  213.1 6.5 %collective-permute-done.52 = f32[4,128,128]{2,1,0:T(8,128)S(1)} collective-permute-done((f32[4,128,128]{2,1,0:T(8,128)S(1)}, f32[4,128,128]{2,1,0:T(8,128)S(1)}, u32[]{:S(2)}, u32[]{:S(2)}) %collective-permute-start.52) | collective-permute-done | bytes 262176 | tf_op jit(solution)/shard_map/ppermute | solution.py:31
  221.9 4.0 %collective-permute-done.56 = f32[128,128]{1,0:T(8,128)S(1)} collective-permute-done((f32[128,128]{1,0:T(8,128)S(1)}, f32[128,128]{1,0:T(8,128)S(1)}, u32[]{:S(2)}, u32[]{:S(2)}) %collective-permute-start.56) | collective-permute-done | bytes 65568 | tf_op jit(solution)/shard_map/ppermute | solution.py:31
  227.8 4.0 %collective-permute-done.57 = f32[128,128]{1,0:T(8,128)S(1)} collective-permute-done((f32[128,128]{1,0:T(8,128)S(1)}, f32[128,128]{1,0:T(8,128)S(1)}, u32[]{:S(2)}, u32[]{:S(2)}) %collective-permute-start.57) | collective-permute-done | bytes 65568 | tf_op jit(solution)/shard_map/ppermute | solution.py:31
  232.0 4.1 %collective-permute-done.58 = f32[128,128]{1,0:T(8,128)S(1)} collective-permute-done((f32[128,128]{1,0:T(8,128)S(1)}, f32[128,128]{1,0:T(8,128)S(1)}, u32[]{:S(2)}, u32[]{:S(2)}) %collective-permute-start.58) | collective-permute-done | bytes 65568 | tf_op jit(solution)/shard_map/ppermute | solution.py:31
  236.1 3.4 %collective-permute-start.59 = (f32[128,128]{1,0:T(8,128)S(1)}, f32[128,128]{1,0:T(8,128)S(1)}, u32[]{:S(2)}, u32[]{:S(2)}) collective-permute-start(f32[128,128]{1,0:T(8,128)S(1)} %add.209), channel_id=1, source_target_pairs={{0,2},{1,3},{2,0},{3,1},{4,6},{5,7},{6,4},{7,5},{8,10},{9,11},{10,... | collective-permute-start | bytes 196616 | tf_op jit(solution)/shard_map/ppermute | solution.py:31
  (167 shorter events, 94.1 us)
Async XLA Ops:
  5.2 16.9 %collective-permute-start.6 = (f32[4,128,128]{2,1,0:T(8,128)S(1)}, f32[4,128,128]{2,1,0:T(8,128)S(1)}, u32[]{:S(2)}, u32[]{:S(2)}) collective-permute-start(f32[4,128,128]{2,1,0:T(8,128)S(1)} %get-tuple-element.40), channel_id=1, source_target_pairs={{0,80},{1,81},{2,82},{3,83},{4,84},{5,85},{6,86},{7,87},{8,88},{9,... | collective-permute-start | bytes 786440 | tf_op jit(solution)/shard_map/ppermute | solution.py:31
  18.8 24.5 %collective-permute-start.5 = (f32[8,128,128]{2,1,0:T(8,128)S(1)}, f32[8,128,128]{2,1,0:T(8,128)S(1)}, u32[]{:S(2)}, u32[]{:S(2)}) collective-permute-start(f32[8,128,128]{2,1,0:T(8,128)S(1)} %pad_maximum_fusion.rest_0_), channel_id=1, source_target_pairs={{0,1},{1,2},{2,3},{3,0},{4,5},{5,6},{6,7},{7,4},{8,9},{9,10},{10,1... | collective-permute-start | bytes 1572872 | tf_op jit(solution)/shard_map/ppermute | solution.py:31
  18.9 27.0 %collective-permute-start.3 = (f32[8,128,128]{2,1,0:T(8,128)S(1)}, f32[8,128,128]{2,1,0:T(8,128)}, u32[]{:S(2)}, u32[]{:S(2)}) collective-permute-start(f32[8,128,128]{2,1,0:T(8,128)S(1)} %pad_maximum_fusion.rest_0_), channel_id=1, source_target_pairs={{0,3},{1,0},{2,1},{3,2},{4,7},{5,4},{6,5},{7,6},{8,11},{9,8},{10,9... | collective-permute-start | bytes 1572872 | tf_op jit(solution)/shard_map/ppermute | solution.py:31
  37.8 16.1 %collective-permute-start.18 = (f32[8,128,128]{2,1,0:T(8,128)S(1)}, f32[8,128,128]{2,1,0:T(8,128)S(1)}, u32[]{:S(2)}, u32[]{:S(2)}) collective-permute-start(f32[8,128,128]{2,1,0:T(8,128)S(1)} %pad_maximum_fusion.2.rest_8_), channel_id=1, source_target_pairs={{0,4},{1,5},{2,6},{3,7},{4,8},{5,9},{6,10},{7,11},{8,12},{9,13},{1... | collective-permute-start | bytes 1572872 | tf_op jit(solution)/shard_map/ppermute | solution.py:31
  45.9 15.9 %collective-permute-start.23 = (f32[8,128,128]{2,1,0:T(8,128)S(1)}, f32[8,128,128]{2,1,0:T(8,128)}, u32[]{:S(2)}, u32[]{:S(2)}) collective-permute-start(f32[8,128,128]{2,1,0:T(8,128)S(1)} %pad_maximum_fusion.3.rest_12_), channel_id=1, source_target_pairs={{0,4},{1,5},{2,6},{3,7},{4,8},{5,9},{6,10},{7,11},{8,12},{9,13},{1... | collective-permute-start | bytes 1572872 | tf_op jit(solution)/shard_map/ppermute | solution.py:31
  54.0 14.5 %collective-permute-start.22 = (f32[8,128,128]{2,1,0:T(8,128)S(1)}, f32[8,128,128]{2,1,0:T(8,128)}, u32[]{:S(2)}, u32[]{:S(2)}) collective-permute-start(f32[8,128,128]{2,1,0:T(8,128)S(1)} %pad_maximum_fusion.3.rest_12_), channel_id=1, source_target_pairs={{0,12},{1,13},{2,14},{3,15},{4,0},{5,1},{6,2},{7,3},{8,4},{9,5},{1... | collective-permute-start | bytes 1572872 | tf_op jit(solution)/shard_map/ppermute | solution.py:31
  55.5 18.6 %collective-permute-start.17 = (f32[8,128,128]{2,1,0:T(8,128)}, f32[8,128,128]{2,1,0:T(8,128)}, u32[]{:S(2)}, u32[]{:S(2)}) collective-permute-start(f32[8,128,128]{2,1,0:T(8,128)} %collective-permute-done.16.rest_9_), channel_id=1, source_target_pairs={{0,12},{1,13},{2,14},{3,15},{4,0},{5,1},{6,2},{7,3},{8,4},{9,5},{1... | collective-permute-start | bytes 1572872 | tf_op jit(solution)/shard_map/ppermute | solution.py:31
  57.2 16.8 %collective-permute-start.12 = (f32[8,128,128]{2,1,0:T(8,128)}, f32[8,128,128]{2,1,0:T(8,128)}, u32[]{:S(2)}, u32[]{:S(2)}) collective-permute-start(f32[8,128,128]{2,1,0:T(8,128)} %collective-permute-done.11.rest_7_), channel_id=1, source_target_pairs={{0,1},{1,2},{2,3},{3,0},{4,5},{5,6},{6,7},{7,4},{8,9},{9,10},{10,1... | collective-permute-start | bytes 1572872 | tf_op jit(solution)/shard_map/ppermute | solution.py:31
  119.5 40.1 %collective-permute-start.28 = (f32[8,128,128]{2,1,0:T(8,128)}, f32[8,128,128]{2,1,0:T(8,128)S(1)}, u32[]{:S(2)}, u32[]{:S(2)}) collective-permute-start(f32[8,128,128]{2,1,0:T(8,128)} %get-tuple-element.21), channel_id=1, source_target_pairs={{0,1},{1,2},{2,3},{3,0},{4,5},{5,6},{6,7},{7,4},{8,9},{9,10},{10,1... | collective-permute-start | bytes 1572872 | tf_op jit(solution)/shard_map/ppermute | solution.py:31
  130.0 30.7 %collective-permute-start.34 = (f32[8,128,128]{2,1,0:T(8,128)}, f32[8,128,128]{2,1,0:T(8,128)S(1)}, u32[]{:S(2)}, u32[]{:S(2)}) collective-permute-start(f32[8,128,128]{2,1,0:T(8,128)} %get-tuple-element.25), channel_id=1, source_target_pairs={{0,4},{1,5},{2,6},{3,7},{4,8},{5,9},{6,10},{7,11},{8,12},{9,13},{1... | collective-permute-start | bytes 1572872 | tf_op jit(solution)/shard_map/ppermute | solution.py:31
  130.1 32.4 %collective-permute-start.41 = (f32[8,128,128]{2,1,0:T(8,128)}, f32[8,128,128]{2,1,0:T(8,128)S(1)}, u32[]{:S(2)}, u32[]{:S(2)}) collective-permute-start(f32[8,128,128]{2,1,0:T(8,128)} %get-tuple-element.30), channel_id=1, source_target_pairs={{0,3},{1,0},{2,1},{3,2},{4,7},{5,4},{6,5},{7,6},{8,11},{9,8},{10,9... | collective-permute-start | bytes 1572872 | tf_op jit(solution)/shard_map/ppermute | solution.py:31
  147.3 17.8 %collective-permute-start.47 = (f32[8,128,128]{2,1,0:T(8,128)}, f32[8,128,128]{2,1,0:T(8,128)S(1)}, u32[]{:S(2)}, u32[]{:S(2)}) collective-permute-start(f32[8,128,128]{2,1,0:T(8,128)} %get-tuple-element.34), channel_id=1, source_target_pairs={{0,12},{1,13},{2,14},{3,15},{4,0},{5,1},{6,2},{7,3},{8,4},{9,5},{1... | collective-permute-start | bytes 1572872 | tf_op jit(solution)/shard_map/ppermute | solution.py:31
  150.9 19.4 %collective-permute-start.30 = (f32[8,128,128]{2,1,0:T(8,128)}, f32[8,128,128]{2,1,0:T(8,128)S(1)}, u32[]{:S(2)}, u32[]{:S(2)}) collective-permute-start(f32[8,128,128]{2,1,0:T(8,128)} %get-tuple-element.22), channel_id=1, source_target_pairs={{0,3},{1,0},{2,1},{3,2},{4,7},{5,4},{6,5},{7,6},{8,11},{9,8},{10,9... | collective-permute-start | bytes 1572872 | tf_op jit(solution)/shard_map/ppermute | solution.py:31
  160.7 16.1 %collective-permute-start.29 = (f32[8,128,128]{2,1,0:T(8,128)S(1)}, f32[8,128,128]{2,1,0:T(8,128)S(1)}, u32[]{:S(2)}, u32[]{:S(2)}) collective-permute-start(f32[8,128,128]{2,1,0:T(8,128)S(1)} %add.182), channel_id=1, source_target_pairs={{0,1},{1,2},{2,3},{3,0},{4,5},{5,6},{6,7},{7,4},{8,9},{9,10},{10,1... | collective-permute-start | bytes 1572872 | tf_op jit(solution)/shard_map/ppermute | solution.py:31
  160.7 17.7 %collective-permute-start.36 = (f32[8,128,128]{2,1,0:T(8,128)}, f32[8,128,128]{2,1,0:T(8,128)S(1)}, u32[]{:S(2)}, u32[]{:S(2)}) collective-permute-start(f32[8,128,128]{2,1,0:T(8,128)} %get-tuple-element.26), channel_id=1, source_target_pairs={{0,12},{1,13},{2,14},{3,15},{4,0},{5,1},{6,2},{7,3},{8,4},{9,5},{1... | collective-permute-start | bytes 1572872 | tf_op jit(solution)/shard_map/ppermute | solution.py:31
  162.5 16.1 %collective-permute-start.35 = (f32[8,128,128]{2,1,0:T(8,128)S(1)}, f32[8,128,128]{2,1,0:T(8,128)S(1)}, u32[]{:S(2)}, u32[]{:S(2)}) collective-permute-start(f32[8,128,128]{2,1,0:T(8,128)S(1)} %add.188), channel_id=1, source_target_pairs={{0,4},{1,5},{2,6},{3,7},{4,8},{5,9},{6,10},{7,11},{8,12},{9,13},{1... | collective-permute-start | bytes 1572872 | tf_op jit(solution)/shard_map/ppermute | solution.py:31
  165.1 21.5 %collective-permute-start.40 = (f32[8,128,128]{2,1,0:T(8,128)}, f32[8,128,128]{2,1,0:T(8,128)S(1)}, u32[]{:S(2)}, u32[]{:S(2)}) collective-permute-start(f32[8,128,128]{2,1,0:T(8,128)} %get-tuple-element.28), channel_id=1, source_target_pairs={{0,1},{1,2},{2,3},{3,0},{4,5},{5,6},{6,7},{7,4},{8,9},{9,10},{10,1... | collective-permute-start | bytes 1572872 | tf_op jit(solution)/shard_map/ppermute | solution.py:31
  170.3 19.0 %collective-permute-start.46 = (f32[8,128,128]{2,1,0:T(8,128)}, f32[8,128,128]{2,1,0:T(8,128)S(1)}, u32[]{:S(2)}, u32[]{:S(2)}) collective-permute-start(f32[8,128,128]{2,1,0:T(8,128)} %get-tuple-element.32), channel_id=1, source_target_pairs={{0,4},{1,5},{2,6},{3,7},{4,8},{5,9},{6,10},{7,11},{8,12},{9,13},{1... | collective-permute-start | bytes 1572872 | tf_op jit(solution)/shard_map/ppermute | solution.py:31
  178.6 15.0 %collective-permute-start.31 = (f32[2,128,128]{2,1,0:T(8,128)S(1)}, f32[2,128,128]{2,1,0:T(8,128)S(1)}, u32[]{:S(2)}, u32[]{:S(2)}) collective-permute-start(f32[2,128,128]{2,1,0:T(8,128)S(1)} %slice.86), channel_id=1, source_target_pairs={{0,4},{1,5},{2,6},{3,7},{4,8},{5,9},{6,10},{7,11},{8,12},{9,13},{1... | collective-permute-start | bytes 393224 | tf_op jit(solution)/shard_map/ppermute | solution.py:31
  193.6 14.5 %collective-permute-start.49 = (f32[2,128,128]{2,1,0:T(8,128)S(1)}, f32[2,128,128]{2,1,0:T(8,128)S(1)}, u32[]{:S(2)}, u32[]{:S(2)}) collective-permute-start(f32[2,128,128]{2,1,0:T(8,128)S(1)} %get-tuple-element.48), channel_id=1, source_target_pairs={{0,1},{1,2},{2,3},{3,0},{4,5},{5,6},{6,7},{7,4},{8,9},{9,10},{10,1... | collective-permute-start | bytes 393224 | tf_op jit(solution)/shard_map/ppermute | solution.py:31
  196.9 15.5 %collective-permute-start.32 = (f32[2,128,128]{2,1,0:T(8,128)S(1)}, f32[2,128,128]{2,1,0:T(8,128)S(1)}, u32[]{:S(2)}, u32[]{:S(2)}) collective-permute-start(f32[2,128,128]{2,1,0:T(8,128)S(1)} %get-tuple-element.42), channel_id=1, source_target_pairs={{0,4},{1,5},{2,6},{3,7},{4,8},{5,9},{6,10},{7,11},{8,12},{9,13},{1... | collective-permute-start | bytes 393224 | tf_op jit(solution)/shard_map/ppermute | solution.py:31
  197.0 15.4 %collective-permute-start.33 = (f32[2,128,128]{2,1,0:T(8,128)S(1)}, f32[2,128,128]{2,1,0:T(8,128)S(1)}, u32[]{:S(2)}, u32[]{:S(2)}) collective-permute-start(f32[2,128,128]{2,1,0:T(8,128)S(1)} %get-tuple-element.43), channel_id=1, source_target_pairs={{0,12},{1,13},{2,14},{3,15},{4,0},{5,1},{6,2},{7,3},{8,4},{9,5},{1... | collective-permute-start | bytes 393224 | tf_op jit(solution)/shard_map/ppermute | solution.py:31
  227.7 20.7 %collective-permute-start.53 = (f32[4,128,128]{2,1,0:T(8,128)S(1)}, f32[4,128,128]{2,1,0:T(8,128)S(1)}, u32[]{:S(2)}, u32[]{:S(2)}) collective-permute-start(f32[4,128,128]{2,1,0:T(8,128)S(1)} %maximum_add_fusion), channel_id=1, source_target_pairs={{0,32},{1,33},{2,34},{3,35},{4,36},{5,37},{6,38},{7,39},{8,40},{9,... | collective-permute-start | bytes 786440 | tf_op jit(solution)/shard_map/ppermute | solution.py:31
  232.0 16.5 %collective-permute-start.55 = (f32[4,128,128]{2,1,0:T(8,128)S(1)}, f32[4,128,128]{2,1,0:T(8,128)S(1)}, u32[]{:S(2)}, u32[]{:S(2)}) collective-permute-start(f32[4,128,128]{2,1,0:T(8,128)S(1)} %collective-permute-done.54), channel_id=1, source_target_pairs={{0,32},{1,33},{2,34},{3,35},{4,36},{5,37},{6,38},{7,39},{8,40},{9,... | collective-permute-start | bytes 786440 | tf_op jit(solution)/shard_map/ppermute | solution.py:31
  (46 other events, 694.4 us)

commit v2 on v1

v2 whole, which is shorter than its diff:
```python
import functools

import jax
import jax.numpy as jnp
from jax import lax
from jax.experimental import pallas as pl
from jax.experimental.pallas import tpu as pltpu
from jax.sharding import PartitionSpec as P

HI = lax.Precision.HIGHEST
AXES = ("loop", "wide")
SIDE = 4
TILE = 128
SLOTS = 256
GROUP = 16
PER = 8
CLASS_BUFFERS = (8, 6, 2)
VMEM_BYTES = 28 * 1024 * 1024


def device_index(y, core, x, z):
    y, x, z = y % SIDE, x % SIDE, z % SIDE
    return (((y & 1) * 2 + core) * 2 + (y >> 1)) * 16 + x * SIDE + z


def permute(value, move):
    pairs = []
    for y in range(SIDE):
        for core in range(2):
            for x in range(SIDE):
                for z in range(SIDE):
                    pairs.append((device_index(y, core, x, z), device_index(*move(y, core, x, z))))
    return lax.ppermute(value, AXES, pairs)


def toward(core):
    return 1 - 2 * core


def x_up(y, core, x, z):
    return (y, core, x + toward(core), z)


def x_down(y, core, x, z):
    return (y, core, x - toward(core), z)


def z_up(y, core, x, z):
    return (y, core, x, z + toward(core))


def z_down(y, core, x, z):
    return (y, core, x, z - toward(core))


def y_partner(y, core, x, z):
    return (3 - y, core, x, z)


def y_pair(y, core, x, z):
    return (y ^ 1, core, x, z)


def y_far(y, core, x, z):
    return (y + 2, core, x, z)


def core_swap(y, core, x, z):
    return (y, 1 - core, x, z)


def after(value, *others):
    return lax.optimization_barrier((value,) + others)[0]


def split_high_low(value):
    high = value.astype(jnp.bfloat16)
    low = (value - high.astype(jnp.float32)).astype(jnp.bfloat16)
    return high, low


def start_groups(tiles_ref, order_ref, held, sems, begin, groups):
    @pl.loop(0, groups)
    def _(group):
        for j in range(GROUP):
            spot = group * GROUP + j
            source = order_ref[jnp.minimum(begin + spot, SLOTS - 1)]
            pltpu.make_async_copy(tiles_ref.at[source], held.at[spot], sems.at[group]).start()


def wait_group(tiles_ref, held, sems, group):
    part = pl.ds(group * GROUP, GROUP)
    pltpu.make_async_copy(tiles_ref.at[pl.ds(0, GROUP)], held.at[part], sems.at[group]).wait()


def class_range(bounds_ref, which):
    begin, end = bounds_ref[which], bounds_ref[which + 1]
    return begin, end, (end - begin + GROUP - 1) // GROUP


def forward_kernel(which, bounds_ref, order_ref, rows_ref, slots_ref, tiles_ref, *rest):
    number = CLASS_BUFFERS[which]
    base = sum(CLASS_BUFFERS[:which]) * PER
    buffers = rest[:number]
    rest = rest[number:]
    prior_ref = rest[0] if which else None
    out_ref, held, pairs, total, sems = rest[-5:]
    nrow = out_ref.shape[0]
    begin, end, groups = class_range(bounds_ref, which)
    start_groups(tiles_ref, order_ref, held, sems, begin, groups)
    if which:
        total[0:nrow] = prior_ref[...]
    else:
        total[0:nrow] = jnp.zeros_like(out_ref)
    for index in range(number):

        @pl.loop(0, PER, unroll=4)
        def _(j):
            high, low = split_high_low(buffers[index][j])
            pairs[index * PER + j, :, :TILE] = high
            pairs[index * PER + j, :, TILE:] = low

    @pl.loop(0, groups)
    def _(group):
        wait_group(tiles_ref, held, sems, group)
        for j in range(GROUP):
            spot = group * GROUP + j
            place = jnp.minimum(begin + spot, SLOTS - 1)
            live = begin + spot < end
            row = jnp.where(live, rows_ref[place], nrow)
            slot = jnp.where(live, slots_ref[place] - base, 0)
            high, low = split_high_low(held[spot])
            right = pairs[slot]
            product = jnp.dot(
                jnp.concatenate([high, low], axis=1),
                jnp.concatenate([right, right], axis=0),
                preferred_element_type=jnp.float32,
            )
            total[row] += product[:, :TILE] + product[:, TILE:]

    out_ref[...] = total[0:nrow]


def backward_kernel(which, bounds_ref, order_ref, rows_ref, slots_ref, tiles_ref, slope_ref, *rest):
    number = CLASS_BUFFERS[which]
    base = sum(CLASS_BUFFERS[:which]) * PER
    buffers = rest[:number]
    held, pairs, total, sems, out_sems = rest[number:]
    begin, end, groups = class_range(bounds_ref, which)
    start_groups(tiles_ref, order_ref, held, sems, begin, groups)
    for row in range(pairs.shape[0]):
        high, low = split_high_low(slope_ref[:, row * TILE : (row + 1) * TILE])
        pairs[row, :, :TILE] = high
        pairs[row, :, TILE:] = low

    @pl.loop(0, number * PER, unroll=4)
    def _(slot):
        total[slot] = jnp.zeros((TILE, TILE), jnp.float32)

    @pl.loop(0, groups)
    def _(group):
        wait_group(tiles_ref, held, sems, group)
        for j in range(GROUP):
            spot = group * GROUP + j
            place = jnp.minimum(begin + spot, SLOTS - 1)
            live = begin + spot < end
            slot = jnp.where(live, slots_ref[place] - base, number * PER)
            high, low = split_high_low(held[spot])
            right = jnp.concatenate([high, low], axis=1)
            product = jnp.dot(
                pairs[rows_ref[place]],
                jnp.concatenate([right, right], axis=0),
                preferred_element_type=jnp.float32,
            )
            total[slot] += product[:, :TILE] + product[:, TILE:]

    copies = []
    for index in range(number):
        copy = pltpu.make_async_copy(
            total.at[pl.ds(index * PER, PER)], buffers[index], out_sems.at[index]
        )
        copy.start()
        copies.append(copy)
    for copy in copies:
        copy.wait()


def smem():
    return pl.BlockSpec(memory_space=pltpu.SMEM)


def vmem():
    return pl.BlockSpec(memory_space=pltpu.VMEM)


def anywhere():
    return pl.BlockSpec(memory_space=pl.ANY)


def cost(which):
    live = (96, 72, 24)[which]
    return pl.CostEstimate(
        flops=live * 8 * TILE**3, bytes_accessed=live * 4 * TILE**2, transcendentals=0
    )


def forward_part(which, plan, tiles, buffers, prior, nrow):
    extra = [prior] if which else []
    number = CLASS_BUFFERS[which]
    return pl.pallas_call(
        functools.partial(forward_kernel, which),
        name="forward_tiles_%d" % which,
        out_shape=jax.ShapeDtypeStruct((nrow, TILE, TILE), jnp.float32),
        in_specs=[smem()] * 4 + [anywhere()] + [vmem()] * (number + len(extra)),
        out_specs=vmem(),
        scratch_shapes=[
            pltpu.VMEM((SLOTS, TILE, TILE), jnp.float32),
            pltpu.VMEM((number * PER, TILE, 2 * TILE), jnp.bfloat16),
            pltpu.VMEM((nrow + 1, TILE, TILE), jnp.float32),
            pltpu.SemaphoreType.DMA((SLOTS // GROUP,)),
        ],
        cost_estimate=cost(which),
        compiler_params=pltpu.CompilerParams(vmem_limit_bytes=VMEM_BYTES),
    )(*plan, tiles, *buffers, *extra)


def backward_part(which, plan, tiles, slope):
    number = CLASS_BUFFERS[which]
    return pl.pallas_call(
        functools.partial(backward_kernel, which),
        name="backward_tiles_%d" % which,
        out_shape=[jax.ShapeDtypeStruct((PER, TILE, TILE), jnp.float32)] * number,
        in_specs=[smem()] * 4 + [anywhere(), vmem()],
        out_specs=[anywhere()] * number,
        scratch_shapes=[
            pltpu.VMEM((SLOTS, TILE, TILE), jnp.float32),
            pltpu.VMEM((slope.shape[1] // TILE, TILE, 2 * TILE), jnp.bfloat16),
            pltpu.VMEM((number * PER + 1, TILE, TILE), jnp.float32),
            pltpu.SemaphoreType.DMA((SLOTS // GROUP,)),
            pltpu.SemaphoreType.DMA((number,)),
        ],
        cost_estimate=cost(which),
        compiler_params=pltpu.CompilerParams(vmem_limit_bytes=VMEM_BYTES),
    )(*plan, tiles, slope)


def make_plan(rows, cols, count, loop, wide):
    sign = 1 - 2 * (loop % 2)
    node_block = cols // 4
    part = cols % 4
    across = (node_block // 16) ^ (wide // 16)
    dx = ((node_block // 4 - wide // 4) * sign) % 4
    dz = ((node_block - wide) * sign) % 4
    is_first = part < 2
    ring = jnp.where(is_first, dz, dx)
    inner = jnp.where(is_first, dx * 2 + part, dz * 2 + part - 2)
    near = jnp.where(is_first, 0, 4) + ring
    apart = jnp.where(is_first, 8, 11) + jnp.where(ring == 3, 2, ring)
    apart = jnp.where(ring == 2, jnp.where(is_first, 14, 15), apart)
    buffer = jnp.where(across == 0, near, apart)
    slots = buffer * PER + inner
    spots = jnp.arange(SLOTS, dtype=jnp.int32)
    kind = jnp.where(buffer < 8, 0, jnp.where(buffer < 14, 1, 2))
    kind = jnp.where(spots < count[0], kind, 3)
    ahead = (kind[None, :] < kind[:, None]) | (
        (kind[None, :] == kind[:, None]) & (spots[None, :] < spots[:, None])
    )
    rank = jnp.sum(ahead.astype(jnp.int32), axis=1)
    here = rank[None, :] == spots[:, None]

    def sort(values):
        return jnp.sum(jnp.where(here, values[None, :], 0), axis=1)

    steps = jnp.arange(4, dtype=jnp.int32)
    bounds = jnp.sum((kind[None, :] < steps[:, None]).astype(jnp.int32), axis=1)
    return bounds, sort(spots), sort(rows), sort(slots)


def gather_ring(value, up, down, near):
    one = permute(value, down)
    three = permute(value, up)
    two = permute(one, down) if near else permute(three, up)
    return [value, one, two, three]


def reduce_ring(parts, up, down, near):
    if near:
        one = parts[1] + permute(parts[2], up)
        three = parts[3]
    else:
        one = parts[1]
        three = parts[3] + permute(parts[2], down)
    return parts[0] + permute(one, up) + permute(three, down)


def quarter_tiles(features, index):
    feats = features.shape[0]
    split = features.reshape(feats, 4, 4, TILE)
    piece = lax.dynamic_index_in_dim(split, index, 1, keepdims=False)
    return jnp.transpose(piece, (1, 2, 0))


def gather_features(features, loop):
    partner = permute(quarter_tiles(features, loop ^ 2), y_partner)
    own = quarter_tiles(features, loop)
    sets = []
    for piece, near in ((own, True), (partner, False)):
        row = jnp.concatenate(gather_ring(piece[:2], x_up, x_down, near), axis=0)
        column = jnp.concatenate(gather_ring(piece[2:], z_up, z_down, near), axis=0)
        first = gather_ring(row, z_up, z_down, near)
        second = gather_ring(column, x_up, x_down, near)
        sets.append((first, second))
    first, second = sets[1]
    return (
        sets[0][0] + sets[0][1],
        [first[0], first[1], first[3], second[0], second[1], second[3]],
        [first[2], second[2]],
    )


def scatter_terms(own, apart, apart_far):
    first = [apart[0], apart[1], apart_far[0], apart[2]]
    second = [apart[3], apart[4], apart_far[1], apart[5]]
    pieces = []
    for row, column, near in ((first, second, False), (own[:4], own[4:], True)):
        row = reduce_ring(row, z_up, z_down, near)
        column = reduce_ring(column, x_up, x_down, near)
        half = reduce_ring([row[2 * i : 2 * i + 2] for i in range(4)], x_up, x_down, near)
        other = reduce_ring([column[2 * i : 2 * i + 2] for i in range(4)], z_up, z_down, near)
        pieces.append(jnp.concatenate([half, other], axis=0))
    return pieces[1] + permute(pieces[0], y_far)


def sum_over_loop(partial, loop):
    core = loop % 2
    half = partial.shape[0] // 2
    kept = lax.dynamic_slice_in_dim(partial, core * half, half, 0)
    given = lax.dynamic_slice_in_dim(partial, (1 - core) * half, half, 0)
    kept = kept + permute(given, core_swap)
    kept = kept + permute(kept, y_pair)
    other = permute(kept, core_swap)
    return jnp.where(
        core == 0,
        jnp.concatenate([kept, other], axis=0),
        jnp.concatenate([other, kept], axis=0),
    )


def sum_over_wide(value):
    for step in (1, 2):
        value = value + permute(value, lambda y, c, x, z: (y, c, x ^ step, z))
    for step in (1, 2):
        value = value + permute(value, lambda y, c, x, z: (y, c, x, z ^ step))
    return value + permute(value, y_far)


def gather_loop(own, loop):
    low, core = loop // 2, loop % 2
    across = permute(own, y_pair)
    own_other = permute(own, core_swap)
    across_other = permute(across, core_swap)
    same = jnp.where(
        core == 0, jnp.stack([own, own_other]), jnp.stack([own_other, own])
    )
    far = jnp.where(
        core == 0, jnp.stack([across, across_other]), jnp.stack([across_other, across])
    )
    whole = jnp.where(low == 0, jnp.stack([same, far]), jnp.stack([far, same]))
    feats = own.shape[1]
    return jnp.transpose(whole.reshape(-1, feats, TILE), (1, 0, 2)).reshape(feats, -1)


def per_device(features, weight, cotangent, tiles, tile_rows, tile_cols, counts):
    feats, shard_nodes = features.shape
    loop = lax.axis_index("loop")
    wide = lax.axis_index("wide")
    nrow = shard_nodes // TILE
    tile_collection = tiles.reshape(SLOTS, TILE, TILE)
    plan = make_plan(
        tile_rows.reshape(SLOTS), tile_cols.reshape(SLOTS), counts.reshape(1), loop, wide
    )

    partial = None
    for which, buffers in enumerate(gather_features(features, loop)):
        partial = forward_part(which, plan, tile_collection, buffers, partial, nrow)
    gathered = sum_over_loop(partial, loop).reshape(shard_nodes, feats)
    aggregated = lax.dot_general(
        weight, gathered, (((0,), (1,)), ((), ())), precision=HI, preferred_element_type=jnp.float32
    )
    activated, pull = jax.vjp(jax.nn.gelu, aggregated)
    slope = pull(cotangent)[0]
    weight_term = lax.dot_general(
        gathered, slope, (((0,), (1,)), ((), ())), precision=HI, preferred_element_type=jnp.float32
    )
    spread = jnp.dot(weight, slope, precision=HI, preferred_element_type=jnp.float32)
    terms = [None, None, None]
    for which in (2, 1, 0):
        terms[which] = backward_part(which, plan, tile_collection, spread)
    weight_grad = sum_over_wide(weight_term)
    input_cols = scatter_terms(*terms)
    input_cols = after(input_cols, weight_grad)
    input_grad = gather_loop(input_cols, loop)
    return (activated, input_grad, weight_grad)


def solution(mesh):
    return jax.shard_map(
        per_device,
        mesh=mesh,
        in_specs=(
            P(None, "wide"),
            P(),
            P(None, "wide"),
            P("loop", "wide", None, None, None),
            P("loop", "wide", None),
            P("loop", "wide", None),
            P("loop", "wide"),
        ),
        out_specs=(P(None, "wide"), P(None, "wide"), P()),
        check_vma=False,
    )
```

time: 251 us -> 273 us (1.088)
  waiting for transfers between devices: 106 us -> 71.9 us
  starting transfers between devices: 97.9 us -> 123 us
  Pallas kernels: 20.8 us -> 45.3 us
  local copies, waits for them, and re-layouts: 5.55 us -> 16.7 us
  other arithmetic: 12.6 us -> 6.45 us
    ppermute x61, waiting for transfers between devices: 106 us -> 71.9 us  [permute(): return lax.ppermute(value, AXES, pairs)]
    ppermute x61, starting transfers between devices: 97.9 us -> 123 us  [permute(): return lax.ppermute(value, AXES, pairs)]
    pallas_call x2 -> x6, Pallas kernels: 20.8 us -> 45.3 us  [the longest x3 24.1 us: forward_part(): pl.pallas_call(functools.partial(forward_kernel, which), name='forward_ti...]
    unnamed x20 -> x14, local copies, waits for them, and re-layouts: 1.67 us -> 13.8 us
    add x21 -> x22, other arithmetic: 9.12 us -> 1.5 us  [the longest x1 0.7 us: make_plan(): slots = buffer * PER + inner]
  transfers between devices with their start and end apart: 61 -> 61, of which waited for: 26 -> 25; matrix products, arithmetic and copies ran while one was open for 6% -> 4% of each run, Pallas kernels for 0% -> 11%
where the time goes in v2:
time: 273 us; the launch traced here: 270 us
  starting transfers between devices  123 us (45%)
  waiting for transfers between devices  71.9 us (26%)
  Pallas kernels  45.3 us (17%)
  local copies, waits for them, and re-layouts  16.7 us (6%)
  other arithmetic  6.45 us (2%)
  matrix products  4.43 us (2%)
    ppermute x61, starting transfers between devices, permute(): return lax.ppermute(value, AXES, pairs)  123 us
    ppermute x61, waiting for transfers between devices, permute(): return lax.ppermute(value, AXES, pairs)  71.9 us
    pallas_call x3, Pallas kernels, forward_part(): pl.pallas_call(functools.partial(forward_kernel, which), name='forward_ti...  24.1 us
    pallas_call x3, Pallas kernels, backward_part(): pl.pallas_call(functools.partial(backward_kernel, which), name='backward_...  21.2 us
    unnamed x14, local copies, waits for them, and re-layouts  13.8 us
  transfers between devices with their start and end apart: 61, of which 25 were waited for; matrix products, arithmetic and copies ran while one was open for 4% of the time, Pallas kernels for 11%

profile of v2, /device:TPU:0, one launch (start us, length us, event | category | flops | bytes accessed | tf_op | source)
XLA Modules:
  0.0 269.8 jit_solution(10876671668284392940)
XLA Ops:
  5.2 4.0 %collective-permute-start.19 = (f32[2,128,128]{2,1,0:T(8,128)S(1)}, f32[2,128,128]{2,1,0:T(8,128)S(1)}, u32[]{:S(2)}, u32[]{:S(2)}) collective-permute-start(f32[2,128,128]{2,1,0:T(8,128)S(1)} %get-tuple-element.62), channel_id=1, source_target_pairs={{0,3},{1,0},{2,1},{3,2},{4,7},{5,4},{6,5},{7,6},{8,11},{9,8},{10,9... | collective-permute-start | bytes 393224 | tf_op jit(solution)/shard_map/ppermute | solution.py:33
  46.7 4.2 %collective-permute-done.18.rest_3_ = f32[8,128,128]{2,1,0:T(8,128)} collective-permute-done((f32[8,128,128]{2,1,0:T(8,128)S(1)}, f32[8,128,128]{2,1,0:T(8,128)}, u32[]{:S(2)}, u32[]{:S(2)}) %collective-permute-start.18) | collective-permute-done | bytes 524320 | tf_op jit(solution)/shard_map/ppermute | solution.py:33
  55.2 5.5 %collective-permute-done.9.rest_5_ = f32[8,128,128]{2,1,0:T(8,128)} collective-permute-done((f32[8,128,128]{2,1,0:T(8,128)S(1)}, f32[8,128,128]{2,1,0:T(8,128)}, u32[]{:S(2)}, u32[]{:S(2)}) %collective-permute-start.9) | collective-permute-done | bytes 524320 | tf_op jit(solution)/shard_map/ppermute | solution.py:33
  67.2 4.3 %collective-permute-done.23.rest_6_ = f32[8,128,128]{2,1,0:T(8,128)} collective-permute-done((f32[8,128,128]{2,1,0:T(8,128)S(1)}, f32[8,128,128]{2,1,0:T(8,128)}, u32[]{:S(2)}, u32[]{:S(2)}) %collective-permute-start.23) | collective-permute-done | bytes 524320 | tf_op jit(solution)/shard_map/ppermute | solution.py:33
  71.5 5.8 %copy-done.1 = f32[1,1,256,128,128]{4,3,2,1,0:T(8,128)S(1)} copy-done((f32[1,1,256,128,128]{4,3,2,1,0:T(8,128)S(1)}, f32[1,1,256,128,128]{4,3,2,1,0:T(8,128)}, u32[]{:S(2)}) %copy-start.1) | copy-done | bytes 16777240
  77.3 12.1 %forward_tiles_0.1.rest_6_ = f32[16,128,128]{2,1,0:T(8,128)S(1)} custom-call(s32[4]{0:T(128)S(1)} %convert_reduce_fusion.1.bounds_ref, s32[256]{0:T(256)S(1)} %get-tuple-element.45.order_ref, s32[256]{0:T(256)S(1)} %get-tuple-element.44.rows_ref, s32[256]{0:T(256)S(1)} %get-tuple-element.43.slots_ref, f32[256,128,128]{2,1,0:T(8,128)S(1)} %bitcast.36, ...), custom_call_target="tpu_custom_call" | custom-call | flops 1610612736 | bytes 6291456 | tf_op jit(solution)/shard_map/forward_tiles_0/pallas_call | solution.py:210
  89.4 8.3 %forward_tiles_1.1.rest_2_ = f32[16,128,128]{2,1,0:T(8,128)S(1)} custom-call(s32[4]{0:T(128)S(1)} %convert_reduce_fusion.1.bounds_ref, s32[256]{0:T(256)S(1)} %get-tuple-element.45.order_ref, s32[256]{0:T(256)S(1)} %get-tuple-element.44.rows_ref, s32[256]{0:T(256)S(1)} %get-tuple-element.43.slots_ref, f32[256,128,128]{2,1,0:T(8,128)S(1)} %bitcast.37, ...), custom_call_target="tpu_custom_call" | custom-call | flops 1207959552 | bytes 4718592 | tf_op jit(solution)/shard_map/forward_tiles_1/pallas_call | solution.py:210
  103.6 15.4 %collective-permute-start.26 = (f32[8,128,128]{2,1,0:T(8,128)S(1)}, f32[8,128,128]{2,1,0:T(8,128)S(1)}, u32[]{:S(2)}, u32[]{:S(2)}) collective-permute-start(f32[8,128,128]{2,1,0:T(8,128)S(1)} %dynamic-slice_add_fusion), channel_id=1, source_target_pairs={{0,64},{1,65},{2,66},{3,67},{4,68},{5,69},{6,70},{7,71},{8,72},{9,... | collective-permute-start | bytes 1572872 | tf_op jit(solution)/shard_map/ppermute | solution.py:33
  119.0 12.2 %collective-permute-done.26 = f32[8,128,128]{2,1,0:T(8,128)S(1)} collective-permute-done((f32[8,128,128]{2,1,0:T(8,128)S(1)}, f32[8,128,128]{2,1,0:T(8,128)S(1)}, u32[]{:S(2)}, u32[]{:S(2)}) %collective-permute-start.26) | collective-permute-done | bytes 524320 | tf_op jit(solution)/shard_map/ppermute | solution.py:33
  136.0 5.8 %copy-done.2 = f32[1,1,256,128,128]{4,3,2,1,0:T(8,128)S(1)} copy-done((f32[1,1,256,128,128]{4,3,2,1,0:T(8,128)S(1)}, f32[1,1,256,128,128]{4,3,2,1,0:T(8,128)}, u32[]{:S(2)}) %copy-start.2) | copy-done | bytes 16777240
  141.8 11.1 %backward_tiles_0.1 = (f32[8,128,128]{2,1,0:T(8,128)S(1)}, f32[8,128,128]{2,1,0:T(8,128)S(1)}, f32[8,128,128]{2,1,0:T(8,128)S(1)}, f32[8,128,128]{2,1,0:T(8,128)...) custom-call(s32[4]{0:T(128)S(1)} %convert_reduce_fusion.1.bounds_ref, ...), custom_call_target="tpu_custom_call" | custom-call | flops 1610612736 | bytes 6291456 | tf_op jit(solution)/shard_map/backward_tiles_0/pallas_call | solution.py:229
  155.1 9.0 %collective-permute-start.34 = (f32[8,128,128]{2,1,0:T(8,128)S(1)}, f32[8,128,128]{2,1,0:T(8,128)S(1)}, u32[]{:S(2)}, u32[]{:S(2)}) collective-permute-start(f32[8,128,128]{2,1,0:T(8,128)S(1)} %get-tuple-element.26), channel_id=1, source_target_pairs={{0,4},{1,5},{2,6},{3,7},{4,8},{5,9},{6,10},{7,11},{8,12},{9,13},{1... | collective-permute-start | bytes 1572872 | tf_op jit(solution)/shard_map/ppermute | solution.py:33
  169.0 4.3 %collective-permute-start.41 = (f32[8,128,128]{2,1,0:T(8,128)S(1)}, f32[8,128,128]{2,1,0:T(8,128)S(1)}, u32[]{:S(2)}, u32[]{:S(2)}) collective-permute-start(f32[8,128,128]{2,1,0:T(8,128)S(1)} %get-tuple-element.31), channel_id=1, source_target_pairs={{0,3},{1,0},{2,1},{3,2},{4,7},{5,4},{6,5},{7,6},{8,11},{9,8},{10,9... | collective-permute-start | bytes 1572872 | tf_op jit(solution)/shard_map/ppermute | solution.py:33
  179.3 4.3 %collective-permute-done.55 = f32[128,128]{1,0:T(8,128)S(1)} collective-permute-done((f32[128,128]{1,0:T(8,128)S(1)}, f32[128,128]{1,0:T(8,128)S(1)}, u32[]{:S(2)}, u32[]{:S(2)}) %collective-permute-start.55) | collective-permute-done | bytes 65568 | tf_op jit(solution)/shard_map/ppermute | solution.py:33
  187.0 4.5 %collective-permute-start.47 = (f32[8,128,128]{2,1,0:T(8,128)S(1)}, f32[8,128,128]{2,1,0:T(8,128)S(1)}, u32[]{:S(2)}, u32[]{:S(2)}) collective-permute-start(f32[8,128,128]{2,1,0:T(8,128)S(1)} %get-tuple-element.35), channel_id=1, source_target_pairs={{0,12},{1,13},{2,14},{3,15},{4,0},{5,1},{6,2},{7,3},{8,4},{9,5},{1... | collective-permute-start | bytes 1572872 | tf_op jit(solution)/shard_map/ppermute | solution.py:33
  195.9 3.8 %collective-permute-done.57 = f32[128,128]{1,0:T(8,128)S(1)} collective-permute-done((f32[128,128]{1,0:T(8,128)S(1)}, f32[128,128]{1,0:T(8,128)S(1)}, u32[]{:S(2)}, u32[]{:S(2)}) %collective-permute-start.57) | collective-permute-done | bytes 65568 | tf_op jit(solution)/shard_map/ppermute | solution.py:33
  199.8 3.7 %collective-permute-start.36 = (f32[8,128,128]{2,1,0:T(8,128)S(1)}, f32[8,128,128]{2,1,0:T(8,128)S(1)}, u32[]{:S(2)}, u32[]{:S(2)}) collective-permute-start(f32[8,128,128]{2,1,0:T(8,128)S(1)} %get-tuple-element.27), channel_id=1, source_target_pairs={{0,12},{1,13},{2,14},{3,15},{4,0},{5,1},{6,2},{7,3},{8,4},{9,5},{1... | collective-permute-start | bytes 1572872 | tf_op jit(solution)/shard_map/ppermute | solution.py:33
  203.5 7.1 %backward_tiles_1.1 = (f32[8,128,128]{2,1,0:T(8,128)S(1)}, f32[8,128,128]{2,1,0:T(8,128)S(1)}, f32[8,128,128]{2,1,0:T(8,128)S(1)}, f32[8,128,128]{2,1,0:T(8,128)...) custom-call(s32[4]{0:T(128)S(1)} %convert_reduce_fusion.1.bounds_ref, s32[256]{0:T(256)S(1)} %get-tuple-element.45.order_ref, ...), custom_call_target="tpu_custom_call" | custom-call | flops 1207959552 | bytes 4718592 | tf_op jit(solution)/shard_map/backward_tiles_1/pallas_call | solution.py:229
  211.9 6.0 %collective-permute-start.46 = (f32[8,128,128]{2,1,0:T(8,128)S(1)}, f32[8,128,128]{2,1,0:T(8,128)S(1)}, u32[]{:S(2)}, u32[]{:S(2)}) collective-permute-start(f32[8,128,128]{2,1,0:T(8,128)S(1)} %get-tuple-element.33), channel_id=1, source_target_pairs={{0,4},{1,5},{2,6},{3,7},{4,8},{5,9},{6,10},{7,11},{8,12},{9,13},{1... | collective-permute-start | bytes 1572872 | tf_op jit(solution)/shard_map/ppermute | solution.py:33
  222.8 4.3 %collective-permute-done.40 = f32[8,128,128]{2,1,0:T(8,128)S(1)} collective-permute-done((f32[8,128,128]{2,1,0:T(8,128)S(1)}, f32[8,128,128]{2,1,0:T(8,128)S(1)}, u32[]{:S(2)}, u32[]{:S(2)}) %collective-permute-start.40) | collective-permute-done | bytes 524320 | tf_op jit(solution)/shard_map/ppermute | solution.py:33
  242.8 3.7 %collective-permute-start.51 = (f32[2,128,128]{2,1,0:T(8,128)S(1)}, f32[2,128,128]{2,1,0:T(8,128)S(1)}, u32[]{:S(2)}, u32[]{:S(2)}) collective-permute-start(f32[2,128,128]{2,1,0:T(8,128)S(1)} %slice_add_fusion), channel_id=1, source_target_pairs={{0,3},{1,0},{2,1},{3,2},{4,7},{5,4},{6,5},{7,6},{8,11},{9,8},{10,9... | collective-permute-start | bytes 393224 | tf_op jit(solution)/shard_map/ppermute | solution.py:33
  249.1 4.8 %collective-permute-start.52 = (f32[4,128,128]{2,1,0:T(8,128)S(1)}, f32[4,128,128]{2,1,0:T(8,128)S(1)}, u32[]{:S(2)}, u32[]{:S(2)}) collective-permute-start(f32[4,128,128]{2,1,0:T(8,128)S(1)} %pad_maximum_fusion.4), channel_id=1, source_target_pairs={{0,16},{1,17},{2,18},{3,19},{4,20},{5,21},{6,22},{7,23},{8,24},{9,... | collective-permute-start | bytes 786440 | tf_op jit(solution)/shard_map/ppermute | solution.py:33
  254.0 6.6 %collective-permute-done.52 = f32[4,128,128]{2,1,0:T(8,128)S(1)} collective-permute-done((f32[4,128,128]{2,1,0:T(8,128)S(1)}, f32[4,128,128]{2,1,0:T(8,128)S(1)}, u32[]{:S(2)}, u32[]{:S(2)}) %collective-permute-start.52) | collective-permute-done | bytes 262176 | tf_op jit(solution)/shard_map/ppermute | solution.py:33
  262.4 4.7 %collective-permute-done.59 = f32[4,128,128]{2,1,0:T(8,128)S(1)} collective-permute-done((f32[4,128,128]{2,1,0:T(8,128)S(1)}, f32[4,128,128]{2,1,0:T(8,128)S(1)}, u32[]{:S(2)}, u32[]{:S(2)}) %collective-permute-start.59) | collective-permute-done | bytes 262176 | tf_op jit(solution)/shard_map/ppermute | solution.py:33
  (170 shorter events, 112.4 us)
Async XLA Ops:
  19.0 22.2 %collective-permute-start.16 = (f32[8,128,128]{2,1,0:T(8,128)S(1)}, f32[8,128,128]{2,1,0:T(8,128)S(1)}, u32[]{:S(2)}, u32[]{:S(2)}) collective-permute-start(f32[8,128,128]{2,1,0:T(8,128)S(1)} %pad_maximum_fusion.2.rest_0_), channel_id=1, source_target_pairs={{0,3},{1,0},{2,1},{3,2},{4,7},{5,4},{6,5},{7,6},{8,11},{9,8},{10,9... | collective-permute-start | bytes 1572872 | tf_op jit(solution)/shard_map/ppermute | solution.py:33
  23.4 19.0 %collective-permute-start.22 = (f32[8,128,128]{2,1,0:T(8,128)S(1)}, f32[8,128,128]{2,1,0:T(8,128)S(1)}, u32[]{:S(2)}, u32[]{:S(2)}) collective-permute-start(f32[8,128,128]{2,1,0:T(8,128)S(1)} %pad_maximum_fusion.3.rest_4_), channel_id=1, source_target_pairs={{0,12},{1,13},{2,14},{3,15},{4,0},{5,1},{6,2},{7,3},{8,4},{9,5},{1... | collective-permute-start | bytes 1572872 | tf_op jit(solution)/shard_map/ppermute | solution.py:33
  36.8 14.0 %collective-permute-start.18 = (f32[8,128,128]{2,1,0:T(8,128)S(1)}, f32[8,128,128]{2,1,0:T(8,128)}, u32[]{:S(2)}, u32[]{:S(2)}) collective-permute-start(f32[8,128,128]{2,1,0:T(8,128)S(1)} %pad_maximum_fusion.2.rest_0_), channel_id=1, source_target_pairs={{0,1},{1,2},{2,3},{3,0},{4,5},{5,6},{6,7},{7,4},{8,9},{9,10},{10,1... | collective-permute-start | bytes 1572872 | tf_op jit(solution)/shard_map/ppermute | solution.py:33
  37.8 15.4 %collective-permute-start.24 = (f32[8,128,128]{2,1,0:T(8,128)S(1)}, f32[8,128,128]{2,1,0:T(8,128)}, u32[]{:S(2)}, u32[]{:S(2)}) collective-permute-start(f32[8,128,128]{2,1,0:T(8,128)S(1)} %pad_maximum_fusion.3.rest_4_), channel_id=1, source_target_pairs={{0,4},{1,5},{2,6},{3,7},{4,8},{5,9},{6,10},{7,11},{8,12},{9,13},{1... | collective-permute-start | bytes 1572872 | tf_op jit(solution)/shard_map/ppermute | solution.py:33
  40.2 20.5 %collective-permute-start.9 = (f32[8,128,128]{2,1,0:T(8,128)S(1)}, f32[8,128,128]{2,1,0:T(8,128)}, u32[]{:S(2)}, u32[]{:S(2)}) collective-permute-start(f32[8,128,128]{2,1,0:T(8,128)S(1)} %pad_maximum_fusion.1.rest_3_), channel_id=1, source_target_pairs={{0,4},{1,5},{2,6},{3,7},{4,8},{5,9},{6,10},{7,11},{8,12},{9,13},{1... | collective-permute-start | bytes 1572872 | tf_op jit(solution)/shard_map/ppermute | solution.py:33
  41.2 20.9 %collective-permute-start.4 = (f32[8,128,128]{2,1,0:T(8,128)S(1)}, f32[8,128,128]{2,1,0:T(8,128)}, u32[]{:S(2)}, u32[]{:S(2)}) collective-permute-start(f32[8,128,128]{2,1,0:T(8,128)S(1)} %pad_maximum_fusion.rest_0_), channel_id=1, source_target_pairs={{0,1},{1,2},{2,3},{3,0},{4,5},{5,6},{6,7},{7,4},{8,9},{9,10},{10,1... | collective-permute-start | bytes 1572872 | tf_op jit(solution)/shard_map/ppermute | solution.py:33
  42.3 22.1 %collective-permute-start.17 = (f32[8,128,128]{2,1,0:T(8,128)S(1)}, f32[8,128,128]{2,1,0:T(8,128)}, u32[]{:S(2)}, u32[]{:S(2)}) collective-permute-start(f32[8,128,128]{2,1,0:T(8,128)S(1)} %collective-permute-done.16.rest_1_), channel_id=1, source_target_pairs={{0,3},{1,0},{2,1},{3,2},{4,7},{5,4},{6,5},{7,6},{8,11},{9,8},{10,9... | collective-permute-start | bytes 1572872 | tf_op jit(solution)/shard_map/ppermute | solution.py:33
  50.9 38.5 %collective-permute-start.12 = (f32[8,128,128]{2,1,0:T(8,128)S(1)}, f32[8,128,128]{2,1,0:T(8,128)}, u32[]{:S(2)}, u32[]{:S(2)}) collective-permute-start(f32[8,128,128]{2,1,0:T(8,128)S(1)} %pad_maximum_fusion.1.rest_3_), channel_id=1, source_target_pairs={{0,12},{1,13},{2,14},{3,15},{4,0},{5,1},{6,2},{7,3},{8,4},{9,5},{1... | collective-permute-start | bytes 1572872 | tf_op jit(solution)/shard_map/ppermute | solution.py:33
  53.2 36.2 %collective-permute-start.11 = (f32[8,128,128]{2,1,0:T(8,128)S(1)}, f32[8,128,128]{2,1,0:T(8,128)}, u32[]{:S(2)}, u32[]{:S(2)}) collective-permute-start(f32[8,128,128]{2,1,0:T(8,128)S(1)} %pad_maximum_fusion.rest_0_), channel_id=1, source_target_pairs={{0,3},{1,0},{2,1},{3,2},{4,7},{5,4},{6,5},{7,6},{8,11},{9,8},{10,9... | collective-permute-start | bytes 1572872 | tf_op jit(solution)/shard_map/ppermute | solution.py:33
  62.1 35.6 %collective-permute-start.10 = (f32[8,128,128]{2,1,0:T(8,128)}, f32[8,128,128]{2,1,0:T(8,128)}, u32[]{:S(2)}, u32[]{:S(2)}) collective-permute-start(f32[8,128,128]{2,1,0:T(8,128)} %collective-permute-done.9.rest_5_), channel_id=1, source_target_pairs={{0,4},{1,5},{2,6},{3,7},{4,8},{5,9},{6,10},{7,11},{8,12},{9,13},{1... | collective-permute-start | bytes 1572872 | tf_op jit(solution)/shard_map/ppermute | solution.py:33
  64.5 33.3 %collective-permute-start.5 = (f32[8,128,128]{2,1,0:T(8,128)}, f32[8,128,128]{2,1,0:T(8,128)}, u32[]{:S(2)}, u32[]{:S(2)}) collective-permute-start(f32[8,128,128]{2,1,0:T(8,128)} %collective-permute-done.4.rest_2_), channel_id=1, source_target_pairs={{0,1},{1,2},{2,3},{3,0},{4,5},{5,6},{6,7},{7,4},{8,9},{9,10},{10,1... | collective-permute-start | bytes 1572872 | tf_op jit(solution)/shard_map/ppermute | solution.py:33
  103.6 27.7 %collective-permute-start.26 = (f32[8,128,128]{2,1,0:T(8,128)S(1)}, f32[8,128,128]{2,1,0:T(8,128)S(1)}, u32[]{:S(2)}, u32[]{:S(2)}) collective-permute-start(f32[8,128,128]{2,1,0:T(8,128)S(1)} %dynamic-slice_add_fusion), channel_id=1, source_target_pairs={{0,64},{1,65},{2,66},{3,67},{4,68},{5,69},{6,70},{7,71},{8,72},{9,... | collective-permute-start | bytes 1572872 | tf_op jit(solution)/shard_map/ppermute | solution.py:33
  152.9 38.6 %collective-permute-start.28 = (f32[8,128,128]{2,1,0:T(8,128)S(1)}, f32[8,128,128]{2,1,0:T(8,128)S(1)}, u32[]{:S(2)}, u32[]{:S(2)}) collective-permute-start(f32[8,128,128]{2,1,0:T(8,128)S(1)} %get-tuple-element.22), channel_id=1, source_target_pairs={{0,1},{1,2},{2,3},{3,0},{4,5},{5,6},{6,7},{7,4},{8,9},{9,10},{10,1... | collective-permute-start | bytes 1572872 | tf_op jit(solution)/shard_map/ppermute | solution.py:33
  155.1 38.9 %collective-permute-start.34 = (f32[8,128,128]{2,1,0:T(8,128)S(1)}, f32[8,128,128]{2,1,0:T(8,128)S(1)}, u32[]{:S(2)}, u32[]{:S(2)}) collective-permute-start(f32[8,128,128]{2,1,0:T(8,128)S(1)} %get-tuple-element.26), channel_id=1, source_target_pairs={{0,4},{1,5},{2,6},{3,7},{4,8},{5,9},{6,10},{7,11},{8,12},{9,13},{1... | collective-permute-start | bytes 1572872 | tf_op jit(solution)/shard_map/ppermute | solution.py:33
  169.0 34.5 %collective-permute-start.41 = (f32[8,128,128]{2,1,0:T(8,128)S(1)}, f32[8,128,128]{2,1,0:T(8,128)S(1)}, u32[]{:S(2)}, u32[]{:S(2)}) collective-permute-start(f32[8,128,128]{2,1,0:T(8,128)S(1)} %get-tuple-element.31), channel_id=1, source_target_pairs={{0,3},{1,0},{2,1},{3,2},{4,7},{5,4},{6,5},{7,6},{8,11},{9,8},{10,9... | collective-permute-start | bytes 1572872 | tf_op jit(solution)/shard_map/ppermute | solution.py:33
  187.0 24.4 %collective-permute-start.47 = (f32[8,128,128]{2,1,0:T(8,128)S(1)}, f32[8,128,128]{2,1,0:T(8,128)S(1)}, u32[]{:S(2)}, u32[]{:S(2)}) collective-permute-start(f32[8,128,128]{2,1,0:T(8,128)S(1)} %get-tuple-element.35), channel_id=1, source_target_pairs={{0,12},{1,13},{2,14},{3,15},{4,0},{5,1},{6,2},{7,3},{8,4},{9,5},{1... | collective-permute-start | bytes 1572872 | tf_op jit(solution)/shard_map/ppermute | solution.py:33
  191.5 20.4 %collective-permute-start.30 = (f32[8,128,128]{2,1,0:T(8,128)S(1)}, f32[8,128,128]{2,1,0:T(8,128)S(1)}, u32[]{:S(2)}, u32[]{:S(2)}) collective-permute-start(f32[8,128,128]{2,1,0:T(8,128)S(1)} %get-tuple-element.23), channel_id=1, source_target_pairs={{0,3},{1,0},{2,1},{3,2},{4,7},{5,4},{6,5},{7,6},{8,11},{9,8},{10,9... | collective-permute-start | bytes 1572872 | tf_op jit(solution)/shard_map/ppermute | solution.py:33
  193.8 24.1 %collective-permute-start.29 = (f32[8,128,128]{2,1,0:T(8,128)S(1)}, f32[8,128,128]{2,1,0:T(8,128)S(1)}, u32[]{:S(2)}, u32[]{:S(2)}) collective-permute-start(f32[8,128,128]{2,1,0:T(8,128)S(1)} %add.279), channel_id=1, source_target_pairs={{0,1},{1,2},{2,3},{3,0},{4,5},{5,6},{6,7},{7,4},{8,9},{9,10},{10,1... | collective-permute-start | bytes 1572872 | tf_op jit(solution)/shard_map/ppermute | solution.py:33
  199.8 20.6 %collective-permute-start.36 = (f32[8,128,128]{2,1,0:T(8,128)S(1)}, f32[8,128,128]{2,1,0:T(8,128)S(1)}, u32[]{:S(2)}, u32[]{:S(2)}) collective-permute-start(f32[8,128,128]{2,1,0:T(8,128)S(1)} %get-tuple-element.27), channel_id=1, source_target_pairs={{0,12},{1,13},{2,14},{3,15},{4,0},{5,1},{6,2},{7,3},{8,4},{9,5},{1... | collective-permute-start | bytes 1572872 | tf_op jit(solution)/shard_map/ppermute | solution.py:33
  203.5 19.2 %collective-permute-start.35 = (f32[8,128,128]{2,1,0:T(8,128)S(1)}, f32[8,128,128]{2,1,0:T(8,128)S(1)}, u32[]{:S(2)}, u32[]{:S(2)}) collective-permute-start(f32[8,128,128]{2,1,0:T(8,128)S(1)} %add.285), channel_id=1, source_target_pairs={{0,4},{1,5},{2,6},{3,7},{4,8},{5,9},{6,10},{7,11},{8,12},{9,13},{1... | collective-permute-start | bytes 1572872 | tf_op jit(solution)/shard_map/ppermute | solution.py:33
  211.3 15.7 %collective-permute-start.40 = (f32[8,128,128]{2,1,0:T(8,128)S(1)}, f32[8,128,128]{2,1,0:T(8,128)S(1)}, u32[]{:S(2)}, u32[]{:S(2)}) collective-permute-start(f32[8,128,128]{2,1,0:T(8,128)S(1)} %get-tuple-element.29), channel_id=1, source_target_pairs={{0,1},{1,2},{2,3},{3,0},{4,5},{5,6},{6,7},{7,4},{8,9},{9,10},{10,1... | collective-permute-start | bytes 1572872 | tf_op jit(solution)/shard_map/ppermute | solution.py:33
  211.9 17.7 %collective-permute-start.46 = (f32[8,128,128]{2,1,0:T(8,128)S(1)}, f32[8,128,128]{2,1,0:T(8,128)S(1)}, u32[]{:S(2)}, u32[]{:S(2)}) collective-permute-start(f32[8,128,128]{2,1,0:T(8,128)S(1)} %get-tuple-element.33), channel_id=1, source_target_pairs={{0,4},{1,5},{2,6},{3,7},{4,8},{5,9},{6,10},{7,11},{8,12},{9,13},{1... | collective-permute-start | bytes 1572872 | tf_op jit(solution)/shard_map/ppermute | solution.py:33
  234.0 19.9 %collective-permute-start.32 = (f32[2,128,128]{2,1,0:T(8,128)S(1)}, f32[2,128,128]{2,1,0:T(8,128)S(1)}, u32[]{:S(2)}, u32[]{:S(2)}) collective-permute-start(f32[2,128,128]{2,1,0:T(8,128)S(1)} %get-tuple-element.54), channel_id=1, source_target_pairs={{0,4},{1,5},{2,6},{3,7},{4,8},{5,9},{6,10},{7,11},{8,12},{9,13},{1... | collective-permute-start | bytes 393224 | tf_op jit(solution)/shard_map/ppermute | solution.py:33
  235.4 18.5 %collective-permute-start.33 = (f32[2,128,128]{2,1,0:T(8,128)S(1)}, f32[2,128,128]{2,1,0:T(8,128)S(1)}, u32[]{:S(2)}, u32[]{:S(2)}) collective-permute-start(f32[2,128,128]{2,1,0:T(8,128)S(1)} %get-tuple-element.55), channel_id=1, source_target_pairs={{0,12},{1,13},{2,14},{3,15},{4,0},{5,1},{6,2},{7,3},{8,4},{9,5},{1... | collective-permute-start | bytes 393224 | tf_op jit(solution)/shard_map/ppermute | solution.py:33
  (43 other events, 464.8 us)

commit v3 on v2

--- a/solution.py
+++ b/solution.py
@@ -13,9 +13,12 @@
 TILE = 128
 SLOTS = 256
 GROUP = 16
+CHUNK = 32
+STAGES = 3
+PAIR_BYTES = 40 * 1024 * 1024
 PER = 8
 CLASS_BUFFERS = (8, 6, 2)
-VMEM_BYTES = 28 * 1024 * 1024
+VMEM_BYTES = 24 * 1024 * 1024
 
 
 def device_index(y, core, x, z):
@@ -79,18 +82,48 @@
     return high, low
 
 
-def start_groups(tiles_ref, order_ref, held, sems, begin, groups):
-    @pl.loop(0, groups)
-    def _(group):
-        for j in range(GROUP):
-            spot = group * GROUP + j
-            source = order_ref[jnp.minimum(begin + spot, SLOTS - 1)]
-            pltpu.make_async_copy(tiles_ref.at[source], held.at[spot], sems.at[group]).start()
-
-
-def wait_group(tiles_ref, held, sems, group):
-    part = pl.ds(group * GROUP, GROUP)
-    pltpu.make_async_copy(tiles_ref.at[pl.ds(0, GROUP)], held.at[part], sems.at[group]).wait()
+def pair_kernel(count_ref, tiles_ref, out_ref, held, sems):
+    count = count_ref[0]
+
+    def copy(chunk):
+        source = tiles_ref.at[pl.ds(chunk * CHUNK, CHUNK)]
+        return pltpu.make_async_copy(source, held.at[chunk % STAGES], sems.at[chunk % STAGES])
+
+    def when_live(chunk):
+        return pl.when(chunk * CHUNK < count)
+
+    for chunk in range(STAGES):
+        when_live(chunk)(copy(chunk).start)
+    for chunk in range(SLOTS // CHUNK):
+
+        @when_live(chunk)
+        def _():
+            copy(chunk).wait()
+
+            @pl.loop(0, CHUNK, unroll=8)
+            def _(j):
+                high, low = split_high_low(held[chunk % STAGES, j])
+                out_ref[chunk * CHUNK + j, :, :TILE] = high
+                out_ref[chunk * CHUNK + j, :, TILE:] = low
+
+            if chunk + STAGES < SLOTS // CHUNK:
+                when_live(chunk + STAGES)(copy(chunk + STAGES).start)
+
+
+def pair_tiles(count, tiles):
+    return pl.pallas_call(
+        pair_kernel,
+        name="pair_tiles",
+        out_shape=pltpu.VMEM((SLOTS, TILE, 2 * TILE), jnp.bfloat16),
+        in_specs=[smem(), anywhere()],
+        out_specs=vmem(),
+        scratch_shapes=[
+            pltpu.VMEM((STAGES, CHUNK, TILE, TILE), jnp.float32),
+            pltpu.SemaphoreType.DMA((STAGES,)),
+        ],
+        cost_estimate=cost(8),
+        compiler_params=pltpu.CompilerParams(vmem_limit_bytes=PAIR_BYTES),
+    )(count, tiles)
 
 
 def class_range(bounds_ref, which):
@@ -104,10 +137,9 @@
     buffers = rest[:number]
     rest = rest[number:]
     prior_ref = rest[0] if which else None
-    out_ref, held, pairs, total, sems = rest[-5:]
+    out_ref, pairs, total = rest[-3:]
     nrow = out_ref.shape[0]
     begin, end, groups = class_range(bounds_ref, which)
-    start_groups(tiles_ref, order_ref, held, sems, begin, groups)
     if which:
         total[0:nrow] = prior_ref[...]
     else:
@@ -122,17 +154,15 @@
 
     @pl.loop(0, groups)
     def _(group):
-        wait_group(tiles_ref, held, sems, group)
         for j in range(GROUP):
             spot = group * GROUP + j
             place = jnp.minimum(begin + spot, SLOTS - 1)
             live = begin + spot < end
             row = jnp.where(live, rows_ref[place], nrow)
             slot = jnp.where(live, slots_ref[place] - base, 0)
-            high, low = split_high_low(held[spot])
             right = pairs[slot]
             product = jnp.dot(
-                jnp.concatenate([high, low], axis=1),
+                tiles_ref[order_ref[place]],
                 jnp.concatenate([right, right], axis=0),
                 preferred_element_type=jnp.float32,
             )
@@ -145,9 +175,8 @@
     number = CLASS_BUFFERS[which]
     base = sum(CLASS_BUFFERS[:which]) * PER
     buffers = rest[:number]
-    held, pairs, total, sems, out_sems = rest[number:]
+    pairs, total, out_sems = rest[number:]
     begin, end, groups = class_range(bounds_ref, which)
-    start_groups(tiles_ref, order_ref, held, sems, begin, groups)
     for row in range(pairs.shape[0]):
         high, low = split_high_low(slope_ref[:, row * TILE : (row + 1) * TILE])
         pairs[row, :, :TILE] = high
@@ -159,14 +188,12 @@
 
     @pl.loop(0, groups)
     def _(group):
-        wait_group(tiles_ref, held, sems, group)
         for j in range(GROUP):
             spot = group * GROUP + j
             place = jnp.minimum(begin + spot, SLOTS - 1)
             live = begin + spot < end
             slot = jnp.where(live, slots_ref[place] - base, number * PER)
-            high, low = split_high_low(held[spot])
-            right = jnp.concatenate([high, low], axis=1)
+            right = tiles_ref[order_ref[place]]
             product = jnp.dot(
                 pairs[rows_ref[place]],
                 jnp.concatenate([right, right], axis=0),
@@ -197,10 +224,9 @@
     return pl.BlockSpec(memory_space=pl.ANY)
 
 
-def cost(which):
-    live = (96, 72, 24)[which]
+def cost(microseconds):
     return pl.CostEstimate(
-        flops=live * 8 * TILE**3, bytes_accessed=live * 4 * TILE**2, transcendentals=0
+        flops=int(microseconds * 1.1e9), bytes_accessed=1 << 20, transcendentals=0
     )
 
 
@@ -211,15 +237,13 @@
         functools.partial(forward_kernel, which),
         name="forward_tiles_%d" % which,
         out_shape=jax.ShapeDtypeStruct((nrow, TILE, TILE), jnp.float32),
-        in_specs=[smem()] * 4 + [anywhere()] + [vmem()] * (number + len(extra)),
+        in_specs=[smem()] * 4 + [vmem()] * (1 + number + len(extra)),
         out_specs=vmem(),
         scratch_shapes=[
-            pltpu.VMEM((SLOTS, TILE, TILE), jnp.float32),
             pltpu.VMEM((number * PER, TILE, 2 * TILE), jnp.bfloat16),
             pltpu.VMEM((nrow + 1, TILE, TILE), jnp.float32),
-            pltpu.SemaphoreType.DMA((SLOTS // GROUP,)),
         ],
-        cost_estimate=cost(which),
+        cost_estimate=cost((6, 5, 2)[which]),
         compiler_params=pltpu.CompilerParams(vmem_limit_bytes=VMEM_BYTES),
     )(*plan, tiles, *buffers, *extra)
 
@@ -230,16 +254,14 @@
         functools.partial(backward_kernel, which),
         name="backward_tiles_%d" % which,
         out_shape=[jax.ShapeDtypeStruct((PER, TILE, TILE), jnp.float32)] * number,
-        in_specs=[smem()] * 4 + [anywhere(), vmem()],
+        in_specs=[smem()] * 4 + [vmem(), vmem()],
         out_specs=[anywhere()] * number,
         scratch_shapes=[
-            pltpu.VMEM((SLOTS, TILE, TILE), jnp.float32),
             pltpu.VMEM((slope.shape[1] // TILE, TILE, 2 * TILE), jnp.bfloat16),
             pltpu.VMEM((number * PER + 1, TILE, TILE), jnp.float32),
-            pltpu.SemaphoreType.DMA((SLOTS // GROUP,)),
             pltpu.SemaphoreType.DMA((number,)),
         ],
-        cost_estimate=cost(which),
+        cost_estimate=cost((6, 5, 2)[which]),
         compiler_params=pltpu.CompilerParams(vmem_limit_bytes=VMEM_BYTES),
     )(*plan, tiles, slope)
 
@@ -276,13 +298,6 @@
     return bounds, sort(spots), sort(rows), sort(slots)
 
 
-def gather_ring(value, up, down, near):
-    one = permute(value, down)
-    three = permute(value, up)
-    two = permute(one, down) if near else permute(three, up)
-    return [value, one, two, three]
-
-
 def reduce_ring(parts, up, down, near):
     if near:
         one = parts[1] + permute(parts[2], up)
@@ -301,21 +316,28 @@
 
 
 def gather_features(features, loop):
+    own = quarter_tiles(features, loop)
     partner = permute(quarter_tiles(features, loop ^ 2), y_partner)
-    own = quarter_tiles(features, loop)
-    sets = []
-    for piece, near in ((own, True), (partner, False)):
-        row = jnp.concatenate(gather_ring(piece[:2], x_up, x_down, near), axis=0)
-        column = jnp.concatenate(gather_ring(piece[2:], z_up, z_down, near), axis=0)
-        first = gather_ring(row, z_up, z_down, near)
-        second = gather_ring(column, x_up, x_down, near)
-        sets.append((first, second))
-    first, second = sets[1]
-    return (
-        sets[0][0] + sets[0][1],
-        [first[0], first[1], first[3], second[0], second[1], second[3]],
-        [first[2], second[2]],
-    )
+    row_one, row_three = permute(own[:2], x_down), permute(own[:2], x_up)
+    column_one, column_three = permute(own[2:], z_down), permute(own[2:], z_up)
+    row_two, column_two = permute(row_one, x_down), permute(column_one, z_down)
+    row = jnp.concatenate([own[:2], row_one, row_two, row_three], axis=0)
+    column = jnp.concatenate([own[2:], column_one, column_two, column_three], axis=0)
+    first_one, second_one = permute(row, z_down), permute(column, x_down)
+    first_three, second_three = permute(row, z_up), permute(column, x_up)
+    first_two, second_two = permute(first_one, z_down), permute(second_one, x_down)
+    near = [row, first_one, first_two, first_three, column, second_one, second_two, second_three]
+
+    partner = after(partner, row, column)
+    row_one, row_three = permute(partner[:2], x_down), permute(partner[:2], x_up)
+    column_one, column_three = permute(partner[2:], z_down), permute(partner[2:], z_up)
+    row_two, column_two = permute(row_three, x_up), permute(column_three, z_up)
+    row = jnp.concatenate([partner[:2], row_one, row_two, row_three], axis=0)
+    column = jnp.concatenate([partner[2:], column_one, column_two, column_three], axis=0)
+    first_one, second_one = permute(row, z_down), permute(column, x_down)
+    first_three, second_three = permute(row, z_up), permute(column, x_up)
+    apart = [row, first_one, first_three, column, second_one, second_three]
+    return near, apart
 
 
 def scatter_terms(own, apart, apart_far):
@@ -380,9 +402,12 @@
         tile_rows.reshape(SLOTS), tile_cols.reshape(SLOTS), counts.reshape(1), loop, wide
     )
 
-    partial = None
-    for which, buffers in enumerate(gather_features(features, loop)):
-        partial = forward_part(which, plan, tile_collection, buffers, partial, nrow)
+    near, apart = gather_features(features, loop)
+    pairs = pair_tiles(after(counts.reshape(1), near[0], near[4]), tile_collection)
+    partial = forward_part(0, plan, pairs, near, None, nrow)
+    far = [permute(after(apart[2], pairs), z_up), permute(after(apart[5], pairs), x_up)]
+    partial = forward_part(1, plan, pairs, apart, partial, nrow)
+    partial = forward_part(2, plan, pairs, far, partial, nrow)
     gathered = sum_over_loop(partial, loop).reshape(shard_nodes, feats)
     aggregated = lax.dot_general(
         weight, gathered, (((0,), (1,)), ((), ())), precision=HI, preferred_element_type=jnp.float32
@@ -393,11 +418,11 @@
         gathered, slope, (((0,), (1,)), ((), ())), precision=HI, preferred_element_type=jnp.float32
     )
     spread = jnp.dot(weight, slope, precision=HI, preferred_element_type=jnp.float32)
-    terms = [None, None, None]
-    for which in (2, 1, 0):
-        terms[which] = backward_part(which, plan, tile_collection, spread)
+    apart_far = backward_part(2, plan, pairs, spread)
+    apart = backward_part(1, plan, pairs, after(spread, *apart_far))
+    own = backward_part(0, plan, pairs, after(spread, *apart))
     weight_grad = sum_over_wide(weight_term)
-    input_cols = scatter_terms(*terms)
+    input_cols = scatter_terms(own, apart, apart_far)
     input_cols = after(input_cols, weight_grad)
     input_grad = gather_loop(input_cols, loop)
     return (activated, input_grad, weight_grad)

time: 273 us -> 239 us (0.88)
  starting transfers between devices: 123 us -> 94 us
  Pallas kernels: 45.3 us -> 20.8 us
  waiting for transfers between devices: 71.9 us -> 82.8 us
  local copies, waits for them, and re-layouts: 16.7 us -> 27.3 us
    ppermute x61, starting transfers between devices: 123 us -> 94 us  [permute(): return lax.ppermute(value, AXES, pairs)]
    pallas_call x3, Pallas kernels: 24.1 us -> 8.38 us  [forward_part(): pl.pallas_call(functools.partial(forward_kernel, which), name='forward_ti...]
    pallas_call x3, Pallas kernels: 21.2 us -> 8.27 us  [backward_part(): pl.pallas_call(functools.partial(backward_kernel, which), name='backward_...]
    ppermute x61, waiting for transfers between devices: 71.9 us -> 82.8 us  [permute(): return lax.ppermute(value, AXES, pairs)]
    unnamed x14 -> x24, local copies, waits for them, and re-layouts: 13.8 us -> 24.5 us
    pallas_call x0 -> x1, Pallas kernels: none -> 4.14 us  [pair_tiles(): pl.pallas_call(pair_kernel, name='pair_tiles', out_shape=pltpu.VMEM((SLOT...]
  transfers between devices with their start and end apart: 61 -> 61, of which waited for: 25 -> 24; matrix products, arithmetic and copies ran while one was open for 4% -> 4% of each run, Pallas kernels for 11% -> 5%
where the time goes in v3:
time: 239 us; the launch traced here: 237 us
  starting transfers between devices  94 us (39%)
  waiting for transfers between devices  82.8 us (35%)
  local copies, waits for them, and re-layouts  27.3 us (11%)
  Pallas kernels  20.8 us (9%)
  other arithmetic  5.54 us (2%)
  matrix products  4.44 us (2%)
    ppermute x61, starting transfers between devices, permute(): return lax.ppermute(value, AXES, pairs)  94 us
    ppermute x61, waiting for transfers between devices, permute(): return lax.ppermute(value, AXES, pairs)  82.8 us
    unnamed x24, local copies, waits for them, and re-layouts  24.5 us
    pallas_call x3, Pallas kernels, forward_part(): pl.pallas_call(functools.partial(forward_kernel, which), name='forward_ti...  8.38 us
    pallas_call x3, Pallas kernels, backward_part(): pl.pallas_call(functools.partial(backward_kernel, which), name='backward_...  8.27 us
  transfers between devices with their start and end apart: 61, of which 24 were waited for; matrix products, arithmetic and copies ran while one was open for 4% of the time, Pallas kernels for 5%

profile of v3, /device:TPU:0, one launch (start us, length us, event | category | flops | bytes accessed | tf_op | source)
XLA Modules:
  0.0 236.8 jit_solution(3923553738134123193)
XLA Ops:
  2.3 4.2 %collective-permute-start.3 = (f32[2,128,128]{2,1,0:T(8,128)S(1)}, f32[2,128,128]{2,1,0:T(8,128)S(1)}, u32[]{:S(2)}, u32[]{:S(2)}) collective-permute-start(f32[2,128,128]{2,1,0:T(8,128)S(1)} %get-tuple-element.76), channel_id=1, source_target_pairs={{0,3},{1,0},{2,1},{3,2},{4,7},{5,4},{6,5},{7,6},{8,11},{9,8},{10,9... | collective-permute-start | bytes 393224 | tf_op jit(solution)/shard_map/ppermute | solution.py:36
  10.2 3.7 %collective-permute-start.4 = (f32[2,128,128]{2,1,0:T(8,128)S(1)}, f32[2,128,128]{2,1,0:T(8,128)S(1)}, u32[]{:S(2)}, u32[]{:S(2)}) collective-permute-start(f32[2,128,128]{2,1,0:T(8,128)S(1)} %collective-permute-done.3), channel_id=1, source_target_pairs={{0,3},{1,0},{2,1},{3,2},{4,7},{5,4},{6,5},{7,6},{8,11},{9,8},{10,9... | collective-permute-start | bytes 393224 | tf_op jit(solution)/shard_map/ppermute | solution.py:36
  33.7 4.1 %collective-permute-start.22 = (f32[8,128,128]{2,1,0:T(8,128)S(1)}, f32[8,128,128]{2,1,0:T(8,128)S(1)}, u32[]{:S(2)}, u32[]{:S(2)}) collective-permute-start(f32[8,128,128]{2,1,0:T(8,128)S(1)} %pad_maximum_fusion.1.rest_4_), channel_id=1, source_target_pairs={{0,12},{1,13},{2,14},{3,15},{4,0},{5,1},{6,2},{7,3},{8,4},{9,5},{1... | collective-permute-start | bytes 1572872 | tf_op jit(solution)/shard_map/ppermute | solution.py:36
  45.0 4.1 %collective-permute-done.7 = f32[2,128,128]{2,1,0:T(8,128)} collective-permute-done((f32[2,128,128]{2,1,0:T(8,128)S(1)}, f32[2,128,128]{2,1,0:T(8,128)}, u32[]{:S(2)}, u32[]{:S(2)}) %collective-permute-start.7) | collective-permute-done | bytes 131104 | tf_op jit(solution)/shard_map/ppermute | solution.py:36
  58.7 4.1 %pair_tiles.1.tiles_ref = bf16[256,128,256]{2,1,0:T(8,128)(2,1)S(1)} custom-call(s32[1]{0:T(128)} %bitcast.36.count_ref, f32[256,128,128]{2,1,0:T(8,128)} %bitcast.38), custom_call_target="tpu_custom_call" | custom-call | flops 8800000000 | bytes 1048576 | tf_op jit(solution)/shard_map/pair_tiles/pallas_call | solution.py:114
  62.9 5.8 %copy-done.1 = bf16[256,128,256]{2,1,0:T(8,128)(2,1)} copy-done((bf16[256,128,256]{2,1,0:T(8,128)(2,1)}, bf16[256,128,256]{2,1,0:T(8,128)(2,1)S(1)}, u32[]{:S(2)}) %copy-start.1) | copy-done | bytes 16777240
  68.6 7.1 %collective-permute-done.10.rest_2_ = f32[8,128,128]{2,1,0:T(8,128)S(1)} collective-permute-done((f32[8,128,128]{2,1,0:T(8,128)S(1)}, f32[8,128,128]{2,1,0:T(8,128)S(1)}, u32[]{:S(2)}, u32[]{:S(2)}) %collective-permute-start.10) | collective-permute-done | bytes 524320 | tf_op jit(solution)/shard_map/ppermute | solution.py:36
  82.2 5.8 %copy-done.2 = bf16[256,128,256]{2,1,0:T(8,128)(2,1)S(1)} copy-done((bf16[256,128,256]{2,1,0:T(8,128)(2,1)S(1)}, bf16[256,128,256]{2,1,0:T(8,128)(2,1)}, u32[]{:S(2)}) %copy-start.2) | copy-done | bytes 16777240
  91.1 3.9 %forward_tiles_0.1.rest_6_ = f32[16,128,128]{2,1,0:T(8,128)S(1)} custom-call(s32[4]{0:T(128)S(1)} %convert_reduce_fusion.1.bounds_ref, s32[256]{0:T(256)S(1)} %get-tuple-element.57.order_ref, s32[256]{0:T(256)S(1)} %get-tuple-element.56.rows_ref, s32[256]{0:T(256)S(1)} %get-tuple-element.55.slots_ref, bf16[256,128,256]{2,1,0:T(8,128)(2,1)S(1)} %copy-done.2, ...), custom_call_target="tpu_custom_call" | custom-call | flops 6600000000 | bytes 1048576 | tf_op jit(solution)/shard_map/forward_tiles_0/pallas_call | solution.py:236
  101.7 14.0 %collective-permute-done.26 = f32[8,128,128]{2,1,0:T(8,128)S(1)} collective-permute-done((f32[8,128,128]{2,1,0:T(8,128)S(1)}, f32[8,128,128]{2,1,0:T(8,128)S(1)}, u32[]{:S(2)}, u32[]{:S(2)}) %collective-permute-start.26) | collective-permute-done | bytes 524320 | tf_op jit(solution)/shard_map/ppermute | solution.py:36
  120.5 5.8 %copy-done.3 = bf16[256,128,256]{2,1,0:T(8,128)(2,1)S(1)} copy-done((bf16[256,128,256]{2,1,0:T(8,128)(2,1)S(1)}, bf16[256,128,256]{2,1,0:T(8,128)(2,1)}, u32[]{:S(2)}) %copy-start.3) | copy-done | bytes 16777240
  130.8 3.8 %backward_tiles_0.1 = (f32[8,128,128]{2,1,0:T(8,128)S(1)}, f32[8,128,128]{2,1,0:T(8,128)S(1)}, f32[8,128,128]{2,1,0:T(8,128)S(1)}, f32[8,128,128]{2,1,0:T(8,128)...) custom-call(s32[4]{0:T(128)S(1)} %convert_reduce_fusion.1.bounds_ref, ...), custom_call_target="tpu_custom_call" | custom-call | flops 6600000000 | bytes 1048576 | tf_op jit(solution)/shard_map/backward_tiles_0/pallas_call | solution.py:253
  136.6 7.7 %collective-permute-start.41 = (f32[8,128,128]{2,1,0:T(8,128)S(1)}, f32[8,128,128]{2,1,0:T(8,128)S(1)}, u32[]{:S(2)}, u32[]{:S(2)}) collective-permute-start(f32[8,128,128]{2,1,0:T(8,128)S(1)} %get-tuple-element.30), channel_id=1, source_target_pairs={{0,3},{1,0},{2,1},{3,2},{4,7},{5,4},{6,5},{7,6},{8,11},{9,8},{10,9... | collective-permute-start | bytes 1572872 | tf_op jit(solution)/shard_map/ppermute | solution.py:36
  144.3 8.9 %collective-permute-start.54 = (f32[128,128]{1,0:T(8,128)S(1)}, f32[128,128]{1,0:T(8,128)S(1)}, u32[]{:S(2)}, u32[]{:S(2)}) collective-permute-start(f32[128,128]{1,0:T(8,128)S(1)} %add.304), channel_id=1, source_target_pairs={{0,8},{1,9},{2,10},{3,11},{4,12},{5,13},{6,14},{7,15},{8,0},{9,1},... | collective-permute-start | bytes 196616 | tf_op jit(solution)/shard_map/ppermute | solution.py:36
  155.5 4.3 %collective-permute-done.55 = f32[128,128]{1,0:T(8,128)S(1)} collective-permute-done((f32[128,128]{1,0:T(8,128)S(1)}, f32[128,128]{1,0:T(8,128)S(1)}, u32[]{:S(2)}, u32[]{:S(2)}) %collective-permute-start.55) | collective-permute-done | bytes 65568 | tf_op jit(solution)/shard_map/ppermute | solution.py:36
  169.2 4.6 %collective-permute-done.57 = f32[128,128]{1,0:T(8,128)S(1)} collective-permute-done((f32[128,128]{1,0:T(8,128)S(1)}, f32[128,128]{1,0:T(8,128)S(1)}, u32[]{:S(2)}, u32[]{:S(2)}) %collective-permute-start.57) | collective-permute-done | bytes 65568 | tf_op jit(solution)/shard_map/ppermute | solution.py:36
  173.8 3.7 %collective-permute-start.36 = (f32[8,128,128]{2,1,0:T(8,128)S(1)}, f32[8,128,128]{2,1,0:T(8,128)S(1)}, u32[]{:S(2)}, u32[]{:S(2)}) collective-permute-start(f32[8,128,128]{2,1,0:T(8,128)S(1)} %get-tuple-element.47), channel_id=1, source_target_pairs={{0,12},{1,13},{2,14},{3,15},{4,0},{5,1},{6,2},{7,3},{8,4},{9,5},{1... | collective-permute-start | bytes 1572872 | tf_op jit(solution)/shard_map/ppermute | solution.py:36
  181.9 8.0 %collective-permute-done.36 = f32[8,128,128]{2,1,0:T(8,128)S(1)} collective-permute-done((f32[8,128,128]{2,1,0:T(8,128)S(1)}, f32[8,128,128]{2,1,0:T(8,128)S(1)}, u32[]{:S(2)}, u32[]{:S(2)}) %collective-permute-start.36) | collective-permute-done | bytes 524320 | tf_op jit(solution)/shard_map/ppermute | solution.py:36
  189.9 3.7 %collective-permute-start.48 = (f32[8,128,128]{2,1,0:T(8,128)S(1)}, f32[8,128,128]{2,1,0:T(8,128)S(1)}, u32[]{:S(2)}, u32[]{:S(2)}) collective-permute-start(f32[8,128,128]{2,1,0:T(8,128)S(1)} %add.298), channel_id=1, source_target_pairs={{0,12},{1,13},{2,14},{3,15},{4,0},{5,1},{6,2},{7,3},{8,4},{9,5},{1... | collective-permute-start | bytes 1572872 | tf_op jit(solution)/shard_map/ppermute | solution.py:36
  194.1 4.1 %collective-permute-done.46 = f32[8,128,128]{2,1,0:T(8,128)S(1)} collective-permute-done((f32[8,128,128]{2,1,0:T(8,128)S(1)}, f32[8,128,128]{2,1,0:T(8,128)S(1)}, u32[]{:S(2)}, u32[]{:S(2)}) %collective-permute-start.46) | collective-permute-done | bytes 524320 | tf_op jit(solution)/shard_map/ppermute | solution.py:36
  204.8 3.8 %collective-permute-start.33 = (f32[2,128,128]{2,1,0:T(8,128)S(1)}, f32[2,128,128]{2,1,0:T(8,128)S(1)}, u32[]{:S(2)}, u32[]{:S(2)}) collective-permute-start(f32[2,128,128]{2,1,0:T(8,128)S(1)} %get-tuple-element.67), channel_id=1, source_target_pairs={{0,12},{1,13},{2,14},{3,15},{4,0},{5,1},{6,2},{7,3},{8,4},{9,5},{1... | collective-permute-start | bytes 393224 | tf_op jit(solution)/shard_map/ppermute | solution.py:36
  213.6 3.4 %collective-permute-start.51 = (f32[2,128,128]{2,1,0:T(8,128)S(1)}, f32[2,128,128]{2,1,0:T(8,128)S(1)}, u32[]{:S(2)}, u32[]{:S(2)}) collective-permute-start(f32[2,128,128]{2,1,0:T(8,128)S(1)} %slice_add_fusion), channel_id=1, source_target_pairs={{0,3},{1,0},{2,1},{3,2},{4,7},{5,4},{6,5},{7,6},{8,11},{9,8},{10,9... | collective-permute-start | bytes 393224 | tf_op jit(solution)/shard_map/ppermute | solution.py:36
  222.1 5.4 %collective-permute-done.52 = f32[4,128,128]{2,1,0:T(8,128)S(1)} collective-permute-done((f32[4,128,128]{2,1,0:T(8,128)S(1)}, f32[4,128,128]{2,1,0:T(8,128)S(1)}, u32[]{:S(2)}, u32[]{:S(2)}) %collective-permute-start.52) | collective-permute-done | bytes 262176 | tf_op jit(solution)/shard_map/ppermute | solution.py:36
  228.0 6.0 %collective-permute-done.59 = f32[4,128,128]{2,1,0:T(8,128)S(1)} collective-permute-done((f32[4,128,128]{2,1,0:T(8,128)S(1)}, f32[4,128,128]{2,1,0:T(8,128)S(1)}, u32[]{:S(2)}, u32[]{:S(2)}) %collective-permute-start.59) | collective-permute-done | bytes 262176 | tf_op jit(solution)/shard_map/ppermute | solution.py:36
  (181 shorter events, 105.1 us)
Async XLA Ops:
  30.4 21.7 %collective-permute-start.19 = (f32[8,128,128]{2,1,0:T(8,128)S(1)}, f32[8,128,128]{2,1,0:T(8,128)S(1)}, u32[]{:S(2)}, u32[]{:S(2)}) collective-permute-start(f32[8,128,128]{2,1,0:T(8,128)S(1)} %pad_maximum_fusion.rest_0_), channel_id=1, source_target_pairs={{0,3},{1,0},{2,1},{3,2},{4,7},{5,4},{6,5},{7,6},{8,11},{9,8},{10,9... | collective-permute-start | bytes 1572872 | tf_op jit(solution)/shard_map/ppermute | solution.py:36
  33.7 18.5 %collective-permute-start.22 = (f32[8,128,128]{2,1,0:T(8,128)S(1)}, f32[8,128,128]{2,1,0:T(8,128)S(1)}, u32[]{:S(2)}, u32[]{:S(2)}) collective-permute-start(f32[8,128,128]{2,1,0:T(8,128)S(1)} %pad_maximum_fusion.1.rest_4_), channel_id=1, source_target_pairs={{0,12},{1,13},{2,14},{3,15},{4,0},{5,1},{6,2},{7,3},{8,4},{9,5},{1... | collective-permute-start | bytes 1572872 | tf_op jit(solution)/shard_map/ppermute | solution.py:36
  37.9 17.6 %collective-permute-start.15 = (f32[8,128,128]{2,1,0:T(8,128)S(1)}, f32[8,128,128]{2,1,0:T(8,128)S(1)}, u32[]{:S(2)}, u32[]{:S(2)}) collective-permute-start(f32[8,128,128]{2,1,0:T(8,128)S(1)} %pad_maximum_fusion.3.rest_3_), channel_id=1, source_target_pairs={{0,4},{1,5},{2,6},{3,7},{4,8},{5,9},{6,10},{7,11},{8,12},{9,13},{1... | collective-permute-start | bytes 1572872 | tf_op jit(solution)/shard_map/ppermute | solution.py:36
  49.1 26.6 %collective-permute-start.21 = (f32[8,128,128]{2,1,0:T(8,128)S(1)}, f32[8,128,128]{2,1,0:T(8,128)S(1)}, u32[]{:S(2)}, u32[]{:S(2)}) collective-permute-start(f32[8,128,128]{2,1,0:T(8,128)S(1)} %pad_maximum_fusion.rest_0_), channel_id=1, source_target_pairs={{0,1},{1,2},{2,3},{3,0},{4,5},{5,6},{6,7},{7,4},{8,9},{9,10},{10,1... | collective-permute-start | bytes 1572872 | tf_op jit(solution)/shard_map/ppermute | solution.py:36
  51.1 24.6 %collective-permute-start.24 = (f32[8,128,128]{2,1,0:T(8,128)S(1)}, f32[8,128,128]{2,1,0:T(8,128)S(1)}, u32[]{:S(2)}, u32[]{:S(2)}) collective-permute-start(f32[8,128,128]{2,1,0:T(8,128)S(1)} %pad_maximum_fusion.1.rest_4_), channel_id=1, source_target_pairs={{0,4},{1,5},{2,6},{3,7},{4,8},{5,9},{6,10},{7,11},{8,12},{9,13},{1... | collective-permute-start | bytes 1572872 | tf_op jit(solution)/shard_map/ppermute | solution.py:36
  52.1 23.6 %collective-permute-start.10 = (f32[8,128,128]{2,1,0:T(8,128)S(1)}, f32[8,128,128]{2,1,0:T(8,128)S(1)}, u32[]{:S(2)}, u32[]{:S(2)}) collective-permute-start(f32[8,128,128]{2,1,0:T(8,128)S(1)} %pad_maximum_fusion.2.rest_0_), channel_id=1, source_target_pairs={{0,1},{1,2},{2,3},{3,0},{4,5},{5,6},{6,7},{7,4},{8,9},{9,10},{10,1... | collective-permute-start | bytes 1572872 | tf_op jit(solution)/shard_map/ppermute | solution.py:36
  52.2 26.3 %collective-permute-start.20 = (f32[8,128,128]{2,1,0:T(8,128)S(1)}, f32[8,128,128]{2,1,0:T(8,128)S(1)}, u32[]{:S(2)}, u32[]{:S(2)}) collective-permute-start(f32[8,128,128]{2,1,0:T(8,128)S(1)} %collective-permute-done.19.rest_1_), channel_id=1, source_target_pairs={{0,3},{1,0},{2,1},{3,2},{4,7},{5,4},{6,5},{7,6},{8,11},{9,8},{10,9... | collective-permute-start | bytes 1572872 | tf_op jit(solution)/shard_map/ppermute | solution.py:36
  55.5 25.9 %collective-permute-start.23 = (f32[8,128,128]{2,1,0:T(8,128)S(1)}, f32[8,128,128]{2,1,0:T(8,128)S(1)}, u32[]{:S(2)}, u32[]{:S(2)}) collective-permute-start(f32[8,128,128]{2,1,0:T(8,128)S(1)} %collective-permute-done.22.rest_5_), channel_id=1, source_target_pairs={{0,12},{1,13},{2,14},{3,15},{4,0},{5,1},{6,2},{7,3},{8,4},{9,5},{1... | collective-permute-start | bytes 1572872 | tf_op jit(solution)/shard_map/ppermute | solution.py:36
  75.7 19.3 %collective-permute-start.17 = (f32[8,128,128]{2,1,0:T(8,128)S(1)}, f32[8,128,128]{2,1,0:T(8,128)S(1)}, u32[]{:S(2)}, u32[]{:S(2)}) collective-permute-start(f32[8,128,128]{2,1,0:T(8,128)S(1)} %pad_maximum_fusion.2.rest_0_), channel_id=1, source_target_pairs={{0,3},{1,0},{2,1},{3,2},{4,7},{5,4},{6,5},{7,6},{8,11},{9,8},{10,9... | collective-permute-start | bytes 1572872 | tf_op jit(solution)/shard_map/ppermute | solution.py:36
  75.7 19.3 %collective-permute-start.18 = (f32[8,128,128]{2,1,0:T(8,128)S(1)}, f32[8,128,128]{2,1,0:T(8,128)S(1)}, u32[]{:S(2)}, u32[]{:S(2)}) collective-permute-start(f32[8,128,128]{2,1,0:T(8,128)S(1)} %pad_maximum_fusion.3.rest_3_), channel_id=1, source_target_pairs={{0,12},{1,13},{2,14},{3,15},{4,0},{5,1},{6,2},{7,3},{8,4},{9,5},{1... | collective-permute-start | bytes 1572872 | tf_op jit(solution)/shard_map/ppermute | solution.py:36
  76.5 21.1 %collective-permute-start.11 = (f32[8,128,128]{2,1,0:T(8,128)S(1)}, f32[8,128,128]{2,1,0:T(8,128)S(1)}, u32[]{:S(2)}, u32[]{:S(2)}) collective-permute-start(f32[8,128,128]{2,1,0:T(8,128)S(1)} %collective-permute-done.10.rest_2_), channel_id=1, source_target_pairs={{0,1},{1,2},{2,3},{3,0},{4,5},{5,6},{6,7},{7,4},{8,9},{9,10},{10,1... | collective-permute-start | bytes 1572872 | tf_op jit(solution)/shard_map/ppermute | solution.py:36
  79.4 18.3 %collective-permute-start.16 = (f32[8,128,128]{2,1,0:T(8,128)S(1)}, f32[8,128,128]{2,1,0:T(8,128)S(1)}, u32[]{:S(2)}, u32[]{:S(2)}) collective-permute-start(f32[8,128,128]{2,1,0:T(8,128)S(1)} %collective-permute-done.15.rest_5_), channel_id=1, source_target_pairs={{0,4},{1,5},{2,6},{3,7},{4,8},{5,9},{6,10},{7,11},{8,12},{9,13},{1... | collective-permute-start | bytes 1572872 | tf_op jit(solution)/shard_map/ppermute | solution.py:36
  134.5 30.0 %collective-permute-start.28 = (f32[8,128,128]{2,1,0:T(8,128)S(1)}, f32[8,128,128]{2,1,0:T(8,128)S(1)}, u32[]{:S(2)}, u32[]{:S(2)}) collective-permute-start(f32[8,128,128]{2,1,0:T(8,128)S(1)} %get-tuple-element.42), channel_id=1, source_target_pairs={{0,1},{1,2},{2,3},{3,0},{4,5},{5,6},{6,7},{7,4},{8,9},{9,10},{10,1... | collective-permute-start | bytes 1572872 | tf_op jit(solution)/shard_map/ppermute | solution.py:36
  134.6 33.3 %collective-permute-start.34 = (f32[8,128,128]{2,1,0:T(8,128)S(1)}, f32[8,128,128]{2,1,0:T(8,128)S(1)}, u32[]{:S(2)}, u32[]{:S(2)}) collective-permute-start(f32[8,128,128]{2,1,0:T(8,128)S(1)} %get-tuple-element.46), channel_id=1, source_target_pairs={{0,4},{1,5},{2,6},{3,7},{4,8},{5,9},{6,10},{7,11},{8,12},{9,13},{1... | collective-permute-start | bytes 1572872 | tf_op jit(solution)/shard_map/ppermute | solution.py:36
  136.6 40.9 %collective-permute-start.41 = (f32[8,128,128]{2,1,0:T(8,128)S(1)}, f32[8,128,128]{2,1,0:T(8,128)S(1)}, u32[]{:S(2)}, u32[]{:S(2)}) collective-permute-start(f32[8,128,128]{2,1,0:T(8,128)S(1)} %get-tuple-element.30), channel_id=1, source_target_pairs={{0,3},{1,0},{2,1},{3,2},{4,7},{5,4},{6,5},{7,6},{8,11},{9,8},{10,9... | collective-permute-start | bytes 1572872 | tf_op jit(solution)/shard_map/ppermute | solution.py:36
  162.4 15.8 %collective-permute-start.47 = (f32[8,128,128]{2,1,0:T(8,128)S(1)}, f32[8,128,128]{2,1,0:T(8,128)S(1)}, u32[]{:S(2)}, u32[]{:S(2)}) collective-permute-start(f32[8,128,128]{2,1,0:T(8,128)S(1)} %get-tuple-element.31), channel_id=1, source_target_pairs={{0,12},{1,13},{2,14},{3,15},{4,0},{5,1},{6,2},{7,3},{8,4},{9,5},{1... | collective-permute-start | bytes 1572872 | tf_op jit(solution)/shard_map/ppermute | solution.py:36
  173.8 16.1 %collective-permute-start.36 = (f32[8,128,128]{2,1,0:T(8,128)S(1)}, f32[8,128,128]{2,1,0:T(8,128)S(1)}, u32[]{:S(2)}, u32[]{:S(2)}) collective-permute-start(f32[8,128,128]{2,1,0:T(8,128)S(1)} %get-tuple-element.47), channel_id=1, source_target_pairs={{0,12},{1,13},{2,14},{3,15},{4,0},{5,1},{6,2},{7,3},{8,4},{9,5},{1... | collective-permute-start | bytes 1572872 | tf_op jit(solution)/shard_map/ppermute | solution.py:36
  177.5 16.1 %collective-permute-start.35 = (f32[8,128,128]{2,1,0:T(8,128)S(1)}, f32[8,128,128]{2,1,0:T(8,128)S(1)}, u32[]{:S(2)}, u32[]{:S(2)}) collective-permute-start(f32[8,128,128]{2,1,0:T(8,128)S(1)} %add.285), channel_id=1, source_target_pairs={{0,4},{1,5},{2,6},{3,7},{4,8},{5,9},{6,10},{7,11},{8,12},{9,13},{1... | collective-permute-start | bytes 1572872 | tf_op jit(solution)/shard_map/ppermute | solution.py:36
  178.2 15.5 %collective-permute-start.40 = (f32[8,128,128]{2,1,0:T(8,128)S(1)}, f32[8,128,128]{2,1,0:T(8,128)S(1)}, u32[]{:S(2)}, u32[]{:S(2)}) collective-permute-start(f32[8,128,128]{2,1,0:T(8,128)S(1)} %get-tuple-element.34), channel_id=1, source_target_pairs={{0,1},{1,2},{2,3},{3,0},{4,5},{5,6},{6,7},{7,4},{8,9},{9,10},{10,1... | collective-permute-start | bytes 1572872 | tf_op jit(solution)/shard_map/ppermute | solution.py:36
  178.4 19.7 %collective-permute-start.46 = (f32[8,128,128]{2,1,0:T(8,128)S(1)}, f32[8,128,128]{2,1,0:T(8,128)S(1)}, u32[]{:S(2)}, u32[]{:S(2)}) collective-permute-start(f32[8,128,128]{2,1,0:T(8,128)S(1)} %get-tuple-element.37), channel_id=1, source_target_pairs={{0,4},{1,5},{2,6},{3,7},{4,8},{5,9},{6,10},{7,11},{8,12},{9,13},{1... | collective-permute-start | bytes 1572872 | tf_op jit(solution)/shard_map/ppermute | solution.py:36
  193.9 16.9 %collective-permute-start.43 = (f32[2,128,128]{2,1,0:T(8,128)S(1)}, f32[2,128,128]{2,1,0:T(8,128)S(1)}, u32[]{:S(2)}, u32[]{:S(2)}) collective-permute-start(f32[2,128,128]{2,1,0:T(8,128)S(1)} %get-tuple-element.70), channel_id=1, source_target_pairs={{0,4},{1,5},{2,6},{3,7},{4,8},{5,9},{6,10},{7,11},{8,12},{9,13},{1... | collective-permute-start | bytes 393224 | tf_op jit(solution)/shard_map/ppermute | solution.py:36
  201.3 15.7 %collective-permute-start.49 = (f32[2,128,128]{2,1,0:T(8,128)S(1)}, f32[2,128,128]{2,1,0:T(8,128)S(1)}, u32[]{:S(2)}, u32[]{:S(2)}) collective-permute-start(f32[2,128,128]{2,1,0:T(8,128)S(1)} %get-tuple-element.72), channel_id=1, source_target_pairs={{0,1},{1,2},{2,3},{3,0},{4,5},{5,6},{6,7},{7,4},{8,9},{9,10},{10,1... | collective-permute-start | bytes 393224 | tf_op jit(solution)/shard_map/ppermute | solution.py:36
  204.7 15.5 %collective-permute-start.32 = (f32[2,128,128]{2,1,0:T(8,128)S(1)}, f32[2,128,128]{2,1,0:T(8,128)S(1)}, u32[]{:S(2)}, u32[]{:S(2)}) collective-permute-start(f32[2,128,128]{2,1,0:T(8,128)S(1)} %get-tuple-element.66), channel_id=1, source_target_pairs={{0,4},{1,5},{2,6},{3,7},{4,8},{5,9},{6,10},{7,11},{8,12},{9,13},{1... | collective-permute-start | bytes 393224 | tf_op jit(solution)/shard_map/ppermute | solution.py:36
  204.8 15.4 %collective-permute-start.33 = (f32[2,128,128]{2,1,0:T(8,128)S(1)}, f32[2,128,128]{2,1,0:T(8,128)S(1)}, u32[]{:S(2)}, u32[]{:S(2)}) collective-permute-start(f32[2,128,128]{2,1,0:T(8,128)S(1)} %get-tuple-element.67), channel_id=1, source_target_pairs={{0,12},{1,13},{2,14},{3,15},{4,0},{5,1},{6,2},{7,3},{8,4},{9,5},{1... | collective-permute-start | bytes 393224 | tf_op jit(solution)/shard_map/ppermute | solution.py:36
  (48 other events, 460.1 us)

commit v4 on v3

--- a/solution.py
+++ b/solution.py
@@ -15,10 +15,10 @@
 GROUP = 16
 CHUNK = 32
 STAGES = 3
-PAIR_BYTES = 40 * 1024 * 1024
+PAIR_BYTES = 8 * 1024 * 1024
 PER = 8
 CLASS_BUFFERS = (8, 6, 2)
-VMEM_BYTES = 24 * 1024 * 1024
+VMEM_BYTES = 8 * 1024 * 1024
 
 
 def device_index(y, core, x, z):
@@ -340,17 +340,39 @@
     return near, apart
 
 
-def scatter_terms(own, apart, apart_far):
-    first = [apart[0], apart[1], apart_far[0], apart[2]]
-    second = [apart[3], apart[4], apart_far[1], apart[5]]
-    pieces = []
-    for row, column, near in ((first, second, False), (own[:4], own[4:], True)):
-        row = reduce_ring(row, z_up, z_down, near)
-        column = reduce_ring(column, x_up, x_down, near)
-        half = reduce_ring([row[2 * i : 2 * i + 2] for i in range(4)], x_up, x_down, near)
-        other = reduce_ring([column[2 * i : 2 * i + 2] for i in range(4)], z_up, z_down, near)
-        pieces.append(jnp.concatenate([half, other], axis=0))
-    return pieces[1] + permute(pieces[0], y_far)
+def scatter_terms(own, apart, apart_far, weight_term):
+    row_sent = permute(apart_far[0], z_down)
+    column_sent = permute(apart_far[1], x_down)
+    weight_term = flip_add(after(weight_term, row_sent), "x", 1)
+    row_one, column_one = permute(apart[1], z_up), permute(apart[4], x_up)
+    row_three = permute(apart[2] + row_sent, z_down)
+    column_three = permute(apart[5] + column_sent, x_down)
+    row = apart[0] + row_one + row_three
+    column = apart[3] + column_one + column_three
+    weight_term = flip_add(after(weight_term, column), "x", 2)
+    apart_half = reduce_ring(split_row(row), x_up, x_down, False)
+    apart_other = reduce_ring(split_row(column), z_up, z_down, False)
+    sent = permute(jnp.concatenate([apart_half, apart_other], axis=0), y_far)
+
+    row = reduce_ring(own[:4], z_up, z_down, True)
+    weight_term = flip_add(after(weight_term, row), "z", 1)
+    column = reduce_ring(own[4:], x_up, x_down, True)
+    weight_term = flip_add(after(weight_term, column), "z", 2)
+    half = reduce_ring(split_row(row), x_up, x_down, True)
+    other = reduce_ring(split_row(column), z_up, z_down, True)
+    kept = jnp.concatenate([half, other], axis=0)
+    total = after(kept, weight_term) + sent
+    return total, weight_term + permute(weight_term, y_far)
+
+
+def split_row(row):
+    return [row[2 * i : 2 * i + 2] for i in range(4)]
+
+
+def flip_add(value, axis, step):
+    if axis == "x":
+        return value + permute(value, lambda y, c, x, z: (y, c, x ^ step, z))
+    return value + permute(value, lambda y, c, x, z: (y, c, x, z ^ step))
 
 
 def sum_over_loop(partial, loop):
@@ -368,14 +390,6 @@
     )
 
 
-def sum_over_wide(value):
-    for step in (1, 2):
-        value = value + permute(value, lambda y, c, x, z: (y, c, x ^ step, z))
-    for step in (1, 2):
-        value = value + permute(value, lambda y, c, x, z: (y, c, x, z ^ step))
-    return value + permute(value, y_far)
-
-
 def gather_loop(own, loop):
     low, core = loop // 2, loop % 2
     across = permute(own, y_pair)
@@ -421,9 +435,7 @@
     apart_far = backward_part(2, plan, pairs, spread)
     apart = backward_part(1, plan, pairs, after(spread, *apart_far))
     own = backward_part(0, plan, pairs, after(spread, *apart))
-    weight_grad = sum_over_wide(weight_term)
-    input_cols = scatter_terms(own, apart, apart_far)
-    input_cols = after(input_cols, weight_grad)
+    input_cols, weight_grad = scatter_terms(own, apart, apart_far, weight_term)
     input_grad = gather_loop(input_cols, loop)
     return (activated, input_grad, weight_grad)
 

time: 239 us -> 220 us (0.921)
  local copies, waits for them, and re-layouts: 27.3 us -> 16 us
  starting transfers between devices: 94 us -> 85.3 us
  Pallas kernels: 20.8 us -> 27 us
  waiting for transfers between devices: 82.8 us -> 79.4 us
    unnamed x24 -> x12, local copies, waits for them, and re-layouts: 24.5 us -> 13.2 us
    ppermute x61, starting transfers between devices: 94 us -> 85.3 us  [permute(): return lax.ppermute(value, AXES, pairs)]
    ppermute x61, waiting for transfers between devices: 82.8 us -> 79.4 us  [permute(): return lax.ppermute(value, AXES, pairs)]
    pallas_call x3, Pallas kernels: 8.27 us -> 11.5 us  [backward_part(): pl.pallas_call(functools.partial(backward_kernel, which), name='backward_...]
    pallas_call x3, Pallas kernels: 8.38 us -> 11.6 us  [forward_part(): pl.pallas_call(functools.partial(forward_kernel, which), name='forward_ti...]
  transfers between devices with their start and end apart: 61 -> 61, of which waited for: 24 -> 25; matrix products, arithmetic and copies ran while one was open for 4% -> 4% of each run, Pallas kernels for 5% -> 10%
where the time goes in v4:
time: 220 us
  starting transfers between devices  85.3 us (39%)
  waiting for transfers between devices  79.4 us (36%)
  Pallas kernels  27 us (12%)
  local copies, waits for them, and re-layouts  16 us (7%)
  other arithmetic  5.56 us (3%)
  matrix products  4.44 us (2%)
    ppermute x61, starting transfers between devices, permute(): return lax.ppermute(value, AXES, pairs)  85.3 us
    ppermute x61, waiting for transfers between devices, permute(): return lax.ppermute(value, AXES, pairs)  79.4 us
    unnamed x12, local copies, waits for them, and re-layouts  13.2 us
    pallas_call x3, Pallas kernels, forward_part(): pl.pallas_call(functools.partial(forward_kernel, which), name='forward_ti...  11.6 us
    pallas_call x3, Pallas kernels, backward_part(): pl.pallas_call(functools.partial(backward_kernel, which), name='backward_...  11.5 us
  transfers between devices with their start and end apart: 61, of which 25 were waited for; matrix products, arithmetic and copies ran while one was open for 4% of the time, Pallas kernels for 10%

profile of v4, /device:TPU:0, one launch (start us, length us, event | category | flops | bytes accessed | tf_op | source)
XLA Modules:
  0.0 219.7 jit_solution(17032976878377867542)
XLA Ops:
  2.3 4.2 %collective-permute-start.3 = (f32[2,128,128]{2,1,0:T(8,128)S(1)}, f32[2,128,128]{2,1,0:T(8,128)S(1)}, u32[]{:S(2)}, u32[]{:S(2)}) collective-permute-start(f32[2,128,128]{2,1,0:T(8,128)S(1)} %get-tuple-element.84), channel_id=1, source_target_pairs={{0,3},{1,0},{2,1},{3,2},{4,7},{5,4},{6,5},{7,6},{8,11},{9,8},{10,9... | collective-permute-start | bytes 393224 | tf_op jit(solution)/shard_map/ppermute | solution.py:36
  10.2 3.7 %collective-permute-start.4 = (f32[2,128,128]{2,1,0:T(8,128)S(1)}, f32[2,128,128]{2,1,0:T(8,128)S(1)}, u32[]{:S(2)}, u32[]{:S(2)}) collective-permute-start(f32[2,128,128]{2,1,0:T(8,128)S(1)} %collective-permute-done.3), channel_id=1, source_target_pairs={{0,3},{1,0},{2,1},{3,2},{4,7},{5,4},{6,5},{7,6},{8,11},{9,8},{10,9... | collective-permute-start | bytes 393224 | tf_op jit(solution)/shard_map/ppermute | solution.py:36
  24.3 3.3 %collective-permute-start.12 = (f32[2,128,128]{2,1,0:T(8,128)S(1)}, f32[2,128,128]{2,1,0:T(8,128)S(1)}, u32[]{:S(2)}, u32[]{:S(2)}) collective-permute-start(f32[2,128,128]{2,1,0:T(8,128)S(1)} %get-tuple-element.82), channel_id=1, source_target_pairs={{0,3},{1,0},{2,1},{3,2},{4,7},{5,4},{6,5},{7,6},{8,11},{9,8},{10,9... | collective-permute-start | bytes 393224 | tf_op jit(solution)/shard_map/ppermute | solution.py:36
  43.9 4.8 %collective-permute-done.7 = f32[2,128,128]{2,1,0:T(8,128)} collective-permute-done((f32[2,128,128]{2,1,0:T(8,128)S(1)}, f32[2,128,128]{2,1,0:T(8,128)}, u32[]{:S(2)}, u32[]{:S(2)}) %collective-permute-start.7) | collective-permute-done | bytes 131104 | tf_op jit(solution)/shard_map/ppermute | solution.py:36
  56.9 5.8 %copy-done.3 = f32[1,1,256,128,128]{4,3,2,1,0:T(8,128)S(1)} copy-done((f32[1,1,256,128,128]{4,3,2,1,0:T(8,128)S(1)}, f32[1,1,256,128,128]{4,3,2,1,0:T(8,128)}, u32[]{:S(2)}) %copy-start.3) | copy-done | bytes 16777240
  62.7 4.0 %pair_tiles.1.tiles_ref = bf16[256,128,256]{2,1,0:T(8,128)(2,1)S(1)} custom-call(s32[1]{0:T(128)} %bitcast.36.count_ref, f32[256,128,128]{2,1,0:T(8,128)S(1)} %bitcast.38), custom_call_target="tpu_custom_call" | custom-call | flops 8800000000 | bytes 1048576 | tf_op jit(solution)/shard_map/pair_tiles/pallas_call | solution.py:114
  66.7 7.2 %collective-permute-done.10.rest_2_ = f32[8,128,128]{2,1,0:T(8,128)S(1)} collective-permute-done((f32[8,128,128]{2,1,0:T(8,128)S(1)}, f32[8,128,128]{2,1,0:T(8,128)S(1)}, u32[]{:S(2)}, u32[]{:S(2)}) %collective-permute-start.10) | collective-permute-done | bytes 524320 | tf_op jit(solution)/shard_map/ppermute | solution.py:36
  78.8 5.3 %forward_tiles_0.1.rest_6_ = f32[16,128,128]{2,1,0:T(8,128)S(1)} custom-call(s32[4]{0:T(128)S(1)} %convert_reduce_fusion.1.bounds_ref, s32[256]{0:T(256)S(1)} %get-tuple-element.65.order_ref, s32[256]{0:T(256)S(1)} %get-tuple-element.64.rows_ref, s32[256]{0:T(256)S(1)} %get-tuple-element.63.slots_ref, bf16[256,128,256]{2,1,0:T(8,128)(2,1)S(1)} %pair_tiles.1.tiles_ref, ...), custom_call_target="tpu_custom_call" | custom-call | flops 6600000000 | bytes 1048576 | tf_op jit(solution)/shard_map/forward_tiles_0/pallas_call | solution.py:236
  85.9 4.0 %forward_tiles_1.1.rest_2_ = f32[16,128,128]{2,1,0:T(8,128)S(1)} custom-call(s32[4]{0:T(128)S(1)} %convert_reduce_fusion.1.bounds_ref, s32[256]{0:T(256)S(1)} %get-tuple-element.65.order_ref, s32[256]{0:T(256)S(1)} %get-tuple-element.64.rows_ref, s32[256]{0:T(256)S(1)} %get-tuple-element.63.slots_ref, bf16[256,128,256]{2,1,0:T(8,128)(2,1)S(1)} %pair_tiles.1.tiles_ref, ...), custom_call_target="tpu_custom_call" | custom-call | flops 5500000256 | bytes 1048576 | tf_op jit(solution)/shard_map/forward_tiles_1/pallas_call | solution.py:236
  94.4 14.0 %collective-permute-done.26 = f32[8,128,128]{2,1,0:T(8,128)S(1)} collective-permute-done((f32[8,128,128]{2,1,0:T(8,128)S(1)}, f32[8,128,128]{2,1,0:T(8,128)S(1)}, u32[]{:S(2)}, u32[]{:S(2)}) %collective-permute-start.26) | collective-permute-done | bytes 524320 | tf_op jit(solution)/shard_map/ppermute | solution.py:36
  113.2 5.8 %copy-done.2 = bf16[256,128,256]{2,1,0:T(8,128)(2,1)S(1)} copy-done((bf16[256,128,256]{2,1,0:T(8,128)(2,1)S(1)}, bf16[256,128,256]{2,1,0:T(8,128)(2,1)}, u32[]{:S(2)}) %copy-start.2) | copy-done | bytes 16777240
  121.9 4.0 %backward_tiles_1.1 = (f32[8,128,128]{2,1,0:T(8,128)S(1)}, f32[8,128,128]{2,1,0:T(8,128)S(1)}, f32[8,128,128]{2,1,0:T(8,128)S(1)}, f32[8,128,128]{2,1,0:T(8,128)...) custom-call(s32[4]{0:T(128)S(1)} %convert_reduce_fusion.1.bounds_ref, s32[256]{0:T(256)S(1)} %get-tuple-element.65.order_ref, ...), custom_call_target="tpu_custom_call" | custom-call | flops 5500000256 | bytes 1048576 | tf_op jit(solution)/shard_map/backward_tiles_1/pallas_call | solution.py:253
  126.0 5.1 %backward_tiles_0.1 = (f32[8,128,128]{2,1,0:T(8,128)S(1)}, f32[8,128,128]{2,1,0:T(8,128)S(1)}, f32[8,128,128]{2,1,0:T(8,128)S(1)}, f32[8,128,128]{2,1,0:T(8,128)...) custom-call(s32[4]{0:T(128)S(1)} %convert_reduce_fusion.1.bounds_ref, ...), custom_call_target="tpu_custom_call" | custom-call | flops 6600000000 | bytes 1048576 | tf_op jit(solution)/shard_map/backward_tiles_0/pallas_call | solution.py:253
  131.4 3.5 %collective-permute-start.44 = (f32[8,128,128]{2,1,0:T(8,128)S(1)}, f32[8,128,128]{2,1,0:T(8,128)S(1)}, u32[]{:S(2)}, u32[]{:S(2)}) collective-permute-start(f32[8,128,128]{2,1,0:T(8,128)S(1)} %add.293), channel_id=1, source_target_pairs={{0,12},{1,13},{2,14},{3,15},{4,0},{5,1},{6,2},{7,3},{8,4},{9,5},{1... | collective-permute-start | bytes 1572872 | tf_op jit(solution)/shard_map/ppermute | solution.py:36
  138.1 3.5 %collective-permute-done.28 = f32[8,128,128]{2,1,0:T(8,128)S(1)} collective-permute-done((f32[8,128,128]{2,1,0:T(8,128)S(1)}, f32[8,128,128]{2,1,0:T(8,128)S(1)}, u32[]{:S(2)}, u32[]{:S(2)}) %collective-permute-start.28) | collective-permute-done | bytes 524320 | tf_op jit(solution)/shard_map/ppermute | solution.py:36
  143.4 6.0 %collective-permute-start.49 = (f32[8,128,128]{2,1,0:T(8,128)S(1)}, f32[8,128,128]{2,1,0:T(8,128)S(1)}, u32[]{:S(2)}, u32[]{:S(2)}) collective-permute-start(f32[8,128,128]{2,1,0:T(8,128)S(1)} %add.299), channel_id=1, source_target_pairs={{0,3},{1,0},{2,1},{3,2},{4,7},{5,4},{6,5},{7,6},{8,11},{9,8},{10,9... | collective-permute-start | bytes 1572872 | tf_op jit(solution)/shard_map/ppermute | solution.py:36
  160.1 6.5 %collective-permute-done.30 = f32[8,128,128]{2,1,0:T(8,128)S(1)} collective-permute-done((f32[8,128,128]{2,1,0:T(8,128)S(1)}, f32[8,128,128]{2,1,0:T(8,128)S(1)}, u32[]{:S(2)}, u32[]{:S(2)}) %collective-permute-start.30) | collective-permute-done | bytes 524320 | tf_op jit(solution)/shard_map/ppermute | solution.py:36
  166.7 3.7 %collective-permute-start.51 = (f32[2,128,128]{2,1,0:T(8,128)S(1)}, f32[2,128,128]{2,1,0:T(8,128)S(1)}, u32[]{:S(2)}, u32[]{:S(2)}) collective-permute-start(f32[2,128,128]{2,1,0:T(8,128)S(1)} %get-tuple-element.75), channel_id=1, source_target_pairs={{0,12},{1,13},{2,14},{3,15},{4,0},{5,1},{6,2},{7,3},{8,4},{9,5},{1... | collective-permute-start | bytes 393224 | tf_op jit(solution)/shard_map/ppermute | solution.py:36
  174.0 4.1 %collective-permute-done.46 = f32[128,128]{1,0:T(8,128)S(1)} collective-permute-done((f32[128,128]{1,0:T(8,128)S(1)}, f32[128,128]{1,0:T(8,128)S(1)}, u32[]{:S(2)}, u32[]{:S(2)}) %collective-permute-start.46) | collective-permute-done | bytes 65568 | tf_op jit(solution)/shard_map/ppermute | solution.py:36
  183.0 3.9 %collective-permute-start.52 = (f32[2,128,128]{2,1,0:T(8,128)S(1)}, f32[2,128,128]{2,1,0:T(8,128)S(1)}, u32[]{:S(2)}, u32[]{:S(2)}) collective-permute-start(f32[2,128,128]{2,1,0:T(8,128)S(1)} %slice_add_fusion.2), channel_id=1, source_target_pairs={{0,12},{1,13},{2,14},{3,15},{4,0},{5,1},{6,2},{7,3},{8,4},{9,5},{1... | collective-permute-start | bytes 393224 | tf_op jit(solution)/shard_map/ppermute | solution.py:36
  188.5 3.2 %collective-permute-start.33 = (f32[2,128,128]{2,1,0:T(8,128)S(1)}, f32[2,128,128]{2,1,0:T(8,128)S(1)}, u32[]{:S(2)}, u32[]{:S(2)}) collective-permute-start(f32[2,128,128]{2,1,0:T(8,128)S(1)} %get-tuple-element.79), channel_id=1, source_target_pairs={{0,12},{1,13},{2,14},{3,15},{4,0},{5,1},{6,2},{7,3},{8,4},{9,5},{1... | collective-permute-start | bytes 393224 | tf_op jit(solution)/shard_map/ppermute | solution.py:36
  198.9 6.4 %collective-permute-done.56 = f32[4,128,128]{2,1,0:T(8,128)S(1)} collective-permute-done((f32[4,128,128]{2,1,0:T(8,128)S(1)}, f32[4,128,128]{2,1,0:T(8,128)S(1)}, u32[]{:S(2)}, u32[]{:S(2)}) %collective-permute-start.56) | collective-permute-done | bytes 262176 | tf_op jit(solution)/shard_map/ppermute | solution.py:36
  205.5 6.3 %collective-permute-done.58 = f32[4,128,128]{2,1,0:T(8,128)S(1)} collective-permute-done((f32[4,128,128]{2,1,0:T(8,128)S(1)}, f32[4,128,128]{2,1,0:T(8,128)S(1)}, u32[]{:S(2)}, u32[]{:S(2)}) %collective-permute-start.58) | collective-permute-done | bytes 262176 | tf_op jit(solution)/shard_map/ppermute | solution.py:36
  213.1 4.7 %collective-permute-done.60 = f32[128,128]{1,0:T(8,128)S(1)} collective-permute-done((f32[128,128]{1,0:T(8,128)S(1)}, f32[128,128]{1,0:T(8,128)S(1)}, u32[]{:S(2)}, u32[]{:S(2)}) %collective-permute-start.60) | collective-permute-done | bytes 65568 | tf_op jit(solution)/shard_map/ppermute | solution.py:36
  (170 shorter events, 94.9 us)
Async XLA Ops:
  30.4 21.1 %collective-permute-start.22 = (f32[8,128,128]{2,1,0:T(8,128)S(1)}, f32[8,128,128]{2,1,0:T(8,128)S(1)}, u32[]{:S(2)}, u32[]{:S(2)}) collective-permute-start(f32[8,128,128]{2,1,0:T(8,128)S(1)} %pad_maximum_fusion.1.rest_4_), channel_id=1, source_target_pairs={{0,12},{1,13},{2,14},{3,15},{4,0},{5,1},{6,2},{7,3},{8,4},{9,5},{1... | collective-permute-start | bytes 1572872 | tf_op jit(solution)/shard_map/ppermute | solution.py:36
  33.5 19.1 %collective-permute-start.19 = (f32[8,128,128]{2,1,0:T(8,128)S(1)}, f32[8,128,128]{2,1,0:T(8,128)S(1)}, u32[]{:S(2)}, u32[]{:S(2)}) collective-permute-start(f32[8,128,128]{2,1,0:T(8,128)S(1)} %pad_maximum_fusion.rest_0_), channel_id=1, source_target_pairs={{0,3},{1,0},{2,1},{3,2},{4,7},{5,4},{6,5},{7,6},{8,11},{9,8},{10,9... | collective-permute-start | bytes 1572872 | tf_op jit(solution)/shard_map/ppermute | solution.py:36
  37.4 17.1 %collective-permute-start.15 = (f32[8,128,128]{2,1,0:T(8,128)S(1)}, f32[8,128,128]{2,1,0:T(8,128)S(1)}, u32[]{:S(2)}, u32[]{:S(2)}) collective-permute-start(f32[8,128,128]{2,1,0:T(8,128)S(1)} %pad_maximum_fusion.3.rest_3_), channel_id=1, source_target_pairs={{0,4},{1,5},{2,6},{3,7},{4,8},{5,9},{6,10},{7,11},{8,12},{9,13},{1... | collective-permute-start | bytes 1572872 | tf_op jit(solution)/shard_map/ppermute | solution.py:36
  48.7 28.0 %collective-permute-start.24 = (f32[8,128,128]{2,1,0:T(8,128)S(1)}, f32[8,128,128]{2,1,0:T(8,128)S(1)}, u32[]{:S(2)}, u32[]{:S(2)}) collective-permute-start(f32[8,128,128]{2,1,0:T(8,128)S(1)} %pad_maximum_fusion.1.rest_4_), channel_id=1, source_target_pairs={{0,4},{1,5},{2,6},{3,7},{4,8},{5,9},{6,10},{7,11},{8,12},{9,13},{1... | collective-permute-start | bytes 1572872 | tf_op jit(solution)/shard_map/ppermute | solution.py:36
  50.6 26.2 %collective-permute-start.21 = (f32[8,128,128]{2,1,0:T(8,128)S(1)}, f32[8,128,128]{2,1,0:T(8,128)S(1)}, u32[]{:S(2)}, u32[]{:S(2)}) collective-permute-start(f32[8,128,128]{2,1,0:T(8,128)S(1)} %pad_maximum_fusion.rest_0_), channel_id=1, source_target_pairs={{0,1},{1,2},{2,3},{3,0},{4,5},{5,6},{6,7},{7,4},{8,9},{9,10},{10,1... | collective-permute-start | bytes 1572872 | tf_op jit(solution)/shard_map/ppermute | solution.py:36
  51.6 22.3 %collective-permute-start.10 = (f32[8,128,128]{2,1,0:T(8,128)S(1)}, f32[8,128,128]{2,1,0:T(8,128)S(1)}, u32[]{:S(2)}, u32[]{:S(2)}) collective-permute-start(f32[8,128,128]{2,1,0:T(8,128)S(1)} %pad_maximum_fusion.2.rest_0_), channel_id=1, source_target_pairs={{0,1},{1,2},{2,3},{3,0},{4,5},{5,6},{6,7},{7,4},{8,9},{9,10},{10,1... | collective-permute-start | bytes 1572872 | tf_op jit(solution)/shard_map/ppermute | solution.py:36
  52.6 24.2 %collective-permute-start.23 = (f32[8,128,128]{2,1,0:T(8,128)S(1)}, f32[8,128,128]{2,1,0:T(8,128)S(1)}, u32[]{:S(2)}, u32[]{:S(2)}) collective-permute-start(f32[8,128,128]{2,1,0:T(8,128)S(1)} %collective-permute-done.22.rest_5_), channel_id=1, source_target_pairs={{0,12},{1,13},{2,14},{3,15},{4,0},{5,1},{6,2},{7,3},{8,4},{9,5},{1... | collective-permute-start | bytes 1572872 | tf_op jit(solution)/shard_map/ppermute | solution.py:36
  54.6 24.3 %collective-permute-start.20 = (f32[8,128,128]{2,1,0:T(8,128)S(1)}, f32[8,128,128]{2,1,0:T(8,128)S(1)}, u32[]{:S(2)}, u32[]{:S(2)}) collective-permute-start(f32[8,128,128]{2,1,0:T(8,128)S(1)} %collective-permute-done.19.rest_1_), channel_id=1, source_target_pairs={{0,3},{1,0},{2,1},{3,2},{4,7},{5,4},{6,5},{7,6},{8,11},{9,8},{10,9... | collective-permute-start | bytes 1572872 | tf_op jit(solution)/shard_map/ppermute | solution.py:36
  76.7 13.2 %collective-permute-start.16 = (f32[8,128,128]{2,1,0:T(8,128)S(1)}, f32[8,128,128]{2,1,0:T(8,128)S(1)}, u32[]{:S(2)}, u32[]{:S(2)}) collective-permute-start(f32[8,128,128]{2,1,0:T(8,128)S(1)} %collective-permute-done.15.rest_5_), channel_id=1, source_target_pairs={{0,4},{1,5},{2,6},{3,7},{4,8},{5,9},{6,10},{7,11},{8,12},{9,13},{1... | collective-permute-start | bytes 1572872 | tf_op jit(solution)/shard_map/ppermute | solution.py:36
  76.8 13.1 %collective-permute-start.11 = (f32[8,128,128]{2,1,0:T(8,128)S(1)}, f32[8,128,128]{2,1,0:T(8,128)S(1)}, u32[]{:S(2)}, u32[]{:S(2)}) collective-permute-start(f32[8,128,128]{2,1,0:T(8,128)S(1)} %collective-permute-done.10.rest_2_), channel_id=1, source_target_pairs={{0,1},{1,2},{2,3},{3,0},{4,5},{5,6},{6,7},{7,4},{8,9},{9,10},{10,1... | collective-permute-start | bytes 1572872 | tf_op jit(solution)/shard_map/ppermute | solution.py:36
  94.3 14.0 %collective-permute-start.26 = (f32[8,128,128]{2,1,0:T(8,128)S(1)}, f32[8,128,128]{2,1,0:T(8,128)S(1)}, u32[]{:S(2)}, u32[]{:S(2)}) collective-permute-start(f32[8,128,128]{2,1,0:T(8,128)S(1)} %dynamic-slice_add_fusion), channel_id=1, source_target_pairs={{0,64},{1,65},{2,66},{3,67},{4,68},{5,69},{6,70},{7,71},{8,72},{9,... | collective-permute-start | bytes 1572872 | tf_op jit(solution)/shard_map/ppermute | solution.py:36
  121.4 15.4 %collective-permute-start.40 = (f32[8,128,128]{2,1,0:T(8,128)S(1)}, f32[8,128,128]{2,1,0:T(8,128)S(1)}, u32[]{:S(2)}, u32[]{:S(2)}) collective-permute-start(f32[8,128,128]{2,1,0:T(8,128)S(1)} %get-tuple-element.34), channel_id=1, source_target_pairs={{0,3},{1,0},{2,1},{3,2},{4,7},{5,4},{6,5},{7,6},{8,11},{9,8},{10,9... | collective-permute-start | bytes 1572872 | tf_op jit(solution)/shard_map/ppermute | solution.py:36
  131.3 22.5 %collective-permute-start.42 = (f32[8,128,128]{2,1,0:T(8,128)S(1)}, f32[8,128,128]{2,1,0:T(8,128)S(1)}, u32[]{:S(2)}, u32[]{:S(2)}) collective-permute-start(f32[8,128,128]{2,1,0:T(8,128)S(1)} %get-tuple-element.41), channel_id=1, source_target_pairs={{0,4},{1,5},{2,6},{3,7},{4,8},{5,9},{6,10},{7,11},{8,12},{9,13},{1... | collective-permute-start | bytes 1572872 | tf_op jit(solution)/shard_map/ppermute | solution.py:36
  131.4 24.8 %collective-permute-start.44 = (f32[8,128,128]{2,1,0:T(8,128)S(1)}, f32[8,128,128]{2,1,0:T(8,128)S(1)}, u32[]{:S(2)}, u32[]{:S(2)}) collective-permute-start(f32[8,128,128]{2,1,0:T(8,128)S(1)} %add.293), channel_id=1, source_target_pairs={{0,12},{1,13},{2,14},{3,15},{4,0},{5,1},{6,2},{7,3},{8,4},{9,5},{1... | collective-permute-start | bytes 1572872 | tf_op jit(solution)/shard_map/ppermute | solution.py:36
  136.7 13.8 %collective-permute-start.41 = (f32[128,128]{1,0:T(8,128)S(1)}, f32[128,128]{1,0:T(8,128)S(1)}, u32[]{:S(2)}, u32[]{:S(2)}) collective-permute-start(f32[128,128]{1,0:T(8,128)S(1)} %fusion.19), channel_id=1, source_target_pairs={{0,4},{1,5},{2,6},{3,7},{4,0},{5,1},{6,2},{7,3},{8,12},{9,13},{10,... | collective-permute-start | bytes 196616 | tf_op jit(solution)/shard_map/ppermute | solution.py:36
  141.6 16.8 %collective-permute-start.48 = (f32[8,128,128]{2,1,0:T(8,128)S(1)}, f32[8,128,128]{2,1,0:T(8,128)S(1)}, u32[]{:S(2)}, u32[]{:S(2)}) collective-permute-start(f32[8,128,128]{2,1,0:T(8,128)S(1)} %get-tuple-element.38), channel_id=1, source_target_pairs={{0,1},{1,2},{2,3},{3,0},{4,5},{5,6},{6,7},{7,4},{8,9},{9,10},{10,1... | collective-permute-start | bytes 1572872 | tf_op jit(solution)/shard_map/ppermute | solution.py:36
  143.4 15.0 %collective-permute-start.49 = (f32[8,128,128]{2,1,0:T(8,128)S(1)}, f32[8,128,128]{2,1,0:T(8,128)S(1)}, u32[]{:S(2)}, u32[]{:S(2)}) collective-permute-start(f32[8,128,128]{2,1,0:T(8,128)S(1)} %add.299), channel_id=1, source_target_pairs={{0,3},{1,0},{2,1},{3,2},{4,7},{5,4},{6,5},{7,6},{8,11},{9,8},{10,9... | collective-permute-start | bytes 1572872 | tf_op jit(solution)/shard_map/ppermute | solution.py:36
  150.6 16.1 %collective-permute-start.30 = (f32[8,128,128]{2,1,0:T(8,128)S(1)}, f32[8,128,128]{2,1,0:T(8,128)S(1)}, u32[]{:S(2)}, u32[]{:S(2)}) collective-permute-start(f32[8,128,128]{2,1,0:T(8,128)S(1)} %get-tuple-element.47), channel_id=1, source_target_pairs={{0,3},{1,0},{2,1},{3,2},{4,7},{5,4},{6,5},{7,6},{8,11},{9,8},{10,9... | collective-permute-start | bytes 1572872 | tf_op jit(solution)/shard_map/ppermute | solution.py:36
  153.8 19.8 %collective-permute-start.36 = (f32[8,128,128]{2,1,0:T(8,128)S(1)}, f32[8,128,128]{2,1,0:T(8,128)S(1)}, u32[]{:S(2)}, u32[]{:S(2)}) collective-permute-start(f32[8,128,128]{2,1,0:T(8,128)S(1)} %get-tuple-element.51), channel_id=1, source_target_pairs={{0,12},{1,13},{2,14},{3,15},{4,0},{5,1},{6,2},{7,3},{8,4},{9,5},{1... | collective-permute-start | bytes 1572872 | tf_op jit(solution)/shard_map/ppermute | solution.py:36
  156.2 14.1 %collective-permute-start.29 = (f32[8,128,128]{2,1,0:T(8,128)S(1)}, f32[8,128,128]{2,1,0:T(8,128)S(1)}, u32[]{:S(2)}, u32[]{:S(2)}) collective-permute-start(f32[8,128,128]{2,1,0:T(8,128)S(1)} %add.279), channel_id=1, source_target_pairs={{0,1},{1,2},{2,3},{3,0},{4,5},{5,6},{6,7},{7,4},{8,9},{9,10},{10,1... | collective-permute-start | bytes 1572872 | tf_op jit(solution)/shard_map/ppermute | solution.py:36
  158.4 15.3 %collective-permute-start.35 = (f32[8,128,128]{2,1,0:T(8,128)S(1)}, f32[8,128,128]{2,1,0:T(8,128)S(1)}, u32[]{:S(2)}, u32[]{:S(2)}) collective-permute-start(f32[8,128,128]{2,1,0:T(8,128)S(1)} %add.285), channel_id=1, source_target_pairs={{0,4},{1,5},{2,6},{3,7},{4,8},{5,9},{6,10},{7,11},{8,12},{9,13},{1... | collective-permute-start | bytes 1572872 | tf_op jit(solution)/shard_map/ppermute | solution.py:36
  166.7 13.2 %collective-permute-start.51 = (f32[2,128,128]{2,1,0:T(8,128)S(1)}, f32[2,128,128]{2,1,0:T(8,128)S(1)}, u32[]{:S(2)}, u32[]{:S(2)}) collective-permute-start(f32[2,128,128]{2,1,0:T(8,128)S(1)} %get-tuple-element.75), channel_id=1, source_target_pairs={{0,12},{1,13},{2,14},{3,15},{4,0},{5,1},{6,2},{7,3},{8,4},{9,5},{1... | collective-permute-start | bytes 393224 | tf_op jit(solution)/shard_map/ppermute | solution.py:36
  170.3 18.2 %collective-permute-start.50 = (f32[2,128,128]{2,1,0:T(8,128)S(1)}, f32[2,128,128]{2,1,0:T(8,128)S(1)}, u32[]{:S(2)}, u32[]{:S(2)}) collective-permute-start(f32[2,128,128]{2,1,0:T(8,128)S(1)} %get-tuple-element.74), channel_id=1, source_target_pairs={{0,4},{1,5},{2,6},{3,7},{4,8},{5,9},{6,10},{7,11},{8,12},{9,13},{1... | collective-permute-start | bytes 393224 | tf_op jit(solution)/shard_map/ppermute | solution.py:36
  178.0 15.8 %collective-permute-start.53 = (f32[2,128,128]{2,1,0:T(8,128)S(1)}, f32[2,128,128]{2,1,0:T(8,128)S(1)}, u32[]{:S(2)}, u32[]{:S(2)}) collective-permute-start(f32[2,128,128]{2,1,0:T(8,128)S(1)} %get-tuple-element.76), channel_id=1, source_target_pairs={{0,1},{1,2},{2,3},{3,0},{4,5},{5,6},{6,7},{7,4},{8,9},{9,10},{10,1... | collective-permute-start | bytes 393224 | tf_op jit(solution)/shard_map/ppermute | solution.py:36
  (42 other events, 468.2 us)

commit v5 on v4

--- a/solution.py
+++ b/solution.py
@@ -8,16 +8,20 @@
 from jax.sharding import PartitionSpec as P
 
 HI = lax.Precision.HIGHEST
+GELU_SCALE = 0.7978845608028654
+GELU_CUBE = 0.044715
 AXES = ("loop", "wide")
 SIDE = 4
 TILE = 128
 SLOTS = 256
 GROUP = 16
 CHUNK = 32
-STAGES = 3
-PAIR_BYTES = 8 * 1024 * 1024
+STAGES = 4
+PAIR_BYTES = 30 * 1024 * 1024
 PER = 8
 CLASS_BUFFERS = (8, 6, 2)
+CORE = 4
+LOW = 5
 VMEM_BYTES = 8 * 1024 * 1024
 
 
@@ -137,13 +141,13 @@
     buffers = rest[:number]
     rest = rest[number:]
     prior_ref = rest[0] if which else None
-    out_ref, pairs, total = rest[-3:]
-    nrow = out_ref.shape[0]
+    pairs, total = rest[-2:]
+    nrow = total.shape[0] - 1
     begin, end, groups = class_range(bounds_ref, which)
     if which:
         total[0:nrow] = prior_ref[...]
     else:
-        total[0:nrow] = jnp.zeros_like(out_ref)
+        total[0:nrow] = jnp.zeros((nrow, TILE, TILE), jnp.float32)
     for index in range(number):
 
         @pl.loop(0, PER, unroll=4)
@@ -168,7 +172,14 @@
             )
             total[row] += product[:, :TILE] + product[:, TILE:]
 
-    out_ref[...] = total[0:nrow]
+    if which == len(CLASS_BUFFERS) - 1:
+        kept_ref, given_ref = rest[-4:-2]
+        core = bounds_ref[CORE]
+        half = nrow // 2
+        kept_ref[...] = total[pl.ds(core * half, half)]
+        given_ref[...] = total[pl.ds((1 - core) * half, half)]
+    else:
+        rest[-3][...] = total[0:nrow]
 
 
 def backward_kernel(which, bounds_ref, order_ref, rows_ref, slots_ref, tiles_ref, slope_ref, *rest):
@@ -233,12 +244,15 @@
 def forward_part(which, plan, tiles, buffers, prior, nrow):
     extra = [prior] if which else []
     number = CLASS_BUFFERS[which]
+    out_shape = [jax.ShapeDtypeStruct((nrow, TILE, TILE), jnp.float32)]
+    if which == len(CLASS_BUFFERS) - 1:
+        out_shape = [jax.ShapeDtypeStruct((nrow // 2, TILE, TILE), jnp.float32)] * 2
     return pl.pallas_call(
         functools.partial(forward_kernel, which),
         name="forward_tiles_%d" % which,
-        out_shape=jax.ShapeDtypeStruct((nrow, TILE, TILE), jnp.float32),
+        out_shape=out_shape,
         in_specs=[smem()] * 4 + [vmem()] * (1 + number + len(extra)),
-        out_specs=vmem(),
+        out_specs=[vmem()] * len(out_shape),
         scratch_shapes=[
             pltpu.VMEM((number * PER, TILE, 2 * TILE), jnp.bfloat16),
             pltpu.VMEM((nrow + 1, TILE, TILE), jnp.float32),
@@ -264,6 +278,80 @@
         cost_estimate=cost((6, 5, 2)[which]),
         compiler_params=pltpu.CompilerParams(vmem_limit_bytes=VMEM_BYTES),
     )(*plan, tiles, slope)
+
+
+def middle_kernel(
+    bounds_ref, across_ref, weight_ref, cotangent_ref, kept_ref, other_ref, pairs_ref,
+    activated_ref, spread_ref, weight_term_ref,
+):
+    core = bounds_ref[CORE]
+    half = kept_ref.shape[0]
+    weight_term = jnp.zeros((TILE, TILE), jnp.float32)
+    for source, place in ((kept_ref, core), (other_ref, 1 - core)):
+        for j in range(half):
+            columns = pl.ds(pl.multiple_of((place * half + j) * TILE, TILE), TILE)
+            block = source[j]
+            value = lax.dot_general(
+                across_ref[...],
+                block,
+                (((1,), (1,)), ((), ())),
+                precision=HI,
+                preferred_element_type=jnp.float32,
+            )
+            square = value * value
+            bend = jnp.tanh(GELU_SCALE * (value + GELU_CUBE * (square * value)))
+            activated_ref[:, columns] = 0.5 * value * (1.0 + bend)
+            rate = 0.5 * (1.0 + bend) + 0.5 * value * (1.0 - bend * bend) * (
+                GELU_SCALE * (1.0 + 3.0 * GELU_CUBE * square)
+            )
+            slope = cotangent_ref[:, columns] * rate
+            weight_term += jnp.dot(
+                slope, block, precision=HI, preferred_element_type=jnp.float32
+            )
+            spread_ref[:, columns] = jnp.dot(
+                weight_ref[...], slope, precision=HI, preferred_element_type=jnp.float32
+            )
+    weight_term_ref[...] = jnp.transpose(weight_term)
+
+
+def middle_part(bounds, across, weight, cotangent, kept, other, pairs):
+    return pl.pallas_call(
+        middle_kernel,
+        name="middle",
+        out_shape=[
+            jax.ShapeDtypeStruct(cotangent.shape, jnp.float32),
+            jax.ShapeDtypeStruct(cotangent.shape, jnp.float32),
+            jax.ShapeDtypeStruct(weight.shape, jnp.float32),
+        ],
+        in_specs=[smem()] + [vmem()] * 6,
+        out_specs=[vmem()] * 3,
+        cost_estimate=cost(4),
+        compiler_params=pltpu.CompilerParams(vmem_limit_bytes=VMEM_BYTES),
+    )(bounds, across, weight, cotangent, kept, other, pairs)
+
+
+def assemble_kernel(bounds_ref, own_ref, own_other_ref, across_ref, across_other_ref, out_ref):
+    core, low = bounds_ref[CORE], bounds_ref[LOW]
+    for source, chip, side in (
+        (own_ref, low, core),
+        (own_other_ref, low, 1 - core),
+        (across_ref, 1 - low, core),
+        (across_other_ref, 1 - low, 1 - core),
+    ):
+        for j in range(source.shape[0]):
+            place = (chip * 2 + side) * source.shape[0] + j
+            out_ref[:, pl.ds(pl.multiple_of(place * TILE, TILE), TILE)] = source[j]
+
+
+def assemble(bounds, parts):
+    return pl.pallas_call(
+        assemble_kernel,
+        name="assemble",
+        out_shape=jax.ShapeDtypeStruct((TILE, 4 * parts[0].shape[0] * TILE), jnp.float32),
+        in_specs=[smem()] + [vmem()] * 4,
+        out_specs=vmem(),
+        compiler_params=pltpu.CompilerParams(vmem_limit_bytes=VMEM_BYTES),
+    )(bounds, *parts)
 
 
 def make_plan(rows, cols, count, loop, wide):
@@ -293,8 +381,9 @@
     def sort(values):
         return jnp.sum(jnp.where(here, values[None, :], 0), axis=1)
 
-    steps = jnp.arange(4, dtype=jnp.int32)
+    steps = jnp.arange(8, dtype=jnp.int32)
     bounds = jnp.sum((kind[None, :] < steps[:, None]).astype(jnp.int32), axis=1)
+    bounds = jnp.where(steps == CORE, loop % 2, jnp.where(steps == LOW, loop // 2, bounds))
     return bounds, sort(spots), sort(rows), sort(slots)
 
 
@@ -323,50 +412,63 @@
     row_two, column_two = permute(row_one, x_down), permute(column_one, z_down)
     row = jnp.concatenate([own[:2], row_one, row_two, row_three], axis=0)
     column = jnp.concatenate([own[2:], column_one, column_two, column_three], axis=0)
+    return row, column, partner
+
+
+def gather_near(row, column):
     first_one, second_one = permute(row, z_down), permute(column, x_down)
     first_three, second_three = permute(row, z_up), permute(column, x_up)
     first_two, second_two = permute(first_one, z_down), permute(second_one, x_down)
-    near = [row, first_one, first_two, first_three, column, second_one, second_two, second_three]
-
-    partner = after(partner, row, column)
-    row_one, row_three = permute(partner[:2], x_down), permute(partner[:2], x_up)
-    column_one, column_three = permute(partner[2:], z_down), permute(partner[2:], z_up)
-    row_two, column_two = permute(row_three, x_up), permute(column_three, z_up)
-    row = jnp.concatenate([partner[:2], row_one, row_two, row_three], axis=0)
-    column = jnp.concatenate([partner[2:], column_one, column_two, column_three], axis=0)
-    first_one, second_one = permute(row, z_down), permute(column, x_down)
-    first_three, second_three = permute(row, z_up), permute(column, x_up)
-    apart = [row, first_one, first_three, column, second_one, second_three]
-    return near, apart
+    return [row, first_one, first_two, first_three, column, second_one, second_two, second_three]
+
+
+def gather_apart(near, partner, pairs):
+    row_sent = permute(near[0][2:], y_far)
+    column_sent = permute(after(near[4][2:], row_sent, pairs), y_far)
+    row = jnp.concatenate([partner[:2], row_sent], axis=0)
+    column = jnp.concatenate([partner[2:], column_sent], axis=0)
+    first_three = permute(after(row, near[3]), z_up)
+    second_three = permute(after(column, near[7]), x_up)
+    first_one = permute(after(row, near[2]), z_down)
+    second_one = permute(after(column, near[6]), x_down)
+    return [row, first_one, first_three, column, second_one, second_three]
 
 
 def scatter_terms(own, apart, apart_far, weight_term):
     row_sent = permute(apart_far[0], z_down)
     column_sent = permute(apart_far[1], x_down)
-    weight_term = flip_add(after(weight_term, row_sent), "x", 1)
+    weight_term = flip_add(after(weight_term, row_sent, apart[0]), "x", 1)
     row_one, column_one = permute(apart[1], z_up), permute(apart[4], x_up)
     row_three = permute(apart[2] + row_sent, z_down)
     column_three = permute(apart[5] + column_sent, x_down)
+    weight_term = flip_add(after(weight_term, row_one), "x", 2)
+
+    own_two = permute(after(own[2], row_one), z_up)
+    own_column_two = permute(after(own[6], column_one), x_up)
+    own_three = permute(after(own[3], row_three), z_down)
+    own_column_three = permute(after(own[7], column_three), x_down)
+    own_one = permute(own[1] + own_two, z_up)
+    own_column_one = permute(own[5] + own_column_two, x_up)
+
     row = apart[0] + row_one + row_three
     column = apart[3] + column_one + column_three
-    weight_term = flip_add(after(weight_term, column), "x", 2)
-    apart_half = reduce_ring(split_row(row), x_up, x_down, False)
-    apart_other = reduce_ring(split_row(column), z_up, z_down, False)
-    sent = permute(jnp.concatenate([apart_half, apart_other], axis=0), y_far)
-
-    row = reduce_ring(own[:4], z_up, z_down, True)
-    weight_term = flip_add(after(weight_term, row), "z", 1)
-    column = reduce_ring(own[4:], x_up, x_down, True)
-    weight_term = flip_add(after(weight_term, column), "z", 2)
-    half = reduce_ring(split_row(row), x_up, x_down, True)
-    other = reduce_ring(split_row(column), z_up, z_down, True)
-    kept = jnp.concatenate([half, other], axis=0)
-    total = after(kept, weight_term) + sent
-    return total, weight_term + permute(weight_term, y_far)
-
-
-def split_row(row):
-    return [row[2 * i : 2 * i + 2] for i in range(4)]
+    weight_term = flip_add(after(weight_term, row_three), "z", 1)
+    row_far = permute(row[2:], y_far)
+    column_far = permute(after(column[2:], row_far), y_far)
+    weight_term = flip_add(after(weight_term, row_far), "z", 2)
+    last_far = permute(jnp.concatenate([row[:2], column[:2]], axis=0), y_far)
+
+    row = own[0] + own_one + own_three
+    column = own[4] + own_column_one + own_column_three
+    rows = [row[:2]] + [row[2 * i : 2 * i + 2] + row_far[2 * i - 2 : 2 * i] for i in (1, 2, 3)]
+    columns = [column[:2]] + [
+        column[2 * i : 2 * i + 2] + column_far[2 * i - 2 : 2 * i] for i in (1, 2, 3)
+    ]
+    half = reduce_ring(rows, x_up, x_down, True)
+    other = reduce_ring(columns, z_up, z_down, True)
+    weight_term = after(weight_term, column_far)
+    weight_term = weight_term + permute(weight_term, y_far)
+    return jnp.concatenate([half, other], axis=0) + last_far, weight_term
 
 
 def flip_add(value, axis, step):
@@ -375,69 +477,38 @@
     return value + permute(value, lambda y, c, x, z: (y, c, x, z ^ step))
 
 
-def sum_over_loop(partial, loop):
-    core = loop % 2
-    half = partial.shape[0] // 2
-    kept = lax.dynamic_slice_in_dim(partial, core * half, half, 0)
-    given = lax.dynamic_slice_in_dim(partial, (1 - core) * half, half, 0)
+def per_device(features, weight, cotangent, tiles, tile_rows, tile_cols, counts):
+    nrow = features.shape[1] // TILE
+    loop = lax.axis_index("loop")
+    wide = lax.axis_index("wide")
+    tile_collection = tiles.reshape(SLOTS, TILE, TILE)
+    count = counts.reshape(1)
+    plan = make_plan(tile_rows.reshape(SLOTS), tile_cols.reshape(SLOTS), count, loop, wide)
+    across = weight.T
+
+    row, column, partner = gather_features(features, loop)
+    near = gather_near(row, column)
+    plan, count, across = lax.optimization_barrier((plan, count, across, row, column))[:3]
+    pairs = pair_tiles(count, tile_collection)
+    apart = gather_apart(near, partner, pairs)
+    partial = forward_part(0, plan, pairs, near, None, nrow)
+    far = [permute(after(apart[2], *partial), z_up), permute(after(apart[5], *partial), x_up)]
+    partial = forward_part(1, plan, pairs, apart, partial[0], nrow)
+    kept, given = forward_part(2, plan, pairs, far, partial[0], nrow)
+
     kept = kept + permute(given, core_swap)
     kept = kept + permute(kept, y_pair)
     other = permute(kept, core_swap)
-    return jnp.where(
-        core == 0,
-        jnp.concatenate([kept, other], axis=0),
-        jnp.concatenate([other, kept], axis=0),
+    activated, spread, weight_term = middle_part(
+        plan[0], across, weight, cotangent, kept, other, pairs
     )
-
-
-def gather_loop(own, loop):
-    low, core = loop // 2, loop % 2
-    across = permute(own, y_pair)
-    own_other = permute(own, core_swap)
-    across_other = permute(across, core_swap)
-    same = jnp.where(
-        core == 0, jnp.stack([own, own_other]), jnp.stack([own_other, own])
-    )
-    far = jnp.where(
-        core == 0, jnp.stack([across, across_other]), jnp.stack([across_other, across])
-    )
-    whole = jnp.where(low == 0, jnp.stack([same, far]), jnp.stack([far, same]))
-    feats = own.shape[1]
-    return jnp.transpose(whole.reshape(-1, feats, TILE), (1, 0, 2)).reshape(feats, -1)
-
-
-def per_device(features, weight, cotangent, tiles, tile_rows, tile_cols, counts):
-    feats, shard_nodes = features.shape
-    loop = lax.axis_index("loop")
-    wide = lax.axis_index("wide")
-    nrow = shard_nodes // TILE
-    tile_collection = tiles.reshape(SLOTS, TILE, TILE)
-    plan = make_plan(
-        tile_rows.reshape(SLOTS), tile_cols.reshape(SLOTS), counts.reshape(1), loop, wide
-    )
-
-    near, apart = gather_features(features, loop)
-    pairs = pair_tiles(after(counts.reshape(1), near[0], near[4]), tile_collection)
-    partial = forward_part(0, plan, pairs, near, None, nrow)
-    far = [permute(after(apart[2], pairs), z_up), permute(after(apart[5], pairs), x_up)]
-    partial = forward_part(1, plan, pairs, apart, partial, nrow)
-    partial = forward_part(2, plan, pairs, far, partial, nrow)
-    gathered = sum_over_loop(partial, loop).reshape(shard_nodes, feats)
-    aggregated = lax.dot_general(
-        weight, gathered, (((0,), (1,)), ((), ())), precision=HI, preferred_element_type=jnp.float32
-    )
-    activated, pull = jax.vjp(jax.nn.gelu, aggregated)
-    slope = pull(cotangent)[0]
-    weight_term = lax.dot_general(
-        gathered, slope, (((0,), (1,)), ((), ())), precision=HI, preferred_element_type=jnp.float32
-    )
-    spread = jnp.dot(weight, slope, precision=HI, preferred_element_type=jnp.float32)
     apart_far = backward_part(2, plan, pairs, spread)
     apart = backward_part(1, plan, pairs, after(spread, *apart_far))
     own = backward_part(0, plan, pairs, after(spread, *apart))
-    input_cols, weight_grad = scatter_terms(own, apart, apart_far, weight_term)
-    input_grad = gather_loop(input_cols, loop)
-    return (activated, input_grad, weight_grad)
+    total, weight_grad = scatter_terms(own, apart, apart_far, weight_term)
+    far_total = permute(total, y_pair)
+    parts = [total, permute(total, core_swap), far_total, permute(far_total, core_swap)]
+    return (activated, assemble(plan[0], parts), weight_grad)
 
 
 def solution(mesh):

time: 220 us -> 227 us (1.032)
  waiting for transfers between devices: 79.4 us -> 87.1 us
  starting transfers between devices: 85.3 us -> 91.4 us
  matrix products: 4.44 us -> 0 us
    pallas_call x0 -> x2, Pallas kernels: none -> 10.8 us  [the longest x1 9.21 us: middle_part(): pl.pallas_call(middle_kernel, name='middle', out_shape=[jax.ShapeDtypeStr...]
    ppermute x61 -> x53, waiting for transfers between devices: 79.4 us -> 87.1 us  [permute(): return lax.ppermute(value, AXES, pairs)]
    ppermute x61 -> x53, starting transfers between devices: 85.3 us -> 91.4 us  [permute(): return lax.ppermute(value, AXES, pairs)]
    pallas_call x3, Pallas kernels: 11.5 us -> 5.93 us  [backward_part(): pl.pallas_call(functools.partial(backward_kernel, which), name='backward_...]
    pallas_call x3, Pallas kernels: 11.6 us -> 6.74 us  [forward_part(): pl.pallas_call(functools.partial(forward_kernel, which), name='forward_ti...]
    dot_general x3 -> x0, matrix products: 4.44 us -> none  [the longest x1 1.81 us: per_device(): lax.dot_general(gathered, slope, (((0,), (1,)), ((), ())), precision=HI,...]
    unnamed x12 -> x23, local copies, waits for them, and re-layouts: 13.2 us -> 11.7 us
  transfers between devices with their start and end apart: 61 -> 53, of which waited for: 25 -> 23; matrix products, arithmetic and copies ran while one was open for 4% -> 3% of each run, Pallas kernels for 10% -> 5%
where the time goes in v5:
time: 227 us
  starting transfers between devices  91.4 us (40%)
  waiting for transfers between devices  87.1 us (38%)
  Pallas kernels  26.2 us (12%)
  local copies, waits for them, and re-layouts  15.1 us (7%)
  other arithmetic  5.07 us (2%)
    ppermute x53, starting transfers between devices, permute(): return lax.ppermute(value, AXES, pairs)  91.4 us
    ppermute x53, waiting for transfers between devices, permute(): return lax.ppermute(value, AXES, pairs)  87.1 us
    unnamed x23, local copies, waits for them, and re-layouts  11.7 us
    pallas_call x1, Pallas kernels, middle_part(): pl.pallas_call(middle_kernel, name='middle', out_shape=[jax.ShapeDtypeStr...  9.21 us
    pallas_call x3, Pallas kernels, forward_part(): pl.pallas_call(functools.partial(forward_kernel, which), name='forward_ti...  6.74 us
    pallas_call x3, Pallas kernels, backward_part(): pl.pallas_call(functools.partial(backward_kernel, which), name='backward_...  5.93 us
  transfers between devices with their start and end apart: 53, of which 23 were waited for; matrix products, arithmetic and copies ran while one was open for 3% of the time, Pallas kernels for 5%

profile of v5, /device:TPU:0, one launch (start us, length us, event | category | flops | bytes accessed | tf_op | source)
XLA Modules:
  0.0 226.6 jit_solution(12865515108188702063)
XLA Ops:
  16.9 5.8 %copy-done = bf16[256,128,256]{2,1,0:T(8,128)(2,1)} copy-done((bf16[256,128,256]{2,1,0:T(8,128)(2,1)}, bf16[256,128,256]{2,1,0:T(8,128)(2,1)S(1)}, u32[]{:S(2)}) %copy-start) | copy-done | bytes 16777240
  24.7 5.5 %collective-permute-start.1 = (f32[2,128,128]{2,1,0:T(8,128)S(1)}, f32[2,128,128]{2,1,0:T(8,128)S(1)}, u32[]{:S(2)}, u32[]{:S(2)}) collective-permute-start(f32[2,128,128]{2,1,0:T(8,128)S(1)} %collective-permute-done), channel_id=1, source_target_pairs={{0,12},{1,13},{2,14},{3,15},{4,0},{5,1},{6,2},{7,3},{8,4},{9,5},{1... | collective-permute-start | bytes 393224 | tf_op jit(solution)/shard_map/ppermute | solution.py:40
  32.8 3.7 %collective-permute-start.10 = (f32[8,128,128]{2,1,0:T(8,128)S(1)}, f32[8,128,128]{2,1,0:T(8,128)S(1)}, u32[]{:S(2)}, u32[]{:S(2)}) collective-permute-start(f32[8,128,128]{2,1,0:T(8,128)S(1)} %pad_maximum_fusion.rest_0_), channel_id=1, source_target_pairs={{0,3},{1,0},{2,1},{3,2},{4,7},{5,4},{6,5},{7,6},{8,11},{9,8},{10,9... | collective-permute-start | bytes 1572872 | tf_op jit(solution)/shard_map/ppermute | solution.py:40
  38.3 7.8 %collective-permute-done.7 = f32[6,128,128]{2,1,0:T(8,128)S(1)} collective-permute-done((f32[6,128,128]{2,1,0:T(8,128)S(1)}, f32[6,128,128]{2,1,0:T(8,128)S(1)}, u32[]{:S(2)}, u32[]{:S(2)}) %collective-permute-start.7) | collective-permute-done | bytes 393248 | tf_op jit(solution)/shard_map/ppermute | solution.py:40
  57.8 4.7 %collective-permute-done.11.rest_2_ = f32[8,128,128]{2,1,0:T(8,128)} collective-permute-done((f32[8,128,128]{2,1,0:T(8,128)S(1)}, f32[8,128,128]{2,1,0:T(8,128)}, u32[]{:S(2)}, u32[]{:S(2)}) %collective-permute-start.11) | collective-permute-done | bytes 524320 | tf_op jit(solution)/shard_map/ppermute | solution.py:40
  68.1 5.8 %copy-done.1 = bf16[256,128,256]{2,1,0:T(8,128)(2,1)S(1)} copy-done((bf16[256,128,256]{2,1,0:T(8,128)(2,1)S(1)}, bf16[256,128,256]{2,1,0:T(8,128)(2,1)}, u32[]{:S(2)}) %copy-start.1) | copy-done | bytes 16777240
  80.4 7.0 %collective-permute-done.15.rest_0_ = f32[8,128,128]{2,1,0:T(8,128)S(1)} collective-permute-done((f32[8,128,128]{2,1,0:T(8,128)S(1)}, f32[8,128,128]{2,1,0:T(8,128)S(1)}, u32[]{:S(2)}, u32[]{:S(2)}) %collective-permute-start.15) | collective-permute-done | bytes 524320 | tf_op jit(solution)/shard_map/ppermute | solution.py:40
  91.0 4.0 %collective-permute-start.22 = (f32[8,128,128]{2,1,0:T(8,128)S(1)}, f32[8,128,128]{2,1,0:T(8,128)S(1)}, u32[]{:S(2)}, u32[]{:S(2)}) collective-permute-start(f32[8,128,128]{2,1,0:T(8,128)S(1)} %add.259), channel_id=1, source_target_pairs={{0,64},{1,65},{2,66},{3,67},{4,68},{5,69},{6,70},{7,71},{8,72},{9,... | collective-permute-start | bytes 1572872 | tf_op jit(solution)/shard_map/ppermute | solution.py:40
  95.1 12.2 %collective-permute-done.22 = f32[8,128,128]{2,1,0:T(8,128)S(1)} collective-permute-done((f32[8,128,128]{2,1,0:T(8,128)S(1)}, f32[8,128,128]{2,1,0:T(8,128)S(1)}, u32[]{:S(2)}, u32[]{:S(2)}) %collective-permute-start.22) | collective-permute-done | bytes 524320 | tf_op jit(solution)/shard_map/ppermute | solution.py:40
  109.4 9.2 %middle.1 = (f32[128,2048]{1,0:T(8,128)}, f32[128,2048]{1,0:T(8,128)S(1)}, f32[128,128]{1,0:T(8,128)S(1)}) custom-call(s32[8]{0:T(128)S(1)} %compare_select_fusion.11.bounds_ref, f32[128,128]{1,0:T(8,128)S(1)} %bitcast.19, f32[128,128]{1,0:T(8,128)S(1)} %copy-done.3, f32[128,2048]{1,0:T(8,128)S(1)} %copy-done.2, f32[8,128,128]{2,1,0:T(8,128)S(1)} %add.260.kept_ref, ...), custom_call_target="tpu_custom_call" | custom-call | flops 4400000000 | bytes 1048576 | tf_op jit(solution)/shard_map/middle/pallas_call | solution.py:318
  120.0 3.2 %collective-permute-start.27 = (f32[8,128,128]{2,1,0:T(8,128)S(1)}, f32[8,128,128]{2,1,0:T(8,128)S(1)}, u32[]{:S(2)}, u32[]{:S(2)}) collective-permute-start(f32[8,128,128]{2,1,0:T(8,128)S(1)} %get-tuple-element.66), channel_id=1, source_target_pairs={{0,3},{1,0},{2,1},{3,2},{4,7},{5,4},{6,5},{7,6},{8,11},{9,8},{10,9... | collective-permute-start | bytes 1572872 | tf_op jit(solution)/shard_map/ppermute | solution.py:40
  132.9 3.8 %collective-permute-start.28 = (f32[8,128,128]{2,1,0:T(8,128)S(1)}, f32[8,128,128]{2,1,0:T(8,128)S(1)}, u32[]{:S(2)}, u32[]{:S(2)}) collective-permute-start(f32[8,128,128]{2,1,0:T(8,128)S(1)} %add.263), channel_id=1, source_target_pairs={{0,3},{1,0},{2,1},{3,2},{4,7},{5,4},{6,5},{7,6},{8,11},{9,8},{10,9... | collective-permute-start | bytes 1572872 | tf_op jit(solution)/shard_map/ppermute | solution.py:40
  140.0 7.2 %collective-permute-done.28 = f32[8,128,128]{2,1,0:T(8,128)S(1)} collective-permute-done((f32[8,128,128]{2,1,0:T(8,128)S(1)}, f32[8,128,128]{2,1,0:T(8,128)S(1)}, u32[]{:S(2)}, u32[]{:S(2)}) %collective-permute-start.28) | collective-permute-done | bytes 524320 | tf_op jit(solution)/shard_map/ppermute | solution.py:40
  147.2 3.7 %collective-permute-start.29 = (f32[8,128,128]{2,1,0:T(8,128)S(1)}, f32[8,128,128]{2,1,0:T(8,128)S(1)}, u32[]{:S(2)}, u32[]{:S(2)}) collective-permute-start(f32[8,128,128]{2,1,0:T(8,128)S(1)} %get-tuple-element.81), channel_id=1, source_target_pairs={{0,3},{1,0},{2,1},{3,2},{4,7},{5,4},{6,5},{7,6},{8,11},{9,8},{10,9... | collective-permute-start | bytes 1572872 | tf_op jit(solution)/shard_map/ppermute | solution.py:40
  154.4 5.7 %collective-permute-start.30 = (f32[6,128,128]{2,1,0:T(8,128)S(1)}, f32[6,128,128]{2,1,0:T(8,128)S(1)}, u32[]{:S(2)}, u32[]{:S(2)}) collective-permute-start(f32[6,128,128]{2,1,0:T(8,128)S(1)} %slice.102), channel_id=1, source_target_pairs={{0,16},{1,17},{2,18},{3,19},{4,20},{5,21},{6,22},{7,23},{8,24},{9,... | collective-permute-start | bytes 1179656 | tf_op jit(solution)/shard_map/ppermute | solution.py:40
  160.5 6.2 %collective-permute-done.30 = f32[6,128,128]{2,1,0:T(8,128)S(1)} collective-permute-done((f32[6,128,128]{2,1,0:T(8,128)S(1)}, f32[6,128,128]{2,1,0:T(8,128)S(1)}, u32[]{:S(2)}, u32[]{:S(2)}) %collective-permute-start.30) | collective-permute-done | bytes 393248 | tf_op jit(solution)/shard_map/ppermute | solution.py:40
  166.6 3.2 %collective-permute-start.44 = (f32[4,128,128]{2,1,0:T(8,128)S(1)}, f32[4,128,128]{2,1,0:T(8,128)S(1)}, u32[]{:S(2)}, u32[]{:S(2)}) collective-permute-start(f32[4,128,128]{2,1,0:T(8,128)S(1)} %pad_maximum_fusion.6), channel_id=1, source_target_pairs={{0,16},{1,17},{2,18},{3,19},{4,20},{5,21},{6,22},{7,23},{8,24},{9,... | collective-permute-start | bytes 786440 | tf_op jit(solution)/shard_map/ppermute | solution.py:40
  170.9 10.5 %collective-permute-done.40 = f32[6,128,128]{2,1,0:T(8,128)S(1)} collective-permute-done((f32[6,128,128]{2,1,0:T(8,128)S(1)}, f32[6,128,128]{2,1,0:T(8,128)S(1)}, u32[]{:S(2)}, u32[]{:S(2)}) %collective-permute-start.40) | collective-permute-done | bytes 393248 | tf_op jit(solution)/shard_map/ppermute | solution.py:40
  182.1 5.3 %collective-permute-start.33 = (f32[2,128,128]{2,1,0:T(8,128)S(1)}, f32[2,128,128]{2,1,0:T(8,128)S(1)}, u32[]{:S(2)}, u32[]{:S(2)}) collective-permute-start(f32[2,128,128]{2,1,0:T(8,128)S(1)} %get-tuple-element.105), channel_id=1, source_target_pairs={{0,12},{1,13},{2,14},{3,15},{4,0},{5,1},{6,2},{7,3},{8,4},{9,5},{1... | collective-permute-start | bytes 393224 | tf_op jit(solution)/shard_map/ppermute | solution.py:40
  194.0 4.2 %collective-permute-start.46 = (f32[4,128,128]{2,1,0:T(8,128)S(1)}, f32[4,128,128]{2,1,0:T(8,128)S(1)}, u32[]{:S(2)}, u32[]{:S(2)}) collective-permute-start(f32[4,128,128]{2,1,0:T(8,128)S(1)} %maximum_add_fusion.own_ref), channel_id=1, source_target_pairs={{0,64},{1,65},{2,66},{3,67},{4,68},{5,69},{6,70},{7,71},{8,72},{9,... | collective-permute-start | bytes 786440 | tf_op jit(solution)/shard_map/ppermute | solution.py:40
  198.2 4.3 %collective-permute-done.48 = f32[128,128]{1,0:T(8,128)S(1)} collective-permute-done((f32[128,128]{1,0:T(8,128)S(1)}, f32[128,128]{1,0:T(8,128)S(1)}, u32[]{:S(2)}, u32[]{:S(2)}) %collective-permute-start.48) | collective-permute-done | bytes 65568 | tf_op jit(solution)/shard_map/ppermute | solution.py:40
  205.1 3.2 %collective-permute-done.49 = f32[128,128]{1,0:T(8,128)S(1)} collective-permute-done((f32[128,128]{1,0:T(8,128)S(1)}, f32[128,128]{1,0:T(8,128)S(1)}, u32[]{:S(2)}, u32[]{:S(2)}) %collective-permute-start.49) | collective-permute-done | bytes 65568 | tf_op jit(solution)/shard_map/ppermute | solution.py:40
  208.4 4.3 %collective-permute-done.50 = f32[128,128]{1,0:T(8,128)S(1)} collective-permute-done((f32[128,128]{1,0:T(8,128)S(1)}, f32[128,128]{1,0:T(8,128)S(1)}, u32[]{:S(2)}, u32[]{:S(2)}) %collective-permute-start.50) | collective-permute-done | bytes 65568 | tf_op jit(solution)/shard_map/ppermute | solution.py:40
  220.0 4.4 %collective-permute-done.52 = f32[128,128]{1,0:T(8,128)S(1)} collective-permute-done((f32[128,128]{1,0:T(8,128)S(1)}, f32[128,128]{1,0:T(8,128)S(1)}, u32[]{:S(2)}, u32[]{:S(2)}) %collective-permute-start.52) | collective-permute-done | bytes 65568 | tf_op jit(solution)/shard_map/ppermute | solution.py:40
  (159 shorter events, 90.0 us)
Async XLA Ops:
  3.0 27.4 %collective-permute-start.5 = (f32[2,128,128]{2,1,0:T(8,128)S(1)}, f32[2,128,128]{2,1,0:T(8,128)S(1)}, u32[]{:S(2)}, u32[]{:S(2)}) collective-permute-start(f32[2,128,128]{2,1,0:T(8,128)S(1)} %get-tuple-element.110), channel_id=1, source_target_pairs={{0,1},{1,2},{2,3},{3,0},{4,5},{5,6},{6,7},{7,4},{8,9},{9,10},{10,1... | collective-permute-start | bytes 393224 | tf_op jit(solution)/shard_map/ppermute | solution.py:40
  5.0 17.7 %collective-permute-start.3 = (f32[2,128,128]{2,1,0:T(8,128)S(1)}, f32[2,128,128]{2,1,0:T(8,128)S(1)}, u32[]{:S(2)}, u32[]{:S(2)}) collective-permute-start(f32[2,128,128]{2,1,0:T(8,128)S(1)} %get-tuple-element.110), channel_id=1, source_target_pairs={{0,3},{1,0},{2,1},{3,2},{4,7},{5,4},{6,5},{7,6},{8,11},{9,8},{10,9... | collective-permute-start | bytes 393224 | tf_op jit(solution)/shard_map/ppermute | solution.py:40
  7.2 25.5 %collective-permute-start.2 = (f32[2,128,128]{2,1,0:T(8,128)S(1)}, f32[2,128,128]{2,1,0:T(8,128)S(1)}, u32[]{:S(2)}, u32[]{:S(2)}) collective-permute-start(f32[2,128,128]{2,1,0:T(8,128)S(1)} %get-tuple-element.111), channel_id=1, source_target_pairs={{0,4},{1,5},{2,6},{3,7},{4,8},{5,9},{6,10},{7,11},{8,12},{9,13},{1... | collective-permute-start | bytes 393224 | tf_op jit(solution)/shard_map/ppermute | solution.py:40
  8.7 16.0 %collective-permute-start = (f32[2,128,128]{2,1,0:T(8,128)S(1)}, f32[2,128,128]{2,1,0:T(8,128)S(1)}, u32[]{:S(2)}, u32[]{:S(2)}) collective-permute-start(f32[2,128,128]{2,1,0:T(8,128)S(1)} %get-tuple-element.111), channel_id=1, source_target_pairs={{0,12},{1,13},{2,14},{3,15},{4,0},{5,1},{6,2},{7,3},{8,4},{9,5},{1... | collective-permute-start | bytes 393224 | tf_op jit(solution)/shard_map/ppermute | solution.py:40
  10.5 35.7 %collective-permute-start.6 = (f32[4,128,128]{2,1,0:T(8,128)}, f32[4,128,128]{2,1,0:T(8,128)}, u32[]{:S(2)}, u32[]{:S(2)}) collective-permute-start(f32[4,128,128]{2,1,0:T(8,128)} %get-tuple-element.102), channel_id=1, source_target_pairs={{0,80},{1,81},{2,82},{3,83},{4,84},{5,85},{6,86},{7,87},{8,88},{9,... | collective-permute-start | bytes 786440 | tf_op jit(solution)/shard_map/ppermute | solution.py:40
  30.4 17.4 %collective-permute-start.12 = (f32[8,128,128]{2,1,0:T(8,128)S(1)}, f32[8,128,128]{2,1,0:T(8,128)S(1)}, u32[]{:S(2)}, u32[]{:S(2)}) collective-permute-start(f32[8,128,128]{2,1,0:T(8,128)S(1)} %pad_maximum_fusion.1.rest_4_), channel_id=1, source_target_pairs={{0,12},{1,13},{2,14},{3,15},{4,0},{5,1},{6,2},{7,3},{8,4},{9,5},{1... | collective-permute-start | bytes 1572872 | tf_op jit(solution)/shard_map/ppermute | solution.py:40
  32.8 17.0 %collective-permute-start.10 = (f32[8,128,128]{2,1,0:T(8,128)S(1)}, f32[8,128,128]{2,1,0:T(8,128)S(1)}, u32[]{:S(2)}, u32[]{:S(2)}) collective-permute-start(f32[8,128,128]{2,1,0:T(8,128)S(1)} %pad_maximum_fusion.rest_0_), channel_id=1, source_target_pairs={{0,3},{1,0},{2,1},{3,2},{4,7},{5,4},{6,5},{7,6},{8,11},{9,8},{10,9... | collective-permute-start | bytes 1572872 | tf_op jit(solution)/shard_map/ppermute | solution.py:40
  37.5 14.9 %collective-permute-start.8 = (f32[8,128,128]{2,1,0:T(8,128)S(1)}, f32[8,128,128]{2,1,0:T(8,128)S(1)}, u32[]{:S(2)}, u32[]{:S(2)}) collective-permute-start(f32[8,128,128]{2,1,0:T(8,128)S(1)} %pad_maximum_fusion.rest_0_), channel_id=1, source_target_pairs={{0,1},{1,2},{2,3},{3,0},{4,5},{5,6},{6,7},{7,4},{8,9},{9,10},{10,1... | collective-permute-start | bytes 1572872 | tf_op jit(solution)/shard_map/ppermute | solution.py:40
  47.8 17.2 %collective-permute-start.13 = (f32[8,128,128]{2,1,0:T(8,128)S(1)}, f32[8,128,128]{2,1,0:T(8,128)}, u32[]{:S(2)}, u32[]{:S(2)}) collective-permute-start(f32[8,128,128]{2,1,0:T(8,128)S(1)} %collective-permute-done.12.rest_5_), channel_id=1, source_target_pairs={{0,12},{1,13},{2,14},{3,15},{4,0},{5,1},{6,2},{7,3},{8,4},{9,5},{1... | collective-permute-start | bytes 1572872 | tf_op jit(solution)/shard_map/ppermute | solution.py:40
  52.4 24.5 %collective-permute-start.9 = (f32[8,128,128]{2,1,0:T(8,128)S(1)}, f32[8,128,128]{2,1,0:T(8,128)S(1)}, u32[]{:S(2)}, u32[]{:S(2)}) collective-permute-start(f32[8,128,128]{2,1,0:T(8,128)S(1)} %pad_maximum_fusion.2.rest_0_), channel_id=1, source_target_pairs={{0,1},{1,2},{2,3},{3,0},{4,5},{5,6},{6,7},{7,4},{8,9},{9,10},{10,1... | collective-permute-start | bytes 1572872 | tf_op jit(solution)/shard_map/ppermute | solution.py:40
  57.2 19.8 %collective-permute-start.17 = (f32[8,128,128]{2,1,0:T(8,128)S(1)}, f32[8,128,128]{2,1,0:T(8,128)S(1)}, u32[]{:S(2)}, u32[]{:S(2)}) collective-permute-start(f32[8,128,128]{2,1,0:T(8,128)S(1)} %pad_maximum_fusion.3.rest_3_), channel_id=1, source_target_pairs={{0,4},{1,5},{2,6},{3,7},{4,8},{5,9},{6,10},{7,11},{8,12},{9,13},{1... | collective-permute-start | bytes 1572872 | tf_op jit(solution)/shard_map/ppermute | solution.py:40
  62.5 15.7 %collective-permute-start.19 = (f32[8,128,128]{2,1,0:T(8,128)S(1)}, f32[8,128,128]{2,1,0:T(8,128)S(1)}, u32[]{:S(2)}, u32[]{:S(2)}) collective-permute-start(f32[8,128,128]{2,1,0:T(8,128)S(1)} %pad_maximum_fusion.2.rest_0_), channel_id=1, source_target_pairs={{0,3},{1,0},{2,1},{3,2},{4,7},{5,4},{6,5},{7,6},{8,11},{9,8},{10,9... | collective-permute-start | bytes 1572872 | tf_op jit(solution)/shard_map/ppermute | solution.py:40
  91.0 16.3 %collective-permute-start.22 = (f32[8,128,128]{2,1,0:T(8,128)S(1)}, f32[8,128,128]{2,1,0:T(8,128)S(1)}, u32[]{:S(2)}, u32[]{:S(2)}) collective-permute-start(f32[8,128,128]{2,1,0:T(8,128)S(1)} %add.259), channel_id=1, source_target_pairs={{0,64},{1,65},{2,66},{3,67},{4,68},{5,69},{6,70},{7,71},{8,72},{9,... | collective-permute-start | bytes 1572872 | tf_op jit(solution)/shard_map/ppermute | solution.py:40
  123.2 13.5 %collective-permute-start.37 = (f32[8,128,128]{2,1,0:T(8,128)S(1)}, f32[8,128,128]{2,1,0:T(8,128)S(1)}, u32[]{:S(2)}, u32[]{:S(2)}) collective-permute-start(f32[8,128,128]{2,1,0:T(8,128)S(1)} %get-tuple-element.67), channel_id=1, source_target_pairs={{0,12},{1,13},{2,14},{3,15},{4,0},{5,1},{6,2},{7,3},{8,4},{9,5},{1... | collective-permute-start | bytes 1572872 | tf_op jit(solution)/shard_map/ppermute | solution.py:40
  132.9 14.3 %collective-permute-start.28 = (f32[8,128,128]{2,1,0:T(8,128)S(1)}, f32[8,128,128]{2,1,0:T(8,128)S(1)}, u32[]{:S(2)}, u32[]{:S(2)}) collective-permute-start(f32[8,128,128]{2,1,0:T(8,128)S(1)} %add.263), channel_id=1, source_target_pairs={{0,3},{1,0},{2,1},{3,2},{4,7},{5,4},{6,5},{7,6},{8,11},{9,8},{10,9... | collective-permute-start | bytes 1572872 | tf_op jit(solution)/shard_map/ppermute | solution.py:40
  136.7 14.2 %collective-permute-start.25 = (f32[8,128,128]{2,1,0:T(8,128)S(1)}, f32[8,128,128]{2,1,0:T(8,128)S(1)}, u32[]{:S(2)}, u32[]{:S(2)}) collective-permute-start(f32[8,128,128]{2,1,0:T(8,128)S(1)} %get-tuple-element.79), channel_id=1, source_target_pairs={{0,1},{1,2},{2,3},{3,0},{4,5},{5,6},{6,7},{7,4},{8,9},{9,10},{10,1... | collective-permute-start | bytes 1572872 | tf_op jit(solution)/shard_map/ppermute | solution.py:40
  136.8 15.6 %collective-permute-start.38 = (f32[8,128,128]{2,1,0:T(8,128)S(1)}, f32[8,128,128]{2,1,0:T(8,128)S(1)}, u32[]{:S(2)}, u32[]{:S(2)}) collective-permute-start(f32[8,128,128]{2,1,0:T(8,128)S(1)} %add.275), channel_id=1, source_target_pairs={{0,12},{1,13},{2,14},{3,15},{4,0},{5,1},{6,2},{7,3},{8,4},{9,5},{1... | collective-permute-start | bytes 1572872 | tf_op jit(solution)/shard_map/ppermute | solution.py:40
  139.6 20.7 %collective-permute-start.35 = (f32[8,128,128]{2,1,0:T(8,128)S(1)}, f32[8,128,128]{2,1,0:T(8,128)S(1)}, u32[]{:S(2)}, u32[]{:S(2)}) collective-permute-start(f32[8,128,128]{2,1,0:T(8,128)S(1)} %get-tuple-element.85), channel_id=1, source_target_pairs={{0,4},{1,5},{2,6},{3,7},{4,8},{5,9},{6,10},{7,11},{8,12},{9,13},{1... | collective-permute-start | bytes 1572872 | tf_op jit(solution)/shard_map/ppermute | solution.py:40
  147.2 22.6 %collective-permute-start.29 = (f32[8,128,128]{2,1,0:T(8,128)S(1)}, f32[8,128,128]{2,1,0:T(8,128)S(1)}, u32[]{:S(2)}, u32[]{:S(2)}) collective-permute-start(f32[8,128,128]{2,1,0:T(8,128)S(1)} %get-tuple-element.81), channel_id=1, source_target_pairs={{0,3},{1,0},{2,1},{3,2},{4,7},{5,4},{6,5},{7,6},{8,11},{9,8},{10,9... | collective-permute-start | bytes 1572872 | tf_op jit(solution)/shard_map/ppermute | solution.py:40
  151.0 19.2 %collective-permute-start.26 = (f32[8,128,128]{2,1,0:T(8,128)S(1)}, f32[8,128,128]{2,1,0:T(8,128)S(1)}, u32[]{:S(2)}, u32[]{:S(2)}) collective-permute-start(f32[8,128,128]{2,1,0:T(8,128)S(1)} %add.261), channel_id=1, source_target_pairs={{0,1},{1,2},{2,3},{3,0},{4,5},{5,6},{6,7},{7,4},{8,9},{9,10},{10,1... | collective-permute-start | bytes 1572872 | tf_op jit(solution)/shard_map/ppermute | solution.py:40
  152.4 18.0 %collective-permute-start.39 = (f32[8,128,128]{2,1,0:T(8,128)S(1)}, f32[8,128,128]{2,1,0:T(8,128)S(1)}, u32[]{:S(2)}, u32[]{:S(2)}) collective-permute-start(f32[8,128,128]{2,1,0:T(8,128)S(1)} %get-tuple-element.87), channel_id=1, source_target_pairs={{0,12},{1,13},{2,14},{3,15},{4,0},{5,1},{6,2},{7,3},{8,4},{9,5},{1... | collective-permute-start | bytes 1572872 | tf_op jit(solution)/shard_map/ppermute | solution.py:40
  166.6 27.3 %collective-permute-start.44 = (f32[4,128,128]{2,1,0:T(8,128)S(1)}, f32[4,128,128]{2,1,0:T(8,128)S(1)}, u32[]{:S(2)}, u32[]{:S(2)}) collective-permute-start(f32[4,128,128]{2,1,0:T(8,128)S(1)} %pad_maximum_fusion.6), channel_id=1, source_target_pairs={{0,16},{1,17},{2,18},{3,19},{4,20},{5,21},{6,22},{7,23},{8,24},{9,... | collective-permute-start | bytes 786440 | tf_op jit(solution)/shard_map/ppermute | solution.py:40
  204.5 20.5 %collective-permute-start.45 = (f32[4,128,128]{2,1,0:T(8,128)S(1)}, f32[4,128,128]{2,1,0:T(8,128)S(1)}, u32[]{:S(2)}, u32[]{:S(2)}) collective-permute-start(f32[4,128,128]{2,1,0:T(8,128)S(1)} %maximum_add_fusion.own_ref), channel_id=1, source_target_pairs={{0,32},{1,33},{2,34},{3,35},{4,36},{5,37},{6,38},{7,39},{8,40},{9,... | collective-permute-start | bytes 786440 | tf_op jit(solution)/shard_map/ppermute | solution.py:40
  204.6 20.5 %collective-permute-start.47 = (f32[4,128,128]{2,1,0:T(8,128)S(1)}, f32[4,128,128]{2,1,0:T(8,128)S(1)}, u32[]{:S(2)}, u32[]{:S(2)}) collective-permute-start(f32[4,128,128]{2,1,0:T(8,128)S(1)} %collective-permute-done.46.across_ref), channel_id=1, source_target_pairs={{0,32},{1,33},{2,34},{3,35},{4,36},{5,37},{6,38},{7,39},{8,40},{9,... | collective-permute-start | bytes 786440 | tf_op jit(solution)/shard_map/ppermute | solution.py:40
  (40 other events, 504.5 us)

commit v6 on v5

--- a/solution.py
+++ b/solution.py
@@ -76,8 +76,8 @@
     return (y, 1 - core, x, z)
 
 
-def after(value, *others):
-    return lax.optimization_barrier((value,) + others)[0]
+def tie(*values):
+    return lax.optimization_barrier(values)
 
 
 def split_high_low(value):
@@ -173,11 +173,11 @@
             total[row] += product[:, :TILE] + product[:, TILE:]
 
     if which == len(CLASS_BUFFERS) - 1:
-        kept_ref, given_ref = rest[-4:-2]
         core = bounds_ref[CORE]
-        half = nrow // 2
-        kept_ref[...] = total[pl.ds(core * half, half)]
-        given_ref[...] = total[pl.ds((1 - core) * half, half)]
+        part = nrow // 4
+        for index, out_ref in enumerate(rest[-6:-2]):
+            side = core if index < 2 else 1 - core
+            out_ref[...] = total[pl.ds((side * 2 + index % 2) * part, part)]
     else:
         rest[-3][...] = total[0:nrow]
 
@@ -186,13 +186,8 @@
     number = CLASS_BUFFERS[which]
     base = sum(CLASS_BUFFERS[:which]) * PER
     buffers = rest[:number]
-    pairs, total, out_sems = rest[number:]
+    total, out_sems = rest[number:]
     begin, end, groups = class_range(bounds_ref, which)
-    for row in range(pairs.shape[0]):
-        high, low = split_high_low(slope_ref[:, row * TILE : (row + 1) * TILE])
-        pairs[row, :, :TILE] = high
-        pairs[row, :, TILE:] = low
-
     @pl.loop(0, number * PER, unroll=4)
     def _(slot):
         total[slot] = jnp.zeros((TILE, TILE), jnp.float32)
@@ -206,7 +201,7 @@
             slot = jnp.where(live, slots_ref[place] - base, number * PER)
             right = tiles_ref[order_ref[place]]
             product = jnp.dot(
-                pairs[rows_ref[place]],
+                slope_ref[rows_ref[place]],
                 jnp.concatenate([right, right], axis=0),
                 preferred_element_type=jnp.float32,
             )
@@ -246,7 +241,7 @@
     number = CLASS_BUFFERS[which]
     out_shape = [jax.ShapeDtypeStruct((nrow, TILE, TILE), jnp.float32)]
     if which == len(CLASS_BUFFERS) - 1:
-        out_shape = [jax.ShapeDtypeStruct((nrow // 2, TILE, TILE), jnp.float32)] * 2
+        out_shape = [jax.ShapeDtypeStruct((nrow // 4, TILE, TILE), jnp.float32)] * 4
     return pl.pallas_call(
         functools.partial(forward_kernel, which),
         name="forward_tiles_%d" % which,
@@ -271,7 +266,6 @@
         in_specs=[smem()] * 4 + [vmem(), vmem()],
         out_specs=[anywhere()] * number,
         scratch_shapes=[
-            pltpu.VMEM((slope.shape[1] // TILE, TILE, 2 * TILE), jnp.bfloat16),
             pltpu.VMEM((number * PER + 1, TILE, TILE), jnp.float32),
             pltpu.SemaphoreType.DMA((number,)),
         ],
@@ -280,54 +274,85 @@
     )(*plan, tiles, slope)
 
 
-def middle_kernel(
-    bounds_ref, across_ref, weight_ref, cotangent_ref, kept_ref, other_ref, pairs_ref,
-    activated_ref, spread_ref, weight_term_ref,
-):
+def triple_left(value):
+    high, low = split_high_low(value)
+    return jnp.concatenate([high, low, high], axis=1)
+
+
+def triple_right(value, axis):
+    high, low = split_high_low(value)
+    return jnp.concatenate([high, high, low], axis=axis)
+
+
+def middle_kernel(which, bounds_ref, across_ref, weight_ref, cotangent_ref, *rest):
+    kept_ref, other_ref = rest[0:2]
     core = bounds_ref[CORE]
-    half = kept_ref.shape[0]
-    weight_term = jnp.zeros((TILE, TILE), jnp.float32)
-    for source, place in ((kept_ref, core), (other_ref, 1 - core)):
-        for j in range(half):
-            columns = pl.ds(pl.multiple_of((place * half + j) * TILE, TILE), TILE)
-            block = source[j]
-            value = lax.dot_general(
-                across_ref[...],
-                block,
-                (((1,), (1,)), ((), ())),
-                precision=HI,
-                preferred_element_type=jnp.float32,
-            )
-            square = value * value
-            bend = jnp.tanh(GELU_SCALE * (value + GELU_CUBE * (square * value)))
-            activated_ref[:, columns] = 0.5 * value * (1.0 + bend)
-            rate = 0.5 * (1.0 + bend) + 0.5 * value * (1.0 - bend * bend) * (
-                GELU_SCALE * (1.0 + 3.0 * GELU_CUBE * square)
-            )
-            slope = cotangent_ref[:, columns] * rate
-            weight_term += jnp.dot(
-                slope, block, precision=HI, preferred_element_type=jnp.float32
-            )
-            spread_ref[:, columns] = jnp.dot(
-                weight_ref[...], slope, precision=HI, preferred_element_type=jnp.float32
-            )
-    weight_term_ref[...] = jnp.transpose(weight_term)
-
-
-def middle_part(bounds, across, weight, cotangent, kept, other, pairs):
+    part = kept_ref.shape[0]
+    across = triple_left(across_ref[...])
+    weight = triple_left(weight_ref[...])
+    if which == 0:
+        activated_ref, spread_ref, weight_term_ref = rest[-3:]
+        weight_term = jnp.zeros((TILE, TILE), jnp.float32)
+    else:
+        early_activated_ref, early_spread_ref, early_term_ref = rest[3:6]
+        activated_ref, spread_ref, weight_term_ref = rest[-3:]
+        weight_term = early_term_ref[...]
+    for index in range(2 * part):
+        source = kept_ref if index < part else other_ref
+        side = core if index < part else 1 - core
+        row = (side * 2 + which) * part + index % part
+        columns = pl.ds(pl.multiple_of(row * TILE, TILE), TILE)
+        block = source[index % part]
+        value = lax.dot_general(
+            across,
+            triple_right(block, 1),
+            (((1,), (1,)), ((), ())),
+            preferred_element_type=jnp.float32,
+        )
+        square = value * value
+        bend = jnp.tanh(GELU_SCALE * (value + GELU_CUBE * (square * value)))
+        activated = 0.5 * value * (1.0 + bend)
+        rate = 0.5 * (1.0 + bend) + 0.5 * value * (1.0 - bend * bend) * (
+            GELU_SCALE * (1.0 + 3.0 * GELU_CUBE * square)
+        )
+        slope = cotangent_ref[:, columns] * rate
+        weight_term += jnp.dot(
+            triple_left(slope), triple_right(block, 0), preferred_element_type=jnp.float32
+        )
+        spread = jnp.dot(weight, triple_right(slope, 0), preferred_element_type=jnp.float32)
+        high, low = split_high_low(spread)
+        if which == 0:
+            activated_ref[index] = activated
+            spread_ref[index, :, :TILE] = high
+            spread_ref[index, :, TILE:] = low
+        else:
+            activated_ref[:, columns] = activated
+            spread_ref[row, :, :TILE] = high
+            spread_ref[row, :, TILE:] = low
+            early = side * 2 * part + index % part
+            early_columns = pl.ds(pl.multiple_of(early * TILE, TILE), TILE)
+            activated_ref[:, early_columns] = early_activated_ref[index]
+            spread_ref[early] = early_spread_ref[index]
+    weight_term_ref[...] = jnp.transpose(weight_term) if which else weight_term
+
+
+def middle_part(which, bounds, across, weight, cotangent, kept, other, pairs, early=()):
+    part = kept.shape[0]
+    rows = 4 * part if which else 2 * part
+    activated = cotangent.shape if which else (rows, TILE, TILE)
     return pl.pallas_call(
-        middle_kernel,
-        name="middle",
+        functools.partial(middle_kernel, which),
+        name="middle_%d" % which,
         out_shape=[
-            jax.ShapeDtypeStruct(cotangent.shape, jnp.float32),
-            jax.ShapeDtypeStruct(cotangent.shape, jnp.float32),
+            jax.ShapeDtypeStruct(activated, jnp.float32),
+            jax.ShapeDtypeStruct((rows, TILE, 2 * TILE), jnp.bfloat16),
             jax.ShapeDtypeStruct(weight.shape, jnp.float32),
         ],
-        in_specs=[smem()] + [vmem()] * 6,
+        in_specs=[smem()] + [vmem()] * (6 + len(early)),
         out_specs=[vmem()] * 3,
-        cost_estimate=cost(4),
+        cost_estimate=cost(2),
         compiler_params=pltpu.CompilerParams(vmem_limit_bytes=VMEM_BYTES),
-    )(bounds, across, weight, cotangent, kept, other, pairs)
+    )(bounds, across, weight, cotangent, kept, other, pairs, *early)
 
 
 def assemble_kernel(bounds_ref, own_ref, own_other_ref, across_ref, across_other_ref, out_ref):
@@ -422,41 +447,61 @@
     return [row, first_one, first_two, first_three, column, second_one, second_two, second_three]
 
 
-def gather_apart(near, partner, pairs):
+def gather_apart(near, partner):
+    near = list(near)
     row_sent = permute(near[0][2:], y_far)
-    column_sent = permute(after(near[4][2:], row_sent, pairs), y_far)
+    column, row_sent = tie(near[4], row_sent)
+    near[4] = column
+    column_sent = permute(column[2:], y_far)
     row = jnp.concatenate([partner[:2], row_sent], axis=0)
     column = jnp.concatenate([partner[2:], column_sent], axis=0)
-    first_three = permute(after(row, near[3]), z_up)
-    second_three = permute(after(column, near[7]), x_up)
-    first_one = permute(after(row, near[2]), z_down)
-    second_one = permute(after(column, near[6]), x_down)
-    return [row, first_one, first_three, column, second_one, second_three]
-
-
-def scatter_terms(own, apart, apart_far, weight_term):
-    row_sent = permute(apart_far[0], z_down)
-    column_sent = permute(apart_far[1], x_down)
-    weight_term = flip_add(after(weight_term, row_sent, apart[0]), "x", 1)
+    row, near[3] = tie(row, near[3])
+    first_three = permute(row, z_up)
+    row, near[2] = tie(row, near[2])
+    first_one = permute(row, z_down)
+    column, near[7] = tie(column, near[7])
+    second_three = permute(column, x_up)
+    column, near[6] = tie(column, near[6])
+    second_one = permute(column, x_down)
+    return near, [row, first_one, first_three, column, second_one, second_three]
+
+
+def scatter_terms(plan, pairs, spread, weight_term):
+    apart_far = backward_part(2, plan, pairs, spread)
+    spread, *apart_far = tie(spread, *apart_far)
+    row_sent, column_sent = permute(apart_far[0], z_down), permute(apart_far[1], x_down)
+    apart = backward_part(1, plan, pairs, spread)
     row_one, column_one = permute(apart[1], z_up), permute(apart[4], x_up)
-    row_three = permute(apart[2] + row_sent, z_down)
-    column_three = permute(apart[5] + column_sent, x_down)
-    weight_term = flip_add(after(weight_term, row_one), "x", 2)
-
-    own_two = permute(after(own[2], row_one), z_up)
-    own_column_two = permute(after(own[6], column_one), x_up)
-    own_three = permute(after(own[3], row_three), z_down)
-    own_column_three = permute(after(own[7], column_three), x_down)
+    row_back, column_back = apart[2] + row_sent, apart[5] + column_sent
+    spread, weight_term, row_back, column_back = tie(spread, weight_term, row_back, column_back)
+    row_three, column_three = permute(row_back, z_down), permute(column_back, x_down)
+    own = list(backward_part(0, plan, pairs, spread))
+    weight_term = flip_add(weight_term, "x", 1)
+
+    own[2], row_one = tie(own[2], row_one)
+    own_two = permute(own[2], z_up)
+    own[6], column_one = tie(own[6], column_one)
+    own_column_two = permute(own[6], x_up)
+    own[3], row_three = tie(own[3], row_three)
+    own_three = permute(own[3], z_down)
+    own[7], column_three = tie(own[7], column_three)
+    own_column_three = permute(own[7], x_down)
+    weight_term, own_two = tie(weight_term, own_two)
+    weight_term = flip_add(weight_term, "x", 2)
     own_one = permute(own[1] + own_two, z_up)
     own_column_one = permute(own[5] + own_column_two, x_up)
 
     row = apart[0] + row_one + row_three
     column = apart[3] + column_one + column_three
-    weight_term = flip_add(after(weight_term, row_three), "z", 1)
     row_far = permute(row[2:], y_far)
-    column_far = permute(after(column[2:], row_far), y_far)
-    weight_term = flip_add(after(weight_term, row_far), "z", 2)
-    last_far = permute(jnp.concatenate([row[:2], column[:2]], axis=0), y_far)
+    column, row_far, weight_term = tie(column, row_far, weight_term)
+    column_far = permute(column[2:], y_far)
+    weight_term = flip_add(weight_term, "z", 1)
+    last, column_far, weight_term = tie(
+        jnp.concatenate([row[:2], column[:2]], axis=0), column_far, weight_term
+    )
+    last_far = permute(last, y_far)
+    weight_term = flip_add(weight_term, "z", 2)
 
     row = own[0] + own_one + own_three
     column = own[4] + own_column_one + own_column_three
@@ -466,9 +511,9 @@
     ]
     half = reduce_ring(rows, x_up, x_down, True)
     other = reduce_ring(columns, z_up, z_down, True)
-    weight_term = after(weight_term, column_far)
-    weight_term = weight_term + permute(weight_term, y_far)
-    return jnp.concatenate([half, other], axis=0) + last_far, weight_term
+    total = jnp.concatenate([half, other], axis=0) + last_far
+    total, weight_term = tie(total, weight_term)
+    return total, weight_term + permute(weight_term, y_far)
 
 
 def flip_add(value, axis, step):
@@ -487,28 +532,30 @@
     across = weight.T
 
     row, column, partner = gather_features(features, loop)
+    plan, across, row, column = tie(plan, across, row, column)
     near = gather_near(row, column)
-    plan, count, across = lax.optimization_barrier((plan, count, across, row, column))[:3]
+    count, near[1], near[5] = tie(count, near[1], near[5])
     pairs = pair_tiles(count, tile_collection)
-    apart = gather_apart(near, partner, pairs)
+    near, apart = gather_apart(near, partner)
     partial = forward_part(0, plan, pairs, near, None, nrow)
-    far = [permute(after(apart[2], *partial), z_up), permute(after(apart[5], *partial), x_up)]
-    partial = forward_part(1, plan, pairs, apart, partial[0], nrow)
-    kept, given = forward_part(2, plan, pairs, far, partial[0], nrow)
-
-    kept = kept + permute(given, core_swap)
-    kept = kept + permute(kept, y_pair)
-    other = permute(kept, core_swap)
+    apart[2], apart[5], partial = tie(apart[2], apart[5], partial[0])
+    far = [permute(apart[2], z_up), permute(apart[5], x_up)]
+    partial = forward_part(1, plan, pairs, apart, partial, nrow)
+    *kept, given_first, given_second = forward_part(2, plan, pairs, far, partial[0], nrow)
+
+    bounds = plan[0]
+    kept = [kept[0] + permute(given_first, core_swap), kept[1] + permute(given_second, core_swap)]
+    kept = [value + permute(value, y_pair) for value in kept]
+    early = middle_part(
+        0, bounds, across, weight, cotangent, kept[0], permute(kept[0], core_swap), pairs
+    )
     activated, spread, weight_term = middle_part(
-        plan[0], across, weight, cotangent, kept, other, pairs
+        1, bounds, across, weight, cotangent, kept[1], permute(kept[1], core_swap), pairs, early
     )
-    apart_far = backward_part(2, plan, pairs, spread)
-    apart = backward_part(1, plan, pairs, after(spread, *apart_far))
-    own = backward_part(0, plan, pairs, after(spread, *apart))
-    total, weight_grad = scatter_terms(own, apart, apart_far, weight_term)
+    total, weight_grad = scatter_terms(plan, pairs, spread, weight_term)
     far_total = permute(total, y_pair)
     parts = [total, permute(total, core_swap), far_total, permute(far_total, core_swap)]
-    return (activated, assemble(plan[0], parts), weight_grad)
+    return (activated, assemble(bounds, parts), weight_grad)
 
 
 def solution(mesh):

time: 227 us -> 198 us (0.87)
  local copies, waits for them, and re-layouts: 15.1 us -> 2.7 us
  waiting for transfers between devices: 87.1 us -> 79.8 us
  starting transfers between devices: 91.4 us -> 85.7 us
  Pallas kernels: 26.2 us -> 22.2 us
    unnamed x23 -> x5, local copies, waits for them, and re-layouts: 11.7 us -> 0.94 us
    ppermute x53 -> x56, waiting for transfers between devices: 87.1 us -> 79.8 us  [permute(): return lax.ppermute(value, AXES, pairs)]
    ppermute x53 -> x56, starting transfers between devices: 91.4 us -> 85.7 us  [permute(): return lax.ppermute(value, AXES, pairs)]
    pallas_call x1 -> x2, Pallas kernels: 9.21 us -> 6.28 us  [middle_part(): pl.pallas_call(functools.partial(middle_kernel, which), name='middle_%d'...]
  transfers between devices with their start and end apart: 53 -> 56, of which waited for: 23 -> 22; matrix products, arithmetic and copies ran while one was open for 3% -> 3% of each run, Pallas kernels for 5% -> 7%
where the time goes in v6:
time: 198 us; the launch traced here: 197 us
  starting transfers between devices  85.7 us (43%)
  waiting for transfers between devices  79.8 us (40%)
  Pallas kernels  22.2 us (11%)
  other arithmetic  4.34 us (2%)
  local copies, waits for them, and re-layouts  2.7 us (1%)
    ppermute x56, starting transfers between devices, permute(): return lax.ppermute(value, AXES, pairs)  85.7 us
    ppermute x56, waiting for transfers between devices, permute(): return lax.ppermute(value, AXES, pairs)  79.8 us
    pallas_call x2, Pallas kernels, middle_part(): pl.pallas_call(functools.partial(middle_kernel, which), name='middle_%d'...  6.28 us
    pallas_call x3, Pallas kernels, forward_part(): pl.pallas_call(functools.partial(forward_kernel, which), name='forward_ti...  6.1 us
    pallas_call x3, Pallas kernels, backward_part(): pl.pallas_call(functools.partial(backward_kernel, which), name='backward_...  5.55 us
  transfers between devices with their start and end apart: 56, of which 22 were waited for; matrix products, arithmetic and copies ran while one was open for 3% of the time, Pallas kernels for 7%

profile of v6, /device:TPU:0, one launch (start us, length us, event | category | flops | bytes accessed | tf_op | source)
XLA Modules:
  0.0 196.5 jit_solution(11122525211606868778)
XLA Ops:
  19.3 3.0 %collective-permute-start.7 = (f32[8,128,128]{2,1,0:T(8,128)S(1)}, f32[8,128,128]{2,1,0:T(8,128)S(1)}, u32[]{:S(2)}, u32[]{:S(2)}) collective-permute-start(f32[8,128,128]{2,1,0:T(8,128)S(1)} %pad_maximum_fusion.1.rest_4_), channel_id=1, source_target_pairs={{0,12},{1,13},{2,14},{3,15},{4,0},{5,1},{6,2},{7,3},{8,4},{9,5},{1... | collective-permute-start | bytes 1572872 | tf_op jit(solution)/shard_map/ppermute | solution.py:40
  24.7 3.3 %collective-permute-start.9 = (f32[6,128,128]{2,1,0:T(8,128)S(1)}, f32[6,128,128]{2,1,0:T(8,128)S(1)}, u32[]{:S(2)}, u32[]{:S(2)}) collective-permute-start(f32[6,128,128]{2,1,0:T(8,128)S(1)} %slice.79), channel_id=1, source_target_pairs={{0,16},{1,17},{2,18},{3,19},{4,20},{5,21},{6,22},{7,23},{8,24},{9,... | collective-permute-start | bytes 1179656 | tf_op jit(solution)/shard_map/ppermute | solution.py:40
  29.0 5.1 %collective-permute-done.9 = f32[6,128,128]{2,1,0:T(8,128)S(1)} collective-permute-done((f32[6,128,128]{2,1,0:T(8,128)S(1)}, f32[6,128,128]{2,1,0:T(8,128)S(1)}, u32[]{:S(2)}, u32[]{:S(2)}) %collective-permute-start.9) | collective-permute-done | bytes 393248 | tf_op jit(solution)/shard_map/ppermute | solution.py:40
  34.2 3.3 %collective-permute-done.8 = f32[4,128,128]{2,1,0:T(8,128)S(1)} collective-permute-done((f32[4,128,128]{2,1,0:T(8,128)S(1)}, f32[4,128,128]{2,1,0:T(8,128)S(1)}, u32[]{:S(2)}, u32[]{:S(2)}) %collective-permute-start.8) | collective-permute-done | bytes 262176 | tf_op jit(solution)/shard_map/ppermute | solution.py:40
  48.4 3.0 %collective-permute-start.11 = (f32[8,128,128]{2,1,0:T(8,128)S(1)}, f32[8,128,128]{2,1,0:T(8,128)S(1)}, u32[]{:S(2)}, u32[]{:S(2)}) collective-permute-start(f32[8,128,128]{2,1,0:T(8,128)S(1)} %pad_maximum_fusion.2.rest_0_), channel_id=1, source_target_pairs={{0,1},{1,2},{2,3},{3,0},{4,5},{5,6},{6,7},{7,4},{8,9},{9,10},{10,1... | collective-permute-start | bytes 1572872 | tf_op jit(solution)/shard_map/ppermute | solution.py:40
  51.6 3.1 %collective-permute-start.20 = (f32[8,128,128]{2,1,0:T(8,128)S(1)}, f32[8,128,128]{2,1,0:T(8,128)S(1)}, u32[]{:S(2)}, u32[]{:S(2)}) collective-permute-start(f32[8,128,128]{2,1,0:T(8,128)S(1)} %pad_maximum_fusion.3.rest_3_), channel_id=1, source_target_pairs={{0,12},{1,13},{2,14},{3,15},{4,0},{5,1},{6,2},{7,3},{8,4},{9,5},{1... | collective-permute-start | bytes 1572872 | tf_op jit(solution)/shard_map/ppermute | solution.py:40
  57.2 3.7 %collective-permute-start.19 = (f32[8,128,128]{2,1,0:T(8,128)S(1)}, f32[8,128,128]{2,1,0:T(8,128)S(1)}, u32[]{:S(2)}, u32[]{:S(2)}) collective-permute-start(f32[8,128,128]{2,1,0:T(8,128)S(1)} %pad_maximum_fusion.2.rest_0_), channel_id=1, source_target_pairs={{0,3},{1,0},{2,1},{3,2},{4,7},{5,4},{6,5},{7,6},{8,11},{9,8},{10,9... | collective-permute-start | bytes 1572872 | tf_op jit(solution)/shard_map/ppermute | solution.py:40
  63.3 3.6 %collective-permute-done.14.rest_5_ = f32[8,128,128]{2,1,0:T(8,128)S(1)} collective-permute-done((f32[8,128,128]{2,1,0:T(8,128)S(1)}, f32[8,128,128]{2,1,0:T(8,128)S(1)}, u32[]{:S(2)}, u32[]{:S(2)}) %collective-permute-start.14) | collective-permute-done | bytes 524320 | tf_op jit(solution)/shard_map/ppermute | solution.py:40
  66.9 3.7 %collective-permute-done.19.rest_1_ = f32[8,128,128]{2,1,0:T(8,128)S(1)} collective-permute-done((f32[8,128,128]{2,1,0:T(8,128)S(1)}, f32[8,128,128]{2,1,0:T(8,128)S(1)}, u32[]{:S(2)}, u32[]{:S(2)}) %collective-permute-start.19) | collective-permute-done | bytes 524320 | tf_op jit(solution)/shard_map/ppermute | solution.py:40
  72.8 4.5 %collective-permute-done.17.rest_0_ = f32[8,128,128]{2,1,0:T(8,128)S(1)} collective-permute-done((f32[8,128,128]{2,1,0:T(8,128)S(1)}, f32[8,128,128]{2,1,0:T(8,128)S(1)}, u32[]{:S(2)}, u32[]{:S(2)}) %collective-permute-start.17) | collective-permute-done | bytes 524320 | tf_op jit(solution)/shard_map/ppermute | solution.py:40
  83.5 6.7 %collective-permute-done.25 = f32[4,128,128]{2,1,0:T(8,128)S(1)} collective-permute-done((f32[4,128,128]{2,1,0:T(8,128)S(1)}, f32[4,128,128]{2,1,0:T(8,128)S(1)}, u32[]{:S(2)}, u32[]{:S(2)}) %collective-permute-start.25) | collective-permute-done | bytes 262176 | tf_op jit(solution)/shard_map/ppermute | solution.py:40
  90.4 5.0 %collective-permute-done.22 = f32[4,128,128]{2,1,0:T(8,128)S(1)} collective-permute-done((f32[4,128,128]{2,1,0:T(8,128)S(1)}, f32[4,128,128]{2,1,0:T(8,128)S(1)}, u32[]{:S(2)}, u32[]{:S(2)}) %collective-permute-start.22) | collective-permute-done | bytes 262176 | tf_op jit(solution)/shard_map/ppermute | solution.py:40
  98.2 3.6 %middle_1.1 = (f32[128,2048]{1,0:T(8,128)}, bf16[16,128,256]{2,1,0:T(8,128)(2,1)S(1)}, f32[128,128]{1,0:T(8,128)S(1)}) custom-call(s32[8]{0:T(128)S(1)} %compare_select_fusion.11.bounds_ref, f32[128,128]{1,0:T(8,128)S(1)} %bitcast.18, f32[128,128]{1,0:T(8,128)S(1)} %copy-done.1, f32[128,2048]{1,0:T(8,128)S(1)} %copy-done, f32[4,128,128]{2,1,0:T(8,128)S(1)} %add.266.rest_0_, ...), custom_call_target="tpu_custom_call" | custom-call | flops 2200000000 | bytes 1048576 | tf_op jit(solution)/shard_map/middle_1/pallas_call | solution.py:343
  103.1 3.7 %collective-permute-start.27 = (f32[8,128,128]{2,1,0:T(8,128)S(1)}, f32[8,128,128]{2,1,0:T(8,128)S(1)}, u32[]{:S(2)}, u32[]{:S(2)}) collective-permute-start(f32[8,128,128]{2,1,0:T(8,128)S(1)} %get-tuple-element.114), channel_id=1, source_target_pairs={{0,3},{1,0},{2,1},{3,2},{4,7},{5,4},{6,5},{7,6},{8,11},{9,8},{10,9... | collective-permute-start | bytes 1572872 | tf_op jit(solution)/shard_map/ppermute | solution.py:40
  113.4 3.9 %collective-permute-done.27 = f32[8,128,128]{2,1,0:T(8,128)S(1)} collective-permute-done((f32[8,128,128]{2,1,0:T(8,128)S(1)}, f32[8,128,128]{2,1,0:T(8,128)S(1)}, u32[]{:S(2)}, u32[]{:S(2)}) %collective-permute-start.27) | collective-permute-done | bytes 524320 | tf_op jit(solution)/shard_map/ppermute | solution.py:40
  127.9 9.7 %collective-permute-done.29 = f32[128,128]{1,0:T(8,128)S(1)} collective-permute-done((f32[128,128]{1,0:T(8,128)S(1)}, f32[128,128]{1,0:T(8,128)S(1)}, u32[]{:S(2)}, u32[]{:S(2)}) %collective-permute-start.29) | collective-permute-done | bytes 65568 | tf_op jit(solution)/shard_map/ppermute | solution.py:40
  144.6 4.1 %collective-permute-done.38 = f32[128,128]{1,0:T(8,128)S(1)} collective-permute-done((f32[128,128]{1,0:T(8,128)S(1)}, f32[128,128]{1,0:T(8,128)S(1)}, u32[]{:S(2)}, u32[]{:S(2)}) %collective-permute-start.38) | collective-permute-done | bytes 65568 | tf_op jit(solution)/shard_map/ppermute | solution.py:40
  150.3 3.3 %collective-permute-done.46 = f32[128,128]{1,0:T(8,128)S(1)} collective-permute-done((f32[128,128]{1,0:T(8,128)S(1)}, f32[128,128]{1,0:T(8,128)S(1)}, u32[]{:S(2)}, u32[]{:S(2)}) %collective-permute-start.46) | collective-permute-done | bytes 65568 | tf_op jit(solution)/shard_map/ppermute | solution.py:40
  159.2 3.7 %collective-permute-done.45 = f32[6,128,128]{2,1,0:T(8,128)S(1)} collective-permute-done((f32[6,128,128]{2,1,0:T(8,128)S(1)}, f32[6,128,128]{2,1,0:T(8,128)S(1)}, u32[]{:S(2)}, u32[]{:S(2)}) %collective-permute-start.45) | collective-permute-done | bytes 393248 | tf_op jit(solution)/shard_map/ppermute | solution.py:40
  164.0 3.2 %collective-permute-start.41 = (f32[2,128,128]{2,1,0:T(8,128)S(1)}, f32[2,128,128]{2,1,0:T(8,128)S(1)}, u32[]{:S(2)}, u32[]{:S(2)}) collective-permute-start(f32[2,128,128]{2,1,0:T(8,128)S(1)} %get-tuple-element.161), channel_id=1, source_target_pairs={{0,12},{1,13},{2,14},{3,15},{4,0},{5,1},{6,2},{7,3},{8,4},{9,5},{1... | collective-permute-start | bytes 393224 | tf_op jit(solution)/shard_map/ppermute | solution.py:40
  172.9 3.2 %collective-permute-start.49 = (f32[2,128,128]{2,1,0:T(8,128)S(1)}, f32[2,128,128]{2,1,0:T(8,128)S(1)}, u32[]{:S(2)}, u32[]{:S(2)}) collective-permute-start(f32[2,128,128]{2,1,0:T(8,128)S(1)} %get-tuple-element.163), channel_id=1, source_target_pairs={{0,3},{1,0},{2,1},{3,2},{4,7},{5,4},{6,5},{7,6},{8,11},{9,8},{10,9... | collective-permute-start | bytes 393224 | tf_op jit(solution)/shard_map/ppermute | solution.py:40
  179.0 4.8 %collective-permute-start.53 = (f32[4,128,128]{2,1,0:T(8,128)S(1)}, f32[4,128,128]{2,1,0:T(8,128)S(1)}, u32[]{:S(2)}, u32[]{:S(2)}) collective-permute-start(f32[4,128,128]{2,1,0:T(8,128)S(1)} %maximum_add_fusion.own_ref), channel_id=1, source_target_pairs={{0,64},{1,65},{2,66},{3,67},{4,68},{5,69},{6,70},{7,71},{8,72},{9,... | collective-permute-start | bytes 786440 | tf_op jit(solution)/shard_map/ppermute | solution.py:40
  183.9 4.3 %collective-permute-done.53.across_ref = f32[4,128,128]{2,1,0:T(8,128)S(1)} collective-permute-done((f32[4,128,128]{2,1,0:T(8,128)S(1)}, f32[4,128,128]{2,1,0:T(8,128)S(1)}, u32[]{:S(2)}, u32[]{:S(2)}) %collective-permute-start.53) | collective-permute-done | bytes 262176 | tf_op jit(solution)/shard_map/ppermute | solution.py:40
  188.6 5.7 %collective-permute-done.55 = f32[128,128]{1,0:T(8,128)S(1)} collective-permute-done((f32[128,128]{1,0:T(8,128)S(1)}, f32[128,128]{1,0:T(8,128)S(1)}, u32[]{:S(2)}, u32[]{:S(2)}) %collective-permute-start.55) | collective-permute-done | bytes 65568 | tf_op jit(solution)/shard_map/ppermute | solution.py:40
  (149 shorter events, 93.5 us)
Async XLA Ops:
  2.3 15.5 %collective-permute-start.5 = (f32[2,128,128]{2,1,0:T(8,128)S(1)}, f32[2,128,128]{2,1,0:T(8,128)S(1)}, u32[]{:S(2)}, u32[]{:S(2)}) collective-permute-start(f32[2,128,128]{2,1,0:T(8,128)S(1)} %get-tuple-element.166), channel_id=1, source_target_pairs={{0,1},{1,2},{2,3},{3,0},{4,5},{5,6},{6,7},{7,4},{8,9},{9,10},{10,1... | collective-permute-start | bytes 393224 | tf_op jit(solution)/shard_map/ppermute | solution.py:40
  19.3 20.6 %collective-permute-start.7 = (f32[8,128,128]{2,1,0:T(8,128)S(1)}, f32[8,128,128]{2,1,0:T(8,128)S(1)}, u32[]{:S(2)}, u32[]{:S(2)}) collective-permute-start(f32[8,128,128]{2,1,0:T(8,128)S(1)} %pad_maximum_fusion.1.rest_4_), channel_id=1, source_target_pairs={{0,12},{1,13},{2,14},{3,15},{4,0},{5,1},{6,2},{7,3},{8,4},{9,5},{1... | collective-permute-start | bytes 1572872 | tf_op jit(solution)/shard_map/ppermute | solution.py:40
  22.3 20.5 %collective-permute-start.6 = (f32[8,128,128]{2,1,0:T(8,128)S(1)}, f32[8,128,128]{2,1,0:T(8,128)S(1)}, u32[]{:S(2)}, u32[]{:S(2)}) collective-permute-start(f32[8,128,128]{2,1,0:T(8,128)S(1)} %pad_maximum_fusion.rest_0_), channel_id=1, source_target_pairs={{0,3},{1,0},{2,1},{3,2},{4,7},{5,4},{6,5},{7,6},{8,11},{9,8},{10,9... | collective-permute-start | bytes 1572872 | tf_op jit(solution)/shard_map/ppermute | solution.py:40
  29.0 22.4 %collective-permute-start.13 = (f32[8,128,128]{2,1,0:T(8,128)S(1)}, f32[8,128,128]{2,1,0:T(8,128)S(1)}, u32[]{:S(2)}, u32[]{:S(2)}) collective-permute-start(f32[8,128,128]{2,1,0:T(8,128)S(1)} %pad_maximum_fusion.1.rest_4_), channel_id=1, source_target_pairs={{0,4},{1,5},{2,6},{3,7},{4,8},{5,9},{6,10},{7,11},{8,12},{9,13},{1... | collective-permute-start | bytes 1572872 | tf_op jit(solution)/shard_map/ppermute | solution.py:40
  34.1 14.3 %collective-permute-start.10 = (f32[8,128,128]{2,1,0:T(8,128)S(1)}, f32[8,128,128]{2,1,0:T(8,128)S(1)}, u32[]{:S(2)}, u32[]{:S(2)}) collective-permute-start(f32[8,128,128]{2,1,0:T(8,128)S(1)} %pad_maximum_fusion.rest_0_), channel_id=1, source_target_pairs={{0,1},{1,2},{2,3},{3,0},{4,5},{5,6},{6,7},{7,4},{8,9},{9,10},{10,1... | collective-permute-start | bytes 1572872 | tf_op jit(solution)/shard_map/ppermute | solution.py:40
  37.4 13.9 %collective-permute-start.12 = (f32[6,128,128]{2,1,0:T(8,128)S(1)}, f32[6,128,128]{2,1,0:T(8,128)S(1)}, u32[]{:S(2)}, u32[]{:S(2)}) collective-permute-start(f32[6,128,128]{2,1,0:T(8,128)S(1)} %slice.81), channel_id=1, source_target_pairs={{0,16},{1,17},{2,18},{3,19},{4,20},{5,21},{6,22},{7,23},{8,24},{9,... | collective-permute-start | bytes 1179656 | tf_op jit(solution)/shard_map/ppermute | solution.py:40
  42.7 14.4 %collective-permute-start.15 = (f32[8,128,128]{2,1,0:T(8,128)S(1)}, f32[8,128,128]{2,1,0:T(8,128)S(1)}, u32[]{:S(2)}, u32[]{:S(2)}) collective-permute-start(f32[8,128,128]{2,1,0:T(8,128)S(1)} %collective-permute-done.6.rest_1_), channel_id=1, source_target_pairs={{0,3},{1,0},{2,1},{3,2},{4,7},{5,4},{6,5},{7,6},{8,11},{9,8},{10,9... | collective-permute-start | bytes 1572872 | tf_op jit(solution)/shard_map/ppermute | solution.py:40
  48.4 14.9 %collective-permute-start.11 = (f32[8,128,128]{2,1,0:T(8,128)S(1)}, f32[8,128,128]{2,1,0:T(8,128)S(1)}, u32[]{:S(2)}, u32[]{:S(2)}) collective-permute-start(f32[8,128,128]{2,1,0:T(8,128)S(1)} %pad_maximum_fusion.2.rest_0_), channel_id=1, source_target_pairs={{0,1},{1,2},{2,3},{3,0},{4,5},{5,6},{6,7},{7,4},{8,9},{9,10},{10,1... | collective-permute-start | bytes 1572872 | tf_op jit(solution)/shard_map/ppermute | solution.py:40
  51.4 15.5 %collective-permute-start.14 = (f32[8,128,128]{2,1,0:T(8,128)S(1)}, f32[8,128,128]{2,1,0:T(8,128)S(1)}, u32[]{:S(2)}, u32[]{:S(2)}) collective-permute-start(f32[8,128,128]{2,1,0:T(8,128)S(1)} %pad_maximum_fusion.3.rest_3_), channel_id=1, source_target_pairs={{0,4},{1,5},{2,6},{3,7},{4,8},{5,9},{6,10},{7,11},{8,12},{9,13},{1... | collective-permute-start | bytes 1572872 | tf_op jit(solution)/shard_map/ppermute | solution.py:40
  51.6 15.3 %collective-permute-start.20 = (f32[8,128,128]{2,1,0:T(8,128)S(1)}, f32[8,128,128]{2,1,0:T(8,128)S(1)}, u32[]{:S(2)}, u32[]{:S(2)}) collective-permute-start(f32[8,128,128]{2,1,0:T(8,128)S(1)} %pad_maximum_fusion.3.rest_3_), channel_id=1, source_target_pairs={{0,12},{1,13},{2,14},{3,15},{4,0},{5,1},{6,2},{7,3},{8,4},{9,5},{1... | collective-permute-start | bytes 1572872 | tf_op jit(solution)/shard_map/ppermute | solution.py:40
  57.2 13.4 %collective-permute-start.19 = (f32[8,128,128]{2,1,0:T(8,128)S(1)}, f32[8,128,128]{2,1,0:T(8,128)S(1)}, u32[]{:S(2)}, u32[]{:S(2)}) collective-permute-start(f32[8,128,128]{2,1,0:T(8,128)S(1)} %pad_maximum_fusion.2.rest_0_), channel_id=1, source_target_pairs={{0,3},{1,0},{2,1},{3,2},{4,7},{5,4},{6,5},{7,6},{8,11},{9,8},{10,9... | collective-permute-start | bytes 1572872 | tf_op jit(solution)/shard_map/ppermute | solution.py:40
  83.2 12.2 %collective-permute-start.22 = (f32[4,128,128]{2,1,0:T(8,128)S(1)}, f32[4,128,128]{2,1,0:T(8,128)S(1)}, u32[]{:S(2)}, u32[]{:S(2)}) collective-permute-start(f32[4,128,128]{2,1,0:T(8,128)S(1)} %add.265), channel_id=1, source_target_pairs={{0,64},{1,65},{2,66},{3,67},{4,68},{5,69},{6,70},{7,71},{8,72},{9,... | collective-permute-start | bytes 786440 | tf_op jit(solution)/shard_map/ppermute | solution.py:40
  103.1 14.2 %collective-permute-start.27 = (f32[8,128,128]{2,1,0:T(8,128)S(1)}, f32[8,128,128]{2,1,0:T(8,128)S(1)}, u32[]{:S(2)}, u32[]{:S(2)}) collective-permute-start(f32[8,128,128]{2,1,0:T(8,128)S(1)} %get-tuple-element.114), channel_id=1, source_target_pairs={{0,3},{1,0},{2,1},{3,2},{4,7},{5,4},{6,5},{7,6},{8,11},{9,8},{10,9... | collective-permute-start | bytes 1572872 | tf_op jit(solution)/shard_map/ppermute | solution.py:40
  106.8 12.3 %collective-permute-start.28 = (f32[8,128,128]{2,1,0:T(8,128)S(1)}, f32[8,128,128]{2,1,0:T(8,128)S(1)}, u32[]{:S(2)}, u32[]{:S(2)}) collective-permute-start(f32[8,128,128]{2,1,0:T(8,128)S(1)} %get-tuple-element.116), channel_id=1, source_target_pairs={{0,12},{1,13},{2,14},{3,15},{4,0},{5,1},{6,2},{7,3},{8,4},{9,5},{1... | collective-permute-start | bytes 1572872 | tf_op jit(solution)/shard_map/ppermute | solution.py:40
  108.9 14.5 %collective-permute-start.30 = (f32[8,128,128]{2,1,0:T(8,128)S(1)}, f32[8,128,128]{2,1,0:T(8,128)S(1)}, u32[]{:S(2)}, u32[]{:S(2)}) collective-permute-start(f32[8,128,128]{2,1,0:T(8,128)S(1)} %get-tuple-element.122), channel_id=1, source_target_pairs={{0,1},{1,2},{2,3},{3,0},{4,5},{5,6},{6,7},{7,4},{8,9},{9,10},{10,1... | collective-permute-start | bytes 1572872 | tf_op jit(solution)/shard_map/ppermute | solution.py:40
  111.2 16.7 %collective-permute-start.35 = (f32[8,128,128]{2,1,0:T(8,128)S(1)}, f32[8,128,128]{2,1,0:T(8,128)S(1)}, u32[]{:S(2)}, u32[]{:S(2)}) collective-permute-start(f32[8,128,128]{2,1,0:T(8,128)S(1)} %get-tuple-element.130), channel_id=1, source_target_pairs={{0,4},{1,5},{2,6},{3,7},{4,8},{5,9},{6,10},{7,11},{8,12},{9,13},{1... | collective-permute-start | bytes 1572872 | tf_op jit(solution)/shard_map/ppermute | solution.py:40
  121.4 16.3 %collective-permute-start.33 = (f32[8,128,128]{2,1,0:T(8,128)S(1)}, f32[8,128,128]{2,1,0:T(8,128)S(1)}, u32[]{:S(2)}, u32[]{:S(2)}) collective-permute-start(f32[8,128,128]{2,1,0:T(8,128)S(1)} %add.269), channel_id=1, source_target_pairs={{0,3},{1,0},{2,1},{3,2},{4,7},{5,4},{6,5},{7,6},{8,11},{9,8},{10,9... | collective-permute-start | bytes 1572872 | tf_op jit(solution)/shard_map/ppermute | solution.py:40
  123.4 14.7 %collective-permute-start.31 = (f32[8,128,128]{2,1,0:T(8,128)S(1)}, f32[8,128,128]{2,1,0:T(8,128)S(1)}, u32[]{:S(2)}, u32[]{:S(2)}) collective-permute-start(f32[8,128,128]{2,1,0:T(8,128)S(1)} %get-tuple-element.123), channel_id=1, source_target_pairs={{0,1},{1,2},{2,3},{3,0},{4,5},{5,6},{6,7},{7,4},{8,9},{9,10},{10,1... | collective-permute-start | bytes 1572872 | tf_op jit(solution)/shard_map/ppermute | solution.py:40
  125.8 16.3 %collective-permute-start.36 = (f32[8,128,128]{2,1,0:T(8,128)S(1)}, f32[8,128,128]{2,1,0:T(8,128)S(1)}, u32[]{:S(2)}, u32[]{:S(2)}) collective-permute-start(f32[8,128,128]{2,1,0:T(8,128)S(1)} %add.270), channel_id=1, source_target_pairs={{0,12},{1,13},{2,14},{3,15},{4,0},{5,1},{6,2},{7,3},{8,4},{9,5},{1... | collective-permute-start | bytes 1572872 | tf_op jit(solution)/shard_map/ppermute | solution.py:40
  127.9 14.4 %collective-permute-start.42 = (f32[8,128,128]{2,1,0:T(8,128)S(1)}, f32[8,128,128]{2,1,0:T(8,128)S(1)}, u32[]{:S(2)}, u32[]{:S(2)}) collective-permute-start(f32[8,128,128]{2,1,0:T(8,128)S(1)} %get-tuple-element.142), channel_id=1, source_target_pairs={{0,4},{1,5},{2,6},{3,7},{4,8},{5,9},{6,10},{7,11},{8,12},{9,13},{1... | collective-permute-start | bytes 1572872 | tf_op jit(solution)/shard_map/ppermute | solution.py:40
  137.7 18.3 %collective-permute-start.34 = (f32[8,128,128]{2,1,0:T(8,128)S(1)}, f32[8,128,128]{2,1,0:T(8,128)S(1)}, u32[]{:S(2)}, u32[]{:S(2)}) collective-permute-start(f32[8,128,128]{2,1,0:T(8,128)S(1)} %get-tuple-element.127), channel_id=1, source_target_pairs={{0,3},{1,0},{2,1},{3,2},{4,7},{5,4},{6,5},{7,6},{8,11},{9,8},{10,9... | collective-permute-start | bytes 1572872 | tf_op jit(solution)/shard_map/ppermute | solution.py:40
  138.1 17.8 %collective-permute-start.32 = (f32[8,128,128]{2,1,0:T(8,128)S(1)}, f32[8,128,128]{2,1,0:T(8,128)S(1)}, u32[]{:S(2)}, u32[]{:S(2)}) collective-permute-start(f32[8,128,128]{2,1,0:T(8,128)S(1)} %add.272), channel_id=1, source_target_pairs={{0,1},{1,2},{2,3},{3,0},{4,5},{5,6},{6,7},{7,4},{8,9},{9,10},{10,1... | collective-permute-start | bytes 1572872 | tf_op jit(solution)/shard_map/ppermute | solution.py:40
  142.3 14.6 %collective-permute-start.44 = (f32[8,128,128]{2,1,0:T(8,128)S(1)}, f32[8,128,128]{2,1,0:T(8,128)S(1)}, u32[]{:S(2)}, u32[]{:S(2)}) collective-permute-start(f32[8,128,128]{2,1,0:T(8,128)S(1)} %get-tuple-element.143), channel_id=1, source_target_pairs={{0,12},{1,13},{2,14},{3,15},{4,0},{5,1},{6,2},{7,3},{8,4},{9,5},{1... | collective-permute-start | bytes 1572872 | tf_op jit(solution)/shard_map/ppermute | solution.py:40
  164.0 12.0 %collective-permute-start.41 = (f32[2,128,128]{2,1,0:T(8,128)S(1)}, f32[2,128,128]{2,1,0:T(8,128)S(1)}, u32[]{:S(2)}, u32[]{:S(2)}) collective-permute-start(f32[2,128,128]{2,1,0:T(8,128)S(1)} %get-tuple-element.161), channel_id=1, source_target_pairs={{0,12},{1,13},{2,14},{3,15},{4,0},{5,1},{6,2},{7,3},{8,4},{9,5},{1... | collective-permute-start | bytes 393224 | tf_op jit(solution)/shard_map/ppermute | solution.py:40
  (34 other events, 316.9 us)

commit v7 on v6

--- a/solution.py
+++ b/solution.py
@@ -10,7 +10,9 @@
 HI = lax.Precision.HIGHEST
 GELU_SCALE = 0.7978845608028654
 GELU_CUBE = 0.044715
-AXES = ("loop", "wide")
+AXES = ("y_lo", "core", "y_hi", "x", "z")
+LOOP = ("y_lo", "core")
+WIDE = ("y_hi", "x", "z")
 SIDE = 4
 TILE = 128
 SLOTS = 256
@@ -18,8 +20,9 @@
 CHUNK = 32
 STAGES = 4
 PAIR_BYTES = 30 * 1024 * 1024
-PER = 8
-CLASS_BUFFERS = (8, 6, 2)
+PER = 16
+HALF = 8
+CLASS_SIZES = ((PER, PER, PER, HALF, HALF), (PER, PER, PER), (HALF, HALF))
 CORE = 4
 LOW = 5
 VMEM_BYTES = 8 * 1024 * 1024
@@ -40,24 +43,17 @@
     return lax.ppermute(value, AXES, pairs)
 
 
-def toward(core):
-    return 1 - 2 * core
-
-
-def x_up(y, core, x, z):
-    return (y, core, x + toward(core), z)
-
-
-def x_down(y, core, x, z):
-    return (y, core, x - toward(core), z)
-
-
-def z_up(y, core, x, z):
-    return (y, core, x, z + toward(core))
-
-
-def z_down(y, core, x, z):
-    return (y, core, x, z - toward(core))
+def along(first, step):
+    def move(y, core, x, z):
+        if (core == 0) == first:
+            return (y, core, x + step, z)
+        return (y, core, x, z + step)
+
+    return move
+
+
+u_up, u_down, u_far = along(True, 1), along(True, -1), along(True, 2)
+v_up, v_down = along(False, 1), along(False, -1)
 
 
 def y_partner(y, core, x, z):
@@ -136,10 +132,10 @@
 
 
 def forward_kernel(which, bounds_ref, order_ref, rows_ref, slots_ref, tiles_ref, *rest):
-    number = CLASS_BUFFERS[which]
-    base = sum(CLASS_BUFFERS[:which]) * PER
-    buffers = rest[:number]
-    rest = rest[number:]
+    sizes = CLASS_SIZES[which]
+    base = sum(sum(part) for part in CLASS_SIZES[:which])
+    buffers = rest[: len(sizes)]
+    rest = rest[len(sizes) :]
     prior_ref = rest[0] if which else None
     pairs, total = rest[-2:]
     nrow = total.shape[0] - 1
@@ -148,13 +144,14 @@
         total[0:nrow] = prior_ref[...]
     else:
         total[0:nrow] = jnp.zeros((nrow, TILE, TILE), jnp.float32)
-    for index in range(number):
-
-        @pl.loop(0, PER, unroll=4)
+    for index, size in enumerate(sizes):
+        first = sum(sizes[:index])
+
+        @pl.loop(0, size, unroll=4)
         def _(j):
             high, low = split_high_low(buffers[index][j])
-            pairs[index * PER + j, :, :TILE] = high
-            pairs[index * PER + j, :, TILE:] = low
+            pairs[first + j, :, :TILE] = high
+            pairs[first + j, :, TILE:] = low
 
     @pl.loop(0, groups)
     def _(group):
@@ -172,7 +169,7 @@
             )
             total[row] += product[:, :TILE] + product[:, TILE:]
 
-    if which == len(CLASS_BUFFERS) - 1:
+    if which == len(CLASS_SIZES) - 1:
         core = bounds_ref[CORE]
         part = nrow // 4
         for index, out_ref in enumerate(rest[-6:-2]):
@@ -183,12 +180,12 @@
 
 
 def backward_kernel(which, bounds_ref, order_ref, rows_ref, slots_ref, tiles_ref, slope_ref, *rest):
-    number = CLASS_BUFFERS[which]
-    base = sum(CLASS_BUFFERS[:which]) * PER
-    buffers = rest[:number]
-    total, out_sems = rest[number:]
+    sizes = CLASS_SIZES[which]
+    base = sum(sum(part) for part in CLASS_SIZES[:which])
+    buffers = rest[: len(sizes)]
+    total, out_sems = rest[len(sizes) :]
     begin, end, groups = class_range(bounds_ref, which)
-    @pl.loop(0, number * PER, unroll=4)
+    @pl.loop(0, sum(sizes), unroll=4)
     def _(slot):
         total[slot] = jnp.zeros((TILE, TILE), jnp.float32)
 
@@ -198,7 +195,7 @@
             spot = group * GROUP + j
             place = jnp.minimum(begin + spot, SLOTS - 1)
             live = begin + spot < end
-            slot = jnp.where(live, slots_ref[place] - base, number * PER)
+            slot = jnp.where(live, slots_ref[place] - base, sum(sizes))
             right = tiles_ref[order_ref[place]]
             product = jnp.dot(
                 slope_ref[rows_ref[place]],
@@ -208,9 +205,9 @@
             total[slot] += product[:, :TILE] + product[:, TILE:]
 
     copies = []
-    for index in range(number):
+    for index, size in enumerate(sizes):
         copy = pltpu.make_async_copy(
-            total.at[pl.ds(index * PER, PER)], buffers[index], out_sems.at[index]
+            total.at[pl.ds(sum(sizes[:index]), size)], buffers[index], out_sems.at[index]
         )
         copy.start()
         copies.append(copy)
@@ -238,18 +235,18 @@
 
 def forward_part(which, plan, tiles, buffers, prior, nrow):
     extra = [prior] if which else []
-    number = CLASS_BUFFERS[which]
+    sizes = CLASS_SIZES[which]
     out_shape = [jax.ShapeDtypeStruct((nrow, TILE, TILE), jnp.float32)]
-    if which == len(CLASS_BUFFERS) - 1:
+    if which == len(CLASS_SIZES) - 1:
         out_shape = [jax.ShapeDtypeStruct((nrow // 4, TILE, TILE), jnp.float32)] * 4
     return pl.pallas_call(
         functools.partial(forward_kernel, which),
         name="forward_tiles_%d" % which,
         out_shape=out_shape,
-        in_specs=[smem()] * 4 + [vmem()] * (1 + number + len(extra)),
+        in_specs=[smem()] * 4 + [vmem()] * (1 + len(sizes) + len(extra)),
         out_specs=[vmem()] * len(out_shape),
         scratch_shapes=[
-            pltpu.VMEM((number * PER, TILE, 2 * TILE), jnp.bfloat16),
+            pltpu.VMEM((sum(sizes), TILE, 2 * TILE), jnp.bfloat16),
             pltpu.VMEM((nrow + 1, TILE, TILE), jnp.float32),
         ],
         cost_estimate=cost((6, 5, 2)[which]),
@@ -258,16 +255,16 @@
 
 
 def backward_part(which, plan, tiles, slope):
-    number = CLASS_BUFFERS[which]
+    sizes = CLASS_SIZES[which]
     return pl.pallas_call(
         functools.partial(backward_kernel, which),
         name="backward_tiles_%d" % which,
-        out_shape=[jax.ShapeDtypeStruct((PER, TILE, TILE), jnp.float32)] * number,
+        out_shape=[jax.ShapeDtypeStruct((size, TILE, TILE), jnp.float32) for size in sizes],
         in_specs=[smem()] * 4 + [vmem(), vmem()],
-        out_specs=[anywhere()] * number,
+        out_specs=[anywhere()] * len(sizes),
         scratch_shapes=[
-            pltpu.VMEM((number * PER + 1, TILE, TILE), jnp.float32),
-            pltpu.SemaphoreType.DMA((number,)),
+            pltpu.VMEM((sum(sizes) + 1, TILE, TILE), jnp.float32),
+            pltpu.SemaphoreType.DMA((len(sizes),)),
         ],
         cost_estimate=cost((6, 5, 2)[which]),
         compiler_params=pltpu.CompilerParams(vmem_limit_bytes=VMEM_BYTES),
@@ -380,22 +377,17 @@
 
 
 def make_plan(rows, cols, count, loop, wide):
-    sign = 1 - 2 * (loop % 2)
+    core = loop % 2
     node_block = cols // 4
-    part = cols % 4
     across = (node_block // 16) ^ (wide // 16)
-    dx = ((node_block // 4 - wide // 4) * sign) % 4
-    dz = ((node_block - wide) * sign) % 4
-    is_first = part < 2
-    ring = jnp.where(is_first, dz, dx)
-    inner = jnp.where(is_first, dx * 2 + part, dz * 2 + part - 2)
-    near = jnp.where(is_first, 0, 4) + ring
-    apart = jnp.where(is_first, 8, 11) + jnp.where(ring == 3, 2, ring)
-    apart = jnp.where(ring == 2, jnp.where(is_first, 14, 15), apart)
-    buffer = jnp.where(across == 0, near, apart)
-    slots = buffer * PER + inner
+    dx = (node_block // 4 - wide // 4) % 4
+    dz = (node_block - wide) % 4
+    du = jnp.where(core == 0, dx, dz)
+    dv = jnp.where(core == 0, dz, dx)
+    place = jnp.where(dv == 2, 3, jnp.where(dv == 3, 2, dv))
+    slots = (across * 4 + place) * PER + du * 4 + cols % 4
     spots = jnp.arange(SLOTS, dtype=jnp.int32)
-    kind = jnp.where(buffer < 8, 0, jnp.where(buffer < 14, 1, 2))
+    kind = jnp.where(across == 0, 0, jnp.where(place < 3, 1, 2))
     kind = jnp.where(spots < count[0], kind, 3)
     ahead = (kind[None, :] < kind[:, None]) | (
         (kind[None, :] == kind[:, None]) & (spots[None, :] < spots[:, None])
@@ -412,16 +404,6 @@
     return bounds, sort(spots), sort(rows), sort(slots)
 
 
-def reduce_ring(parts, up, down, near):
-    if near:
-        one = parts[1] + permute(parts[2], up)
-        three = parts[3]
-    else:
-        one = parts[1]
-        three = parts[3] + permute(parts[2], down)
-    return parts[0] + permute(one, up) + permute(three, down)
-
-
 def quarter_tiles(features, index):
     feats = features.shape[0]
     split = features.reshape(feats, 4, 4, TILE)
@@ -429,118 +411,64 @@
     return jnp.transpose(piece, (1, 2, 0))
 
 
-def gather_features(features, loop):
+def gather_own(features, loop):
     own = quarter_tiles(features, loop)
+    one, three, two = permute(own, u_down), permute(own, u_up), permute(own, u_far)
     partner = permute(quarter_tiles(features, loop ^ 2), y_partner)
-    row_one, row_three = permute(own[:2], x_down), permute(own[:2], x_up)
-    column_one, column_three = permute(own[2:], z_down), permute(own[2:], z_up)
-    row_two, column_two = permute(row_one, x_down), permute(column_one, z_down)
-    row = jnp.concatenate([own[:2], row_one, row_two, row_three], axis=0)
-    column = jnp.concatenate([own[2:], column_one, column_two, column_three], axis=0)
-    return row, column, partner
-
-
-def gather_near(row, column):
-    first_one, second_one = permute(row, z_down), permute(column, x_down)
-    first_three, second_three = permute(row, z_up), permute(column, x_up)
-    first_two, second_two = permute(first_one, z_down), permute(second_one, x_down)
-    return [row, first_one, first_two, first_three, column, second_one, second_two, second_three]
-
-
-def gather_apart(near, partner):
-    near = list(near)
-    row_sent = permute(near[0][2:], y_far)
-    column, row_sent = tie(near[4], row_sent)
-    near[4] = column
-    column_sent = permute(column[2:], y_far)
-    row = jnp.concatenate([partner[:2], row_sent], axis=0)
-    column = jnp.concatenate([partner[2:], column_sent], axis=0)
-    row, near[3] = tie(row, near[3])
-    first_three = permute(row, z_up)
-    row, near[2] = tie(row, near[2])
-    first_one = permute(row, z_down)
-    column, near[7] = tie(column, near[7])
-    second_three = permute(column, x_up)
-    column, near[6] = tie(column, near[6])
-    second_one = permute(column, x_down)
-    return near, [row, first_one, first_three, column, second_one, second_three]
-
-
-def scatter_terms(plan, pairs, spread, weight_term):
-    apart_far = backward_part(2, plan, pairs, spread)
-    spread, *apart_far = tie(spread, *apart_far)
-    row_sent, column_sent = permute(apart_far[0], z_down), permute(apart_far[1], x_down)
-    apart = backward_part(1, plan, pairs, spread)
-    row_one, column_one = permute(apart[1], z_up), permute(apart[4], x_up)
-    row_back, column_back = apart[2] + row_sent, apart[5] + column_sent
-    spread, weight_term, row_back, column_back = tie(spread, weight_term, row_back, column_back)
-    row_three, column_three = permute(row_back, z_down), permute(column_back, x_down)
-    own = list(backward_part(0, plan, pairs, spread))
-    weight_term = flip_add(weight_term, "x", 1)
-
-    own[2], row_one = tie(own[2], row_one)
-    own_two = permute(own[2], z_up)
-    own[6], column_one = tie(own[6], column_one)
-    own_column_two = permute(own[6], x_up)
-    own[3], row_three = tie(own[3], row_three)
-    own_three = permute(own[3], z_down)
-    own[7], column_three = tie(own[7], column_three)
-    own_column_three = permute(own[7], x_down)
-    weight_term, own_two = tie(weight_term, own_two)
-    weight_term = flip_add(weight_term, "x", 2)
-    own_one = permute(own[1] + own_two, z_up)
-    own_column_one = permute(own[5] + own_column_two, x_up)
-
-    row = apart[0] + row_one + row_three
-    column = apart[3] + column_one + column_three
-    row_far = permute(row[2:], y_far)
-    column, row_far, weight_term = tie(column, row_far, weight_term)
-    column_far = permute(column[2:], y_far)
-    weight_term = flip_add(weight_term, "z", 1)
-    last, column_far, weight_term = tie(
-        jnp.concatenate([row[:2], column[:2]], axis=0), column_far, weight_term
-    )
-    last_far = permute(last, y_far)
-    weight_term = flip_add(weight_term, "z", 2)
-
-    row = own[0] + own_one + own_three
-    column = own[4] + own_column_one + own_column_three
-    rows = [row[:2]] + [row[2 * i : 2 * i + 2] + row_far[2 * i - 2 : 2 * i] for i in (1, 2, 3)]
-    columns = [column[:2]] + [
-        column[2 * i : 2 * i + 2] + column_far[2 * i - 2 : 2 * i] for i in (1, 2, 3)
-    ]
-    half = reduce_ring(rows, x_up, x_down, True)
-    other = reduce_ring(columns, z_up, z_down, True)
-    total = jnp.concatenate([half, other], axis=0) + last_far
-    total, weight_term = tie(total, weight_term)
-    return total, weight_term + permute(weight_term, y_far)
-
-
-def flip_add(value, axis, step):
-    if axis == "x":
-        return value + permute(value, lambda y, c, x, z: (y, c, x ^ step, z))
-    return value + permute(value, lambda y, c, x, z: (y, c, x, z ^ step))
+    return jnp.concatenate([own, one, two, three], axis=0), partner
+
+
+def add_low(value, part):
+    return lax.dynamic_update_slice_in_dim(value, value[:HALF] + part, 0, 0)
+
+
+def add_high(value, part):
+    return lax.dynamic_update_slice_in_dim(value, value[HALF:] + part, HALF, 0)
+
+
+def scatter_terms(plan, pairs, spread):
+    *far, spread = tie(*backward_part(2, plan, pairs, spread), spread)
+    low, high = permute(far[0], v_up), permute(far[1], v_down)
+    zero, one, three = backward_part(1, plan, pairs, spread)
+    one, three, spread = tie(add_low(one, low), add_high(three, high), spread)
+    one, three = permute(one, v_up), permute(three, v_down)
+    own, own_one, own_three, low, high = backward_part(0, plan, pairs, spread)
+    low, high = permute(low, v_up), permute(high, v_down)
+    apart = zero + one + three
+    apart_far = permute(apart[4:], y_far)
+    own_one = permute(add_low(own_one, low), v_up)
+    own_three = permute(add_high(own_three, high), v_down)
+    last, apart_far = tie(apart[:4], apart_far)
+    last = permute(last, y_far)
+    total = own + own_one + own_three
+    one = permute(total[4:8] + apart_far[0:4], u_up)
+    two = permute(total[8:12] + apart_far[4:8], u_far)
+    three = permute(total[12:16] + apart_far[8:12], u_down)
+    return total[:4] + last + one + two + three
 
 
 def per_device(features, weight, cotangent, tiles, tile_rows, tile_cols, counts):
     nrow = features.shape[1] // TILE
-    loop = lax.axis_index("loop")
-    wide = lax.axis_index("wide")
+    loop = lax.axis_index(LOOP)
+    wide = lax.axis_index(WIDE)
     tile_collection = tiles.reshape(SLOTS, TILE, TILE)
     count = counts.reshape(1)
     plan = make_plan(tile_rows.reshape(SLOTS), tile_cols.reshape(SLOTS), count, loop, wide)
     across = weight.T
 
-    row, column, partner = gather_features(features, loop)
-    plan, across, row, column = tie(plan, across, row, column)
-    near = gather_near(row, column)
-    count, near[1], near[5] = tie(count, near[1], near[5])
+    row, partner = gather_own(features, loop)
+    plan, across, row, partner = tie(plan, across, row, partner)
+    one, three = permute(row, v_down), permute(row, v_up)
+    row_far = permute(row[4:], y_far)
+    count, one = tie(count, one)
     pairs = pair_tiles(count, tile_collection)
-    near, apart = gather_apart(near, partner)
+    near = [row, one, three, permute(one[:HALF], v_down), permute(three[HALF:], v_up)]
+    row = jnp.concatenate([partner, row_far], axis=0)
+    one, three = permute(row, v_down), permute(row, v_up)
     partial = forward_part(0, plan, pairs, near, None, nrow)
-    apart[2], apart[5], partial = tie(apart[2], apart[5], partial[0])
-    far = [permute(apart[2], z_up), permute(apart[5], x_up)]
-    partial = forward_part(1, plan, pairs, apart, partial, nrow)
+    one, three, partial = tie(one, three, partial[0])
+    far = [permute(one[:HALF], v_down), permute(three[HALF:], v_up)]
+    partial = forward_part(1, plan, pairs, [row, one, three], partial, nrow)
     *kept, given_first, given_second = forward_part(2, plan, pairs, far, partial[0], nrow)
 
     bounds = plan[0]
@@ -552,25 +480,27 @@
     activated, spread, weight_term = middle_part(
         1, bounds, across, weight, cotangent, kept[1], permute(kept[1], core_swap), pairs, early
     )
-    total, weight_grad = scatter_terms(plan, pairs, spread, weight_term)
+    weight_grad = lax.psum(lax.psum(lax.psum(weight_term, "x"), "z"), "y_hi")
+    total = scatter_terms(plan, pairs, spread)
     far_total = permute(total, y_pair)
     parts = [total, permute(total, core_swap), far_total, permute(far_total, core_swap)]
     return (activated, assemble(bounds, parts), weight_grad)
 
 
 def solution(mesh):
+    split = jax.sharding.Mesh(mesh.devices.reshape(2, 2, 2, SIDE, SIDE), AXES)
     return jax.shard_map(
         per_device,
-        mesh=mesh,
+        mesh=split,
         in_specs=(
-            P(None, "wide"),
+            P(None, WIDE),
             P(),
-            P(None, "wide"),
-            P("loop", "wide", None, None, None),
-            P("loop", "wide", None),
-            P("loop", "wide", None),
-            P("loop", "wide"),
+            P(None, WIDE),
+            P(LOOP, WIDE, None, None, None),
+            P(LOOP, WIDE, None),
+            P(LOOP, WIDE, None),
+            P(LOOP, WIDE),
         ),
-        out_specs=(P(None, "wide"), P(None, "wide"), P()),
+        out_specs=(P(None, WIDE), P(None, WIDE), P()),
         check_vma=False,
     )

time: 198 us -> 315 us (1.59)
  waiting for transfers between devices: 79.8 us -> 215 us
  starting transfers between devices: 85.7 us -> 49.9 us
  between operations: 1.82 us -> 14.8 us
  Pallas kernels: 22.2 us -> 26.9 us
    psum x0 -> x3, waiting for transfers between devices: none -> 116 us  [per_device(): weight_grad = lax.psum(lax.psum(lax.psum(weight_term, 'x'), 'z'), 'y_hi')]
    ppermute x56 -> x35, starting transfers between devices: 85.7 us -> 49.8 us  [permute(): return lax.ppermute(value, AXES, pairs)]
    ppermute x56 -> x35, waiting for transfers between devices: 79.8 us -> 99.7 us  [permute(): return lax.ppermute(value, AXES, pairs)]
  transfers between devices with their start and end apart: 56 -> 38, of which waited for: 22 -> 25; matrix products, arithmetic and copies ran while one was open for 3% -> 1% of each run, Pallas kernels for 7% -> 5%
where the time goes in v7:
time: 315 us
  waiting for transfers between devices  215 us (68%)
  starting transfers between devices  49.9 us (16%)
  Pallas kernels  26.9 us (9%)
  between operations  14.8 us (5%)
  local copies, waits for them, and re-layouts  4.35 us (1%)
  other arithmetic  3.28 us (1%)
    psum x3, waiting for transfers between devices, per_device(): weight_grad = lax.psum(lax.psum(lax.psum(weight_term, 'x'), 'z'), 'y_hi')  116 us
    ppermute x35, waiting for transfers between devices, permute(): return lax.ppermute(value, AXES, pairs)  99.7 us
    ppermute x35, starting transfers between devices, permute(): return lax.ppermute(value, AXES, pairs)  49.8 us
    pallas_call x3, Pallas kernels, forward_part(): pl.pallas_call(functools.partial(forward_kernel, which), name='forward_ti...  7.76 us
    pallas_call x3, Pallas kernels, backward_part(): pl.pallas_call(functools.partial(backward_kernel, which), name='backward_...  7.41 us
  transfers between devices with their start and end apart: 38, of which 25 were waited for; matrix products, arithmetic and copies ran while one was open for 1% of the time, Pallas kernels for 5%

profile of v7, /device:TPU:0, one launch (start us, length us, event | category | flops | bytes accessed | tf_op | source)
XLA Modules:
  0.0 314.6 jit_solution(9817066908398937609)
XLA Ops:
  22.8 3.9 %collective-permute-start.4 = (f32[16,128,128]{2,1,0:T(8,128)S(1)}, f32[16,128,128]{2,1,0:T(8,128)S(1)}, u32[]{:S(2)}, u32[]{:S(2)}) collective-permute-start(f32[16,128,128]{2,1,0:T(8,128)S(1)} %pad_maximum_fusion.rest_0_), channel_id=1, source_target_pairs={{0,3},{1,0},{2,1},{3,2},{4,7},{5,4},{6,5},{7,6},{8,11},{9,8},{10,9... | collective-permute-start | bytes 3145736 | tf_op jit(solution)/shard_map/ppermute | solution.py:43
  26.7 3.3 %collective-permute-start.5 = (f32[12,128,128]{2,1,0:T(8,128)S(1)}, f32[12,128,128]{2,1,0:T(8,128)S(1)}, u32[]{:S(2)}, u32[]{:S(2)}) collective-permute-start(f32[12,128,128]{2,1,0:T(8,128)S(1)} %slice.54), channel_id=1, source_target_pairs={{0,16},{1,17},{2,18},{3,19},{4,20},{5,21},{6,22},{7,23},{8,24},{9,... | collective-permute-start | bytes 2359304 | tf_op jit(solution)/shard_map/ppermute | solution.py:43
  30.0 15.9 %collective-permute-done.5 = f32[12,128,128]{2,1,0:T(8,128)S(1)} collective-permute-done((f32[12,128,128]{2,1,0:T(8,128)S(1)}, f32[12,128,128]{2,1,0:T(8,128)S(1)}, u32[]{:S(2)}, u32[]{:S(2)}) %collective-permute-start.5) | collective-permute-done | bytes 786464 | tf_op jit(solution)/shard_map/ppermute | solution.py:43
  50.8 3.9 %pair_tiles.1.tiles_ref.rest_2_ = bf16[256,128,256]{2,1,0:T(8,128)(2,1)S(1)} custom-call(s32[1]{0:T(128)} %bitcast.15.count_ref, f32[256,128,128]{2,1,0:T(8,128)} %bitcast.19), custom_call_target="tpu_custom_call" | custom-call | flops 8800000000 | bytes 1048576 | tf_op jit(solution)/shard_map/pair_tiles/pallas_call | solution.py:114
  54.7 12.2 %collective-permute-done.9.rest_3_ = f32[8,128,128]{2,1,0:T(8,128)S(1)} collective-permute-done((f32[8,128,128]{2,1,0:T(8,128)S(1)}, f32[8,128,128]{2,1,0:T(8,128)S(1)}, u32[]{:S(2)}, u32[]{:S(2)}) %collective-permute-start.9) | collective-permute-done | bytes 524320 | tf_op jit(solution)/shard_map/ppermute | solution.py:43
  68.5 3.3 %forward_tiles_0.1.rest_3_ = f32[16,128,128]{2,1,0:T(8,128)S(1)} custom-call(s32[8]{0:T(128)S(1)} %compare_select_fusion.10.bounds_ref, s32[256]{0:T(256)S(1)} %get-tuple-element.45.order_ref, s32[256]{0:T(256)S(1)} %get-tuple-element.46.rows_ref, s32[256]{0:T(256)S(1)} %get-tuple-element.47.slots_ref, ...), custom_call_target="tpu_custom_call" | custom-call | flops 6600000000 | bytes 1048576 | tf_op jit(solution)/shard_map/forward_tiles_0/pallas_call | solution.py:242
  71.9 3.3 %collective-permute-start.11 = (f32[8,128,128]{2,1,0:T(8,128)S(1)}, f32[8,128,128]{2,1,0:T(8,128)S(1)}, u32[]{:S(2)}, u32[]{:S(2)}) collective-permute-start(f32[8,128,128]{2,1,0:T(8,128)S(1)} %slice.57), channel_id=1, source_target_pairs={{0,3},{1,0},{2,1},{3,2},{4,7},{5,4},{6,5},{7,6},{8,11},{9,8},{10,9... | collective-permute-start | bytes 1572872 | tf_op jit(solution)/shard_map/ppermute | solution.py:43
  78.0 3.9 %collective-permute-done.11.rest_0_ = f32[8,128,128]{2,1,0:T(8,128)S(1)} collective-permute-done((f32[8,128,128]{2,1,0:T(8,128)S(1)}, f32[8,128,128]{2,1,0:T(8,128)S(1)}, u32[]{:S(2)}, u32[]{:S(2)}) %collective-permute-start.11) | collective-permute-done | bytes 524320 | tf_op jit(solution)/shard_map/ppermute | solution.py:43
  81.9 3.8 %collective-permute-done.12.rest_1_ = f32[8,128,128]{2,1,0:T(8,128)S(1)} collective-permute-done((f32[8,128,128]{2,1,0:T(8,128)S(1)}, f32[8,128,128]{2,1,0:T(8,128)S(1)}, u32[]{:S(2)}, u32[]{:S(2)}) %collective-permute-start.12) | collective-permute-done | bytes 524320 | tf_op jit(solution)/shard_map/ppermute | solution.py:43
  91.4 7.0 %collective-permute-done.17 = f32[4,128,128]{2,1,0:T(8,128)S(1)} collective-permute-done((f32[4,128,128]{2,1,0:T(8,128)S(1)}, f32[4,128,128]{2,1,0:T(8,128)S(1)}, u32[]{:S(2)}, u32[]{:S(2)}) %collective-permute-start.17) | collective-permute-done | bytes 262176 | tf_op jit(solution)/shard_map/ppermute | solution.py:43
  98.6 4.7 %collective-permute-done.14 = f32[4,128,128]{2,1,0:T(8,128)S(1)} collective-permute-done((f32[4,128,128]{2,1,0:T(8,128)S(1)}, f32[4,128,128]{2,1,0:T(8,128)S(1)}, u32[]{:S(2)}, u32[]{:S(2)}) %collective-permute-start.14) | collective-permute-done | bytes 262176 | tf_op jit(solution)/shard_map/ppermute | solution.py:43
  106.3 3.6 %middle_1.1 = (f32[128,2048]{1,0:T(8,128)}, bf16[16,128,256]{2,1,0:T(8,128)(2,1)S(1)}, f32[128,128]{1,0:T(8,128)}) custom-call(s32[8]{0:T(128)S(1)} %compare_select_fusion.10.bounds_ref, f32[128,128]{1,0:T(8,128)S(1)} %bitcast.18, f32[128,128]{1,0:T(8,128)S(1)} %copy-done.1, f32[128,2048]{1,0:T(8,128)S(1)} %copy-done, f32[4,128,128]{2,1,0:T(8,128)S(1)} %add.197.rest_0_, ...), custom_call_target="tpu_custom_call" | custom-call | flops 2200000000 | bytes 1048576 | tf_op jit(solution)/shard_map/middle_1/pallas_call | solution.py:340
  116.3 4.6 %collective-permute-done.20 = f32[8,128,128]{2,1,0:T(8,128)S(1)} collective-permute-done((f32[8,128,128]{2,1,0:T(8,128)S(1)}, f32[8,128,128]{2,1,0:T(8,128)S(1)}, u32[]{:S(2)}, u32[]{:S(2)}) %collective-permute-start.20) | collective-permute-done | bytes 524320 | tf_op jit(solution)/shard_map/ppermute | solution.py:43
  130.0 3.2 %collective-permute-start.26 = (f32[16,128,128]{2,1,0:T(8,128)S(1)}, f32[16,128,128]{2,1,0:T(8,128)S(1)}, u32[]{:S(2)}, u32[]{:S(2)}) collective-permute-start(f32[16,128,128]{2,1,0:T(8,128)S(1)} %add_dynamic-update-slice_fusion.2), channel_id=1, source_target_pairs={{0,3},{1,0},{2,1},{3,2},{4,7},{5,4},{6,5},{7,6},{8,11},{9,8},{10,9... | collective-permute-start | bytes 3145736 | tf_op jit(solution)/shard_map/ppermute | solution.py:43
  133.2 3.9 %collective-permute-done.21 = f32[8,128,128]{2,1,0:T(8,128)S(1)} collective-permute-done((f32[8,128,128]{2,1,0:T(8,128)S(1)}, f32[8,128,128]{2,1,0:T(8,128)S(1)}, u32[]{:S(2)}, u32[]{:S(2)}) %collective-permute-start.21) | collective-permute-done | bytes 524320 | tf_op jit(solution)/shard_map/ppermute | solution.py:43
  137.5 3.3 %collective-permute-start.24 = (f32[16,128,128]{2,1,0:T(8,128)S(1)}, f32[16,128,128]{2,1,0:T(8,128)S(1)}, u32[]{:S(2)}, u32[]{:S(2)}) collective-permute-start(f32[16,128,128]{2,1,0:T(8,128)S(1)} %add_dynamic-update-slice_fusion), channel_id=1, source_target_pairs={{0,3},{1,0},{2,1},{3,2},{4,7},{5,4},{6,5},{7,6},{8,11},{9,8},{10,9... | collective-permute-start | bytes 3145736 | tf_op jit(solution)/shard_map/ppermute | solution.py:43
  140.8 7.6 %collective-permute-done.25 = f32[16,128,128]{2,1,0:T(8,128)S(1)} collective-permute-done((f32[16,128,128]{2,1,0:T(8,128)S(1)}, f32[16,128,128]{2,1,0:T(8,128)S(1)}, u32[]{:S(2)}, u32[]{:S(2)}) %collective-permute-start.25) | collective-permute-done | bytes 1048608 | tf_op jit(solution)/shard_map/ppermute | solution.py:43
  148.7 4.0 %collective-permute-start.27 = (f32[12,128,128]{2,1,0:T(8,128)S(1)}, f32[12,128,128]{2,1,0:T(8,128)S(1)}, u32[]{:S(2)}, u32[]{:S(2)}) collective-permute-start(f32[12,128,128]{2,1,0:T(8,128)S(1)} %slice.75), channel_id=1, source_target_pairs={{0,16},{1,17},{2,18},{3,19},{4,20},{5,21},{6,22},{7,23},{8,24},{9,... | collective-permute-start | bytes 2359304 | tf_op jit(solution)/shard_map/ppermute | solution.py:43
  152.7 7.0 %collective-permute-done.22 = f32[16,128,128]{2,1,0:T(8,128)S(1)} collective-permute-done((f32[16,128,128]{2,1,0:T(8,128)S(1)}, f32[16,128,128]{2,1,0:T(8,128)S(1)}, u32[]{:S(2)}, u32[]{:S(2)}) %collective-permute-start.22) | collective-permute-done | bytes 1048608 | tf_op jit(solution)/shard_map/ppermute | solution.py:43
  159.9 10.6 %collective-permute-done.27 = f32[12,128,128]{2,1,0:T(8,128)S(1)} collective-permute-done((f32[12,128,128]{2,1,0:T(8,128)S(1)}, f32[12,128,128]{2,1,0:T(8,128)S(1)}, u32[]{:S(2)}, u32[]{:S(2)}) %collective-permute-start.27) | collective-permute-done | bytes 786464 | tf_op jit(solution)/shard_map/ppermute | solution.py:43
  183.8 5.4 %collective-permute-done.33.across_ref = f32[4,128,128]{2,1,0:T(8,128)S(1)} collective-permute-done((f32[4,128,128]{2,1,0:T(8,128)S(1)}, f32[4,128,128]{2,1,0:T(8,128)S(1)}, u32[]{:S(2)}, u32[]{:S(2)}) %collective-permute-start.33) | collective-permute-done | bytes 262176 | tf_op jit(solution)/shard_map/ppermute | solution.py:43
  189.3 41.8 %all-reduce.4.cloned.1.call-done = f32[128,128]{1,0:T(8,128)} async-done(((f32[128,128]{1,0:T(8,128)}), f32[128,128]{1,0:T(8,128)}) %all-reduce.4.cloned.1.call-update) | async-done | bytes 65552 | tf_op jit(solution)/shard_map/psum | solution.py:483
  231.2 43.9 %all-reduce.6.cloned.1.call-done = f32[128,128]{1,0:T(8,128)} async-done(((f32[128,128]{1,0:T(8,128)}), f32[128,128]{1,0:T(8,128)}) %all-reduce.6.cloned.1.call-update) | async-done | bytes 65552 | tf_op jit(solution)/shard_map/psum | solution.py:483
  276.7 29.9 %all-reduce.8.cloned.1.call-done = f32[128,128]{1,0:T(8,128)} async-done(((f32[128,128]{1,0:T(8,128)}), f32[128,128]{1,0:T(8,128)}) %all-reduce.8.cloned.1.call-update) | async-done | bytes 65552 | tf_op jit(solution)/shard_map/psum | solution.py:483
  (101 shorter events, 65.9 us)
Async XLA Ops:
  7.2 223.9 %all-reduce.4.cloned.1.call-start = ((), (), s32[]{:S(2)}) async-start(), calls=%async_computation | async-start | bytes 131072 | tf_op jit(solution)/shard_map/psum | solution.py:483
  8.8 11.2 %collective-permute-start = (f32[4,128,128]{2,1,0:T(8,128)S(1)}, f32[4,128,128]{2,1,0:T(8,128)S(1)}, u32[]{:S(2)}, u32[]{:S(2)}) collective-permute-start(f32[4,128,128]{2,1,0:T(8,128)S(1)} %get-tuple-element.93), channel_id=1, source_target_pairs={{0,12},{1,13},{2,14},{3,15},{4,0},{5,1},{6,2},{7,3},{8,4},{9,5},{1... | collective-permute-start | bytes 786440 | tf_op jit(solution)/shard_map/ppermute | solution.py:43
  22.8 25.8 %collective-permute-start.4 = (f32[16,128,128]{2,1,0:T(8,128)S(1)}, f32[16,128,128]{2,1,0:T(8,128)S(1)}, u32[]{:S(2)}, u32[]{:S(2)}) collective-permute-start(f32[16,128,128]{2,1,0:T(8,128)S(1)} %pad_maximum_fusion.rest_0_), channel_id=1, source_target_pairs={{0,3},{1,0},{2,1},{3,2},{4,7},{5,4},{6,5},{7,6},{8,11},{9,8},{10,9... | collective-permute-start | bytes 3145736 | tf_op jit(solution)/shard_map/ppermute | solution.py:43
  26.6 23.6 %collective-permute-start.8 = (f32[16,128,128]{2,1,0:T(8,128)S(1)}, f32[16,128,128]{2,1,0:T(8,128)S(1)}, u32[]{:S(2)}, u32[]{:S(2)}) collective-permute-start(f32[16,128,128]{2,1,0:T(8,128)S(1)} %pad_maximum_fusion.rest_0_), channel_id=1, source_target_pairs={{0,1},{1,2},{2,3},{3,0},{4,5},{5,6},{6,7},{7,4},{8,9},{9,10},{10,1... | collective-permute-start | bytes 3145736 | tf_op jit(solution)/shard_map/ppermute | solution.py:43
  26.7 19.2 %collective-permute-start.5 = (f32[12,128,128]{2,1,0:T(8,128)S(1)}, f32[12,128,128]{2,1,0:T(8,128)S(1)}, u32[]{:S(2)}, u32[]{:S(2)}) collective-permute-start(f32[12,128,128]{2,1,0:T(8,128)S(1)} %slice.54), channel_id=1, source_target_pairs={{0,16},{1,17},{2,18},{3,19},{4,20},{5,21},{6,22},{7,23},{8,24},{9,... | collective-permute-start | bytes 2359304 | tf_op jit(solution)/shard_map/ppermute | solution.py:43
  45.9 25.9 %collective-permute-start.6 = (f32[16,128,128]{2,1,0:T(8,128)S(1)}, f32[16,128,128]{2,1,0:T(8,128)S(1)}, u32[]{:S(2)}, u32[]{:S(2)}) collective-permute-start(f32[16,128,128]{2,1,0:T(8,128)S(1)} %constant_dynamic-update-slice_fusion.rest_0_), channel_id=1, source_target_pairs={{0,3},{1,0},{2,1},{3,2},{4,7},{5,4},{6,5},{7,6},{8,11},{9,8},{10,9... | collective-permute-start | bytes 3145736 | tf_op jit(solution)/shard_map/ppermute | solution.py:43
  46.9 24.9 %collective-permute-start.7 = (f32[16,128,128]{2,1,0:T(8,128)S(1)}, f32[16,128,128]{2,1,0:T(8,128)S(1)}, u32[]{:S(2)}, u32[]{:S(2)}) collective-permute-start(f32[16,128,128]{2,1,0:T(8,128)S(1)} %constant_dynamic-update-slice_fusion.rest_0_), channel_id=1, source_target_pairs={{0,1},{1,2},{2,3},{3,0},{4,5},{5,6},{6,7},{7,4},{8,9},{9,10},{10,1... | collective-permute-start | bytes 3145736 | tf_op jit(solution)/shard_map/ppermute | solution.py:43
  48.6 18.3 %collective-permute-start.9 = (f32[8,128,128]{2,1,0:T(8,128)S(1)}, f32[8,128,128]{2,1,0:T(8,128)S(1)}, u32[]{:S(2)}, u32[]{:S(2)}) collective-permute-start(f32[8,128,128]{2,1,0:T(8,128)S(1)} %slice.55), channel_id=1, source_target_pairs={{0,3},{1,0},{2,1},{3,2},{4,7},{5,4},{6,5},{7,6},{8,11},{9,8},{10,9... | collective-permute-start | bytes 1572872 | tf_op jit(solution)/shard_map/ppermute | solution.py:43
  50.3 18.2 %collective-permute-start.10 = (f32[8,128,128]{2,1,0:T(8,128)S(1)}, f32[8,128,128]{2,1,0:T(8,128)S(1)}, u32[]{:S(2)}, u32[]{:S(2)}) collective-permute-start(f32[8,128,128]{2,1,0:T(8,128)S(1)} %slice.72), channel_id=1, source_target_pairs={{0,1},{1,2},{2,3},{3,0},{4,5},{5,6},{6,7},{7,4},{8,9},{9,10},{10,1... | collective-permute-start | bytes 1572872 | tf_op jit(solution)/shard_map/ppermute | solution.py:43
  75.3 10.5 %collective-permute-start.12 = (f32[8,128,128]{2,1,0:T(8,128)S(1)}, f32[8,128,128]{2,1,0:T(8,128)S(1)}, u32[]{:S(2)}, u32[]{:S(2)}) collective-permute-start(f32[8,128,128]{2,1,0:T(8,128)S(1)} %slice.58), channel_id=1, source_target_pairs={{0,1},{1,2},{2,3},{3,0},{4,5},{5,6},{6,7},{7,4},{8,9},{9,10},{10,1... | collective-permute-start | bytes 1572872 | tf_op jit(solution)/shard_map/ppermute | solution.py:43
  89.6 13.7 %collective-permute-start.14 = (f32[4,128,128]{2,1,0:T(8,128)S(1)}, f32[4,128,128]{2,1,0:T(8,128)S(1)}, u32[]{:S(2)}, u32[]{:S(2)}) collective-permute-start(f32[4,128,128]{2,1,0:T(8,128)S(1)} %add.196), channel_id=1, source_target_pairs={{0,64},{1,65},{2,66},{3,67},{4,68},{5,69},{6,70},{7,71},{8,72},{9,... | collective-permute-start | bytes 786440 | tf_op jit(solution)/shard_map/ppermute | solution.py:43
  113.0 10.4 %collective-permute-start.19 = (f32[8,128,128]{2,1,0:T(8,128)S(1)}, f32[8,128,128]{2,1,0:T(8,128)S(1)}, u32[]{:S(2)}, u32[]{:S(2)}) collective-permute-start(f32[8,128,128]{2,1,0:T(8,128)S(1)} %get-tuple-element.68), channel_id=1, source_target_pairs={{0,1},{1,2},{2,3},{3,0},{4,5},{5,6},{6,7},{7,4},{8,9},{9,10},{10,1... | collective-permute-start | bytes 1572872 | tf_op jit(solution)/shard_map/ppermute | solution.py:43
  126.7 10.5 %collective-permute-start.21 = (f32[8,128,128]{2,1,0:T(8,128)S(1)}, f32[8,128,128]{2,1,0:T(8,128)S(1)}, u32[]{:S(2)}, u32[]{:S(2)}) collective-permute-start(f32[8,128,128]{2,1,0:T(8,128)S(1)} %get-tuple-element.74), channel_id=1, source_target_pairs={{0,1},{1,2},{2,3},{3,0},{4,5},{5,6},{6,7},{7,4},{8,9},{9,10},{10,1... | collective-permute-start | bytes 1572872 | tf_op jit(solution)/shard_map/ppermute | solution.py:43
  126.8 10.6 %collective-permute-start.23 = (f32[8,128,128]{2,1,0:T(8,128)S(1)}, f32[8,128,128]{2,1,0:T(8,128)S(1)}, u32[]{:S(2)}, u32[]{:S(2)}) collective-permute-start(f32[8,128,128]{2,1,0:T(8,128)S(1)} %get-tuple-element.76), channel_id=1, source_target_pairs={{0,3},{1,0},{2,1},{3,2},{4,7},{5,4},{6,5},{7,6},{8,11},{9,8},{10,9... | collective-permute-start | bytes 1572872 | tf_op jit(solution)/shard_map/ppermute | solution.py:43
  130.0 18.4 %collective-permute-start.25 = (f32[16,128,128]{2,1,0:T(8,128)S(1)}, f32[16,128,128]{2,1,0:T(8,128)S(1)}, u32[]{:S(2)}, u32[]{:S(2)}) collective-permute-start(f32[16,128,128]{2,1,0:T(8,128)S(1)} %add_dynamic-update-slice_fusion.3), channel_id=1, source_target_pairs={{0,1},{1,2},{2,3},{3,0},{4,5},{5,6},{6,7},{7,4},{8,9},{9,10},{10,1... | collective-permute-start | bytes 3145736 | tf_op jit(solution)/shard_map/ppermute | solution.py:43
  130.0 18.4 %collective-permute-start.26 = (f32[16,128,128]{2,1,0:T(8,128)S(1)}, f32[16,128,128]{2,1,0:T(8,128)S(1)}, u32[]{:S(2)}, u32[]{:S(2)}) collective-permute-start(f32[16,128,128]{2,1,0:T(8,128)S(1)} %add_dynamic-update-slice_fusion.2), channel_id=1, source_target_pairs={{0,3},{1,0},{2,1},{3,2},{4,7},{5,4},{6,5},{7,6},{8,11},{9,8},{10,9... | collective-permute-start | bytes 3145736 | tf_op jit(solution)/shard_map/ppermute | solution.py:43
  137.3 22.3 %collective-permute-start.22 = (f32[16,128,128]{2,1,0:T(8,128)S(1)}, f32[16,128,128]{2,1,0:T(8,128)S(1)}, u32[]{:S(2)}, u32[]{:S(2)}) collective-permute-start(f32[16,128,128]{2,1,0:T(8,128)S(1)} %add_dynamic-update-slice_fusion.1), channel_id=1, source_target_pairs={{0,1},{1,2},{2,3},{3,0},{4,5},{5,6},{6,7},{7,4},{8,9},{9,10},{10,1... | collective-permute-start | bytes 3145736 | tf_op jit(solution)/shard_map/ppermute | solution.py:43
  137.5 22.1 %collective-permute-start.24 = (f32[16,128,128]{2,1,0:T(8,128)S(1)}, f32[16,128,128]{2,1,0:T(8,128)S(1)}, u32[]{:S(2)}, u32[]{:S(2)}) collective-permute-start(f32[16,128,128]{2,1,0:T(8,128)S(1)} %add_dynamic-update-slice_fusion), channel_id=1, source_target_pairs={{0,3},{1,0},{2,1},{3,2},{4,7},{5,4},{6,5},{7,6},{8,11},{9,8},{10,9... | collective-permute-start | bytes 3145736 | tf_op jit(solution)/shard_map/ppermute | solution.py:43
  148.7 21.8 %collective-permute-start.27 = (f32[12,128,128]{2,1,0:T(8,128)S(1)}, f32[12,128,128]{2,1,0:T(8,128)S(1)}, u32[]{:S(2)}, u32[]{:S(2)}) collective-permute-start(f32[12,128,128]{2,1,0:T(8,128)S(1)} %slice.75), channel_id=1, source_target_pairs={{0,16},{1,17},{2,18},{3,19},{4,20},{5,21},{6,22},{7,23},{8,24},{9,... | collective-permute-start | bytes 2359304 | tf_op jit(solution)/shard_map/ppermute | solution.py:43
  170.6 10.4 %collective-permute-start.30 = (f32[4,128,128]{2,1,0:T(8,128)S(1)}, f32[4,128,128]{2,1,0:T(8,128)S(1)}, u32[]{:S(2)}, u32[]{:S(2)}) collective-permute-start(f32[4,128,128]{2,1,0:T(8,128)S(1)} %get-tuple-element.91), channel_id=1, source_target_pairs={{0,8},{1,9},{2,10},{3,11},{4,12},{5,13},{6,14},{7,15},{8,0},{9,1},... | collective-permute-start | bytes 786440 | tf_op jit(solution)/shard_map/ppermute | solution.py:43
  183.8 91.3 %collective-permute-start.32 = (f32[4,128,128]{2,1,0:T(8,128)S(1)}, f32[4,128,128]{2,1,0:T(8,128)S(1)}, u32[]{:S(2)}, u32[]{:S(2)}) collective-permute-start(f32[4,128,128]{2,1,0:T(8,128)S(1)} %fusion.2.own_ref), channel_id=1, source_target_pairs={{0,32},{1,33},{2,34},{3,35},{4,36},{5,37},{6,38},{7,39},{8,40},{9,... | collective-permute-start | bytes 786440 | tf_op jit(solution)/shard_map/ppermute | solution.py:43
  189.2 85.9 %collective-permute-start.34 = (f32[4,128,128]{2,1,0:T(8,128)S(1)}, f32[4,128,128]{2,1,0:T(8,128)S(1)}, u32[]{:S(2)}, u32[]{:S(2)}) collective-permute-start(f32[4,128,128]{2,1,0:T(8,128)S(1)} %collective-permute-done.33.across_ref), channel_id=1, source_target_pairs={{0,32},{1,33},{2,34},{3,35},{4,36},{5,37},{6,38},{7,39},{8,40},{9,... | collective-permute-start | bytes 786440 | tf_op jit(solution)/shard_map/ppermute | solution.py:43
  189.2 85.8 %all-reduce.6.cloned.1.call-start = ((), (), s32[]{:S(2)}) async-start(), calls=%async_computation.1 | async-start | bytes 131072 | tf_op jit(solution)/shard_map/psum | solution.py:483
  231.1 75.5 %all-reduce.8.cloned.1.call-start = ((), (), s32[]{:S(2)}) async-start(), calls=%async_computation.2 | async-start | bytes 131072 | tf_op jit(solution)/shard_map/psum | solution.py:483
  (16 other events, 154.4 us)
Sparse Core Ops, SparseCore 0:
  189.3 41.7 all-reduce.3
  233.5 41.4 all-reduce.5
  277.4 29.0 all-reduce.7

commit v8 on v7

--- a/solution.py
+++ b/solution.py
@@ -22,9 +22,17 @@
 PAIR_BYTES = 30 * 1024 * 1024
 PER = 16
 HALF = 8
-CLASS_SIZES = ((PER, PER, PER, HALF, HALF), (PER, PER, PER), (HALF, HALF))
-CORE = 4
-LOW = 5
+FORWARD = (
+    (1, 3, 48, (PER, PER, PER, HALF, HALF)),
+    (0, 1, 0, (PER, PER, PER)),
+    (3, 4, 112, (HALF, HALF)),
+)
+BACKWARD = (
+    (2, 4, 96, (HALF, HALF, HALF, HALF)),
+    (0, 2, 0, (PER, PER, PER, PER, PER, PER)),
+)
+CORE = 5
+LOW = 6
 VMEM_BYTES = 8 * 1024 * 1024
 
 
@@ -126,32 +134,31 @@
     )(count, tiles)
 
 
-def class_range(bounds_ref, which):
-    begin, end = bounds_ref[which], bounds_ref[which + 1]
+def class_range(bounds_ref, first, last):
+    begin, end = bounds_ref[first], bounds_ref[last]
     return begin, end, (end - begin + GROUP - 1) // GROUP
 
 
 def forward_kernel(which, bounds_ref, order_ref, rows_ref, slots_ref, tiles_ref, *rest):
-    sizes = CLASS_SIZES[which]
-    base = sum(sum(part) for part in CLASS_SIZES[:which])
+    first, last, base, sizes = FORWARD[which]
     buffers = rest[: len(sizes)]
     rest = rest[len(sizes) :]
     prior_ref = rest[0] if which else None
     pairs, total = rest[-2:]
     nrow = total.shape[0] - 1
-    begin, end, groups = class_range(bounds_ref, which)
+    begin, end, groups = class_range(bounds_ref, first, last)
     if which:
         total[0:nrow] = prior_ref[...]
     else:
         total[0:nrow] = jnp.zeros((nrow, TILE, TILE), jnp.float32)
     for index, size in enumerate(sizes):
-        first = sum(sizes[:index])
+        start = sum(sizes[:index])
 
         @pl.loop(0, size, unroll=4)
         def _(j):
             high, low = split_high_low(buffers[index][j])
-            pairs[first + j, :, :TILE] = high
-            pairs[first + j, :, TILE:] = low
+            pairs[start + j, :, :TILE] = high
+            pairs[start + j, :, TILE:] = low
 
     @pl.loop(0, groups)
     def _(group):
@@ -169,7 +176,7 @@
             )
             total[row] += product[:, :TILE] + product[:, TILE:]
 
-    if which == len(CLASS_SIZES) - 1:
+    if which == len(FORWARD) - 1:
         core = bounds_ref[CORE]
         part = nrow // 4
         for index, out_ref in enumerate(rest[-6:-2]):
@@ -180,11 +187,10 @@
 
 
 def backward_kernel(which, bounds_ref, order_ref, rows_ref, slots_ref, tiles_ref, slope_ref, *rest):
-    sizes = CLASS_SIZES[which]
-    base = sum(sum(part) for part in CLASS_SIZES[:which])
+    first, last, base, sizes = BACKWARD[which]
     buffers = rest[: len(sizes)]
     total, out_sems = rest[len(sizes) :]
-    begin, end, groups = class_range(bounds_ref, which)
+    begin, end, groups = class_range(bounds_ref, first, last)
     @pl.loop(0, sum(sizes), unroll=4)
     def _(slot):
         total[slot] = jnp.zeros((TILE, TILE), jnp.float32)
@@ -235,9 +241,9 @@
 
 def forward_part(which, plan, tiles, buffers, prior, nrow):
     extra = [prior] if which else []
-    sizes = CLASS_SIZES[which]
+    sizes = FORWARD[which][-1]
     out_shape = [jax.ShapeDtypeStruct((nrow, TILE, TILE), jnp.float32)]
-    if which == len(CLASS_SIZES) - 1:
+    if which == len(FORWARD) - 1:
         out_shape = [jax.ShapeDtypeStruct((nrow // 4, TILE, TILE), jnp.float32)] * 4
     return pl.pallas_call(
         functools.partial(forward_kernel, which),
@@ -255,7 +261,7 @@
 
 
 def backward_part(which, plan, tiles, slope):
-    sizes = CLASS_SIZES[which]
+    sizes = BACKWARD[which][-1]
     return pl.pallas_call(
         functools.partial(backward_kernel, which),
         name="backward_tiles_%d" % which,
@@ -385,10 +391,13 @@
     du = jnp.where(core == 0, dx, dz)
     dv = jnp.where(core == 0, dz, dx)
     place = jnp.where(dv == 2, 3, jnp.where(dv == 3, 2, dv))
-    slots = (across * 4 + place) * PER + du * 4 + cols % 4
+    start = jnp.where(
+        place < 3, (1 - across) * 48 + place * PER, 96 + across * PER
+    )
+    slots = start + du * 4 + cols % 4
     spots = jnp.arange(SLOTS, dtype=jnp.int32)
-    kind = jnp.where(across == 0, 0, jnp.where(place < 3, 1, 2))
-    kind = jnp.where(spots < count[0], kind, 3)
+    kind = jnp.where(place < 3, 1 - across, 2 + across)
+    kind = jnp.where(spots < count[0], kind, 4)
     ahead = (kind[None, :] < kind[:, None]) | (
         (kind[None, :] == kind[:, None]) & (spots[None, :] < spots[:, None])
     )
@@ -426,25 +435,34 @@
     return lax.dynamic_update_slice_in_dim(value, value[HALF:] + part, HALF, 0)
 
 
-def scatter_terms(plan, pairs, spread):
-    *far, spread = tie(*backward_part(2, plan, pairs, spread), spread)
-    low, high = permute(far[0], v_up), permute(far[1], v_down)
-    zero, one, three = backward_part(1, plan, pairs, spread)
-    one, three, spread = tie(add_low(one, low), add_high(three, high), spread)
-    one, three = permute(one, v_up), permute(three, v_down)
-    own, own_one, own_three, low, high = backward_part(0, plan, pairs, spread)
-    low, high = permute(low, v_up), permute(high, v_down)
+def flip_add(value, axis, step):
+    if axis == "x":
+        return value + permute(value, lambda y, c, x, z: (y, c, x ^ step, z))
+    return value + permute(value, lambda y, c, x, z: (y, c, x, z ^ step))
+
+
+def scatter_terms(plan, pairs, spread, weight_term):
+    *far, spread = tie(*backward_part(0, plan, pairs, spread), spread)
+    low, high = permute(far[2], v_up), permute(far[3], v_down)
+    own_low, own_high = permute(far[0], v_up), permute(far[1], v_down)
+    zero, one, three, own, own_one, own_three = backward_part(1, plan, pairs, spread)
+    one, three = permute(add_low(one, low), v_up), permute(add_high(three, high), v_down)
+    own_one = permute(add_low(own_one, own_low), v_up)
+    own_three = permute(add_high(own_three, own_high), v_down)
     apart = zero + one + three
     apart_far = permute(apart[4:], y_far)
-    own_one = permute(add_low(own_one, low), v_up)
-    own_three = permute(add_high(own_three, high), v_down)
     last, apart_far = tie(apart[:4], apart_far)
     last = permute(last, y_far)
+    own_three, weight_term = tie(own_three, weight_term)
+    weight_term = flip_add(flip_add(weight_term, "x", 1), "x", 2)
     total = own + own_one + own_three
+    total, weight_term = tie(total, weight_term)
     one = permute(total[4:8] + apart_far[0:4], u_up)
     two = permute(total[8:12] + apart_far[4:8], u_far)
     three = permute(total[12:16] + apart_far[8:12], u_down)
-    return total[:4] + last + one + two + three
+    total = total[:4] + last + one + two + three
+    weight_term = flip_add(flip_add(weight_term, "z", 1), "z", 2)
+    return total, weight_term + permute(weight_term, y_far)
 
 
 def per_device(features, weight, cotangent, tiles, tile_rows, tile_cols, counts):
@@ -463,6 +481,7 @@
     count, one = tie(count, one)
     pairs = pair_tiles(count, tile_collection)
     near = [row, one, three, permute(one[:HALF], v_down), permute(three[HALF:], v_up)]
+    row_far, near[3], near[4] = tie(row_far, near[3], near[4])
     row = jnp.concatenate([partner, row_far], axis=0)
     one, three = permute(row, v_down), permute(row, v_up)
     partial = forward_part(0, plan, pairs, near, None, nrow)
@@ -480,8 +499,7 @@
     activated, spread, weight_term = middle_part(
         1, bounds, across, weight, cotangent, kept[1], permute(kept[1], core_swap), pairs, early
     )
-    weight_grad = lax.psum(lax.psum(lax.psum(weight_term, "x"), "z"), "y_hi")
-    total = scatter_terms(plan, pairs, spread)
+    total, weight_grad = scatter_terms(plan, pairs, spread, weight_term)
     far_total = permute(total, y_pair)
     parts = [total, permute(total, core_swap), far_total, permute(far_total, core_swap)]
     return (activated, assemble(bounds, parts), weight_grad)

time: 315 us -> 193 us (0.61)
  waiting for transfers between devices: 215 us -> 107 us
  between operations: 14.8 us -> 1.72 us
    psum x3 -> x0, waiting for transfers between devices: 116 us -> none  [per_device(): weight_grad = lax.psum(lax.psum(lax.psum(weight_term, 'x'), 'z'), 'y_hi')]
    ppermute x35 -> x40, waiting for transfers between devices: 99.7 us -> 107 us  [permute(): return lax.ppermute(value, AXES, pairs)]
    ppermute x35 -> x40, starting transfers between devices: 49.8 us -> 51.2 us  [permute(): return lax.ppermute(value, AXES, pairs)]
    pallas_call x3 -> x2, Pallas kernels: 7.41 us -> 6.61 us  [backward_part(): pl.pallas_call(functools.partial(backward_kernel, which), name='backward_...]
  transfers between devices with their start and end apart: 38 -> 40, of which waited for: 25 -> 27; matrix products, arithmetic and copies ran while one was open for 1% -> 3% of each run, Pallas kernels for 5% -> 9%
where the time goes in v8:
time: 193 us
  waiting for transfers between devices  107 us (55%)
  starting transfers between devices  51.2 us (27%)
  Pallas kernels  26.1 us (14%)
  other arithmetic  3.91 us (2%)
  local copies, waits for them, and re-layouts  2.87 us (1%)
    ppermute x40, waiting for transfers between devices, permute(): return lax.ppermute(value, AXES, pairs)  107 us
    ppermute x40, starting transfers between devices, permute(): return lax.ppermute(value, AXES, pairs)  51.2 us
    pallas_call x3, Pallas kernels, forward_part(): pl.pallas_call(functools.partial(forward_kernel, which), name='forward_ti...  7.75 us
    pallas_call x2, Pallas kernels, backward_part(): pl.pallas_call(functools.partial(backward_kernel, which), name='backward_...  6.61 us
    pallas_call x2, Pallas kernels, middle_part(): pl.pallas_call(functools.partial(middle_kernel, which), name='middle_%d'...  6.28 us
    pallas_call x1, Pallas kernels, pair_tiles(): pl.pallas_call(pair_kernel, name='pair_tiles', out_shape=pltpu.VMEM((SLOT...  3.87 us
  transfers between devices with their start and end apart: 40, of which 27 were waited for; matrix products, arithmetic and copies ran while one was open for 3% of the time, Pallas kernels for 9%

profile of v8, /device:TPU:0, one launch (start us, length us, event | category | flops | bytes accessed | tf_op | source)
XLA Modules:
  0.0 193.1 jit_solution(13655612746336596229)
XLA Ops:
  22.7 10.7 %collective-permute-done.7.rest_2_ = f32[16,128,128]{2,1,0:T(8,128)S(1)} collective-permute-done((f32[16,128,128]{2,1,0:T(8,128)S(1)}, f32[16,128,128]{2,1,0:T(8,128)S(1)}, u32[]{:S(2)}, u32[]{:S(2)}) %collective-permute-start.7) | collective-permute-done | bytes 1048608 | tf_op jit(solution)/shard_map/ppermute | solution.py:51
  36.9 3.3 %collective-permute-done.5 = f32[12,128,128]{2,1,0:T(8,128)S(1)} collective-permute-done((f32[12,128,128]{2,1,0:T(8,128)S(1)}, f32[12,128,128]{2,1,0:T(8,128)S(1)}, u32[]{:S(2)}, u32[]{:S(2)}) %collective-permute-start.5) | collective-permute-done | bytes 786464 | tf_op jit(solution)/shard_map/ppermute | solution.py:51
  40.2 3.7 %collective-permute-done.8.rest_4_ = f32[8,128,128]{2,1,0:T(8,128)S(1)} collective-permute-done((f32[8,128,128]{2,1,0:T(8,128)S(1)}, f32[8,128,128]{2,1,0:T(8,128)S(1)}, u32[]{:S(2)}, u32[]{:S(2)}) %collective-permute-start.8) | collective-permute-done | bytes 524320 | tf_op jit(solution)/shard_map/ppermute | solution.py:51
  44.1 3.4 %collective-permute-start.9 = (f32[16,128,128]{2,1,0:T(8,128)S(1)}, f32[16,128,128]{2,1,0:T(8,128)S(1)}, u32[]{:S(2)}, u32[]{:S(2)}) collective-permute-start(f32[16,128,128]{2,1,0:T(8,128)S(1)} %constant_dynamic-update-slice_fusion.rest_0_), channel_id=1, source_target_pairs={{0,3},{1,0},{2,1},{3,2},{4,7},{5,4},{6,5},{7,6},{8,11},{9,8},{10,9... | collective-permute-start | bytes 3145736 | tf_op jit(solution)/shard_map/ppermute | solution.py:51
  47.5 3.9 %pair_tiles.1.tiles_ref.rest_2_ = bf16[256,128,256]{2,1,0:T(8,128)(2,1)S(1)} custom-call(s32[1]{0:T(128)} %bitcast.15.count_ref, f32[256,128,128]{2,1,0:T(8,128)} %bitcast.19), custom_call_target="tpu_custom_call" | custom-call | flops 8800000000 | bytes 1048576 | tf_op jit(solution)/shard_map/pair_tiles/pallas_call | solution.py:122
  51.3 3.3 %forward_tiles_0.1.rest_3_ = f32[16,128,128]{2,1,0:T(8,128)S(1)} custom-call(s32[8]{0:T(128)S(1)} %compare_select_fusion.8.bounds_ref, s32[256]{0:T(256)S(1)} %get-tuple-element.51.order_ref, s32[256]{0:T(256)S(1)} %get-tuple-element.52.rows_ref, s32[256]{0:T(256)S(1)} %get-tuple-element.53.slots_ref, ...), custom_call_target="tpu_custom_call" | custom-call | flops 6600000000 | bytes 1048576 | tf_op jit(solution)/shard_map/forward_tiles_0/pallas_call | solution.py:248
  54.6 5.5 %collective-permute-done.10.rest_2_ = f32[16,128,128]{2,1,0:T(8,128)S(1)} collective-permute-done((f32[16,128,128]{2,1,0:T(8,128)S(1)}, f32[16,128,128]{2,1,0:T(8,128)S(1)}, u32[]{:S(2)}, u32[]{:S(2)}) %collective-permute-start.10) | collective-permute-done | bytes 1048608 | tf_op jit(solution)/shard_map/ppermute | solution.py:51
  60.3 3.4 %collective-permute-start.11 = (f32[8,128,128]{2,1,0:T(8,128)S(1)}, f32[8,128,128]{2,1,0:T(8,128)S(1)}, u32[]{:S(2)}, u32[]{:S(2)}) collective-permute-start(f32[8,128,128]{2,1,0:T(8,128)S(1)} %slice.57), channel_id=1, source_target_pairs={{0,3},{1,0},{2,1},{3,2},{4,7},{5,4},{6,5},{7,6},{8,11},{9,8},{10,9... | collective-permute-start | bytes 1572872 | tf_op jit(solution)/shard_map/ppermute | solution.py:51
  66.8 3.6 %collective-permute-done.11.rest_0_ = f32[8,128,128]{2,1,0:T(8,128)S(1)} collective-permute-done((f32[8,128,128]{2,1,0:T(8,128)S(1)}, f32[8,128,128]{2,1,0:T(8,128)S(1)}, u32[]{:S(2)}, u32[]{:S(2)}) %collective-permute-start.11) | collective-permute-done | bytes 524320 | tf_op jit(solution)/shard_map/ppermute | solution.py:51
  70.4 3.7 %collective-permute-done.12.rest_1_ = f32[8,128,128]{2,1,0:T(8,128)S(1)} collective-permute-done((f32[8,128,128]{2,1,0:T(8,128)S(1)}, f32[8,128,128]{2,1,0:T(8,128)S(1)}, u32[]{:S(2)}, u32[]{:S(2)}) %collective-permute-start.12) | collective-permute-done | bytes 524320 | tf_op jit(solution)/shard_map/ppermute | solution.py:51
  79.3 7.0 %collective-permute-done.17 = f32[4,128,128]{2,1,0:T(8,128)S(1)} collective-permute-done((f32[4,128,128]{2,1,0:T(8,128)S(1)}, f32[4,128,128]{2,1,0:T(8,128)S(1)}, u32[]{:S(2)}, u32[]{:S(2)}) %collective-permute-start.17) | collective-permute-done | bytes 262176 | tf_op jit(solution)/shard_map/ppermute | solution.py:51
  86.4 4.7 %collective-permute-done.14 = f32[4,128,128]{2,1,0:T(8,128)S(1)} collective-permute-done((f32[4,128,128]{2,1,0:T(8,128)S(1)}, f32[4,128,128]{2,1,0:T(8,128)S(1)}, u32[]{:S(2)}, u32[]{:S(2)}) %collective-permute-start.14) | collective-permute-done | bytes 262176 | tf_op jit(solution)/shard_map/ppermute | solution.py:51
  94.1 3.6 %middle_1.1 = (f32[128,2048]{1,0:T(8,128)}, bf16[16,128,256]{2,1,0:T(8,128)(2,1)S(1)}, f32[128,128]{1,0:T(8,128)S(1)}) custom-call(s32[8]{0:T(128)S(1)} %compare_select_fusion.8.bounds_ref, f32[128,128]{1,0:T(8,128)S(1)} %bitcast.18, f32[128,128]{1,0:T(8,128)S(1)} %copy-done.1, f32[128,2048]{1,0:T(8,128)S(1)} %copy-done, f32[4,128,128]{2,1,0:T(8,128)S(1)} %add.230.rest_0_, ...), custom_call_target="tpu_custom_call" | custom-call | flops 2200000000 | bytes 1048576 | tf_op jit(solution)/shard_map/middle_1/pallas_call | solution.py:346
  104.8 4.3 %backward_tiles_1.1 = (f32[16,128,128]{2,1,0:T(8,128)S(1)}, f32[16,128,128]{2,1,0:T(8,128)S(1)}, f32[16,128,128]{2,1,0:T(8,128)S(1)}, f32[16,128,128]{2,1,0:T(8,...) custom-call(s32[8]{0:T(128)S(1)} %compare_select_fusion.8.bounds_ref, ...), custom_call_target="tpu_custom_call" | custom-call | flops 5500000256 | bytes 1048576 | tf_op jit(solution)/shard_map/backward_tiles_1/pallas_call | solution.py:265
  109.4 5.8 %collective-permute-start.28 = (f32[16,128,128]{2,1,0:T(8,128)S(1)}, f32[16,128,128]{2,1,0:T(8,128)S(1)}, u32[]{:S(2)}, u32[]{:S(2)}) collective-permute-start(f32[16,128,128]{2,1,0:T(8,128)S(1)} %add_dynamic-update-slice_fusion), channel_id=1, source_target_pairs={{0,3},{1,0},{2,1},{3,2},{4,7},{5,4},{6,5},{7,6},{8,11},{9,8},{10,9... | collective-permute-start | bytes 3145736 | tf_op jit(solution)/shard_map/ppermute | solution.py:51
  121.4 6.2 %collective-permute-done.28 = f32[16,128,128]{2,1,0:T(8,128)S(1)} collective-permute-done((f32[16,128,128]{2,1,0:T(8,128)S(1)}, f32[16,128,128]{2,1,0:T(8,128)S(1)}, u32[]{:S(2)}, u32[]{:S(2)}) %collective-permute-start.28) | collective-permute-done | bytes 1048608 | tf_op jit(solution)/shard_map/ppermute | solution.py:51
  127.6 6.2 %collective-permute-done.26 = f32[16,128,128]{2,1,0:T(8,128)S(1)} collective-permute-done((f32[16,128,128]{2,1,0:T(8,128)S(1)}, f32[16,128,128]{2,1,0:T(8,128)S(1)}, u32[]{:S(2)}, u32[]{:S(2)}) %collective-permute-start.26) | collective-permute-done | bytes 1048608 | tf_op jit(solution)/shard_map/ppermute | solution.py:51
  138.8 4.3 %collective-permute-done.23 = f32[128,128]{1,0:T(8,128)S(1)} collective-permute-done((f32[128,128]{1,0:T(8,128)S(1)}, f32[128,128]{1,0:T(8,128)S(1)}, u32[]{:S(2)}, u32[]{:S(2)}) %collective-permute-start.23) | collective-permute-done | bytes 65568 | tf_op jit(solution)/shard_map/ppermute | solution.py:51
  145.2 3.7 %collective-permute-done.24 = f32[128,128]{1,0:T(8,128)S(1)} collective-permute-done((f32[128,128]{1,0:T(8,128)S(1)}, f32[128,128]{1,0:T(8,128)S(1)}, u32[]{:S(2)}, u32[]{:S(2)}) %collective-permute-start.24) | collective-permute-done | bytes 65568 | tf_op jit(solution)/shard_map/ppermute | solution.py:51
  149.0 4.5 %collective-permute-done.29 = f32[12,128,128]{2,1,0:T(8,128)S(1)} collective-permute-done((f32[12,128,128]{2,1,0:T(8,128)S(1)}, f32[12,128,128]{2,1,0:T(8,128)S(1)}, u32[]{:S(2)}, u32[]{:S(2)}) %collective-permute-start.29) | collective-permute-done | bytes 786464 | tf_op jit(solution)/shard_map/ppermute | solution.py:51
  168.3 6.3 %collective-permute-done.35.across_ref = f32[4,128,128]{2,1,0:T(8,128)S(1)} collective-permute-done((f32[4,128,128]{2,1,0:T(8,128)S(1)}, f32[4,128,128]{2,1,0:T(8,128)S(1)}, u32[]{:S(2)}, u32[]{:S(2)}) %collective-permute-start.35) | collective-permute-done | bytes 262176 | tf_op jit(solution)/shard_map/ppermute | solution.py:51
  174.6 4.5 %collective-permute-done.37 = f32[128,128]{1,0:T(8,128)S(1)} collective-permute-done((f32[128,128]{1,0:T(8,128)S(1)}, f32[128,128]{1,0:T(8,128)S(1)}, u32[]{:S(2)}, u32[]{:S(2)}) %collective-permute-start.37) | collective-permute-done | bytes 65568 | tf_op jit(solution)/shard_map/ppermute | solution.py:51
  179.8 5.1 %collective-permute-done.38 = f32[128,128]{1,0:T(8,128)S(1)} collective-permute-done((f32[128,128]{1,0:T(8,128)S(1)}, f32[128,128]{1,0:T(8,128)S(1)}, u32[]{:S(2)}, u32[]{:S(2)}) %collective-permute-start.38) | collective-permute-done | bytes 65568 | tf_op jit(solution)/shard_map/ppermute | solution.py:51
  185.3 5.5 %collective-permute-done.39 = f32[128,128]{1,0:T(8,128)S(1)} collective-permute-done((f32[128,128]{1,0:T(8,128)S(1)}, f32[128,128]{1,0:T(8,128)S(1)}, u32[]{:S(2)}, u32[]{:S(2)}) %collective-permute-start.39) | collective-permute-done | bytes 65568 | tf_op jit(solution)/shard_map/ppermute | solution.py:51
  (105 shorter events, 75.2 us)
Async XLA Ops:
  2.3 12.4 %collective-permute-start.2 = (f32[4,128,128]{2,1,0:T(8,128)S(1)}, f32[4,128,128]{2,1,0:T(8,128)S(1)}, u32[]{:S(2)}, u32[]{:S(2)}) collective-permute-start(f32[4,128,128]{2,1,0:T(8,128)S(1)} %get-tuple-element.105), channel_id=1, source_target_pairs={{0,4},{1,5},{2,6},{3,7},{4,8},{5,9},{6,10},{7,11},{8,12},{9,13},{1... | collective-permute-start | bytes 786440 | tf_op jit(solution)/shard_map/ppermute | solution.py:51
  3.9 10.7 %collective-permute-start.1 = (f32[4,128,128]{2,1,0:T(8,128)S(1)}, f32[4,128,128]{2,1,0:T(8,128)S(1)}, u32[]{:S(2)}, u32[]{:S(2)}) collective-permute-start(f32[4,128,128]{2,1,0:T(8,128)S(1)} %get-tuple-element.105), channel_id=1, source_target_pairs={{0,8},{1,9},{2,10},{3,11},{4,12},{5,13},{6,14},{7,15},{8,0},{9,1},... | collective-permute-start | bytes 786440 | tf_op jit(solution)/shard_map/ppermute | solution.py:51
  8.1 9.3 %collective-permute-start.3 = (f32[4,128,128]{2,1,0:T(8,128)S(1)}, f32[4,128,128]{2,1,0:T(8,128)S(1)}, u32[]{:S(2)}, u32[]{:S(2)}) collective-permute-start(f32[4,128,128]{2,1,0:T(8,128)S(1)} %get-tuple-element.104), channel_id=1, source_target_pairs={{0,80},{1,81},{2,82},{3,83},{4,84},{5,85},{6,86},{7,87},{8,88},{9,... | collective-permute-start | bytes 786440 | tf_op jit(solution)/shard_map/ppermute | solution.py:51
  17.4 16.0 %collective-permute-start.7 = (f32[16,128,128]{2,1,0:T(8,128)S(1)}, f32[16,128,128]{2,1,0:T(8,128)S(1)}, u32[]{:S(2)}, u32[]{:S(2)}) collective-permute-start(f32[16,128,128]{2,1,0:T(8,128)S(1)} %pad_maximum_fusion.rest_0_), channel_id=1, source_target_pairs={{0,1},{1,2},{2,3},{3,0},{4,5},{5,6},{6,7},{7,4},{8,9},{9,10},{10,1... | collective-permute-start | bytes 3145736 | tf_op jit(solution)/shard_map/ppermute | solution.py:51
  18.4 15.1 %collective-permute-start.4 = (f32[16,128,128]{2,1,0:T(8,128)S(1)}, f32[16,128,128]{2,1,0:T(8,128)S(1)}, u32[]{:S(2)}, u32[]{:S(2)}) collective-permute-start(f32[16,128,128]{2,1,0:T(8,128)S(1)} %pad_maximum_fusion.rest_0_), channel_id=1, source_target_pairs={{0,3},{1,0},{2,1},{3,2},{4,7},{5,4},{6,5},{7,6},{8,11},{9,8},{10,9... | collective-permute-start | bytes 3145736 | tf_op jit(solution)/shard_map/ppermute | solution.py:51
  20.7 19.5 %collective-permute-start.5 = (f32[12,128,128]{2,1,0:T(8,128)S(1)}, f32[12,128,128]{2,1,0:T(8,128)S(1)}, u32[]{:S(2)}, u32[]{:S(2)}) collective-permute-start(f32[12,128,128]{2,1,0:T(8,128)S(1)} %slice.54), channel_id=1, source_target_pairs={{0,16},{1,17},{2,18},{3,19},{4,20},{5,21},{6,22},{7,23},{8,24},{9,... | collective-permute-start | bytes 2359304 | tf_op jit(solution)/shard_map/ppermute | solution.py:51
  33.4 10.5 %collective-permute-start.8 = (f32[8,128,128]{2,1,0:T(8,128)S(1)}, f32[8,128,128]{2,1,0:T(8,128)S(1)}, u32[]{:S(2)}, u32[]{:S(2)}) collective-permute-start(f32[8,128,128]{2,1,0:T(8,128)S(1)} %slice.72), channel_id=1, source_target_pairs={{0,1},{1,2},{2,3},{3,0},{4,5},{5,6},{6,7},{7,4},{8,9},{9,10},{10,1... | collective-permute-start | bytes 1572872 | tf_op jit(solution)/shard_map/ppermute | solution.py:51
  33.6 10.3 %collective-permute-start.6 = (f32[8,128,128]{2,1,0:T(8,128)S(1)}, f32[8,128,128]{2,1,0:T(8,128)S(1)}, u32[]{:S(2)}, u32[]{:S(2)}) collective-permute-start(f32[8,128,128]{2,1,0:T(8,128)S(1)} %slice.55), channel_id=1, source_target_pairs={{0,3},{1,0},{2,1},{3,2},{4,7},{5,4},{6,5},{7,6},{8,11},{9,8},{10,9... | collective-permute-start | bytes 1572872 | tf_op jit(solution)/shard_map/ppermute | solution.py:51
  44.0 16.2 %collective-permute-start.10 = (f32[16,128,128]{2,1,0:T(8,128)S(1)}, f32[16,128,128]{2,1,0:T(8,128)S(1)}, u32[]{:S(2)}, u32[]{:S(2)}) collective-permute-start(f32[16,128,128]{2,1,0:T(8,128)S(1)} %constant_dynamic-update-slice_fusion.rest_0_), channel_id=1, source_target_pairs={{0,1},{1,2},{2,3},{3,0},{4,5},{5,6},{6,7},{7,4},{8,9},{9,10},{10,1... | collective-permute-start | bytes 3145736 | tf_op jit(solution)/shard_map/ppermute | solution.py:51
  44.1 16.1 %collective-permute-start.9 = (f32[16,128,128]{2,1,0:T(8,128)S(1)}, f32[16,128,128]{2,1,0:T(8,128)S(1)}, u32[]{:S(2)}, u32[]{:S(2)}) collective-permute-start(f32[16,128,128]{2,1,0:T(8,128)S(1)} %constant_dynamic-update-slice_fusion.rest_0_), channel_id=1, source_target_pairs={{0,3},{1,0},{2,1},{3,2},{4,7},{5,4},{6,5},{7,6},{8,11},{9,8},{10,9... | collective-permute-start | bytes 3145736 | tf_op jit(solution)/shard_map/ppermute | solution.py:51
  60.3 10.1 %collective-permute-start.11 = (f32[8,128,128]{2,1,0:T(8,128)S(1)}, f32[8,128,128]{2,1,0:T(8,128)S(1)}, u32[]{:S(2)}, u32[]{:S(2)}) collective-permute-start(f32[8,128,128]{2,1,0:T(8,128)S(1)} %slice.57), channel_id=1, source_target_pairs={{0,3},{1,0},{2,1},{3,2},{4,7},{5,4},{6,5},{7,6},{8,11},{9,8},{10,9... | collective-permute-start | bytes 1572872 | tf_op jit(solution)/shard_map/ppermute | solution.py:51
  63.7 10.4 %collective-permute-start.12 = (f32[8,128,128]{2,1,0:T(8,128)S(1)}, f32[8,128,128]{2,1,0:T(8,128)S(1)}, u32[]{:S(2)}, u32[]{:S(2)}) collective-permute-start(f32[8,128,128]{2,1,0:T(8,128)S(1)} %slice.58), channel_id=1, source_target_pairs={{0,1},{1,2},{2,3},{3,0},{4,5},{5,6},{6,7},{7,4},{8,9},{9,10},{10,1... | collective-permute-start | bytes 1572872 | tf_op jit(solution)/shard_map/ppermute | solution.py:51
  77.5 13.6 %collective-permute-start.14 = (f32[4,128,128]{2,1,0:T(8,128)S(1)}, f32[4,128,128]{2,1,0:T(8,128)S(1)}, u32[]{:S(2)}, u32[]{:S(2)}) collective-permute-start(f32[4,128,128]{2,1,0:T(8,128)S(1)} %add.229), channel_id=1, source_target_pairs={{0,64},{1,65},{2,66},{3,67},{4,68},{5,69},{6,70},{7,71},{8,72},{9,... | collective-permute-start | bytes 786440 | tf_op jit(solution)/shard_map/ppermute | solution.py:51
  101.5 19.6 %collective-permute-start.19 = (f32[8,128,128]{2,1,0:T(8,128)S(1)}, f32[8,128,128]{2,1,0:T(8,128)S(1)}, u32[]{:S(2)}, u32[]{:S(2)}) collective-permute-start(f32[8,128,128]{2,1,0:T(8,128)S(1)} %get-tuple-element.80), channel_id=1, source_target_pairs={{0,1},{1,2},{2,3},{3,0},{4,5},{5,6},{6,7},{7,4},{8,9},{9,10},{10,1... | collective-permute-start | bytes 1572872 | tf_op jit(solution)/shard_map/ppermute | solution.py:51
  102.2 15.6 %collective-permute-start.21 = (f32[8,128,128]{2,1,0:T(8,128)S(1)}, f32[8,128,128]{2,1,0:T(8,128)S(1)}, u32[]{:S(2)}, u32[]{:S(2)}) collective-permute-start(f32[8,128,128]{2,1,0:T(8,128)S(1)} %get-tuple-element.82), channel_id=1, source_target_pairs={{0,3},{1,0},{2,1},{3,2},{4,7},{5,4},{6,5},{7,6},{8,11},{9,8},{10,9... | collective-permute-start | bytes 1572872 | tf_op jit(solution)/shard_map/ppermute | solution.py:51
  104.8 12.8 %collective-permute-start.25 = (f32[8,128,128]{2,1,0:T(8,128)S(1)}, f32[8,128,128]{2,1,0:T(8,128)S(1)}, u32[]{:S(2)}, u32[]{:S(2)}) collective-permute-start(f32[8,128,128]{2,1,0:T(8,128)S(1)} %get-tuple-element.89), channel_id=1, source_target_pairs={{0,1},{1,2},{2,3},{3,0},{4,5},{5,6},{6,7},{7,4},{8,9},{9,10},{10,1... | collective-permute-start | bytes 1572872 | tf_op jit(solution)/shard_map/ppermute | solution.py:51
  109.4 18.1 %collective-permute-start.28 = (f32[16,128,128]{2,1,0:T(8,128)S(1)}, f32[16,128,128]{2,1,0:T(8,128)S(1)}, u32[]{:S(2)}, u32[]{:S(2)}) collective-permute-start(f32[16,128,128]{2,1,0:T(8,128)S(1)} %add_dynamic-update-slice_fusion), channel_id=1, source_target_pairs={{0,3},{1,0},{2,1},{3,2},{4,7},{5,4},{6,5},{7,6},{8,11},{9,8},{10,9... | collective-permute-start | bytes 3145736 | tf_op jit(solution)/shard_map/ppermute | solution.py:51
  117.7 16.1 %collective-permute-start.26 = (f32[16,128,128]{2,1,0:T(8,128)S(1)}, f32[16,128,128]{2,1,0:T(8,128)S(1)}, u32[]{:S(2)}, u32[]{:S(2)}) collective-permute-start(f32[16,128,128]{2,1,0:T(8,128)S(1)} %add_dynamic-update-slice_fusion.1), channel_id=1, source_target_pairs={{0,1},{1,2},{2,3},{3,0},{4,5},{5,6},{6,7},{7,4},{8,9},{9,10},{10,1... | collective-permute-start | bytes 3145736 | tf_op jit(solution)/shard_map/ppermute | solution.py:51
  117.9 20.9 %collective-permute-start.22 = (f32[16,128,128]{2,1,0:T(8,128)S(1)}, f32[16,128,128]{2,1,0:T(8,128)S(1)}, u32[]{:S(2)}, u32[]{:S(2)}) collective-permute-start(f32[16,128,128]{2,1,0:T(8,128)S(1)} %add_dynamic-update-slice_fusion.2), channel_id=1, source_target_pairs={{0,3},{1,0},{2,1},{3,2},{4,7},{5,4},{6,5},{7,6},{8,11},{9,8},{10,9... | collective-permute-start | bytes 3145736 | tf_op jit(solution)/shard_map/ppermute | solution.py:51
  121.3 23.7 %collective-permute-start.20 = (f32[16,128,128]{2,1,0:T(8,128)S(1)}, f32[16,128,128]{2,1,0:T(8,128)S(1)}, u32[]{:S(2)}, u32[]{:S(2)}) collective-permute-start(f32[16,128,128]{2,1,0:T(8,128)S(1)} %add_dynamic-update-slice_fusion.3), channel_id=1, source_target_pairs={{0,1},{1,2},{2,3},{3,0},{4,5},{5,6},{6,7},{7,4},{8,9},{9,10},{10,1... | collective-permute-start | bytes 3145736 | tf_op jit(solution)/shard_map/ppermute | solution.py:51
  134.0 19.5 %collective-permute-start.29 = (f32[12,128,128]{2,1,0:T(8,128)S(1)}, f32[12,128,128]{2,1,0:T(8,128)S(1)}, u32[]{:S(2)}, u32[]{:S(2)}) collective-permute-start(f32[12,128,128]{2,1,0:T(8,128)S(1)} %slice.74), channel_id=1, source_target_pairs={{0,16},{1,17},{2,18},{3,19},{4,20},{5,21},{6,22},{7,23},{8,24},{9,... | collective-permute-start | bytes 2359304 | tf_op jit(solution)/shard_map/ppermute | solution.py:51
  156.9 9.9 %collective-permute-start.33 = (f32[4,128,128]{2,1,0:T(8,128)S(1)}, f32[4,128,128]{2,1,0:T(8,128)S(1)}, u32[]{:S(2)}, u32[]{:S(2)}) collective-permute-start(f32[4,128,128]{2,1,0:T(8,128)S(1)} %get-tuple-element.102), channel_id=1, source_target_pairs={{0,12},{1,13},{2,14},{3,15},{4,0},{5,1},{6,2},{7,3},{8,4},{9,5},{1... | collective-permute-start | bytes 786440 | tf_op jit(solution)/shard_map/ppermute | solution.py:51
  168.2 23.2 %collective-permute-start.34 = (f32[4,128,128]{2,1,0:T(8,128)S(1)}, f32[4,128,128]{2,1,0:T(8,128)S(1)}, u32[]{:S(2)}, u32[]{:S(2)}) collective-permute-start(f32[4,128,128]{2,1,0:T(8,128)S(1)} %add_add_fusion.2.own_ref), channel_id=1, source_target_pairs={{0,32},{1,33},{2,34},{3,35},{4,36},{5,37},{6,38},{7,39},{8,40},{9,... | collective-permute-start | bytes 786440 | tf_op jit(solution)/shard_map/ppermute | solution.py:51
  174.6 16.9 %collective-permute-start.36 = (f32[4,128,128]{2,1,0:T(8,128)S(1)}, f32[4,128,128]{2,1,0:T(8,128)S(1)}, u32[]{:S(2)}, u32[]{:S(2)}) collective-permute-start(f32[4,128,128]{2,1,0:T(8,128)S(1)} %collective-permute-done.35.across_ref), channel_id=1, source_target_pairs={{0,32},{1,33},{2,34},{3,35},{4,36},{5,37},{6,38},{7,39},{8,40},{9,... | collective-permute-start | bytes 786440 | tf_op jit(solution)/shard_map/ppermute | solution.py:51
  (18 other events, 157.5 us)

commit v9 on v8

--- a/solution.py
+++ b/solution.py
@@ -23,13 +23,13 @@
 PER = 16
 HALF = 8
 FORWARD = (
-    (1, 3, 48, (PER, PER, PER, HALF, HALF)),
-    (0, 1, 0, (PER, PER, PER)),
-    (3, 4, 112, (HALF, HALF)),
+    (1, 3, 48, (HALF,) * 8),
+    (0, 1, 0, (HALF,) * 6),
+    (3, 4, 112, (HALF,) * 2),
 )
 BACKWARD = (
-    (2, 4, 96, (HALF, HALF, HALF, HALF)),
-    (0, 2, 0, (PER, PER, PER, PER, PER, PER)),
+    (2, 4, 96, (HALF,) * 4),
+    (0, 2, 0, (PER,) * 6),
 )
 CORE = 5
 LOW = 6
@@ -300,12 +300,11 @@
         early_activated_ref, early_spread_ref, early_term_ref = rest[3:6]
         activated_ref, spread_ref, weight_term_ref = rest[-3:]
         weight_term = early_term_ref[...]
-    for index in range(2 * part):
-        source = kept_ref if index < part else other_ref
-        side = core if index < part else 1 - core
-        row = (side * 2 + which) * part + index % part
-        columns = pl.ds(pl.multiple_of(row * TILE, TILE), TILE)
-        block = source[index % part]
+    for index, source in enumerate((kept_ref, other_ref)):
+        side = core if index == 0 else 1 - core
+        row = (side * 2 + which) * part
+        columns = pl.ds(pl.multiple_of(row * TILE, part * TILE), part * TILE)
+        block = source[...].reshape(part * TILE, TILE)
         value = lax.dot_general(
             across,
             triple_right(block, 1),
@@ -324,25 +323,25 @@
         )
         spread = jnp.dot(weight, triple_right(slope, 0), preferred_element_type=jnp.float32)
         high, low = split_high_low(spread)
+        place = index * part if which == 0 else row
+        for j in range(part):
+            spread_ref[place + j, :, :TILE] = high[:, j * TILE : (j + 1) * TILE]
+            spread_ref[place + j, :, TILE:] = low[:, j * TILE : (j + 1) * TILE]
         if which == 0:
             activated_ref[index] = activated
-            spread_ref[index, :, :TILE] = high
-            spread_ref[index, :, TILE:] = low
         else:
             activated_ref[:, columns] = activated
-            spread_ref[row, :, :TILE] = high
-            spread_ref[row, :, TILE:] = low
-            early = side * 2 * part + index % part
-            early_columns = pl.ds(pl.multiple_of(early * TILE, TILE), TILE)
+            early = side * 2 * part
+            early_columns = pl.ds(pl.multiple_of(early * TILE, part * TILE), part * TILE)
             activated_ref[:, early_columns] = early_activated_ref[index]
-            spread_ref[early] = early_spread_ref[index]
+            spread_ref[pl.ds(early, part)] = early_spread_ref[index * part : (index + 1) * part]
     weight_term_ref[...] = jnp.transpose(weight_term) if which else weight_term
 
 
 def middle_part(which, bounds, across, weight, cotangent, kept, other, pairs, early=()):
     part = kept.shape[0]
     rows = 4 * part if which else 2 * part
-    activated = cotangent.shape if which else (rows, TILE, TILE)
+    activated = cotangent.shape if which else (2, TILE, part * TILE)
     return pl.pallas_call(
         functools.partial(middle_kernel, which),
         name="middle_%d" % which,
@@ -424,7 +423,17 @@
     own = quarter_tiles(features, loop)
     one, three, two = permute(own, u_down), permute(own, u_up), permute(own, u_far)
     partner = permute(quarter_tiles(features, loop ^ 2), y_partner)
-    return jnp.concatenate([own, one, two, three], axis=0), partner
+    return own, one, two, three, partner
+
+
+def gather_near(first, second):
+    one_first, three_second = permute(first, v_down), permute(second, v_up)
+    one_second, three_first = permute(second, v_down), permute(first, v_up)
+    return [first, second, one_first, one_second, three_first, three_second]
+
+
+def gather_far(near):
+    return [permute(near[2], v_down), permute(near[5], v_up)]
 
 
 def add_low(value, part):
@@ -442,27 +451,26 @@
 
 
 def scatter_terms(plan, pairs, spread, weight_term):
+    weight_term = weight_term + permute(weight_term, y_far)
     *far, spread = tie(*backward_part(0, plan, pairs, spread), spread)
     low, high = permute(far[2], v_up), permute(far[3], v_down)
     own_low, own_high = permute(far[0], v_up), permute(far[1], v_down)
     zero, one, three, own, own_one, own_three = backward_part(1, plan, pairs, spread)
+    low, weight_term = tie(low, weight_term)
     one, three = permute(add_low(one, low), v_up), permute(add_high(three, high), v_down)
     own_one = permute(add_low(own_one, own_low), v_up)
     own_three = permute(add_high(own_three, own_high), v_down)
     apart = zero + one + three
-    apart_far = permute(apart[4:], y_far)
-    last, apart_far = tie(apart[:4], apart_far)
-    last = permute(last, y_far)
+    far_two = permute(apart[8:12], u_far)
+    far_one, far_three = permute(apart[4:8], y_far), permute(apart[12:16], y_far)
+    last = permute(apart[:4] + far_two, y_far)
     own_three, weight_term = tie(own_three, weight_term)
     weight_term = flip_add(flip_add(weight_term, "x", 1), "x", 2)
     total = own + own_one + own_three
-    total, weight_term = tie(total, weight_term)
-    one = permute(total[4:8] + apart_far[0:4], u_up)
-    two = permute(total[8:12] + apart_far[4:8], u_far)
-    three = permute(total[12:16] + apart_far[8:12], u_down)
-    total = total[:4] + last + one + two + three
-    weight_term = flip_add(flip_add(weight_term, "z", 1), "z", 2)
-    return total, weight_term + permute(weight_term, y_far)
+    two = permute(total[8:12], u_far)
+    one = permute(total[4:8] + far_one, u_up)
+    three = permute(total[12:16] + far_three, u_down)
+    return total[:4] + last + one + two + three, flip_add(weight_term, "z", 1)
 
 
 def per_device(features, weight, cotangent, tiles, tile_rows, tile_cols, counts):
@@ -474,20 +482,21 @@
     plan = make_plan(tile_rows.reshape(SLOTS), tile_cols.reshape(SLOTS), count, loop, wide)
     across = weight.T
 
-    row, partner = gather_own(features, loop)
-    plan, across, row, partner = tie(plan, across, row, partner)
-    one, three = permute(row, v_down), permute(row, v_up)
-    row_far = permute(row[4:], y_far)
-    count, one = tie(count, one)
+    own, one, two, three, partner = gather_own(features, loop)
+    first = jnp.concatenate([own, one], axis=0)
+    second = jnp.concatenate([two, three], axis=0)
+    plan, across, first, second, one, partner = tie(plan, across, first, second, one, partner)
+    near = gather_near(first, second)
+    second_far, first_far = permute(second, y_far), permute(one, y_far)
+    count, near[2] = tie(count, near[2])
     pairs = pair_tiles(count, tile_collection)
-    near = [row, one, three, permute(one[:HALF], v_down), permute(three[HALF:], v_up)]
-    row_far, near[3], near[4] = tie(row_far, near[3], near[4])
-    row = jnp.concatenate([partner, row_far], axis=0)
-    one, three = permute(row, v_down), permute(row, v_up)
-    partial = forward_part(0, plan, pairs, near, None, nrow)
-    one, three, partial = tie(one, three, partial[0])
-    far = [permute(one[:HALF], v_down), permute(three[HALF:], v_up)]
-    partial = forward_part(1, plan, pairs, [row, one, three], partial, nrow)
+    far = gather_far(near)
+    second_far, first_far, *far = tie(second_far, first_far, *far)
+    apart = gather_near(jnp.concatenate([partner, first_far], axis=0), second_far)
+    partial = forward_part(0, plan, pairs, near + far, None, nrow)
+    apart[2], apart[5], partial = tie(apart[2], apart[5], partial[0])
+    far = gather_far(apart)
+    partial = forward_part(1, plan, pairs, apart, partial, nrow)
     *kept, given_first, given_second = forward_part(2, plan, pairs, far, partial[0], nrow)
 
     bounds = plan[0]
@@ -499,8 +508,8 @@
     activated, spread, weight_term = middle_part(
         1, bounds, across, weight, cotangent, kept[1], permute(kept[1], core_swap), pairs, early
     )
-    total, weight_grad = scatter_terms(plan, pairs, spread, weight_term)
-    far_total = permute(total, y_pair)
+    total, weight_term = tie(*scatter_terms(plan, pairs, spread, weight_term))
+    far_total, weight_grad = tie(permute(total, y_pair), flip_add(weight_term, "z", 2))
     parts = [total, permute(total, core_swap), far_total, permute(far_total, core_swap)]
     return (activated, assemble(bounds, parts), weight_grad)
 

time: 193 us -> 190 us (0.984)
  starting transfers between devices: 51.2 us -> 68.4 us
  waiting for transfers between devices: 107 us -> 93.3 us
  Pallas kernels: 26.1 us -> 19.5 us
    ppermute x40 -> x47, starting transfers between devices: 51.2 us -> 68.4 us  [permute(): return lax.ppermute(value, AXES, pairs)]
    ppermute x40 -> x47, waiting for transfers between devices: 107 us -> 93.3 us  [permute(): return lax.ppermute(value, AXES, pairs)]
  transfers between devices with their start and end apart: 40 -> 47, of which waited for: 27 -> 23; matrix products, arithmetic and copies ran while one was open for 3% -> 3% of each run, Pallas kernels for 9% -> 6%
where the time goes in v9:
time: 190 us; the launch traced here: 189 us
  waiting for transfers between devices  93.3 us (49%)
  starting transfers between devices  68.4 us (36%)
  Pallas kernels  19.5 us (10%)
  other arithmetic  3.95 us (2%)
  local copies, waits for them, and re-layouts  2.59 us (1%)
    ppermute x47, waiting for transfers between devices, permute(): return lax.ppermute(value, AXES, pairs)  93.3 us
    ppermute x47, starting transfers between devices, permute(): return lax.ppermute(value, AXES, pairs)  68.4 us
    pallas_call x3, Pallas kernels, forward_part(): pl.pallas_call(functools.partial(forward_kernel, which), name='forward_ti...  5.92 us
    pallas_call x2, Pallas kernels, backward_part(): pl.pallas_call(functools.partial(backward_kernel, which), name='backward_...  4.78 us
    pallas_call x2, Pallas kernels, middle_part(): pl.pallas_call(functools.partial(middle_kernel, which), name='middle_%d'...  4.51 us
  transfers between devices with their start and end apart: 47, of which 23 were waited for; matrix products, arithmetic and copies ran while one was open for 3% of the time, Pallas kernels for 6%

profile of v9, /device:TPU:0, one launch (start us, length us, event | category | flops | bytes accessed | tf_op | source)
XLA Modules:
  0.0 189.5 jit_solution(12701915582383132667)
XLA Ops:
  3.9 2.7 %collective-permute-start.1 = (f32[4,128,128]{2,1,0:T(8,128)S(1)}, f32[4,128,128]{2,1,0:T(8,128)S(1)}, u32[]{:S(2)}, u32[]{:S(2)}) collective-permute-start(f32[4,128,128]{2,1,0:T(8,128)S(1)} %get-tuple-element.118), channel_id=1, source_target_pairs={{0,8},{1,9},{2,10},{3,11},{4,12},{5,13},{6,14},{7,15},{8,0},{9,1},... | collective-permute-start | bytes 786440 | tf_op jit(solution)/shard_map/ppermute | solution.py:51
  8.1 3.0 %collective-permute-start.3 = (f32[4,128,128]{2,1,0:T(8,128)S(1)}, f32[4,128,128]{2,1,0:T(8,128)S(1)}, u32[]{:S(2)}, u32[]{:S(2)}) collective-permute-start(f32[4,128,128]{2,1,0:T(8,128)S(1)} %get-tuple-element.117), channel_id=1, source_target_pairs={{0,80},{1,81},{2,82},{3,83},{4,84},{5,85},{6,86},{7,87},{8,88},{9,... | collective-permute-start | bytes 786440 | tf_op jit(solution)/shard_map/ppermute | solution.py:51
  28.5 4.0 %collective-permute-start.7 = (f32[8,128,128]{2,1,0:T(8,128)S(1)}, f32[8,128,128]{2,1,0:T(8,128)S(1)}, u32[]{:S(2)}, u32[]{:S(2)}) collective-permute-start(f32[8,128,128]{2,1,0:T(8,128)S(1)} %collective-permute-done.4.rest_2_), channel_id=1, source_target_pairs={{0,3},{1,0},{2,1},{3,2},{4,7},{5,4},{6,5},{7,6},{8,11},{9,8},{10,9... | collective-permute-start | bytes 1572872 | tf_op jit(solution)/shard_map/ppermute | solution.py:51
  35.2 5.6 %collective-permute-done.5.rest_1_ = f32[8,128,128]{2,1,0:T(8,128)S(1)} collective-permute-done((f32[8,128,128]{2,1,0:T(8,128)S(1)}, f32[8,128,128]{2,1,0:T(8,128)S(1)}, u32[]{:S(2)}, u32[]{:S(2)}) %collective-permute-start.5) | collective-permute-done | bytes 524320 | tf_op jit(solution)/shard_map/ppermute | solution.py:51
  43.0 3.2 %collective-permute-start.10 = (f32[8,128,128]{2,1,0:T(8,128)S(1)}, f32[8,128,128]{2,1,0:T(8,128)S(1)}, u32[]{:S(2)}, u32[]{:S(2)}) collective-permute-start(f32[8,128,128]{2,1,0:T(8,128)S(1)} %constant_dynamic-update-slice_fusion.rest_0_), channel_id=1, source_target_pairs={{0,3},{1,0},{2,1},{3,2},{4,7},{5,4},{6,5},{7,6},{8,11},{9,8},{10,9... | collective-permute-start | bytes 1572872 | tf_op jit(solution)/shard_map/ppermute | solution.py:51
  52.9 6.1 %collective-permute-done.11.rest_5_ = f32[8,128,128]{2,1,0:T(8,128)S(1)} collective-permute-done((f32[8,128,128]{2,1,0:T(8,128)S(1)}, f32[8,128,128]{2,1,0:T(8,128)S(1)}, u32[]{:S(2)}, u32[]{:S(2)}) %collective-permute-start.11) | collective-permute-done | bytes 524320 | tf_op jit(solution)/shard_map/ppermute | solution.py:51
  63.2 5.0 %collective-permute-done.14.rest_0_ = f32[8,128,128]{2,1,0:T(8,128)S(1)} collective-permute-done((f32[8,128,128]{2,1,0:T(8,128)S(1)}, f32[8,128,128]{2,1,0:T(8,128)S(1)}, u32[]{:S(2)}, u32[]{:S(2)}) %collective-permute-start.14) | collective-permute-done | bytes 524320 | tf_op jit(solution)/shard_map/ppermute | solution.py:51
  74.6 7.0 %collective-permute-done.22 = f32[4,128,128]{2,1,0:T(8,128)S(1)} collective-permute-done((f32[4,128,128]{2,1,0:T(8,128)S(1)}, f32[4,128,128]{2,1,0:T(8,128)S(1)}, u32[]{:S(2)}, u32[]{:S(2)}) %collective-permute-start.22) | collective-permute-done | bytes 262176 | tf_op jit(solution)/shard_map/ppermute | solution.py:51
  81.9 4.5 %collective-permute-done.19 = f32[4,128,128]{2,1,0:T(8,128)S(1)} collective-permute-done((f32[4,128,128]{2,1,0:T(8,128)S(1)}, f32[4,128,128]{2,1,0:T(8,128)S(1)}, u32[]{:S(2)}, u32[]{:S(2)}) %collective-permute-start.19) | collective-permute-done | bytes 262176 | tf_op jit(solution)/shard_map/ppermute | solution.py:51
  88.4 2.7 %middle_1.1 = (f32[128,2048]{1,0:T(8,128)}, bf16[16,128,256]{2,1,0:T(8,128)(2,1)S(1)}, f32[128,128]{1,0:T(8,128)S(1)}) custom-call(s32[8]{0:T(128)S(1)} %compare_select_fusion.8.bounds_ref, f32[128,128]{1,0:T(8,128)S(1)} %bitcast.18, f32[128,128]{1,0:T(8,128)S(1)} %copy-done.1, f32[128,2048]{1,0:T(8,128)S(1)} %copy-done, f32[4,128,128]{2,1,0:T(8,128)S(1)} %add.230.rest_0_, ...), custom_call_target="tpu_custom_call" | custom-call | flops 2200000000 | bytes 1048576 | tf_op jit(solution)/shard_map/middle_1/pallas_call | solution.py:345
  98.6 2.9 %backward_tiles_1.1 = (f32[16,128,128]{2,1,0:T(8,128)S(1)}, f32[16,128,128]{2,1,0:T(8,128)S(1)}, f32[16,128,128]{2,1,0:T(8,128)S(1)}, f32[16,128,128]{2,1,0:T(8,...) custom-call(s32[8]{0:T(128)S(1)} %compare_select_fusion.8.bounds_ref, ...), custom_call_target="tpu_custom_call" | custom-call | flops 5500000256 | bytes 1048576 | tf_op jit(solution)/shard_map/backward_tiles_1/pallas_call | solution.py:265
  103.6 4.9 %collective-permute-start.32 = (f32[16,128,128]{2,1,0:T(8,128)S(1)}, f32[16,128,128]{2,1,0:T(8,128)S(1)}, u32[]{:S(2)}, u32[]{:S(2)}) collective-permute-start(f32[16,128,128]{2,1,0:T(8,128)S(1)} %add_dynamic-update-slice_fusion), channel_id=1, source_target_pairs={{0,3},{1,0},{2,1},{3,2},{4,7},{5,4},{6,5},{7,6},{8,11},{9,8},{10,9... | collective-permute-start | bytes 3145736 | tf_op jit(solution)/shard_map/ppermute | solution.py:51
  110.9 4.3 %collective-permute-start.27 = (f32[16,128,128]{2,1,0:T(8,128)S(1)}, f32[16,128,128]{2,1,0:T(8,128)S(1)}, u32[]{:S(2)}, u32[]{:S(2)}) collective-permute-start(f32[16,128,128]{2,1,0:T(8,128)S(1)} %add_dynamic-update-slice_fusion.2), channel_id=1, source_target_pairs={{0,3},{1,0},{2,1},{3,2},{4,7},{5,4},{6,5},{7,6},{8,11},{9,8},{10,9... | collective-permute-start | bytes 3145736 | tf_op jit(solution)/shard_map/ppermute | solution.py:51
  115.2 15.2 %collective-permute-done.24 = f32[8,128,128]{2,1,0:T(8,128)S(1)} collective-permute-done((f32[8,128,128]{2,1,0:T(8,128)S(1)}, f32[8,128,128]{2,1,0:T(8,128)S(1)}, u32[]{:S(2)}, u32[]{:S(2)}) %collective-permute-start.24) | collective-permute-done | bytes 524320 | tf_op jit(solution)/shard_map/ppermute | solution.py:51
  130.9 5.6 %collective-permute-start.33 = (f32[4,128,128]{2,1,0:T(8,128)S(1)}, f32[4,128,128]{2,1,0:T(8,128)S(1)}, u32[]{:S(2)}, u32[]{:S(2)}) collective-permute-start(f32[4,128,128]{2,1,0:T(8,128)S(1)} %slice.50), channel_id=1, source_target_pairs={{0,8},{1,9},{2,10},{3,11},{4,12},{5,13},{6,14},{7,15},{8,0},{9,1},... | collective-permute-start | bytes 786440 | tf_op jit(solution)/shard_map/ppermute | solution.py:51
  136.4 6.7 %collective-permute-done.33 = f32[4,128,128]{2,1,0:T(8,128)S(1)} collective-permute-done((f32[4,128,128]{2,1,0:T(8,128)S(1)}, f32[4,128,128]{2,1,0:T(8,128)S(1)}, u32[]{:S(2)}, u32[]{:S(2)}) %collective-permute-start.33) | collective-permute-done | bytes 262176 | tf_op jit(solution)/shard_map/ppermute | solution.py:51
  143.3 3.5 %collective-permute-start.35 = (f32[4,128,128]{2,1,0:T(8,128)S(1)}, f32[4,128,128]{2,1,0:T(8,128)S(1)}, u32[]{:S(2)}, u32[]{:S(2)}) collective-permute-start(f32[4,128,128]{2,1,0:T(8,128)S(1)} %get-tuple-element.113), channel_id=1, source_target_pairs={{0,16},{1,17},{2,18},{3,19},{4,20},{5,21},{6,22},{7,23},{8,24},{9,... | collective-permute-start | bytes 786440 | tf_op jit(solution)/shard_map/ppermute | solution.py:51
  147.1 2.9 %collective-permute-start.34 = (f32[4,128,128]{2,1,0:T(8,128)S(1)}, f32[4,128,128]{2,1,0:T(8,128)S(1)}, u32[]{:S(2)}, u32[]{:S(2)}) collective-permute-start(f32[4,128,128]{2,1,0:T(8,128)S(1)} %get-tuple-element.111), channel_id=1, source_target_pairs={{0,16},{1,17},{2,18},{3,19},{4,20},{5,21},{6,22},{7,23},{8,24},{9,... | collective-permute-start | bytes 786440 | tf_op jit(solution)/shard_map/ppermute | solution.py:51
  152.3 4.5 %collective-permute-done.35 = f32[4,128,128]{2,1,0:T(8,128)S(1)} collective-permute-done((f32[4,128,128]{2,1,0:T(8,128)S(1)}, f32[4,128,128]{2,1,0:T(8,128)S(1)}, u32[]{:S(2)}, u32[]{:S(2)}) %collective-permute-start.35) | collective-permute-done | bytes 262176 | tf_op jit(solution)/shard_map/ppermute | solution.py:51
  157.0 3.2 %collective-permute-start.39 = (f32[4,128,128]{2,1,0:T(8,128)S(1)}, f32[4,128,128]{2,1,0:T(8,128)S(1)}, u32[]{:S(2)}, u32[]{:S(2)}) collective-permute-start(f32[4,128,128]{2,1,0:T(8,128)S(1)} %get-tuple-element.115), channel_id=1, source_target_pairs={{0,12},{1,13},{2,14},{3,15},{4,0},{5,1},{6,2},{7,3},{8,4},{9,5},{1... | collective-permute-start | bytes 786440 | tf_op jit(solution)/shard_map/ppermute | solution.py:51
  161.1 7.3 %collective-permute-done.40 = f32[128,128]{1,0:T(8,128)S(1)} collective-permute-done((f32[128,128]{1,0:T(8,128)S(1)}, f32[128,128]{1,0:T(8,128)S(1)}, u32[]{:S(2)}, u32[]{:S(2)}) %collective-permute-start.40) | collective-permute-done | bytes 65568 | tf_op jit(solution)/shard_map/ppermute | solution.py:51
  170.4 3.9 %collective-permute-done.41 = f32[128,128]{1,0:T(8,128)S(1)} collective-permute-done((f32[128,128]{1,0:T(8,128)S(1)}, f32[128,128]{1,0:T(8,128)S(1)}, u32[]{:S(2)}, u32[]{:S(2)}) %collective-permute-start.41) | collective-permute-done | bytes 65568 | tf_op jit(solution)/shard_map/ppermute | solution.py:51
  174.4 4.2 %collective-permute-done.42 = f32[128,128]{1,0:T(8,128)S(1)} collective-permute-done((f32[128,128]{1,0:T(8,128)S(1)}, f32[128,128]{1,0:T(8,128)S(1)}, u32[]{:S(2)}, u32[]{:S(2)}) %collective-permute-start.42) | collective-permute-done | bytes 65568 | tf_op jit(solution)/shard_map/ppermute | solution.py:51
  181.0 4.7 %collective-permute-done.45 = f32[128,128]{1,0:T(8,128)S(1)} collective-permute-done((f32[128,128]{1,0:T(8,128)S(1)}, f32[128,128]{1,0:T(8,128)S(1)}, u32[]{:S(2)}, u32[]{:S(2)}) %collective-permute-start.45) | collective-permute-done | bytes 65568 | tf_op jit(solution)/shard_map/ppermute | solution.py:51
  (115 shorter events, 70.0 us)
Async XLA Ops:
  2.3 12.4 %collective-permute-start.2 = (f32[4,128,128]{2,1,0:T(8,128)S(1)}, f32[4,128,128]{2,1,0:T(8,128)S(1)}, u32[]{:S(2)}, u32[]{:S(2)}) collective-permute-start(f32[4,128,128]{2,1,0:T(8,128)S(1)} %get-tuple-element.118), channel_id=1, source_target_pairs={{0,4},{1,5},{2,6},{3,7},{4,8},{5,9},{6,10},{7,11},{8,12},{9,13},{1... | collective-permute-start | bytes 786440 | tf_op jit(solution)/shard_map/ppermute | solution.py:51
  3.9 10.8 %collective-permute-start.1 = (f32[4,128,128]{2,1,0:T(8,128)S(1)}, f32[4,128,128]{2,1,0:T(8,128)S(1)}, u32[]{:S(2)}, u32[]{:S(2)}) collective-permute-start(f32[4,128,128]{2,1,0:T(8,128)S(1)} %get-tuple-element.118), channel_id=1, source_target_pairs={{0,8},{1,9},{2,10},{3,11},{4,12},{5,13},{6,14},{7,15},{8,0},{9,1},... | collective-permute-start | bytes 786440 | tf_op jit(solution)/shard_map/ppermute | solution.py:51
  19.7 12.8 %collective-permute-start.8 = (f32[8,128,128]{2,1,0:T(8,128)S(1)}, f32[8,128,128]{2,1,0:T(8,128)S(1)}, u32[]{:S(2)}, u32[]{:S(2)}) collective-permute-start(f32[8,128,128]{2,1,0:T(8,128)S(1)} %pad_maximum_fusion.1.rest_1_), channel_id=1, source_target_pairs={{0,1},{1,2},{2,3},{3,0},{4,5},{5,6},{6,7},{7,4},{8,9},{9,10},{10,1... | collective-permute-start | bytes 1572872 | tf_op jit(solution)/shard_map/ppermute | solution.py:51
  21.7 24.6 %collective-permute-start.13 = (f32[8,128,128]{2,1,0:T(8,128)S(1)}, f32[8,128,128]{2,1,0:T(8,128)S(1)}, u32[]{:S(2)}, u32[]{:S(2)}) collective-permute-start(f32[8,128,128]{2,1,0:T(8,128)S(1)} %pad_maximum_fusion.rest_0_), channel_id=1, source_target_pairs={{0,1},{1,2},{2,3},{3,0},{4,5},{5,6},{6,7},{7,4},{8,9},{9,10},{10,1... | collective-permute-start | bytes 1572872 | tf_op jit(solution)/shard_map/ppermute | solution.py:51
  22.4 25.9 %collective-permute-start.12 = (f32[8,128,128]{2,1,0:T(8,128)S(1)}, f32[8,128,128]{2,1,0:T(8,128)S(1)}, u32[]{:S(2)}, u32[]{:S(2)}) collective-permute-start(f32[8,128,128]{2,1,0:T(8,128)S(1)} %pad_maximum_fusion.1.rest_1_), channel_id=1, source_target_pairs={{0,3},{1,0},{2,1},{3,2},{4,7},{5,4},{6,5},{7,6},{8,11},{9,8},{10,9... | collective-permute-start | bytes 1572872 | tf_op jit(solution)/shard_map/ppermute | solution.py:51
  26.6 14.2 %collective-permute-start.5 = (f32[8,128,128]{2,1,0:T(8,128)S(1)}, f32[8,128,128]{2,1,0:T(8,128)S(1)}, u32[]{:S(2)}, u32[]{:S(2)}) collective-permute-start(f32[8,128,128]{2,1,0:T(8,128)S(1)} %pad_maximum_fusion.1.rest_1_), channel_id=1, source_target_pairs={{0,16},{1,17},{2,18},{3,19},{4,20},{5,21},{6,22},{7,23},{8,24},{9,... | collective-permute-start | bytes 1572872 | tf_op jit(solution)/shard_map/ppermute | solution.py:51
  28.5 12.3 %collective-permute-start.7 = (f32[8,128,128]{2,1,0:T(8,128)S(1)}, f32[8,128,128]{2,1,0:T(8,128)S(1)}, u32[]{:S(2)}, u32[]{:S(2)}) collective-permute-start(f32[8,128,128]{2,1,0:T(8,128)S(1)} %collective-permute-done.4.rest_2_), channel_id=1, source_target_pairs={{0,3},{1,0},{2,1},{3,2},{4,7},{5,4},{6,5},{7,6},{8,11},{9,8},{10,9... | collective-permute-start | bytes 1572872 | tf_op jit(solution)/shard_map/ppermute | solution.py:51
  32.5 10.4 %collective-permute-start.9 = (f32[8,128,128]{2,1,0:T(8,128)S(1)}, f32[8,128,128]{2,1,0:T(8,128)S(1)}, u32[]{:S(2)}, u32[]{:S(2)}) collective-permute-start(f32[8,128,128]{2,1,0:T(8,128)S(1)} %collective-permute-done.8.rest_5_), channel_id=1, source_target_pairs={{0,1},{1,2},{2,3},{3,0},{4,5},{5,6},{6,7},{7,4},{8,9},{9,10},{10,1... | collective-permute-start | bytes 1572872 | tf_op jit(solution)/shard_map/ppermute | solution.py:51
  42.9 18.1 %collective-permute-start.17 = (f32[8,128,128]{2,1,0:T(8,128)S(1)}, f32[8,128,128]{2,1,0:T(8,128)S(1)}, u32[]{:S(2)}, u32[]{:S(2)}) collective-permute-start(f32[8,128,128]{2,1,0:T(8,128)S(1)} %constant_dynamic-update-slice_fusion.rest_0_), channel_id=1, source_target_pairs={{0,1},{1,2},{2,3},{3,0},{4,5},{5,6},{6,7},{7,4},{8,9},{9,10},{10,1... | collective-permute-start | bytes 1572872 | tf_op jit(solution)/shard_map/ppermute | solution.py:51
  46.2 14.8 %collective-permute-start.16 = (f32[8,128,128]{2,1,0:T(8,128)S(1)}, f32[8,128,128]{2,1,0:T(8,128)S(1)}, u32[]{:S(2)}, u32[]{:S(2)}) collective-permute-start(f32[8,128,128]{2,1,0:T(8,128)S(1)} %collective-permute-done.5.rest_1_), channel_id=1, source_target_pairs={{0,3},{1,0},{2,1},{3,2},{4,7},{5,4},{6,5},{7,6},{8,11},{9,8},{10,9... | collective-permute-start | bytes 1572872 | tf_op jit(solution)/shard_map/ppermute | solution.py:51
  46.3 12.7 %collective-permute-start.11 = (f32[8,128,128]{2,1,0:T(8,128)S(1)}, f32[8,128,128]{2,1,0:T(8,128)S(1)}, u32[]{:S(2)}, u32[]{:S(2)}) collective-permute-start(f32[8,128,128]{2,1,0:T(8,128)S(1)} %collective-permute-done.5.rest_1_), channel_id=1, source_target_pairs={{0,1},{1,2},{2,3},{3,0},{4,5},{5,6},{6,7},{7,4},{8,9},{9,10},{10,1... | collective-permute-start | bytes 1572872 | tf_op jit(solution)/shard_map/ppermute | solution.py:51
  74.0 12.5 %collective-permute-start.19 = (f32[4,128,128]{2,1,0:T(8,128)S(1)}, f32[4,128,128]{2,1,0:T(8,128)S(1)}, u32[]{:S(2)}, u32[]{:S(2)}) collective-permute-start(f32[4,128,128]{2,1,0:T(8,128)S(1)} %add.229), channel_id=1, source_target_pairs={{0,64},{1,65},{2,66},{3,67},{4,68},{5,69},{6,70},{7,71},{8,72},{9,... | collective-permute-start | bytes 786440 | tf_op jit(solution)/shard_map/ppermute | solution.py:51
  93.0 10.5 %collective-permute-start.28 = (f32[8,128,128]{2,1,0:T(8,128)S(1)}, f32[8,128,128]{2,1,0:T(8,128)S(1)}, u32[]{:S(2)}, u32[]{:S(2)}) collective-permute-start(f32[8,128,128]{2,1,0:T(8,128)S(1)} %get-tuple-element.91), channel_id=1, source_target_pairs={{0,1},{1,2},{2,3},{3,0},{4,5},{5,6},{6,7},{7,4},{8,9},{9,10},{10,1... | collective-permute-start | bytes 1572872 | tf_op jit(solution)/shard_map/ppermute | solution.py:51
  103.6 27.0 %collective-permute-start.32 = (f32[16,128,128]{2,1,0:T(8,128)S(1)}, f32[16,128,128]{2,1,0:T(8,128)S(1)}, u32[]{:S(2)}, u32[]{:S(2)}) collective-permute-start(f32[16,128,128]{2,1,0:T(8,128)S(1)} %add_dynamic-update-slice_fusion), channel_id=1, source_target_pairs={{0,3},{1,0},{2,1},{3,2},{4,7},{5,4},{6,5},{7,6},{8,11},{9,8},{10,9... | collective-permute-start | bytes 3145736 | tf_op jit(solution)/shard_map/ppermute | solution.py:51
  108.7 21.9 %collective-permute-start.30 = (f32[16,128,128]{2,1,0:T(8,128)S(1)}, f32[16,128,128]{2,1,0:T(8,128)S(1)}, u32[]{:S(2)}, u32[]{:S(2)}) collective-permute-start(f32[16,128,128]{2,1,0:T(8,128)S(1)} %add_dynamic-update-slice_fusion.1), channel_id=1, source_target_pairs={{0,1},{1,2},{2,3},{3,0},{4,5},{5,6},{6,7},{7,4},{8,9},{9,10},{10,1... | collective-permute-start | bytes 3145736 | tf_op jit(solution)/shard_map/ppermute | solution.py:51
  108.8 21.6 %collective-permute-start.24 = (f32[8,128,128]{2,1,0:T(8,128)S(1)}, f32[8,128,128]{2,1,0:T(8,128)S(1)}, u32[]{:S(2)}, u32[]{:S(2)}) collective-permute-start(f32[8,128,128]{2,1,0:T(8,128)S(1)} %get-tuple-element.88), channel_id=1, source_target_pairs={{0,1},{1,2},{2,3},{3,0},{4,5},{5,6},{6,7},{7,4},{8,9},{9,10},{10,1... | collective-permute-start | bytes 1572872 | tf_op jit(solution)/shard_map/ppermute | solution.py:51
  110.9 25.5 %collective-permute-start.27 = (f32[16,128,128]{2,1,0:T(8,128)S(1)}, f32[16,128,128]{2,1,0:T(8,128)S(1)}, u32[]{:S(2)}, u32[]{:S(2)}) collective-permute-start(f32[16,128,128]{2,1,0:T(8,128)S(1)} %add_dynamic-update-slice_fusion.2), channel_id=1, source_target_pairs={{0,3},{1,0},{2,1},{3,2},{4,7},{5,4},{6,5},{7,6},{8,11},{9,8},{10,9... | collective-permute-start | bytes 3145736 | tf_op jit(solution)/shard_map/ppermute | solution.py:51
  130.5 16.4 %collective-permute-start.25 = (f32[16,128,128]{2,1,0:T(8,128)S(1)}, f32[16,128,128]{2,1,0:T(8,128)S(1)}, u32[]{:S(2)}, u32[]{:S(2)}) collective-permute-start(f32[16,128,128]{2,1,0:T(8,128)S(1)} %add_dynamic-update-slice_fusion.3), channel_id=1, source_target_pairs={{0,1},{1,2},{2,3},{3,0},{4,5},{5,6},{6,7},{7,4},{8,9},{9,10},{10,1... | collective-permute-start | bytes 3145736 | tf_op jit(solution)/shard_map/ppermute | solution.py:51
  130.9 12.3 %collective-permute-start.33 = (f32[4,128,128]{2,1,0:T(8,128)S(1)}, f32[4,128,128]{2,1,0:T(8,128)S(1)}, u32[]{:S(2)}, u32[]{:S(2)}) collective-permute-start(f32[4,128,128]{2,1,0:T(8,128)S(1)} %slice.50), channel_id=1, source_target_pairs={{0,8},{1,9},{2,10},{3,11},{4,12},{5,13},{6,14},{7,15},{8,0},{9,1},... | collective-permute-start | bytes 786440 | tf_op jit(solution)/shard_map/ppermute | solution.py:51
  143.3 13.5 %collective-permute-start.35 = (f32[4,128,128]{2,1,0:T(8,128)S(1)}, f32[4,128,128]{2,1,0:T(8,128)S(1)}, u32[]{:S(2)}, u32[]{:S(2)}) collective-permute-start(f32[4,128,128]{2,1,0:T(8,128)S(1)} %get-tuple-element.113), channel_id=1, source_target_pairs={{0,16},{1,17},{2,18},{3,19},{4,20},{5,21},{6,22},{7,23},{8,24},{9,... | collective-permute-start | bytes 786440 | tf_op jit(solution)/shard_map/ppermute | solution.py:51
  147.1 31.5 %collective-permute-start.34 = (f32[4,128,128]{2,1,0:T(8,128)S(1)}, f32[4,128,128]{2,1,0:T(8,128)S(1)}, u32[]{:S(2)}, u32[]{:S(2)}) collective-permute-start(f32[4,128,128]{2,1,0:T(8,128)S(1)} %get-tuple-element.111), channel_id=1, source_target_pairs={{0,16},{1,17},{2,18},{3,19},{4,20},{5,21},{6,22},{7,23},{8,24},{9,... | collective-permute-start | bytes 786440 | tf_op jit(solution)/shard_map/ppermute | solution.py:51
  156.9 21.7 %collective-permute-start.36 = (f32[4,128,128]{2,1,0:T(8,128)S(1)}, f32[4,128,128]{2,1,0:T(8,128)S(1)}, u32[]{:S(2)}, u32[]{:S(2)}) collective-permute-start(f32[4,128,128]{2,1,0:T(8,128)S(1)} %get-tuple-element.114), channel_id=1, source_target_pairs={{0,4},{1,5},{2,6},{3,7},{4,8},{5,9},{6,10},{7,11},{8,12},{9,13},{1... | collective-permute-start | bytes 786440 | tf_op jit(solution)/shard_map/ppermute | solution.py:51
  157.0 21.7 %collective-permute-start.39 = (f32[4,128,128]{2,1,0:T(8,128)S(1)}, f32[4,128,128]{2,1,0:T(8,128)S(1)}, u32[]{:S(2)}, u32[]{:S(2)}) collective-permute-start(f32[4,128,128]{2,1,0:T(8,128)S(1)} %get-tuple-element.115), channel_id=1, source_target_pairs={{0,12},{1,13},{2,14},{3,15},{4,0},{5,1},{6,2},{7,3},{8,4},{9,5},{1... | collective-permute-start | bytes 786440 | tf_op jit(solution)/shard_map/ppermute | solution.py:51
  160.2 18.4 %collective-permute-start.37 = (f32[4,128,128]{2,1,0:T(8,128)S(1)}, f32[4,128,128]{2,1,0:T(8,128)S(1)}, u32[]{:S(2)}, u32[]{:S(2)}) collective-permute-start(f32[4,128,128]{2,1,0:T(8,128)S(1)} %get-tuple-element.116), channel_id=1, source_target_pairs={{0,8},{1,9},{2,10},{3,11},{4,12},{5,13},{6,14},{7,15},{8,0},{9,1},... | collective-permute-start | bytes 786440 | tf_op jit(solution)/shard_map/ppermute | solution.py:51
  (25 other events, 230.2 us)

commit v10 on v9

--- a/solution.py
+++ b/solution.py
@@ -28,11 +28,12 @@
     (3, 4, 112, (HALF,) * 2),
 )
 BACKWARD = (
-    (2, 4, 96, (HALF,) * 4),
-    (0, 2, 0, (PER,) * 6),
+    (2, 4, 96, (PER, PER), (1, 1)),
+    (0, 2, 0, (PER,) * 6, (0, 1, 0, 0, 0, 0)),
 )
 CORE = 5
 LOW = 6
+FIRST = 7
 VMEM_BYTES = 8 * 1024 * 1024
 
 
@@ -187,9 +188,19 @@
 
 
 def backward_kernel(which, bounds_ref, order_ref, rows_ref, slots_ref, tiles_ref, slope_ref, *rest):
-    first, last, base, sizes = BACKWARD[which]
+    first, last, base, sizes, extra = BACKWARD[which]
+    if which == 0:
+        weight_term_ref, *rest = rest
     buffers = rest[: len(sizes)]
-    total, out_sems = rest[len(sizes) :]
+    total, out_sems, *rest = rest[len(sizes) :]
+    if which == 0:
+        (term_sems,) = rest
+        term_copies = [
+            pltpu.make_async_copy(weight_term_ref, buffer.at[PER], term_sems.at[index])
+            for index, buffer in enumerate(buffers)
+        ]
+        for copy in term_copies:
+            copy.start()
     begin, end, groups = class_range(bounds_ref, first, last)
     @pl.loop(0, sum(sizes), unroll=4)
     def _(slot):
@@ -213,10 +224,14 @@
     copies = []
     for index, size in enumerate(sizes):
         copy = pltpu.make_async_copy(
-            total.at[pl.ds(sum(sizes[:index]), size)], buffers[index], out_sems.at[index]
+            total.at[pl.ds(sum(sizes[:index]), size)],
+            buffers[index].at[pl.ds(0, size)],
+            out_sems.at[index],
         )
         copy.start()
         copies.append(copy)
+    if which == 0:
+        copies += term_copies
     for copy in copies:
         copy.wait()
 
@@ -260,21 +275,25 @@
     )(*plan, tiles, *buffers, *extra)
 
 
-def backward_part(which, plan, tiles, slope):
-    sizes = BACKWARD[which][-1]
+def backward_part(which, plan, tiles, slope, weight_term=()):
+    sizes, extra = BACKWARD[which][-2:]
     return pl.pallas_call(
         functools.partial(backward_kernel, which),
         name="backward_tiles_%d" % which,
-        out_shape=[jax.ShapeDtypeStruct((size, TILE, TILE), jnp.float32) for size in sizes],
-        in_specs=[smem()] * 4 + [vmem(), vmem()],
+        out_shape=[
+            jax.ShapeDtypeStruct((size + more, TILE, TILE), jnp.float32)
+            for size, more in zip(sizes, extra)
+        ],
+        in_specs=[smem()] * 4 + [vmem()] * (2 + len(weight_term)),
         out_specs=[anywhere()] * len(sizes),
         scratch_shapes=[
             pltpu.VMEM((sum(sizes) + 1, TILE, TILE), jnp.float32),
             pltpu.SemaphoreType.DMA((len(sizes),)),
-        ],
-        cost_estimate=cost((6, 5, 2)[which]),
+        ]
+        + [pltpu.SemaphoreType.DMA((2,))] * len(weight_term),
+        cost_estimate=cost((3, 8)[which]),
         compiler_params=pltpu.CompilerParams(vmem_limit_bytes=VMEM_BYTES),
-    )(*plan, tiles, slope)
+    )(*plan, tiles, slope, *weight_term)
 
 
 def triple_left(value):
@@ -357,7 +376,30 @@
     )(bounds, across, weight, cotangent, kept, other, pairs, *early)
 
 
-def assemble_kernel(bounds_ref, own_ref, own_other_ref, across_ref, across_other_ref, out_ref):
+def ring_sum_kernel(which, bounds_ref, own_ref, one_ref, two_ref, three_ref, out_ref):
+    refs = (own_ref, one_ref, two_ref, three_ref)
+    for place in range(SIDE):
+
+        @pl.when(bounds_ref[FIRST + which] == place)
+        def _():
+            parts = [refs[(index - place) % SIDE] for index in range(SIDE)]
+            out_ref[...] = (parts[0][...] + parts[1][...]) + (parts[2][...] + parts[3][...])
+
+
+def ring_sum(which, bounds, parts):
+    return pl.pallas_call(
+        functools.partial(ring_sum_kernel, which),
+        name="ring_sum_%d" % which,
+        out_shape=jax.ShapeDtypeStruct((TILE, TILE), jnp.float32),
+        in_specs=[smem()] + [vmem()] * SIDE,
+        out_specs=vmem(),
+        compiler_params=pltpu.CompilerParams(vmem_limit_bytes=VMEM_BYTES),
+    )(bounds, *parts)
+
+
+def assemble_kernel(
+    bounds_ref, own_ref, own_other_ref, across_ref, across_other_ref, term_ref, out_ref, sum_ref
+):
     core, low = bounds_ref[CORE], bounds_ref[LOW]
     for source, chip, side in (
         (own_ref, low, core),
@@ -365,18 +407,29 @@
         (across_ref, 1 - low, core),
         (across_other_ref, 1 - low, 1 - core),
     ):
-        for j in range(source.shape[0]):
-            place = (chip * 2 + side) * source.shape[0] + j
+        for j in range(4):
+            place = (chip * 2 + side) * 4 + j
             out_ref[:, pl.ds(pl.multiple_of(place * TILE, TILE), TILE)] = source[j]
+
+    @pl.when(core == 0)
+    def _():
+        sum_ref[...] = term_ref[...]
+
+    @pl.when(core == 1)
+    def _():
+        sum_ref[...] = own_other_ref[4]
 
 
 def assemble(bounds, parts):
     return pl.pallas_call(
         assemble_kernel,
         name="assemble",
-        out_shape=jax.ShapeDtypeStruct((TILE, 4 * parts[0].shape[0] * TILE), jnp.float32),
-        in_specs=[smem()] + [vmem()] * 4,
-        out_specs=vmem(),
+        out_shape=[
+            jax.ShapeDtypeStruct((TILE, 16 * TILE), jnp.float32),
+            jax.ShapeDtypeStruct((TILE, TILE), jnp.float32),
+        ],
+        in_specs=[smem()] + [vmem()] * 5,
+        out_specs=[vmem()] * 2,
         compiler_params=pltpu.CompilerParams(vmem_limit_bytes=VMEM_BYTES),
     )(bounds, *parts)
 
@@ -406,10 +459,17 @@
     def sort(values):
         return jnp.sum(jnp.where(here, values[None, :], 0), axis=1)
 
-    steps = jnp.arange(8, dtype=jnp.int32)
+    inner = du * 4 + cols % 4
+    back_slots = jnp.where(
+        place < 3, slots, 96 + (inner // HALF) * PER + across * HALF + inner % HALF
+    )
+    steps = jnp.arange(9, dtype=jnp.int32)
     bounds = jnp.sum((kind[None, :] < steps[:, None]).astype(jnp.int32), axis=1)
     bounds = jnp.where(steps == CORE, loop % 2, jnp.where(steps == LOW, loop // 2, bounds))
-    return bounds, sort(spots), sort(rows), sort(slots)
+    ring = jnp.where(core == 0, wide // 4 % 4, wide % 4)
+    other_ring = jnp.where(core == 0, wide % 4, wide // 4 % 4)
+    bounds = jnp.where(steps == FIRST, ring, jnp.where(steps == FIRST + 1, other_ring, bounds))
+    return bounds, sort(spots), sort(rows), sort(slots), sort(back_slots)
 
 
 def quarter_tiles(features, index):
@@ -426,51 +486,40 @@
     return own, one, two, three, partner
 
 
-def gather_near(first, second):
-    one_first, three_second = permute(first, v_down), permute(second, v_up)
-    one_second, three_first = permute(second, v_down), permute(first, v_up)
-    return [first, second, one_first, one_second, three_first, three_second]
-
-
-def gather_far(near):
-    return [permute(near[2], v_down), permute(near[5], v_up)]
-
-
-def add_low(value, part):
-    return lax.dynamic_update_slice_in_dim(value, value[:HALF] + part, 0, 0)
-
-
-def add_high(value, part):
-    return lax.dynamic_update_slice_in_dim(value, value[HALF:] + part, HALF, 0)
-
-
-def flip_add(value, axis, step):
-    if axis == "x":
-        return value + permute(value, lambda y, c, x, z: (y, c, x ^ step, z))
-    return value + permute(value, lambda y, c, x, z: (y, c, x, z ^ step))
+def with_tile(value, tile):
+    return jnp.concatenate([value, tile[None]], axis=0)
+
+
+def add_part(value, part, start):
+    size = part.shape[0]
+    return lax.dynamic_update_slice_in_dim(value, value[start : start + size] + part, start, 0)
 
 
 def scatter_terms(plan, pairs, spread, weight_term):
-    weight_term = weight_term + permute(weight_term, y_far)
-    *far, spread = tie(*backward_part(0, plan, pairs, spread), spread)
-    low, high = permute(far[2], v_up), permute(far[3], v_down)
-    own_low, own_high = permute(far[0], v_up), permute(far[1], v_down)
-    zero, one, three, own, own_one, own_three = backward_part(1, plan, pairs, spread)
-    low, weight_term = tie(low, weight_term)
-    one, three = permute(add_low(one, low), v_up), permute(add_high(three, high), v_down)
-    own_one = permute(add_low(own_one, own_low), v_up)
-    own_three = permute(add_high(own_three, own_high), v_down)
-    apart = zero + one + three
-    far_two = permute(apart[8:12], u_far)
-    far_one, far_three = permute(apart[4:8], y_far), permute(apart[12:16], y_far)
-    last = permute(apart[:4] + far_two, y_far)
-    own_three, weight_term = tie(own_three, weight_term)
-    weight_term = flip_add(flip_add(weight_term, "x", 1), "x", 2)
+    back_plan = plan[:3] + plan[4:]
+    up, down, spread = tie(*backward_part(0, back_plan, pairs, spread, (weight_term,)), spread)
+    up, down = permute(up, v_up), permute(down, v_down)
+    zero, one, three, own, own_one, own_three = backward_part(1, back_plan, pairs, spread)
+    one = lax.dynamic_update_slice_in_dim(add_part(one, up[HALF:PER], 0), up[PER:], PER, 0)
+    three = add_part(three, down[HALF:PER], HALF)
+    one, three = permute(one, v_up), permute(three, v_down)
+    own_one = permute(add_part(own_one, up[:HALF], 0), v_up)
+    own_three = permute(add_part(own_three, down[:HALF], HALF), v_down)
+    weight_term = ring_sum(1, plan[0], (weight_term, down[PER], one[PER], up[PER]))
+    apart = zero + one[:PER] + three
+    apart_two = permute(apart[8:12], u_far)
+    apart_far = permute(
+        jnp.concatenate([apart[4:8], apart[12:16], weight_term[None]], axis=0), y_far
+    )
+    last, apart_far = tie(apart[:4] + apart_two, apart_far)
+    last = permute(last, y_far)
+    weight_term = weight_term + apart_far[8]
     total = own + own_one + own_three
-    two = permute(total[8:12], u_far)
-    one = permute(total[4:8] + far_one, u_up)
-    three = permute(total[12:16] + far_three, u_down)
-    return total[:4] + last + one + two + three, flip_add(weight_term, "z", 1)
+    two = permute(with_tile(total[8:12], weight_term), u_far)
+    one = permute(with_tile(total[4:8] + apart_far[:4], weight_term), u_up)
+    three = permute(with_tile(total[12:16] + apart_far[4:8], weight_term), u_down)
+    weight_term = ring_sum(0, plan[0], (weight_term, three[4], two[4], one[4]))
+    return total[:4] + last + one[:4] + two[:4] + three[:4], weight_term
 
 
 def per_device(features, weight, cotangent, tiles, tile_rows, tile_cols, counts):
@@ -486,18 +535,25 @@
     first = jnp.concatenate([own, one], axis=0)
     second = jnp.concatenate([two, three], axis=0)
     plan, across, first, second, one, partner = tie(plan, across, first, second, one, partner)
-    near = gather_near(first, second)
-    second_far, first_far = permute(second, y_far), permute(one, y_far)
-    count, near[2] = tie(count, near[2])
+    one_first, three_second = permute(first, v_down), permute(second, v_up)
+    second_far = permute(second, y_far)
+    count, first = tie(count, first)
     pairs = pair_tiles(count, tile_collection)
-    far = gather_far(near)
+    first, second, one, pairs = tie(first, second, one, pairs)
+    one_second, three_first = permute(second, v_down), permute(first, v_up)
+    first_far = permute(one, y_far)
+    near = [first, second, one_first, one_second, three_first, three_second]
+    far = [permute(one_first, v_down), permute(three_second, v_up)]
     second_far, first_far, *far = tie(second_far, first_far, *far)
-    apart = gather_near(jnp.concatenate([partner, first_far], axis=0), second_far)
-    partial = forward_part(0, plan, pairs, near + far, None, nrow)
-    apart[2], apart[5], partial = tie(apart[2], apart[5], partial[0])
-    far = gather_far(apart)
-    partial = forward_part(1, plan, pairs, apart, partial, nrow)
-    *kept, given_first, given_second = forward_part(2, plan, pairs, far, partial[0], nrow)
+    first, second = jnp.concatenate([partner, first_far], axis=0), second_far
+    one_first, three_second = permute(first, v_down), permute(second, v_up)
+    partial = forward_part(0, plan[:4], pairs, near + far, None, nrow)
+    first, second, partial = tie(first, second, partial[0])
+    one_second, three_first = permute(second, v_down), permute(first, v_up)
+    apart = [first, second, one_first, one_second, three_first, three_second]
+    far = [permute(one_first, v_down), permute(three_second, v_up)]
+    partial = forward_part(1, plan[:4], pairs, apart, partial, nrow)
+    *kept, given_first, given_second = forward_part(2, plan[:4], pairs, far, partial[0], nrow)
 
     bounds = plan[0]
     kept = [kept[0] + permute(given_first, core_swap), kept[1] + permute(given_second, core_swap)]
@@ -508,10 +564,11 @@
     activated, spread, weight_term = middle_part(
         1, bounds, across, weight, cotangent, kept[1], permute(kept[1], core_swap), pairs, early
     )
-    total, weight_term = tie(*scatter_terms(plan, pairs, spread, weight_term))
-    far_total, weight_grad = tie(permute(total, y_pair), flip_add(weight_term, "z", 2))
-    parts = [total, permute(total, core_swap), far_total, permute(far_total, core_swap)]
-    return (activated, assemble(bounds, parts), weight_grad)
+    total, weight_term = scatter_terms(plan, pairs, spread, weight_term)
+    far_total = permute(total, y_pair)
+    own_other = permute(with_tile(total, weight_term), core_swap)
+    parts = [total, own_other, far_total, permute(far_total, core_swap), weight_term]
+    return (activated, *assemble(bounds, parts))
 
 
 def solution(mesh):

time: 190 us -> 170 us (0.89)
  starting transfers between devices: 68.4 us -> 50.7 us
  Pallas kernels: 19.5 us -> 35.6 us
  waiting for transfers between devices: 93.3 us -> 77.3 us
    ppermute x47 -> x39, starting transfers between devices: 68.4 us -> 50.7 us  [permute(): return lax.ppermute(value, AXES, pairs)]
    ppermute x47 -> x39, waiting for transfers between devices: 93.3 us -> 77.3 us  [permute(): return lax.ppermute(value, AXES, pairs)]
    pallas_call x2, Pallas kernels: 4.78 us -> 10.5 us  [backward_part(): pl.pallas_call(functools.partial(backward_kernel, which), name='backward_...]
    pallas_call x3, Pallas kernels: 5.92 us -> 11.4 us  [forward_part(): pl.pallas_call(functools.partial(forward_kernel, which), name='forward_ti...]
    pallas_call x1, Pallas kernels: 2.63 us -> 6.48 us  [pair_tiles(): pl.pallas_call(pair_kernel, name='pair_tiles', out_shape=pltpu.VMEM((SLOT...]
  transfers between devices with their start and end apart: 47 -> 39, of which waited for: 23 -> 22; matrix products, arithmetic and copies ran while one was open for 3% -> 1% of each run, Pallas kernels for 6% -> 15%
where the time goes in v10:
time: 170 us; the launch traced here: 169 us
  waiting for transfers between devices  77.3 us (45%)
  starting transfers between devices  50.7 us (30%)
  Pallas kernels  35.6 us (21%)
  other arithmetic  2.11 us (1%)
  local copies, waits for them, and re-layouts  1.83 us (1%)
  between operations  1.74 us (1%)
    ppermute x39, waiting for transfers between devices, permute(): return lax.ppermute(value, AXES, pairs)  77.3 us
    ppermute x39, starting transfers between devices, permute(): return lax.ppermute(value, AXES, pairs)  50.7 us
    pallas_call x3, Pallas kernels, forward_part(): pl.pallas_call(functools.partial(forward_kernel, which), name='forward_ti...  11.4 us
    pallas_call x2, Pallas kernels, backward_part(): pl.pallas_call(functools.partial(backward_kernel, which), name='backward_...  10.5 us
    pallas_call x1, Pallas kernels, pair_tiles(): pl.pallas_call(pair_kernel, name='pair_tiles', out_shape=pltpu.VMEM((SLOT...  6.48 us
    pallas_call x2, Pallas kernels, middle_part(): pl.pallas_call(functools.partial(middle_kernel, which), name='middle_%d'...  4.52 us
  transfers between devices with their start and end apart: 39, of which 22 were waited for; matrix products, arithmetic and copies ran while one was open for 1% of the time, Pallas kernels for 15%

profile of v10, /device:TPU:0, one launch (start us, length us, event | category | flops | bytes accessed | tf_op | source)
XLA Modules:
  0.0 169.3 jit_solution(13983786529666097697)
XLA Ops:
  3.9 2.7 %collective-permute-start.1 = (f32[4,128,128]{2,1,0:T(8,128)S(1)}, f32[4,128,128]{2,1,0:T(8,128)S(1)}, u32[]{:S(2)}, u32[]{:S(2)}) collective-permute-start(f32[4,128,128]{2,1,0:T(8,128)S(1)} %get-tuple-element.121), channel_id=1, source_target_pairs={{0,8},{1,9},{2,10},{3,11},{4,12},{5,13},{6,14},{7,15},{8,0},{9,1},... | collective-permute-start | bytes 786440 | tf_op jit(solution)/shard_map/ppermute | solution.py:52
  8.1 3.0 %collective-permute-start.3 = (f32[4,128,128]{2,1,0:T(8,128)S(1)}, f32[4,128,128]{2,1,0:T(8,128)S(1)}, u32[]{:S(2)}, u32[]{:S(2)}) collective-permute-start(f32[4,128,128]{2,1,0:T(8,128)S(1)} %get-tuple-element.120), channel_id=1, source_target_pairs={{0,80},{1,81},{2,82},{3,83},{4,84},{5,85},{6,86},{7,87},{8,88},{9,... | collective-permute-start | bytes 786440 | tf_op jit(solution)/shard_map/ppermute | solution.py:52
  13.9 3.6 %collective-permute-done.3 = f32[4,128,128]{2,1,0:T(8,128)S(1)} collective-permute-done((f32[4,128,128]{2,1,0:T(8,128)S(1)}, f32[4,128,128]{2,1,0:T(8,128)S(1)}, u32[]{:S(2)}, u32[]{:S(2)}) %collective-permute-start.3) | collective-permute-done | bytes 262176 | tf_op jit(solution)/shard_map/ppermute | solution.py:52
  19.7 6.5 %pair_tiles.1.tiles_ref.rest_2_ = bf16[256,128,256]{2,1,0:T(8,128)(2,1)S(1)} custom-call(s32[1]{0:T(128)} %bitcast.32.count_ref, f32[256,128,128]{2,1,0:T(8,128)} %bitcast.39), custom_call_target="tpu_custom_call" | custom-call | flops 8800000000 | bytes 1048576 | tf_op jit(solution)/shard_map/pair_tiles/pallas_call | solution.py:123
  29.8 3.2 %collective-permute-start.7 = (f32[8,128,128]{2,1,0:T(8,128)S(1)}, f32[8,128,128]{2,1,0:T(8,128)S(1)}, u32[]{:S(2)}, u32[]{:S(2)}) collective-permute-start(f32[8,128,128]{2,1,0:T(8,128)S(1)} %collective-permute-done.6.rest_2_), channel_id=1, source_target_pairs={{0,3},{1,0},{2,1},{3,2},{4,7},{5,4},{6,5},{7,6},{8,11},{9,8},{10,9... | collective-permute-start | bytes 1572872 | tf_op jit(solution)/shard_map/ppermute | solution.py:52
  33.1 3.8 %collective-permute-done.5 = f32[4,128,128]{2,1,0:T(8,128)S(1)} collective-permute-done((f32[4,128,128]{2,1,0:T(8,128)S(1)}, f32[4,128,128]{2,1,0:T(8,128)S(1)}, u32[]{:S(2)}, u32[]{:S(2)}) %collective-permute-start.5) | collective-permute-done | bytes 262176 | tf_op jit(solution)/shard_map/ppermute | solution.py:52
  38.3 6.6 %collective-permute-done.4.rest_1_ = f32[8,128,128]{2,1,0:T(8,128)S(1)} collective-permute-done((f32[8,128,128]{2,1,0:T(8,128)S(1)}, f32[8,128,128]{2,1,0:T(8,128)S(1)}, u32[]{:S(2)}, u32[]{:S(2)}) %collective-permute-start.4) | collective-permute-done | bytes 524320 | tf_op jit(solution)/shard_map/ppermute | solution.py:52
  49.1 4.6 %forward_tiles_0.1.rest_6_ = f32[16,128,128]{2,1,0:T(8,128)S(1)} custom-call(s32[9]{0:T(128)S(1)} %compare_select_fusion.10.bounds_ref, s32[256]{0:T(256)S(1)} %get-tuple-element.53.order_ref, s32[256]{0:T(256)S(1)} %get-tuple-element.54.rows_ref, s32[256]{0:T(256)S(1)} %get-tuple-element.55.slots_ref, ...), custom_call_target="tpu_custom_call" | custom-call | flops 6600000000 | bytes 1048576 | tf_op jit(solution)/shard_map/forward_tiles_0/pallas_call | solution.py:263
  53.8 3.2 %collective-permute-start.16 = (f32[8,128,128]{2,1,0:T(8,128)S(1)}, f32[8,128,128]{2,1,0:T(8,128)S(1)}, u32[]{:S(2)}, u32[]{:S(2)}) collective-permute-start(f32[8,128,128]{2,1,0:T(8,128)S(1)} %collective-permute-done.4.rest_1_), channel_id=1, source_target_pairs={{0,3},{1,0},{2,1},{3,2},{4,7},{5,4},{6,5},{7,6},{8,11},{9,8},{10,9... | collective-permute-start | bytes 1572872 | tf_op jit(solution)/shard_map/ppermute | solution.py:52
  59.1 5.1 %collective-permute-done.17.rest_4_ = f32[8,128,128]{2,1,0:T(8,128)S(1)} collective-permute-done((f32[8,128,128]{2,1,0:T(8,128)S(1)}, f32[8,128,128]{2,1,0:T(8,128)S(1)}, u32[]{:S(2)}, u32[]{:S(2)}) %collective-permute-start.17) | collective-permute-done | bytes 524320 | tf_op jit(solution)/shard_map/ppermute | solution.py:52
  64.2 4.5 %forward_tiles_1.1.rest_2_ = f32[16,128,128]{2,1,0:T(8,128)S(1)} custom-call(s32[9]{0:T(128)S(1)} %compare_select_fusion.10.bounds_ref, s32[256]{0:T(256)S(1)} %get-tuple-element.53.order_ref, s32[256]{0:T(256)S(1)} %get-tuple-element.54.rows_ref, s32[256]{0:T(256)S(1)} %get-tuple-element.55.slots_ref, ...), custom_call_target="tpu_custom_call" | custom-call | flops 5500000256 | bytes 1048576 | tf_op jit(solution)/shard_map/forward_tiles_1/pallas_call | solution.py:263
  76.1 6.8 %collective-permute-done.22 = f32[4,128,128]{2,1,0:T(8,128)S(1)} collective-permute-done((f32[4,128,128]{2,1,0:T(8,128)S(1)}, f32[4,128,128]{2,1,0:T(8,128)S(1)}, u32[]{:S(2)}, u32[]{:S(2)}) %collective-permute-start.22) | collective-permute-done | bytes 262176 | tf_op jit(solution)/shard_map/ppermute | solution.py:52
  83.1 4.7 %collective-permute-done.19 = f32[4,128,128]{2,1,0:T(8,128)S(1)} collective-permute-done((f32[4,128,128]{2,1,0:T(8,128)S(1)}, f32[4,128,128]{2,1,0:T(8,128)S(1)}, u32[]{:S(2)}, u32[]{:S(2)}) %collective-permute-start.19) | collective-permute-done | bytes 262176 | tf_op jit(solution)/shard_map/ppermute | solution.py:52
  92.5 3.4 %backward_tiles_0.1 = (f32[17,128,128]{2,1,0:T(8,128)S(1)}, f32[17,128,128]{2,1,0:T(8,128)S(1)}) custom-call(s32[9]{0:T(128)S(1)} %compare_select_fusion.10.bounds_ref, s32[256]{0:T(256)S(1)} %get-tuple-element.53.order_ref, s32[256]{0:T(256)S(1)} %get-tuple-element.54.rows_ref, s32[256]{0:T(256)S(1)} %get-tuple-element.81.slots_ref, ...), custom_call_target="tpu_custom_call" | custom-call | flops 3300000000 | bytes 1048576 | tf_op jit(solution)/shard_map/backward_tiles_0/pallas_call | solution.py:280
  96.0 3.2 %collective-permute-start.26 = (f32[17,128,128]{2,1,0:T(8,128)S(1)}, f32[17,128,128]{2,1,0:T(8,128)S(1)}, u32[]{:S(2)}, u32[]{:S(2)}) collective-permute-start(f32[17,128,128]{2,1,0:T(8,128)S(1)} %get-tuple-element.91), channel_id=1, source_target_pairs={{0,3},{1,0},{2,1},{3,2},{4,7},{5,4},{6,5},{7,6},{8,11},{9,8},{10,9... | collective-permute-start | bytes 3342344 | tf_op jit(solution)/shard_map/ppermute | solution.py:52
  99.2 7.1 %backward_tiles_1.1 = (f32[16,128,128]{2,1,0:T(8,128)S(1)}, f32[17,128,128]{2,1,0:T(8,128)S(1)}, f32[16,128,128]{2,1,0:T(8,128)S(1)}, f32[16,128,128]{2,1,0:T(8,...) custom-call(s32[9]{0:T(128)S(1)} %compare_select_fusion.10.bounds_ref, ...), custom_call_target="tpu_custom_call" | custom-call | flops 8800000000 | bytes 1048576 | tf_op jit(solution)/shard_map/backward_tiles_1/pallas_call | solution.py:280
  106.3 6.4 %collective-permute-done.24 = f32[17,128,128]{2,1,0:T(8,128)S(1)} collective-permute-done((f32[17,128,128]{2,1,0:T(8,128)S(1)}, f32[17,128,128]{2,1,0:T(8,128)S(1)}, u32[]{:S(2)}, u32[]{:S(2)}) %collective-permute-start.24) | collective-permute-done | bytes 1114144 | tf_op jit(solution)/shard_map/ppermute | solution.py:52
  113.3 3.3 %collective-permute-start.29 = (f32[16,128,128]{2,1,0:T(8,128)S(1)}, f32[16,128,128]{2,1,0:T(8,128)S(1)}, u32[]{:S(2)}, u32[]{:S(2)}) collective-permute-start(f32[16,128,128]{2,1,0:T(8,128)S(1)} %get-tuple-element.113), channel_id=1, source_target_pairs={{0,3},{1,0},{2,1},{3,2},{4,7},{5,4},{6,5},{7,6},{8,11},{9,8},{10,9... | collective-permute-start | bytes 3145736 | tf_op jit(solution)/shard_map/ppermute | solution.py:52
  116.6 3.2 %collective-permute-start.27 = (f32[16,128,128]{2,1,0:T(8,128)S(1)}, f32[16,128,128]{2,1,0:T(8,128)S(1)}, u32[]{:S(2)}, u32[]{:S(2)}) collective-permute-start(f32[16,128,128]{2,1,0:T(8,128)S(1)} %get-tuple-element.112), channel_id=1, source_target_pairs={{0,3},{1,0},{2,1},{3,2},{4,7},{5,4},{6,5},{7,6},{8,11},{9,8},{10,9... | collective-permute-start | bytes 3145736 | tf_op jit(solution)/shard_map/ppermute | solution.py:52
  119.8 9.9 %collective-permute-done.28 = f32[17,128,128]{2,1,0:T(8,128)S(1)} collective-permute-done((f32[17,128,128]{2,1,0:T(8,128)S(1)}, f32[17,128,128]{2,1,0:T(8,128)S(1)}, u32[]{:S(2)}, u32[]{:S(2)}) %collective-permute-start.28) | collective-permute-done | bytes 1114144 | tf_op jit(solution)/shard_map/ppermute | solution.py:52
  133.8 9.9 %collective-permute-done.25 = f32[16,128,128]{2,1,0:T(8,128)S(1)} collective-permute-done((f32[16,128,128]{2,1,0:T(8,128)S(1)}, f32[16,128,128]{2,1,0:T(8,128)S(1)}, u32[]{:S(2)}, u32[]{:S(2)}) %collective-permute-start.25) | collective-permute-done | bytes 1048608 | tf_op jit(solution)/shard_map/ppermute | solution.py:52
  148.9 3.2 %collective-permute-start.32 = (f32[4,128,128]{2,1,0:T(8,128)S(1)}, f32[4,128,128]{2,1,0:T(8,128)S(1)}, u32[]{:S(2)}, u32[]{:S(2)}) collective-permute-start(f32[4,128,128]{2,1,0:T(8,128)S(1)} %slice_add_fusion.10), channel_id=1, source_target_pairs={{0,16},{1,17},{2,18},{3,19},{4,20},{5,21},{6,22},{7,23},{8,24},{9,... | collective-permute-start | bytes 786440 | tf_op jit(solution)/shard_map/ppermute | solution.py:52
  152.2 4.6 %collective-permute-done.32 = f32[4,128,128]{2,1,0:T(8,128)S(1)} collective-permute-done((f32[4,128,128]{2,1,0:T(8,128)S(1)}, f32[4,128,128]{2,1,0:T(8,128)S(1)}, u32[]{:S(2)}, u32[]{:S(2)}) %collective-permute-start.32) | collective-permute-done | bytes 262176 | tf_op jit(solution)/shard_map/ppermute | solution.py:52
  160.5 5.5 %collective-permute-done.37.across_ref = f32[4,128,128]{2,1,0:T(8,128)S(1)} collective-permute-done((f32[4,128,128]{2,1,0:T(8,128)S(1)}, f32[4,128,128]{2,1,0:T(8,128)S(1)}, u32[]{:S(2)}, u32[]{:S(2)}) %collective-permute-start.37) | collective-permute-done | bytes 262176 | tf_op jit(solution)/shard_map/ppermute | solution.py:52
  (108 shorter events, 49.3 us)
Async XLA Ops:
  2.3 11.4 %collective-permute-start.2 = (f32[4,128,128]{2,1,0:T(8,128)S(1)}, f32[4,128,128]{2,1,0:T(8,128)S(1)}, u32[]{:S(2)}, u32[]{:S(2)}) collective-permute-start(f32[4,128,128]{2,1,0:T(8,128)S(1)} %get-tuple-element.121), channel_id=1, source_target_pairs={{0,4},{1,5},{2,6},{3,7},{4,8},{5,9},{6,10},{7,11},{8,12},{9,13},{1... | collective-permute-start | bytes 786440 | tf_op jit(solution)/shard_map/ppermute | solution.py:52
  17.4 12.4 %collective-permute-start.6 = (f32[8,128,128]{2,1,0:T(8,128)S(1)}, f32[8,128,128]{2,1,0:T(8,128)S(1)}, u32[]{:S(2)}, u32[]{:S(2)}) collective-permute-start(f32[8,128,128]{2,1,0:T(8,128)S(1)} %pad_maximum_fusion.4.rest_0_), channel_id=1, source_target_pairs={{0,3},{1,0},{2,1},{3,2},{4,7},{5,4},{6,5},{7,6},{8,11},{9,8},{10,9... | collective-permute-start | bytes 1572872 | tf_op jit(solution)/shard_map/ppermute | solution.py:52
  19.7 13.3 %collective-permute-start.8 = (f32[8,128,128]{2,1,0:T(8,128)S(1)}, f32[8,128,128]{2,1,0:T(8,128)S(1)}, u32[]{:S(2)}, u32[]{:S(2)}) collective-permute-start(f32[8,128,128]{2,1,0:T(8,128)S(1)} %pad_maximum_fusion.5.rest_1_), channel_id=1, source_target_pairs={{0,1},{1,2},{2,3},{3,0},{4,5},{5,6},{6,7},{7,4},{8,9},{9,10},{10,1... | collective-permute-start | bytes 1572872 | tf_op jit(solution)/shard_map/ppermute | solution.py:52
  26.2 10.7 %collective-permute-start.5 = (f32[4,128,128]{2,1,0:T(8,128)S(1)}, f32[4,128,128]{2,1,0:T(8,128)S(1)}, u32[]{:S(2)}, u32[]{:S(2)}) collective-permute-start(f32[4,128,128]{2,1,0:T(8,128)S(1)} %collective-permute-done), channel_id=1, source_target_pairs={{0,16},{1,17},{2,18},{3,19},{4,20},{5,21},{6,22},{7,23},{8,24},{9,... | collective-permute-start | bytes 786440 | tf_op jit(solution)/shard_map/ppermute | solution.py:52
  28.3 16.6 %collective-permute-start.4 = (f32[8,128,128]{2,1,0:T(8,128)S(1)}, f32[8,128,128]{2,1,0:T(8,128)S(1)}, u32[]{:S(2)}, u32[]{:S(2)}) collective-permute-start(f32[8,128,128]{2,1,0:T(8,128)S(1)} %pad_maximum_fusion.5.rest_1_), channel_id=1, source_target_pairs={{0,16},{1,17},{2,18},{3,19},{4,20},{5,21},{6,22},{7,23},{8,24},{9,... | collective-permute-start | bytes 1572872 | tf_op jit(solution)/shard_map/ppermute | solution.py:52
  29.8 15.1 %collective-permute-start.7 = (f32[8,128,128]{2,1,0:T(8,128)S(1)}, f32[8,128,128]{2,1,0:T(8,128)S(1)}, u32[]{:S(2)}, u32[]{:S(2)}) collective-permute-start(f32[8,128,128]{2,1,0:T(8,128)S(1)} %collective-permute-done.6.rest_2_), channel_id=1, source_target_pairs={{0,3},{1,0},{2,1},{3,2},{4,7},{5,4},{6,5},{7,6},{8,11},{9,8},{10,9... | collective-permute-start | bytes 1572872 | tf_op jit(solution)/shard_map/ppermute | solution.py:52
  33.1 11.8 %collective-permute-start.9 = (f32[8,128,128]{2,1,0:T(8,128)S(1)}, f32[8,128,128]{2,1,0:T(8,128)S(1)}, u32[]{:S(2)}, u32[]{:S(2)}) collective-permute-start(f32[8,128,128]{2,1,0:T(8,128)S(1)} %collective-permute-done.8.rest_5_), channel_id=1, source_target_pairs={{0,1},{1,2},{2,3},{3,0},{4,5},{5,6},{6,7},{7,4},{8,9},{9,10},{10,1... | collective-permute-start | bytes 1572872 | tf_op jit(solution)/shard_map/ppermute | solution.py:52
  33.1 16.0 %collective-permute-start.15 = (f32[8,128,128]{2,1,0:T(8,128)S(1)}, f32[8,128,128]{2,1,0:T(8,128)S(1)}, u32[]{:S(2)}, u32[]{:S(2)}) collective-permute-start(f32[8,128,128]{2,1,0:T(8,128)S(1)} %pad_maximum_fusion.4.rest_0_), channel_id=1, source_target_pairs={{0,1},{1,2},{2,3},{3,0},{4,5},{5,6},{6,7},{7,4},{8,9},{9,10},{10,1... | collective-permute-start | bytes 1572872 | tf_op jit(solution)/shard_map/ppermute | solution.py:52
  36.9 12.2 %collective-permute-start.14 = (f32[8,128,128]{2,1,0:T(8,128)S(1)}, f32[8,128,128]{2,1,0:T(8,128)S(1)}, u32[]{:S(2)}, u32[]{:S(2)}) collective-permute-start(f32[8,128,128]{2,1,0:T(8,128)S(1)} %pad_maximum_fusion.5.rest_1_), channel_id=1, source_target_pairs={{0,3},{1,0},{2,1},{3,2},{4,7},{5,4},{6,5},{7,6},{8,11},{9,8},{10,9... | collective-permute-start | bytes 1572872 | tf_op jit(solution)/shard_map/ppermute | solution.py:52
  44.9 12.1 %collective-permute-start.10 = (f32[8,128,128]{2,1,0:T(8,128)S(1)}, f32[8,128,128]{2,1,0:T(8,128)S(1)}, u32[]{:S(2)}, u32[]{:S(2)}) collective-permute-start(f32[8,128,128]{2,1,0:T(8,128)S(1)} %constant_dynamic-update-slice_fusion.rest_0_), channel_id=1, source_target_pairs={{0,3},{1,0},{2,1},{3,2},{4,7},{5,4},{6,5},{7,6},{8,11},{9,8},{10,9... | collective-permute-start | bytes 1572872 | tf_op jit(solution)/shard_map/ppermute | solution.py:52
  45.0 12.1 %collective-permute-start.12 = (f32[8,128,128]{2,1,0:T(8,128)S(1)}, f32[8,128,128]{2,1,0:T(8,128)S(1)}, u32[]{:S(2)}, u32[]{:S(2)}) collective-permute-start(f32[8,128,128]{2,1,0:T(8,128)S(1)} %collective-permute-done.4.rest_1_), channel_id=1, source_target_pairs={{0,1},{1,2},{2,3},{3,0},{4,5},{5,6},{6,7},{7,4},{8,9},{9,10},{10,1... | collective-permute-start | bytes 1572872 | tf_op jit(solution)/shard_map/ppermute | solution.py:52
  57.0 12.3 %collective-permute-start.11 = (f32[8,128,128]{2,1,0:T(8,128)S(1)}, f32[8,128,128]{2,1,0:T(8,128)S(1)}, u32[]{:S(2)}, u32[]{:S(2)}) collective-permute-start(f32[8,128,128]{2,1,0:T(8,128)S(1)} %collective-permute-done.10.rest_2_), channel_id=1, source_target_pairs={{0,3},{1,0},{2,1},{3,2},{4,7},{5,4},{6,5},{7,6},{8,11},{9,8},{10,9... | collective-permute-start | bytes 1572872 | tf_op jit(solution)/shard_map/ppermute | solution.py:52
  57.1 12.7 %collective-permute-start.13 = (f32[8,128,128]{2,1,0:T(8,128)S(1)}, f32[8,128,128]{2,1,0:T(8,128)S(1)}, u32[]{:S(2)}, u32[]{:S(2)}) collective-permute-start(f32[8,128,128]{2,1,0:T(8,128)S(1)} %collective-permute-done.12.rest_5_), channel_id=1, source_target_pairs={{0,1},{1,2},{2,3},{3,0},{4,5},{5,6},{6,7},{7,4},{8,9},{9,10},{10,1... | collective-permute-start | bytes 1572872 | tf_op jit(solution)/shard_map/ppermute | solution.py:52
  74.1 13.7 %collective-permute-start.19 = (f32[4,128,128]{2,1,0:T(8,128)S(1)}, f32[4,128,128]{2,1,0:T(8,128)S(1)}, u32[]{:S(2)}, u32[]{:S(2)}) collective-permute-start(f32[4,128,128]{2,1,0:T(8,128)S(1)} %add.301), channel_id=1, source_target_pairs={{0,64},{1,65},{2,66},{3,67},{4,68},{5,69},{6,70},{7,71},{8,72},{9,... | collective-permute-start | bytes 786440 | tf_op jit(solution)/shard_map/ppermute | solution.py:52
  95.9 16.8 %collective-permute-start.24 = (f32[17,128,128]{2,1,0:T(8,128)S(1)}, f32[17,128,128]{2,1,0:T(8,128)S(1)}, u32[]{:S(2)}, u32[]{:S(2)}) collective-permute-start(f32[17,128,128]{2,1,0:T(8,128)S(1)} %get-tuple-element.89), channel_id=1, source_target_pairs={{0,1},{1,2},{2,3},{3,0},{4,5},{5,6},{6,7},{7,4},{8,9},{9,10},{10,1... | collective-permute-start | bytes 3342344 | tf_op jit(solution)/shard_map/ppermute | solution.py:52
  96.0 17.1 %collective-permute-start.26 = (f32[17,128,128]{2,1,0:T(8,128)S(1)}, f32[17,128,128]{2,1,0:T(8,128)S(1)}, u32[]{:S(2)}, u32[]{:S(2)}) collective-permute-start(f32[17,128,128]{2,1,0:T(8,128)S(1)} %get-tuple-element.91), channel_id=1, source_target_pairs={{0,3},{1,0},{2,1},{3,2},{4,7},{5,4},{6,5},{7,6},{8,11},{9,8},{10,9... | collective-permute-start | bytes 3342344 | tf_op jit(solution)/shard_map/ppermute | solution.py:52
  113.0 16.8 %collective-permute-start.28 = (f32[17,128,128]{2,1,0:T(8,128)S(1)}, f32[17,128,128]{2,1,0:T(8,128)S(1)}, u32[]{:S(2)}, u32[]{:S(2)}) collective-permute-start(f32[17,128,128]{2,1,0:T(8,128)S(1)} %get-tuple-element.115), channel_id=1, source_target_pairs={{0,1},{1,2},{2,3},{3,0},{4,5},{5,6},{6,7},{7,4},{8,9},{9,10},{10,1... | collective-permute-start | bytes 3342344 | tf_op jit(solution)/shard_map/ppermute | solution.py:52
  113.3 17.0 %collective-permute-start.29 = (f32[16,128,128]{2,1,0:T(8,128)S(1)}, f32[16,128,128]{2,1,0:T(8,128)S(1)}, u32[]{:S(2)}, u32[]{:S(2)}) collective-permute-start(f32[16,128,128]{2,1,0:T(8,128)S(1)} %get-tuple-element.113), channel_id=1, source_target_pairs={{0,3},{1,0},{2,1},{3,2},{4,7},{5,4},{6,5},{7,6},{8,11},{9,8},{10,9... | collective-permute-start | bytes 3145736 | tf_op jit(solution)/shard_map/ppermute | solution.py:52
  116.6 27.2 %collective-permute-start.25 = (f32[16,128,128]{2,1,0:T(8,128)S(1)}, f32[16,128,128]{2,1,0:T(8,128)S(1)}, u32[]{:S(2)}, u32[]{:S(2)}) collective-permute-start(f32[16,128,128]{2,1,0:T(8,128)S(1)} %get-tuple-element.110), channel_id=1, source_target_pairs={{0,1},{1,2},{2,3},{3,0},{4,5},{5,6},{6,7},{7,4},{8,9},{9,10},{10,1... | collective-permute-start | bytes 3145736 | tf_op jit(solution)/shard_map/ppermute | solution.py:52
  116.6 27.2 %collective-permute-start.27 = (f32[16,128,128]{2,1,0:T(8,128)S(1)}, f32[16,128,128]{2,1,0:T(8,128)S(1)}, u32[]{:S(2)}, u32[]{:S(2)}) collective-permute-start(f32[16,128,128]{2,1,0:T(8,128)S(1)} %get-tuple-element.112), channel_id=1, source_target_pairs={{0,3},{1,0},{2,1},{3,2},{4,7},{5,4},{6,5},{7,6},{8,11},{9,8},{10,9... | collective-permute-start | bytes 3145736 | tf_op jit(solution)/shard_map/ppermute | solution.py:52
  130.6 14.8 %collective-permute-start.31 = (f32[9,128,128]{2,1,0:T(8,128)S(1)}, f32[9,128,128]{2,1,0:T(8,128)S(1)}, u32[]{:S(2)}, u32[]{:S(2)}) collective-permute-start(f32[9,128,128]{2,1,0:T(8,128)S(1)} %pad_maximum_fusion), channel_id=1, source_target_pairs={{0,16},{1,17},{2,18},{3,19},{4,20},{5,21},{6,22},{7,23},{8,24},{9,... | collective-permute-start | bytes 1769480 | tf_op jit(solution)/shard_map/ppermute | solution.py:52
  133.2 10.8 %collective-permute-start.30 = (f32[4,128,128]{2,1,0:T(8,128)S(1)}, f32[4,128,128]{2,1,0:T(8,128)S(1)}, u32[]{:S(2)}, u32[]{:S(2)}) collective-permute-start(f32[4,128,128]{2,1,0:T(8,128)S(1)} %get-tuple-element.119), channel_id=1, source_target_pairs={{0,8},{1,9},{2,10},{3,11},{4,12},{5,13},{6,14},{7,15},{8,0},{9,1},... | collective-permute-start | bytes 786440 | tf_op jit(solution)/shard_map/ppermute | solution.py:52
  145.6 11.9 %collective-permute-start.33 = (f32[5,128,128]{2,1,0:T(8,128)S(1)}, f32[5,128,128]{2,1,0:T(8,128)S(1)}, u32[]{:S(2)}, u32[]{:S(2)}) collective-permute-start(f32[5,128,128]{2,1,0:T(8,128)S(1)} %get-tuple-element.122), channel_id=1, source_target_pairs={{0,4},{1,5},{2,6},{3,7},{4,8},{5,9},{6,10},{7,11},{8,12},{9,13},{1... | collective-permute-start | bytes 983048 | tf_op jit(solution)/shard_map/ppermute | solution.py:52
  145.7 11.8 %collective-permute-start.34 = (f32[5,128,128]{2,1,0:T(8,128)S(1)}, f32[5,128,128]{2,1,0:T(8,128)S(1)}, u32[]{:S(2)}, u32[]{:S(2)}) collective-permute-start(f32[5,128,128]{2,1,0:T(8,128)S(1)} %get-tuple-element.123), channel_id=1, source_target_pairs={{0,8},{1,9},{2,10},{3,11},{4,12},{5,13},{6,14},{7,15},{8,0},{9,1},... | collective-permute-start | bytes 983048 | tf_op jit(solution)/shard_map/ppermute | solution.py:52
  (19 other events, 142.8 us)

commit v11 on v10

--- a/solution.py
+++ b/solution.py
@@ -534,18 +534,17 @@
     own, one, two, three, partner = gather_own(features, loop)
     first = jnp.concatenate([own, one], axis=0)
     second = jnp.concatenate([two, three], axis=0)
-    plan, across, first, second, one, partner = tie(plan, across, first, second, one, partner)
+    plan, across, first, second, partner = tie(plan, across, first, second, partner)
     one_first, three_second = permute(first, v_down), permute(second, v_up)
     second_far = permute(second, y_far)
-    count, first = tie(count, first)
+    one_second, three_first = permute(second, v_down), permute(first, v_up)
+    partner_one = permute(partner, u_down)
+    count, one_first = tie(count, one_first)
     pairs = pair_tiles(count, tile_collection)
-    first, second, one, pairs = tie(first, second, one, pairs)
-    one_second, three_first = permute(second, v_down), permute(first, v_up)
-    first_far = permute(one, y_far)
     near = [first, second, one_first, one_second, three_first, three_second]
     far = [permute(one_first, v_down), permute(three_second, v_up)]
-    second_far, first_far, *far = tie(second_far, first_far, *far)
-    first, second = jnp.concatenate([partner, first_far], axis=0), second_far
+    second_far, partner_one, *far = tie(second_far, partner_one, *far)
+    first, second = jnp.concatenate([partner, partner_one], axis=0), second_far
     one_first, three_second = permute(first, v_down), permute(second, v_up)
     partial = forward_part(0, plan[:4], pairs, near + far, None, nrow)
     first, second, partial = tie(first, second, partial[0])

time: 170 us -> 168 us (0.988)
  Pallas kernels: 35.6 us -> 21.3 us
  starting transfers between devices: 50.7 us -> 56.6 us
  waiting for transfers between devices: 77.3 us -> 82.5 us
    ppermute x39, starting transfers between devices: 50.7 us -> 56.6 us  [permute(): return lax.ppermute(value, AXES, pairs)]
    pallas_call x2, Pallas kernels: 10.5 us -> 4.95 us  [backward_part(): pl.pallas_call(functools.partial(backward_kernel, which), name='backward_...]
    ppermute x39, waiting for transfers between devices: 77.3 us -> 82.5 us  [permute(): return lax.ppermute(value, AXES, pairs)]
    pallas_call x3, Pallas kernels: 11.4 us -> 6.37 us  [forward_part(): pl.pallas_call(functools.partial(forward_kernel, which), name='forward_ti...]
    pallas_call x1, Pallas kernels: 6.48 us -> 2.63 us  [pair_tiles(): pl.pallas_call(pair_kernel, name='pair_tiles', out_shape=pltpu.VMEM((SLOT...]
  transfers between devices with their start and end apart: 39 -> 39, of which waited for: 22 -> 21; matrix products, arithmetic and copies ran while one was open for 1% -> 1% of each run, Pallas kernels for 15% -> 8%
where the time goes in v11:
time: 168 us; the launch traced here: 166 us
  waiting for transfers between devices  82.5 us (49%)
  starting transfers between devices  56.6 us (34%)
  Pallas kernels  21.3 us (13%)
  other arithmetic  2.1 us (1%)
  local copies, waits for them, and re-layouts  1.83 us (1%)
  between operations  1.75 us (1%)
    ppermute x39, waiting for transfers between devices, permute(): return lax.ppermute(value, AXES, pairs)  82.5 us
    ppermute x39, starting transfers between devices, permute(): return lax.ppermute(value, AXES, pairs)  56.6 us
    pallas_call x3, Pallas kernels, forward_part(): pl.pallas_call(functools.partial(forward_kernel, which), name='forward_ti...  6.37 us
    pallas_call x2, Pallas kernels, backward_part(): pl.pallas_call(functools.partial(backward_kernel, which), name='backward_...  4.95 us
    pallas_call x2, Pallas kernels, middle_part(): pl.pallas_call(functools.partial(middle_kernel, which), name='middle_%d'...  4.52 us
  transfers between devices with their start and end apart: 39, of which 21 were waited for; matrix products, arithmetic and copies ran while one was open for 1% of the time, Pallas kernels for 8%

profile of v11, /device:TPU:0, one launch (start us, length us, event | category | flops | bytes accessed | tf_op | source)
XLA Modules:
  0.0 166.2 jit_solution(14695250355631445260)
XLA Ops:
  3.9 2.7 %collective-permute-start.1 = (f32[4,128,128]{2,1,0:T(8,128)S(1)}, f32[4,128,128]{2,1,0:T(8,128)S(1)}, u32[]{:S(2)}, u32[]{:S(2)}) collective-permute-start(f32[4,128,128]{2,1,0:T(8,128)S(1)} %get-tuple-element.111), channel_id=1, source_target_pairs={{0,8},{1,9},{2,10},{3,11},{4,12},{5,13},{6,14},{7,15},{8,0},{9,1},... | collective-permute-start | bytes 786440 | tf_op jit(solution)/shard_map/ppermute | solution.py:52
  8.1 3.0 %collective-permute-start.3 = (f32[4,128,128]{2,1,0:T(8,128)S(1)}, f32[4,128,128]{2,1,0:T(8,128)S(1)}, u32[]{:S(2)}, u32[]{:S(2)}) collective-permute-start(f32[4,128,128]{2,1,0:T(8,128)S(1)} %get-tuple-element.110), channel_id=1, source_target_pairs={{0,80},{1,81},{2,82},{3,83},{4,84},{5,85},{6,86},{7,87},{8,88},{9,... | collective-permute-start | bytes 786440 | tf_op jit(solution)/shard_map/ppermute | solution.py:52
  13.9 3.6 %collective-permute-done.3 = f32[4,128,128]{2,1,0:T(8,128)S(1)} collective-permute-done((f32[4,128,128]{2,1,0:T(8,128)S(1)}, f32[4,128,128]{2,1,0:T(8,128)S(1)}, u32[]{:S(2)}, u32[]{:S(2)}) %collective-permute-start.3) | collective-permute-done | bytes 262176 | tf_op jit(solution)/shard_map/ppermute | solution.py:52
  23.8 5.6 %collective-permute-done.4.rest_2_ = f32[8,128,128]{2,1,0:T(8,128)S(1)} collective-permute-done((f32[8,128,128]{2,1,0:T(8,128)S(1)}, f32[8,128,128]{2,1,0:T(8,128)S(1)}, u32[]{:S(2)}, u32[]{:S(2)}) %collective-permute-start.4) | collective-permute-done | bytes 524320 | tf_op jit(solution)/shard_map/ppermute | solution.py:52
  31.3 3.0 %collective-permute-start.7 = (f32[8,128,128]{2,1,0:T(8,128)S(1)}, f32[8,128,128]{2,1,0:T(8,128)S(1)}, u32[]{:S(2)}, u32[]{:S(2)}) collective-permute-start(f32[8,128,128]{2,1,0:T(8,128)S(1)} %collective-permute-done.4.rest_2_), channel_id=1, source_target_pairs={{0,3},{1,0},{2,1},{3,2},{4,7},{5,4},{6,5},{7,6},{8,11},{9,8},{10,9... | collective-permute-start | bytes 1572872 | tf_op jit(solution)/shard_map/ppermute | solution.py:52
  37.0 5.8 %collective-permute-done.5.rest_1_ = f32[8,128,128]{2,1,0:T(8,128)S(1)} collective-permute-done((f32[8,128,128]{2,1,0:T(8,128)S(1)}, f32[8,128,128]{2,1,0:T(8,128)S(1)}, u32[]{:S(2)}, u32[]{:S(2)}) %collective-permute-start.5) | collective-permute-done | bytes 524320 | tf_op jit(solution)/shard_map/ppermute | solution.py:52
  46.9 2.8 %forward_tiles_0.1.rest_6_ = f32[16,128,128]{2,1,0:T(8,128)S(1)} custom-call(s32[9]{0:T(128)S(1)} %compare_select_fusion.10.bounds_ref, s32[256]{0:T(256)S(1)} %get-tuple-element.48.order_ref, s32[256]{0:T(256)S(1)} %get-tuple-element.49.rows_ref, s32[256]{0:T(256)S(1)} %get-tuple-element.50.slots_ref, ...), custom_call_target="tpu_custom_call" | custom-call | flops 6600000000 | bytes 1048576 | tf_op jit(solution)/shard_map/forward_tiles_0/pallas_call | solution.py:263
  49.7 2.8 %collective-permute-start.17 = (f32[8,128,128]{2,1,0:T(8,128)S(1)}, f32[8,128,128]{2,1,0:T(8,128)S(1)}, u32[]{:S(2)}, u32[]{:S(2)}) collective-permute-start(f32[8,128,128]{2,1,0:T(8,128)S(1)} %constant_dynamic-update-slice_fusion.rest_0_), channel_id=1, source_target_pairs={{0,1},{1,2},{2,3},{3,0},{4,5},{5,6},{6,7},{7,4},{8,9},{9,10},{10,1... | collective-permute-start | bytes 1572872 | tf_op jit(solution)/shard_map/ppermute | solution.py:52
  56.0 4.9 %collective-permute-done.17.rest_4_ = f32[8,128,128]{2,1,0:T(8,128)S(1)} collective-permute-done((f32[8,128,128]{2,1,0:T(8,128)S(1)}, f32[8,128,128]{2,1,0:T(8,128)S(1)}, u32[]{:S(2)}, u32[]{:S(2)}) %collective-permute-start.17) | collective-permute-done | bytes 524320 | tf_op jit(solution)/shard_map/ppermute | solution.py:52
  63.9 3.4 %collective-permute-done.11.rest_0_ = f32[8,128,128]{2,1,0:T(8,128)S(1)} collective-permute-done((f32[8,128,128]{2,1,0:T(8,128)S(1)}, f32[8,128,128]{2,1,0:T(8,128)S(1)}, u32[]{:S(2)}, u32[]{:S(2)}) %collective-permute-start.11) | collective-permute-done | bytes 524320 | tf_op jit(solution)/shard_map/ppermute | solution.py:52
  72.7 6.8 %collective-permute-done.22 = f32[4,128,128]{2,1,0:T(8,128)S(1)} collective-permute-done((f32[4,128,128]{2,1,0:T(8,128)S(1)}, f32[4,128,128]{2,1,0:T(8,128)S(1)}, u32[]{:S(2)}, u32[]{:S(2)}) %collective-permute-start.22) | collective-permute-done | bytes 262176 | tf_op jit(solution)/shard_map/ppermute | solution.py:52
  79.7 4.7 %collective-permute-done.19 = f32[4,128,128]{2,1,0:T(8,128)S(1)} collective-permute-done((f32[4,128,128]{2,1,0:T(8,128)S(1)}, f32[4,128,128]{2,1,0:T(8,128)S(1)}, u32[]{:S(2)}, u32[]{:S(2)}) %collective-permute-start.19) | collective-permute-done | bytes 262176 | tf_op jit(solution)/shard_map/ppermute | solution.py:52
  93.2 2.9 %collective-permute-start.26 = (f32[17,128,128]{2,1,0:T(8,128)S(1)}, f32[17,128,128]{2,1,0:T(8,128)S(1)}, u32[]{:S(2)}, u32[]{:S(2)}) collective-permute-start(f32[17,128,128]{2,1,0:T(8,128)S(1)} %get-tuple-element.81), channel_id=1, source_target_pairs={{0,3},{1,0},{2,1},{3,2},{4,7},{5,4},{6,5},{7,6},{8,11},{9,8},{10,9... | collective-permute-start | bytes 3342344 | tf_op jit(solution)/shard_map/ppermute | solution.py:52
  96.1 2.9 %backward_tiles_1.1 = (f32[16,128,128]{2,1,0:T(8,128)S(1)}, f32[17,128,128]{2,1,0:T(8,128)S(1)}, f32[16,128,128]{2,1,0:T(8,128)S(1)}, f32[16,128,128]{2,1,0:T(8,...) custom-call(s32[9]{0:T(128)S(1)} %compare_select_fusion.10.bounds_ref, ...), custom_call_target="tpu_custom_call" | custom-call | flops 8800000000 | bytes 1048576 | tf_op jit(solution)/shard_map/backward_tiles_1/pallas_call | solution.py:280
  99.0 10.5 %collective-permute-done.24 = f32[17,128,128]{2,1,0:T(8,128)S(1)} collective-permute-done((f32[17,128,128]{2,1,0:T(8,128)S(1)}, f32[17,128,128]{2,1,0:T(8,128)S(1)}, u32[]{:S(2)}, u32[]{:S(2)}) %collective-permute-start.24) | collective-permute-done | bytes 1114144 | tf_op jit(solution)/shard_map/ppermute | solution.py:52
  110.1 3.3 %collective-permute-start.29 = (f32[16,128,128]{2,1,0:T(8,128)S(1)}, f32[16,128,128]{2,1,0:T(8,128)S(1)}, u32[]{:S(2)}, u32[]{:S(2)}) collective-permute-start(f32[16,128,128]{2,1,0:T(8,128)S(1)} %get-tuple-element.103), channel_id=1, source_target_pairs={{0,3},{1,0},{2,1},{3,2},{4,7},{5,4},{6,5},{7,6},{8,11},{9,8},{10,9... | collective-permute-start | bytes 3145736 | tf_op jit(solution)/shard_map/ppermute | solution.py:52
  113.4 3.2 %collective-permute-start.27 = (f32[16,128,128]{2,1,0:T(8,128)S(1)}, f32[16,128,128]{2,1,0:T(8,128)S(1)}, u32[]{:S(2)}, u32[]{:S(2)}) collective-permute-start(f32[16,128,128]{2,1,0:T(8,128)S(1)} %get-tuple-element.102), channel_id=1, source_target_pairs={{0,3},{1,0},{2,1},{3,2},{4,7},{5,4},{6,5},{7,6},{8,11},{9,8},{10,9... | collective-permute-start | bytes 3145736 | tf_op jit(solution)/shard_map/ppermute | solution.py:52
  116.7 9.9 %collective-permute-done.28 = f32[17,128,128]{2,1,0:T(8,128)S(1)} collective-permute-done((f32[17,128,128]{2,1,0:T(8,128)S(1)}, f32[17,128,128]{2,1,0:T(8,128)S(1)}, u32[]{:S(2)}, u32[]{:S(2)}) %collective-permute-start.28) | collective-permute-done | bytes 1114144 | tf_op jit(solution)/shard_map/ppermute | solution.py:52
  127.6 3.2 %collective-permute-start.30 = (f32[4,128,128]{2,1,0:T(8,128)S(1)}, f32[4,128,128]{2,1,0:T(8,128)S(1)}, u32[]{:S(2)}, u32[]{:S(2)}) collective-permute-start(f32[4,128,128]{2,1,0:T(8,128)S(1)} %get-tuple-element.109), channel_id=1, source_target_pairs={{0,8},{1,9},{2,10},{3,11},{4,12},{5,13},{6,14},{7,15},{8,0},{9,1},... | collective-permute-start | bytes 786440 | tf_op jit(solution)/shard_map/ppermute | solution.py:52
  130.8 9.8 %collective-permute-done.25 = f32[16,128,128]{2,1,0:T(8,128)S(1)} collective-permute-done((f32[16,128,128]{2,1,0:T(8,128)S(1)}, f32[16,128,128]{2,1,0:T(8,128)S(1)}, u32[]{:S(2)}, u32[]{:S(2)}) %collective-permute-start.25) | collective-permute-done | bytes 1048608 | tf_op jit(solution)/shard_map/ppermute | solution.py:52
  141.8 3.3 %collective-permute-start.34 = (f32[5,128,128]{2,1,0:T(8,128)S(1)}, f32[5,128,128]{2,1,0:T(8,128)S(1)}, u32[]{:S(2)}, u32[]{:S(2)}) collective-permute-start(f32[5,128,128]{2,1,0:T(8,128)S(1)} %get-tuple-element.113), channel_id=1, source_target_pairs={{0,8},{1,9},{2,10},{3,11},{4,12},{5,13},{6,14},{7,15},{8,0},{9,1},... | collective-permute-start | bytes 983048 | tf_op jit(solution)/shard_map/ppermute | solution.py:52
  147.1 4.9 %collective-permute-start.32 = (f32[4,128,128]{2,1,0:T(8,128)S(1)}, f32[4,128,128]{2,1,0:T(8,128)S(1)}, u32[]{:S(2)}, u32[]{:S(2)}) collective-permute-start(f32[4,128,128]{2,1,0:T(8,128)S(1)} %slice_add_fusion.10), channel_id=1, source_target_pairs={{0,16},{1,17},{2,18},{3,19},{4,20},{5,21},{6,22},{7,23},{8,24},{9,... | collective-permute-start | bytes 786440 | tf_op jit(solution)/shard_map/ppermute | solution.py:52
  151.9 4.5 %collective-permute-done.32 = f32[4,128,128]{2,1,0:T(8,128)S(1)} collective-permute-done((f32[4,128,128]{2,1,0:T(8,128)S(1)}, f32[4,128,128]{2,1,0:T(8,128)S(1)}, u32[]{:S(2)}, u32[]{:S(2)}) %collective-permute-start.32) | collective-permute-done | bytes 262176 | tf_op jit(solution)/shard_map/ppermute | solution.py:52
  157.4 5.6 %collective-permute-done.37.across_ref = f32[4,128,128]{2,1,0:T(8,128)S(1)} collective-permute-done((f32[4,128,128]{2,1,0:T(8,128)S(1)}, f32[4,128,128]{2,1,0:T(8,128)S(1)}, u32[]{:S(2)}, u32[]{:S(2)}) %collective-permute-start.37) | collective-permute-done | bytes 262176 | tf_op jit(solution)/shard_map/ppermute | solution.py:52
  (108 shorter events, 51.2 us)
Async XLA Ops:
  2.3 11.4 %collective-permute-start.2 = (f32[4,128,128]{2,1,0:T(8,128)S(1)}, f32[4,128,128]{2,1,0:T(8,128)S(1)}, u32[]{:S(2)}, u32[]{:S(2)}) collective-permute-start(f32[4,128,128]{2,1,0:T(8,128)S(1)} %get-tuple-element.111), channel_id=1, source_target_pairs={{0,4},{1,5},{2,6},{3,7},{4,8},{5,9},{6,10},{7,11},{8,12},{9,13},{1... | collective-permute-start | bytes 786440 | tf_op jit(solution)/shard_map/ppermute | solution.py:52
  17.4 12.0 %collective-permute-start.4 = (f32[8,128,128]{2,1,0:T(8,128)S(1)}, f32[8,128,128]{2,1,0:T(8,128)S(1)}, u32[]{:S(2)}, u32[]{:S(2)}) collective-permute-start(f32[8,128,128]{2,1,0:T(8,128)S(1)} %pad_maximum_fusion.4.rest_0_), channel_id=1, source_target_pairs={{0,3},{1,0},{2,1},{3,2},{4,7},{5,4},{6,5},{7,6},{8,11},{9,8},{10,9... | collective-permute-start | bytes 1572872 | tf_op jit(solution)/shard_map/ppermute | solution.py:52
  19.7 14.6 %collective-permute-start.8 = (f32[8,128,128]{2,1,0:T(8,128)S(1)}, f32[8,128,128]{2,1,0:T(8,128)S(1)}, u32[]{:S(2)}, u32[]{:S(2)}) collective-permute-start(f32[8,128,128]{2,1,0:T(8,128)S(1)} %pad_maximum_fusion.5.rest_1_), channel_id=1, source_target_pairs={{0,1},{1,2},{2,3},{3,0},{4,5},{5,6},{6,7},{7,4},{8,9},{9,10},{10,1... | collective-permute-start | bytes 1572872 | tf_op jit(solution)/shard_map/ppermute | solution.py:52
  19.7 11.6 %collective-permute-start.6 = (f32[4,128,128]{2,1,0:T(8,128)S(1)}, f32[4,128,128]{2,1,0:T(8,128)S(1)}, u32[]{:S(2)}, u32[]{:S(2)}) collective-permute-start(f32[4,128,128]{2,1,0:T(8,128)S(1)} %collective-permute-done.3), channel_id=1, source_target_pairs={{0,12},{1,13},{2,14},{3,15},{4,0},{5,1},{6,2},{7,3},{8,4},{9,5},{1... | collective-permute-start | bytes 786440 | tf_op jit(solution)/shard_map/ppermute | solution.py:52
  20.6 26.3 %collective-permute-start.15 = (f32[8,128,128]{2,1,0:T(8,128)S(1)}, f32[8,128,128]{2,1,0:T(8,128)S(1)}, u32[]{:S(2)}, u32[]{:S(2)}) collective-permute-start(f32[8,128,128]{2,1,0:T(8,128)S(1)} %pad_maximum_fusion.4.rest_0_), channel_id=1, source_target_pairs={{0,1},{1,2},{2,3},{3,0},{4,5},{5,6},{6,7},{7,4},{8,9},{9,10},{10,1... | collective-permute-start | bytes 1572872 | tf_op jit(solution)/shard_map/ppermute | solution.py:52
  21.7 25.2 %collective-permute-start.14 = (f32[8,128,128]{2,1,0:T(8,128)S(1)}, f32[8,128,128]{2,1,0:T(8,128)S(1)}, u32[]{:S(2)}, u32[]{:S(2)}) collective-permute-start(f32[8,128,128]{2,1,0:T(8,128)S(1)} %pad_maximum_fusion.5.rest_1_), channel_id=1, source_target_pairs={{0,3},{1,0},{2,1},{3,2},{4,7},{5,4},{6,5},{7,6},{8,11},{9,8},{10,9... | collective-permute-start | bytes 1572872 | tf_op jit(solution)/shard_map/ppermute | solution.py:52
  29.4 13.4 %collective-permute-start.5 = (f32[8,128,128]{2,1,0:T(8,128)S(1)}, f32[8,128,128]{2,1,0:T(8,128)S(1)}, u32[]{:S(2)}, u32[]{:S(2)}) collective-permute-start(f32[8,128,128]{2,1,0:T(8,128)S(1)} %pad_maximum_fusion.5.rest_1_), channel_id=1, source_target_pairs={{0,16},{1,17},{2,18},{3,19},{4,20},{5,21},{6,22},{7,23},{8,24},{9,... | collective-permute-start | bytes 1572872 | tf_op jit(solution)/shard_map/ppermute | solution.py:52
  31.3 11.4 %collective-permute-start.7 = (f32[8,128,128]{2,1,0:T(8,128)S(1)}, f32[8,128,128]{2,1,0:T(8,128)S(1)}, u32[]{:S(2)}, u32[]{:S(2)}) collective-permute-start(f32[8,128,128]{2,1,0:T(8,128)S(1)} %collective-permute-done.4.rest_2_), channel_id=1, source_target_pairs={{0,3},{1,0},{2,1},{3,2},{4,7},{5,4},{6,5},{7,6},{8,11},{9,8},{10,9... | collective-permute-start | bytes 1572872 | tf_op jit(solution)/shard_map/ppermute | solution.py:52
  44.8 11.0 %collective-permute-start.12 = (f32[8,128,128]{2,1,0:T(8,128)S(1)}, f32[8,128,128]{2,1,0:T(8,128)S(1)}, u32[]{:S(2)}, u32[]{:S(2)}) collective-permute-start(f32[8,128,128]{2,1,0:T(8,128)S(1)} %collective-permute-done.5.rest_1_), channel_id=1, source_target_pairs={{0,1},{1,2},{2,3},{3,0},{4,5},{5,6},{6,7},{7,4},{8,9},{9,10},{10,1... | collective-permute-start | bytes 1572872 | tf_op jit(solution)/shard_map/ppermute | solution.py:52
  49.7 11.2 %collective-permute-start.17 = (f32[8,128,128]{2,1,0:T(8,128)S(1)}, f32[8,128,128]{2,1,0:T(8,128)S(1)}, u32[]{:S(2)}, u32[]{:S(2)}) collective-permute-start(f32[8,128,128]{2,1,0:T(8,128)S(1)} %constant_dynamic-update-slice_fusion.rest_0_), channel_id=1, source_target_pairs={{0,1},{1,2},{2,3},{3,0},{4,5},{5,6},{6,7},{7,4},{8,9},{9,10},{10,1... | collective-permute-start | bytes 1572872 | tf_op jit(solution)/shard_map/ppermute | solution.py:52
  54.0 13.3 %collective-permute-start.11 = (f32[8,128,128]{2,1,0:T(8,128)S(1)}, f32[8,128,128]{2,1,0:T(8,128)S(1)}, u32[]{:S(2)}, u32[]{:S(2)}) collective-permute-start(f32[8,128,128]{2,1,0:T(8,128)S(1)} %collective-permute-done.10.rest_2_), channel_id=1, source_target_pairs={{0,3},{1,0},{2,1},{3,2},{4,7},{5,4},{6,5},{7,6},{8,11},{9,8},{10,9... | collective-permute-start | bytes 1572872 | tf_op jit(solution)/shard_map/ppermute | solution.py:52
  55.8 11.5 %collective-permute-start.13 = (f32[8,128,128]{2,1,0:T(8,128)S(1)}, f32[8,128,128]{2,1,0:T(8,128)S(1)}, u32[]{:S(2)}, u32[]{:S(2)}) collective-permute-start(f32[8,128,128]{2,1,0:T(8,128)S(1)} %collective-permute-done.12.rest_5_), channel_id=1, source_target_pairs={{0,1},{1,2},{2,3},{3,0},{4,5},{5,6},{6,7},{7,4},{8,9},{9,10},{10,1... | collective-permute-start | bytes 1572872 | tf_op jit(solution)/shard_map/ppermute | solution.py:52
  70.7 13.7 %collective-permute-start.19 = (f32[4,128,128]{2,1,0:T(8,128)S(1)}, f32[4,128,128]{2,1,0:T(8,128)S(1)}, u32[]{:S(2)}, u32[]{:S(2)}) collective-permute-start(f32[4,128,128]{2,1,0:T(8,128)S(1)} %add.301), channel_id=1, source_target_pairs={{0,64},{1,65},{2,66},{3,67},{4,68},{5,69},{6,70},{7,71},{8,72},{9,... | collective-permute-start | bytes 786440 | tf_op jit(solution)/shard_map/ppermute | solution.py:52
  91.1 18.4 %collective-permute-start.24 = (f32[17,128,128]{2,1,0:T(8,128)S(1)}, f32[17,128,128]{2,1,0:T(8,128)S(1)}, u32[]{:S(2)}, u32[]{:S(2)}) collective-permute-start(f32[17,128,128]{2,1,0:T(8,128)S(1)} %get-tuple-element.79), channel_id=1, source_target_pairs={{0,1},{1,2},{2,3},{3,0},{4,5},{5,6},{6,7},{7,4},{8,9},{9,10},{10,1... | collective-permute-start | bytes 3342344 | tf_op jit(solution)/shard_map/ppermute | solution.py:52
  93.2 16.7 %collective-permute-start.26 = (f32[17,128,128]{2,1,0:T(8,128)S(1)}, f32[17,128,128]{2,1,0:T(8,128)S(1)}, u32[]{:S(2)}, u32[]{:S(2)}) collective-permute-start(f32[17,128,128]{2,1,0:T(8,128)S(1)} %get-tuple-element.81), channel_id=1, source_target_pairs={{0,3},{1,0},{2,1},{3,2},{4,7},{5,4},{6,5},{7,6},{8,11},{9,8},{10,9... | collective-permute-start | bytes 3342344 | tf_op jit(solution)/shard_map/ppermute | solution.py:52
  109.8 16.8 %collective-permute-start.28 = (f32[17,128,128]{2,1,0:T(8,128)S(1)}, f32[17,128,128]{2,1,0:T(8,128)S(1)}, u32[]{:S(2)}, u32[]{:S(2)}) collective-permute-start(f32[17,128,128]{2,1,0:T(8,128)S(1)} %get-tuple-element.105), channel_id=1, source_target_pairs={{0,1},{1,2},{2,3},{3,0},{4,5},{5,6},{6,7},{7,4},{8,9},{9,10},{10,1... | collective-permute-start | bytes 3342344 | tf_op jit(solution)/shard_map/ppermute | solution.py:52
  110.1 17.0 %collective-permute-start.29 = (f32[16,128,128]{2,1,0:T(8,128)S(1)}, f32[16,128,128]{2,1,0:T(8,128)S(1)}, u32[]{:S(2)}, u32[]{:S(2)}) collective-permute-start(f32[16,128,128]{2,1,0:T(8,128)S(1)} %get-tuple-element.103), channel_id=1, source_target_pairs={{0,3},{1,0},{2,1},{3,2},{4,7},{5,4},{6,5},{7,6},{8,11},{9,8},{10,9... | collective-permute-start | bytes 3145736 | tf_op jit(solution)/shard_map/ppermute | solution.py:52
  113.4 27.2 %collective-permute-start.25 = (f32[16,128,128]{2,1,0:T(8,128)S(1)}, f32[16,128,128]{2,1,0:T(8,128)S(1)}, u32[]{:S(2)}, u32[]{:S(2)}) collective-permute-start(f32[16,128,128]{2,1,0:T(8,128)S(1)} %get-tuple-element.100), channel_id=1, source_target_pairs={{0,1},{1,2},{2,3},{3,0},{4,5},{5,6},{6,7},{7,4},{8,9},{9,10},{10,1... | collective-permute-start | bytes 3145736 | tf_op jit(solution)/shard_map/ppermute | solution.py:52
  113.4 27.2 %collective-permute-start.27 = (f32[16,128,128]{2,1,0:T(8,128)S(1)}, f32[16,128,128]{2,1,0:T(8,128)S(1)}, u32[]{:S(2)}, u32[]{:S(2)}) collective-permute-start(f32[16,128,128]{2,1,0:T(8,128)S(1)} %get-tuple-element.102), channel_id=1, source_target_pairs={{0,3},{1,0},{2,1},{3,2},{4,7},{5,4},{6,5},{7,6},{8,11},{9,8},{10,9... | collective-permute-start | bytes 3145736 | tf_op jit(solution)/shard_map/ppermute | solution.py:52
  127.5 14.0 %collective-permute-start.31 = (f32[9,128,128]{2,1,0:T(8,128)S(1)}, f32[9,128,128]{2,1,0:T(8,128)S(1)}, u32[]{:S(2)}, u32[]{:S(2)}) collective-permute-start(f32[9,128,128]{2,1,0:T(8,128)S(1)} %pad_maximum_fusion), channel_id=1, source_target_pairs={{0,16},{1,17},{2,18},{3,19},{4,20},{5,21},{6,22},{7,23},{8,24},{9,... | collective-permute-start | bytes 1769480 | tf_op jit(solution)/shard_map/ppermute | solution.py:52
  127.6 13.3 %collective-permute-start.30 = (f32[4,128,128]{2,1,0:T(8,128)S(1)}, f32[4,128,128]{2,1,0:T(8,128)S(1)}, u32[]{:S(2)}, u32[]{:S(2)}) collective-permute-start(f32[4,128,128]{2,1,0:T(8,128)S(1)} %get-tuple-element.109), channel_id=1, source_target_pairs={{0,8},{1,9},{2,10},{3,11},{4,12},{5,13},{6,14},{7,15},{8,0},{9,1},... | collective-permute-start | bytes 786440 | tf_op jit(solution)/shard_map/ppermute | solution.py:52
  141.6 14.8 %collective-permute-start.33 = (f32[5,128,128]{2,1,0:T(8,128)S(1)}, f32[5,128,128]{2,1,0:T(8,128)S(1)}, u32[]{:S(2)}, u32[]{:S(2)}) collective-permute-start(f32[5,128,128]{2,1,0:T(8,128)S(1)} %get-tuple-element.112), channel_id=1, source_target_pairs={{0,4},{1,5},{2,6},{3,7},{4,8},{5,9},{6,10},{7,11},{8,12},{9,13},{1... | collective-permute-start | bytes 983048 | tf_op jit(solution)/shard_map/ppermute | solution.py:52
  141.8 14.6 %collective-permute-start.34 = (f32[5,128,128]{2,1,0:T(8,128)S(1)}, f32[5,128,128]{2,1,0:T(8,128)S(1)}, u32[]{:S(2)}, u32[]{:S(2)}) collective-permute-start(f32[5,128,128]{2,1,0:T(8,128)S(1)} %get-tuple-element.113), channel_id=1, source_target_pairs={{0,8},{1,9},{2,10},{3,11},{4,12},{5,13},{6,14},{7,15},{8,0},{9,1},... | collective-permute-start | bytes 983048 | tf_op jit(solution)/shard_map/ppermute | solution.py:52
  145.1 11.3 %collective-permute-start.35 = (f32[5,128,128]{2,1,0:T(8,128)S(1)}, f32[5,128,128]{2,1,0:T(8,128)S(1)}, u32[]{:S(2)}, u32[]{:S(2)}) collective-permute-start(f32[5,128,128]{2,1,0:T(8,128)S(1)} %get-tuple-element.114), channel_id=1, source_target_pairs={{0,12},{1,13},{2,14},{3,15},{4,0},{5,1},{6,2},{7,3},{8,4},{9,5},{1... | collective-permute-start | bytes 983048 | tf_op jit(solution)/shard_map/ppermute | solution.py:52
  (19 other events, 141.2 us)

commit v12 on v11

--- a/solution.py
+++ b/solution.py
@@ -538,8 +538,8 @@
     one_first, three_second = permute(first, v_down), permute(second, v_up)
     second_far = permute(second, y_far)
     one_second, three_first = permute(second, v_down), permute(first, v_up)
+    count, one_first, partner = tie(count, one_first, partner)
     partner_one = permute(partner, u_down)
-    count, one_first = tie(count, one_first)
     pairs = pair_tiles(count, tile_collection)
     near = [first, second, one_first, one_second, three_first, three_second]
     far = [permute(one_first, v_down), permute(three_second, v_up)]

time: 168 us -> 168 us (level)
  Pallas kernels: 21.3 us -> 36.1 us
  starting transfers between devices: 56.6 us -> 46.2 us
  waiting for transfers between devices: 82.5 us -> 78.5 us
    ppermute x39, starting transfers between devices: 56.6 us -> 46.2 us  [permute(): return lax.ppermute(value, AXES, pairs)]
    pallas_call x2, Pallas kernels: 4.95 us -> 10.5 us  [backward_part(): pl.pallas_call(functools.partial(backward_kernel, which), name='backward_...]
    pallas_call x3, Pallas kernels: 6.37 us -> 11.8 us  [forward_part(): pl.pallas_call(functools.partial(forward_kernel, which), name='forward_ti...]
    ppermute x39, waiting for transfers between devices: 82.5 us -> 78.5 us  [permute(): return lax.ppermute(value, AXES, pairs)]
    pallas_call x1, Pallas kernels: 2.63 us -> 6.48 us  [pair_tiles(): pl.pallas_call(pair_kernel, name='pair_tiles', out_shape=pltpu.VMEM((SLOT...]
  transfers between devices with their start and end apart: 39 -> 39, of which waited for: 21 -> 22; matrix products, arithmetic and copies ran while one was open for 1% -> 1% of each run, Pallas kernels for 8% -> 16%
where the time goes in v12:
time: 168 us; the launch traced here: 166 us
  waiting for transfers between devices  78.5 us (47%)
  starting transfers between devices  46.2 us (28%)
  Pallas kernels  36.1 us (21%)
  other arithmetic  2.1 us (1%)
  local copies, waits for them, and re-layouts  1.83 us (1%)
  between operations  1.77 us (1%)
    ppermute x39, waiting for transfers between devices, permute(): return lax.ppermute(value, AXES, pairs)  78.5 us
    ppermute x39, starting transfers between devices, permute(): return lax.ppermute(value, AXES, pairs)  46.2 us
    pallas_call x3, Pallas kernels, forward_part(): pl.pallas_call(functools.partial(forward_kernel, which), name='forward_ti...  11.8 us
    pallas_call x2, Pallas kernels, backward_part(): pl.pallas_call(functools.partial(backward_kernel, which), name='backward_...  10.5 us
    pallas_call x1, Pallas kernels, pair_tiles(): pl.pallas_call(pair_kernel, name='pair_tiles', out_shape=pltpu.VMEM((SLOT...  6.48 us
    pallas_call x2, Pallas kernels, middle_part(): pl.pallas_call(functools.partial(middle_kernel, which), name='middle_%d'...  4.52 us
  transfers between devices with their start and end apart: 39, of which 22 were waited for; matrix products, arithmetic and copies ran while one was open for 1% of the time, Pallas kernels for 16%

profile of v12, /device:TPU:0, one launch (start us, length us, event | category | flops | bytes accessed | tf_op | source)
XLA Modules:
  0.0 166.5 jit_solution(4897787614573071293)
XLA Ops:
  3.9 2.7 %collective-permute-start.1 = (f32[4,128,128]{2,1,0:T(8,128)S(1)}, f32[4,128,128]{2,1,0:T(8,128)S(1)}, u32[]{:S(2)}, u32[]{:S(2)}) collective-permute-start(f32[4,128,128]{2,1,0:T(8,128)S(1)} %get-tuple-element.113), channel_id=1, source_target_pairs={{0,8},{1,9},{2,10},{3,11},{4,12},{5,13},{6,14},{7,15},{8,0},{9,1},... | collective-permute-start | bytes 786440 | tf_op jit(solution)/shard_map/ppermute | solution.py:52
  8.1 3.0 %collective-permute-start.3 = (f32[4,128,128]{2,1,0:T(8,128)S(1)}, f32[4,128,128]{2,1,0:T(8,128)S(1)}, u32[]{:S(2)}, u32[]{:S(2)}) collective-permute-start(f32[4,128,128]{2,1,0:T(8,128)S(1)} %get-tuple-element.112), channel_id=1, source_target_pairs={{0,80},{1,81},{2,82},{3,83},{4,84},{5,85},{6,86},{7,87},{8,88},{9,... | collective-permute-start | bytes 786440 | tf_op jit(solution)/shard_map/ppermute | solution.py:52
  13.9 3.6 %collective-permute-done.3 = f32[4,128,128]{2,1,0:T(8,128)S(1)} collective-permute-done((f32[4,128,128]{2,1,0:T(8,128)S(1)}, f32[4,128,128]{2,1,0:T(8,128)S(1)}, u32[]{:S(2)}, u32[]{:S(2)}) %collective-permute-start.3) | collective-permute-done | bytes 262176 | tf_op jit(solution)/shard_map/ppermute | solution.py:52
  27.3 2.8 %collective-permute-done.8.rest_5_ = f32[8,128,128]{2,1,0:T(8,128)S(1)} collective-permute-done((f32[8,128,128]{2,1,0:T(8,128)S(1)}, f32[8,128,128]{2,1,0:T(8,128)S(1)}, u32[]{:S(2)}, u32[]{:S(2)}) %collective-permute-start.8) | collective-permute-done | bytes 524320 | tf_op jit(solution)/shard_map/ppermute | solution.py:52
  31.0 2.9 %collective-permute-done.5.rest_1_ = f32[8,128,128]{2,1,0:T(8,128)S(1)} collective-permute-done((f32[8,128,128]{2,1,0:T(8,128)S(1)}, f32[8,128,128]{2,1,0:T(8,128)S(1)}, u32[]{:S(2)}, u32[]{:S(2)}) %collective-permute-start.5) | collective-permute-done | bytes 524320 | tf_op jit(solution)/shard_map/ppermute | solution.py:52
  35.3 6.5 %pair_tiles.1.tiles_ref.rest_2_ = bf16[256,128,256]{2,1,0:T(8,128)(2,1)S(1)} custom-call(s32[1]{0:T(128)} %bitcast.32.count_ref, f32[256,128,128]{2,1,0:T(8,128)} %bitcast.39), custom_call_target="tpu_custom_call" | custom-call | flops 8800000000 | bytes 1048576 | tf_op jit(solution)/shard_map/pair_tiles/pallas_call | solution.py:123
  46.4 5.6 %forward_tiles_0.1.rest_6_ = f32[16,128,128]{2,1,0:T(8,128)S(1)} custom-call(s32[9]{0:T(128)S(1)} %compare_select_fusion.10.bounds_ref, s32[256]{0:T(256)S(1)} %get-tuple-element.49.order_ref, s32[256]{0:T(256)S(1)} %get-tuple-element.50.rows_ref, s32[256]{0:T(256)S(1)} %get-tuple-element.51.slots_ref, ...), custom_call_target="tpu_custom_call" | custom-call | flops 6600000000 | bytes 1048576 | tf_op jit(solution)/shard_map/forward_tiles_0/pallas_call | solution.py:263
  52.1 3.2 %collective-permute-start.16 = (f32[8,128,128]{2,1,0:T(8,128)S(1)}, f32[8,128,128]{2,1,0:T(8,128)S(1)}, u32[]{:S(2)}, u32[]{:S(2)}) collective-permute-start(f32[8,128,128]{2,1,0:T(8,128)S(1)} %collective-permute-done.5.rest_1_), channel_id=1, source_target_pairs={{0,3},{1,0},{2,1},{3,2},{4,7},{5,4},{6,5},{7,6},{8,11},{9,8},{10,9... | collective-permute-start | bytes 1572872 | tf_op jit(solution)/shard_map/ppermute | solution.py:52
  57.4 5.1 %collective-permute-done.17.rest_4_ = f32[8,128,128]{2,1,0:T(8,128)S(1)} collective-permute-done((f32[8,128,128]{2,1,0:T(8,128)S(1)}, f32[8,128,128]{2,1,0:T(8,128)S(1)}, u32[]{:S(2)}, u32[]{:S(2)}) %collective-permute-start.17) | collective-permute-done | bytes 524320 | tf_op jit(solution)/shard_map/ppermute | solution.py:52
  62.5 4.5 %forward_tiles_1.1.rest_2_ = f32[16,128,128]{2,1,0:T(8,128)S(1)} custom-call(s32[9]{0:T(128)S(1)} %compare_select_fusion.10.bounds_ref, s32[256]{0:T(256)S(1)} %get-tuple-element.49.order_ref, s32[256]{0:T(256)S(1)} %get-tuple-element.50.rows_ref, s32[256]{0:T(256)S(1)} %get-tuple-element.51.slots_ref, ...), custom_call_target="tpu_custom_call" | custom-call | flops 5500000256 | bytes 1048576 | tf_op jit(solution)/shard_map/forward_tiles_1/pallas_call | solution.py:263
  74.0 6.8 %collective-permute-done.22 = f32[4,128,128]{2,1,0:T(8,128)S(1)} collective-permute-done((f32[4,128,128]{2,1,0:T(8,128)S(1)}, f32[4,128,128]{2,1,0:T(8,128)S(1)}, u32[]{:S(2)}, u32[]{:S(2)}) %collective-permute-start.22) | collective-permute-done | bytes 262176 | tf_op jit(solution)/shard_map/ppermute | solution.py:52
  80.9 4.7 %collective-permute-done.19 = f32[4,128,128]{2,1,0:T(8,128)S(1)} collective-permute-done((f32[4,128,128]{2,1,0:T(8,128)S(1)}, f32[4,128,128]{2,1,0:T(8,128)S(1)}, u32[]{:S(2)}, u32[]{:S(2)}) %collective-permute-start.19) | collective-permute-done | bytes 262176 | tf_op jit(solution)/shard_map/ppermute | solution.py:52
  87.6 2.7 %middle_1.1 = (f32[128,2048]{1,0:T(8,128)}, bf16[16,128,256]{2,1,0:T(8,128)(2,1)S(1)}, f32[128,128]{1,0:T(8,128)S(1)}) custom-call(s32[9]{0:T(128)S(1)} %compare_select_fusion.10.bounds_ref, f32[128,128]{1,0:T(8,128)S(1)} %bitcast.35, f32[128,128]{1,0:T(8,128)S(1)} %copy-done.1, f32[128,2048]{1,0:T(8,128)S(1)} %copy-done, f32[4,128,128]{2,1,0:T(8,128)S(1)} %add.302.rest_0_, ...), custom_call_target="tpu_custom_call" | custom-call | flops 2200000000 | bytes 1048576 | tf_op jit(solution)/shard_map/middle_1/pallas_call | solution.py:364
  90.3 3.4 %backward_tiles_0.1 = (f32[17,128,128]{2,1,0:T(8,128)S(1)}, f32[17,128,128]{2,1,0:T(8,128)S(1)}) custom-call(s32[9]{0:T(128)S(1)} %compare_select_fusion.10.bounds_ref, s32[256]{0:T(256)S(1)} %get-tuple-element.49.order_ref, s32[256]{0:T(256)S(1)} %get-tuple-element.50.rows_ref, s32[256]{0:T(256)S(1)} %get-tuple-element.73.slots_ref, ...), custom_call_target="tpu_custom_call" | custom-call | flops 3300000000 | bytes 1048576 | tf_op jit(solution)/shard_map/backward_tiles_0/pallas_call | solution.py:280
  93.8 3.2 %collective-permute-start.26 = (f32[17,128,128]{2,1,0:T(8,128)S(1)}, f32[17,128,128]{2,1,0:T(8,128)S(1)}, u32[]{:S(2)}, u32[]{:S(2)}) collective-permute-start(f32[17,128,128]{2,1,0:T(8,128)S(1)} %get-tuple-element.83), channel_id=1, source_target_pairs={{0,3},{1,0},{2,1},{3,2},{4,7},{5,4},{6,5},{7,6},{8,11},{9,8},{10,9... | collective-permute-start | bytes 3342344 | tf_op jit(solution)/shard_map/ppermute | solution.py:52
  97.0 7.1 %backward_tiles_1.1 = (f32[16,128,128]{2,1,0:T(8,128)S(1)}, f32[17,128,128]{2,1,0:T(8,128)S(1)}, f32[16,128,128]{2,1,0:T(8,128)S(1)}, f32[16,128,128]{2,1,0:T(8,...) custom-call(s32[9]{0:T(128)S(1)} %compare_select_fusion.10.bounds_ref, ...), custom_call_target="tpu_custom_call" | custom-call | flops 8800000000 | bytes 1048576 | tf_op jit(solution)/shard_map/backward_tiles_1/pallas_call | solution.py:280
  104.1 6.4 %collective-permute-done.24 = f32[17,128,128]{2,1,0:T(8,128)S(1)} collective-permute-done((f32[17,128,128]{2,1,0:T(8,128)S(1)}, f32[17,128,128]{2,1,0:T(8,128)S(1)}, u32[]{:S(2)}, u32[]{:S(2)}) %collective-permute-start.24) | collective-permute-done | bytes 1114144 | tf_op jit(solution)/shard_map/ppermute | solution.py:52
  111.1 3.3 %collective-permute-start.29 = (f32[16,128,128]{2,1,0:T(8,128)S(1)}, f32[16,128,128]{2,1,0:T(8,128)S(1)}, u32[]{:S(2)}, u32[]{:S(2)}) collective-permute-start(f32[16,128,128]{2,1,0:T(8,128)S(1)} %get-tuple-element.105), channel_id=1, source_target_pairs={{0,3},{1,0},{2,1},{3,2},{4,7},{5,4},{6,5},{7,6},{8,11},{9,8},{10,9... | collective-permute-start | bytes 3145736 | tf_op jit(solution)/shard_map/ppermute | solution.py:52
  114.4 3.2 %collective-permute-start.27 = (f32[16,128,128]{2,1,0:T(8,128)S(1)}, f32[16,128,128]{2,1,0:T(8,128)S(1)}, u32[]{:S(2)}, u32[]{:S(2)}) collective-permute-start(f32[16,128,128]{2,1,0:T(8,128)S(1)} %get-tuple-element.104), channel_id=1, source_target_pairs={{0,3},{1,0},{2,1},{3,2},{4,7},{5,4},{6,5},{7,6},{8,11},{9,8},{10,9... | collective-permute-start | bytes 3145736 | tf_op jit(solution)/shard_map/ppermute | solution.py:52
  117.7 9.9 %collective-permute-done.28 = f32[17,128,128]{2,1,0:T(8,128)S(1)} collective-permute-done((f32[17,128,128]{2,1,0:T(8,128)S(1)}, f32[17,128,128]{2,1,0:T(8,128)S(1)}, u32[]{:S(2)}, u32[]{:S(2)}) %collective-permute-start.28) | collective-permute-done | bytes 1114144 | tf_op jit(solution)/shard_map/ppermute | solution.py:52
  130.2 11.4 %collective-permute-done.25 = f32[16,128,128]{2,1,0:T(8,128)S(1)} collective-permute-done((f32[16,128,128]{2,1,0:T(8,128)S(1)}, f32[16,128,128]{2,1,0:T(8,128)S(1)}, u32[]{:S(2)}, u32[]{:S(2)}) %collective-permute-start.25) | collective-permute-done | bytes 1048608 | tf_op jit(solution)/shard_map/ppermute | solution.py:52
  143.9 3.4 %collective-permute-start.34 = (f32[5,128,128]{2,1,0:T(8,128)S(1)}, f32[5,128,128]{2,1,0:T(8,128)S(1)}, u32[]{:S(2)}, u32[]{:S(2)}) collective-permute-start(f32[5,128,128]{2,1,0:T(8,128)S(1)} %get-tuple-element.115), channel_id=1, source_target_pairs={{0,8},{1,9},{2,10},{3,11},{4,12},{5,13},{6,14},{7,15},{8,0},{9,1},... | collective-permute-start | bytes 983048 | tf_op jit(solution)/shard_map/ppermute | solution.py:52
  148.1 7.8 %collective-permute-done.32 = f32[4,128,128]{2,1,0:T(8,128)S(1)} collective-permute-done((f32[4,128,128]{2,1,0:T(8,128)S(1)}, f32[4,128,128]{2,1,0:T(8,128)S(1)}, u32[]{:S(2)}, u32[]{:S(2)}) %collective-permute-start.32) | collective-permute-done | bytes 262176 | tf_op jit(solution)/shard_map/ppermute | solution.py:52
  158.4 4.9 %collective-permute-done.37.across_ref = f32[4,128,128]{2,1,0:T(8,128)S(1)} collective-permute-done((f32[4,128,128]{2,1,0:T(8,128)S(1)}, f32[4,128,128]{2,1,0:T(8,128)S(1)}, u32[]{:S(2)}, u32[]{:S(2)}) %collective-permute-start.37) | collective-permute-done | bytes 262176 | tf_op jit(solution)/shard_map/ppermute | solution.py:52
  (108 shorter events, 46.6 us)
Async XLA Ops:
  2.3 11.4 %collective-permute-start.2 = (f32[4,128,128]{2,1,0:T(8,128)S(1)}, f32[4,128,128]{2,1,0:T(8,128)S(1)}, u32[]{:S(2)}, u32[]{:S(2)}) collective-permute-start(f32[4,128,128]{2,1,0:T(8,128)S(1)} %get-tuple-element.113), channel_id=1, source_target_pairs={{0,4},{1,5},{2,6},{3,7},{4,8},{5,9},{6,10},{7,11},{8,12},{9,13},{1... | collective-permute-start | bytes 786440 | tf_op jit(solution)/shard_map/ppermute | solution.py:52
  19.7 10.4 %collective-permute-start.8 = (f32[8,128,128]{2,1,0:T(8,128)S(1)}, f32[8,128,128]{2,1,0:T(8,128)S(1)}, u32[]{:S(2)}, u32[]{:S(2)}) collective-permute-start(f32[8,128,128]{2,1,0:T(8,128)S(1)} %pad_maximum_fusion.5.rest_1_), channel_id=1, source_target_pairs={{0,1},{1,2},{2,3},{3,0},{4,5},{5,6},{6,7},{7,4},{8,9},{9,10},{10,1... | collective-permute-start | bytes 1572872 | tf_op jit(solution)/shard_map/ppermute | solution.py:52
  19.7 14.2 %collective-permute-start.5 = (f32[8,128,128]{2,1,0:T(8,128)S(1)}, f32[8,128,128]{2,1,0:T(8,128)S(1)}, u32[]{:S(2)}, u32[]{:S(2)}) collective-permute-start(f32[8,128,128]{2,1,0:T(8,128)S(1)} %pad_maximum_fusion.5.rest_1_), channel_id=1, source_target_pairs={{0,16},{1,17},{2,18},{3,19},{4,20},{5,21},{6,22},{7,23},{8,24},{9,... | collective-permute-start | bytes 1572872 | tf_op jit(solution)/shard_map/ppermute | solution.py:52
  21.7 24.7 %collective-permute-start.15 = (f32[8,128,128]{2,1,0:T(8,128)S(1)}, f32[8,128,128]{2,1,0:T(8,128)S(1)}, u32[]{:S(2)}, u32[]{:S(2)}) collective-permute-start(f32[8,128,128]{2,1,0:T(8,128)S(1)} %pad_maximum_fusion.4.rest_0_), channel_id=1, source_target_pairs={{0,1},{1,2},{2,3},{3,0},{4,5},{5,6},{6,7},{7,4},{8,9},{9,10},{10,1... | collective-permute-start | bytes 1572872 | tf_op jit(solution)/shard_map/ppermute | solution.py:52
  22.4 24.0 %collective-permute-start.14 = (f32[8,128,128]{2,1,0:T(8,128)S(1)}, f32[8,128,128]{2,1,0:T(8,128)S(1)}, u32[]{:S(2)}, u32[]{:S(2)}) collective-permute-start(f32[8,128,128]{2,1,0:T(8,128)S(1)} %pad_maximum_fusion.5.rest_1_), channel_id=1, source_target_pairs={{0,3},{1,0},{2,1},{3,2},{4,7},{5,4},{6,5},{7,6},{8,11},{9,8},{10,9... | collective-permute-start | bytes 1572872 | tf_op jit(solution)/shard_map/ppermute | solution.py:52
  26.9 14.9 %collective-permute-start.6 = (f32[4,128,128]{2,1,0:T(8,128)S(1)}, f32[4,128,128]{2,1,0:T(8,128)S(1)}, u32[]{:S(2)}, u32[]{:S(2)}) collective-permute-start(f32[4,128,128]{2,1,0:T(8,128)S(1)} %collective-permute-done.3), channel_id=1, source_target_pairs={{0,12},{1,13},{2,14},{3,15},{4,0},{5,1},{6,2},{7,3},{8,4},{9,5},{1... | collective-permute-start | bytes 786440 | tf_op jit(solution)/shard_map/ppermute | solution.py:52
  30.1 11.7 %collective-permute-start.7 = (f32[8,128,128]{2,1,0:T(8,128)S(1)}, f32[8,128,128]{2,1,0:T(8,128)S(1)}, u32[]{:S(2)}, u32[]{:S(2)}) collective-permute-start(f32[8,128,128]{2,1,0:T(8,128)S(1)} %collective-permute-done.4.rest_2_), channel_id=1, source_target_pairs={{0,3},{1,0},{2,1},{3,2},{4,7},{5,4},{6,5},{7,6},{8,11},{9,8},{10,9... | collective-permute-start | bytes 1572872 | tf_op jit(solution)/shard_map/ppermute | solution.py:52
  33.9 10.4 %collective-permute-start.9 = (f32[8,128,128]{2,1,0:T(8,128)S(1)}, f32[8,128,128]{2,1,0:T(8,128)S(1)}, u32[]{:S(2)}, u32[]{:S(2)}) collective-permute-start(f32[8,128,128]{2,1,0:T(8,128)S(1)} %collective-permute-done.8.rest_5_), channel_id=1, source_target_pairs={{0,1},{1,2},{2,3},{3,0},{4,5},{5,6},{6,7},{7,4},{8,9},{9,10},{10,1... | collective-permute-start | bytes 1572872 | tf_op jit(solution)/shard_map/ppermute | solution.py:52
  44.3 11.0 %collective-permute-start.10 = (f32[8,128,128]{2,1,0:T(8,128)S(1)}, f32[8,128,128]{2,1,0:T(8,128)S(1)}, u32[]{:S(2)}, u32[]{:S(2)}) collective-permute-start(f32[8,128,128]{2,1,0:T(8,128)S(1)} %constant_dynamic-update-slice_fusion.rest_0_), channel_id=1, source_target_pairs={{0,3},{1,0},{2,1},{3,2},{4,7},{5,4},{6,5},{7,6},{8,11},{9,8},{10,9... | collective-permute-start | bytes 1572872 | tf_op jit(solution)/shard_map/ppermute | solution.py:52
  44.4 10.9 %collective-permute-start.12 = (f32[8,128,128]{2,1,0:T(8,128)S(1)}, f32[8,128,128]{2,1,0:T(8,128)S(1)}, u32[]{:S(2)}, u32[]{:S(2)}) collective-permute-start(f32[8,128,128]{2,1,0:T(8,128)S(1)} %collective-permute-done.5.rest_1_), channel_id=1, source_target_pairs={{0,1},{1,2},{2,3},{3,0},{4,5},{5,6},{6,7},{7,4},{8,9},{9,10},{10,1... | collective-permute-start | bytes 1572872 | tf_op jit(solution)/shard_map/ppermute | solution.py:52
  52.0 10.5 %collective-permute-start.17 = (f32[8,128,128]{2,1,0:T(8,128)S(1)}, f32[8,128,128]{2,1,0:T(8,128)S(1)}, u32[]{:S(2)}, u32[]{:S(2)}) collective-permute-start(f32[8,128,128]{2,1,0:T(8,128)S(1)} %constant_dynamic-update-slice_fusion.rest_0_), channel_id=1, source_target_pairs={{0,1},{1,2},{2,3},{3,0},{4,5},{5,6},{6,7},{7,4},{8,9},{9,10},{10,1... | collective-permute-start | bytes 1572872 | tf_op jit(solution)/shard_map/ppermute | solution.py:52
  55.3 12.3 %collective-permute-start.11 = (f32[8,128,128]{2,1,0:T(8,128)S(1)}, f32[8,128,128]{2,1,0:T(8,128)S(1)}, u32[]{:S(2)}, u32[]{:S(2)}) collective-permute-start(f32[8,128,128]{2,1,0:T(8,128)S(1)} %collective-permute-done.10.rest_2_), channel_id=1, source_target_pairs={{0,3},{1,0},{2,1},{3,2},{4,7},{5,4},{6,5},{7,6},{8,11},{9,8},{10,9... | collective-permute-start | bytes 1572872 | tf_op jit(solution)/shard_map/ppermute | solution.py:52
  55.4 12.7 %collective-permute-start.13 = (f32[8,128,128]{2,1,0:T(8,128)S(1)}, f32[8,128,128]{2,1,0:T(8,128)S(1)}, u32[]{:S(2)}, u32[]{:S(2)}) collective-permute-start(f32[8,128,128]{2,1,0:T(8,128)S(1)} %collective-permute-done.12.rest_5_), channel_id=1, source_target_pairs={{0,1},{1,2},{2,3},{3,0},{4,5},{5,6},{6,7},{7,4},{8,9},{9,10},{10,1... | collective-permute-start | bytes 1572872 | tf_op jit(solution)/shard_map/ppermute | solution.py:52
  72.0 13.7 %collective-permute-start.19 = (f32[4,128,128]{2,1,0:T(8,128)S(1)}, f32[4,128,128]{2,1,0:T(8,128)S(1)}, u32[]{:S(2)}, u32[]{:S(2)}) collective-permute-start(f32[4,128,128]{2,1,0:T(8,128)S(1)} %add.301), channel_id=1, source_target_pairs={{0,64},{1,65},{2,66},{3,67},{4,68},{5,69},{6,70},{7,71},{8,72},{9,... | collective-permute-start | bytes 786440 | tf_op jit(solution)/shard_map/ppermute | solution.py:52
  93.7 16.8 %collective-permute-start.24 = (f32[17,128,128]{2,1,0:T(8,128)S(1)}, f32[17,128,128]{2,1,0:T(8,128)S(1)}, u32[]{:S(2)}, u32[]{:S(2)}) collective-permute-start(f32[17,128,128]{2,1,0:T(8,128)S(1)} %get-tuple-element.81), channel_id=1, source_target_pairs={{0,1},{1,2},{2,3},{3,0},{4,5},{5,6},{6,7},{7,4},{8,9},{9,10},{10,1... | collective-permute-start | bytes 3342344 | tf_op jit(solution)/shard_map/ppermute | solution.py:52
  93.8 17.1 %collective-permute-start.26 = (f32[17,128,128]{2,1,0:T(8,128)S(1)}, f32[17,128,128]{2,1,0:T(8,128)S(1)}, u32[]{:S(2)}, u32[]{:S(2)}) collective-permute-start(f32[17,128,128]{2,1,0:T(8,128)S(1)} %get-tuple-element.83), channel_id=1, source_target_pairs={{0,3},{1,0},{2,1},{3,2},{4,7},{5,4},{6,5},{7,6},{8,11},{9,8},{10,9... | collective-permute-start | bytes 3342344 | tf_op jit(solution)/shard_map/ppermute | solution.py:52
  110.8 16.8 %collective-permute-start.28 = (f32[17,128,128]{2,1,0:T(8,128)S(1)}, f32[17,128,128]{2,1,0:T(8,128)S(1)}, u32[]{:S(2)}, u32[]{:S(2)}) collective-permute-start(f32[17,128,128]{2,1,0:T(8,128)S(1)} %get-tuple-element.107), channel_id=1, source_target_pairs={{0,1},{1,2},{2,3},{3,0},{4,5},{5,6},{6,7},{7,4},{8,9},{9,10},{10,1... | collective-permute-start | bytes 3342344 | tf_op jit(solution)/shard_map/ppermute | solution.py:52
  111.1 17.0 %collective-permute-start.29 = (f32[16,128,128]{2,1,0:T(8,128)S(1)}, f32[16,128,128]{2,1,0:T(8,128)S(1)}, u32[]{:S(2)}, u32[]{:S(2)}) collective-permute-start(f32[16,128,128]{2,1,0:T(8,128)S(1)} %get-tuple-element.105), channel_id=1, source_target_pairs={{0,3},{1,0},{2,1},{3,2},{4,7},{5,4},{6,5},{7,6},{8,11},{9,8},{10,9... | collective-permute-start | bytes 3145736 | tf_op jit(solution)/shard_map/ppermute | solution.py:52
  114.4 27.2 %collective-permute-start.25 = (f32[16,128,128]{2,1,0:T(8,128)S(1)}, f32[16,128,128]{2,1,0:T(8,128)S(1)}, u32[]{:S(2)}, u32[]{:S(2)}) collective-permute-start(f32[16,128,128]{2,1,0:T(8,128)S(1)} %get-tuple-element.102), channel_id=1, source_target_pairs={{0,1},{1,2},{2,3},{3,0},{4,5},{5,6},{6,7},{7,4},{8,9},{9,10},{10,1... | collective-permute-start | bytes 3145736 | tf_op jit(solution)/shard_map/ppermute | solution.py:52
  114.4 27.2 %collective-permute-start.27 = (f32[16,128,128]{2,1,0:T(8,128)S(1)}, f32[16,128,128]{2,1,0:T(8,128)S(1)}, u32[]{:S(2)}, u32[]{:S(2)}) collective-permute-start(f32[16,128,128]{2,1,0:T(8,128)S(1)} %get-tuple-element.104), channel_id=1, source_target_pairs={{0,3},{1,0},{2,1},{3,2},{4,7},{5,4},{6,5},{7,6},{8,11},{9,8},{10,9... | collective-permute-start | bytes 3145736 | tf_op jit(solution)/shard_map/ppermute | solution.py:52
  128.5 15.1 %collective-permute-start.31 = (f32[9,128,128]{2,1,0:T(8,128)S(1)}, f32[9,128,128]{2,1,0:T(8,128)S(1)}, u32[]{:S(2)}, u32[]{:S(2)}) collective-permute-start(f32[9,128,128]{2,1,0:T(8,128)S(1)} %pad_maximum_fusion), channel_id=1, source_target_pairs={{0,16},{1,17},{2,18},{3,19},{4,20},{5,21},{6,22},{7,23},{8,24},{9,... | collective-permute-start | bytes 1769480 | tf_op jit(solution)/shard_map/ppermute | solution.py:52
  128.6 13.3 %collective-permute-start.30 = (f32[4,128,128]{2,1,0:T(8,128)S(1)}, f32[4,128,128]{2,1,0:T(8,128)S(1)}, u32[]{:S(2)}, u32[]{:S(2)}) collective-permute-start(f32[4,128,128]{2,1,0:T(8,128)S(1)} %get-tuple-element.111), channel_id=1, source_target_pairs={{0,8},{1,9},{2,10},{3,11},{4,12},{5,13},{6,14},{7,15},{8,0},{9,1},... | collective-permute-start | bytes 786440 | tf_op jit(solution)/shard_map/ppermute | solution.py:52
  143.8 12.1 %collective-permute-start.33 = (f32[5,128,128]{2,1,0:T(8,128)S(1)}, f32[5,128,128]{2,1,0:T(8,128)S(1)}, u32[]{:S(2)}, u32[]{:S(2)}) collective-permute-start(f32[5,128,128]{2,1,0:T(8,128)S(1)} %get-tuple-element.114), channel_id=1, source_target_pairs={{0,4},{1,5},{2,6},{3,7},{4,8},{5,9},{6,10},{7,11},{8,12},{9,13},{1... | collective-permute-start | bytes 983048 | tf_op jit(solution)/shard_map/ppermute | solution.py:52
  143.9 12.0 %collective-permute-start.34 = (f32[5,128,128]{2,1,0:T(8,128)S(1)}, f32[5,128,128]{2,1,0:T(8,128)S(1)}, u32[]{:S(2)}, u32[]{:S(2)}) collective-permute-start(f32[5,128,128]{2,1,0:T(8,128)S(1)} %get-tuple-element.115), channel_id=1, source_target_pairs={{0,8},{1,9},{2,10},{3,11},{4,12},{5,13},{6,14},{7,15},{8,0},{9,1},... | collective-permute-start | bytes 983048 | tf_op jit(solution)/shard_map/ppermute | solution.py:52
  (19 other events, 140.2 us)

commit v13 on v11

--- a/solution.py
+++ b/solution.py
@@ -507,19 +507,17 @@
     own_three = permute(add_part(own_three, down[:HALF], HALF), v_down)
     weight_term = ring_sum(1, plan[0], (weight_term, down[PER], one[PER], up[PER]))
     apart = zero + one[:PER] + three
-    apart_two = permute(apart[8:12], u_far)
-    apart_far = permute(
-        jnp.concatenate([apart[4:8], apart[12:16], weight_term[None]], axis=0), y_far
-    )
-    last, apart_far = tie(apart[:4] + apart_two, apart_far)
-    last = permute(last, y_far)
-    weight_term = weight_term + apart_far[8]
+    apart_one = permute(with_tile(apart[4:8], weight_term), u_up)
+    apart_two = permute(with_tile(apart[8:12], weight_term), u_far)
+    apart_three = permute(with_tile(apart[12:16], weight_term), u_down)
+    weight_term = ring_sum(0, plan[0], (weight_term, apart_three[4], apart_two[4], apart_one[4]))
+    last = apart[:4] + apart_one[:4] + apart_two[:4] + apart_three[:4]
+    last = permute(with_tile(last, weight_term), y_far)
     total = own + own_one + own_three
-    two = permute(with_tile(total[8:12], weight_term), u_far)
-    one = permute(with_tile(total[4:8] + apart_far[:4], weight_term), u_up)
-    three = permute(with_tile(total[12:16] + apart_far[4:8], weight_term), u_down)
-    weight_term = ring_sum(0, plan[0], (weight_term, three[4], two[4], one[4]))
-    return total[:4] + last + one[:4] + two[:4] + three[:4], weight_term
+    one = permute(total[4:8], u_up)
+    two = permute(total[8:12], u_far)
+    three = permute(total[12:16], u_down)
+    return total[:4] + last[:4] + one + two + three, weight_term + last[4]
 
 
 def per_device(features, weight, cotangent, tiles, tile_rows, tile_cols, counts):
@@ -556,12 +554,15 @@
 
     bounds = plan[0]
     kept = [kept[0] + permute(given_first, core_swap), kept[1] + permute(given_second, core_swap)]
-    kept = [value + permute(value, y_pair) for value in kept]
+    received = [permute(value, y_pair) for value in kept]
+    first = kept[0] + received[0]
     early = middle_part(
-        0, bounds, across, weight, cotangent, kept[0], permute(kept[0], core_swap), pairs
-    )
+        0, bounds, across, weight, cotangent, first, permute(first, core_swap), pairs
+    )
+    received, *early = tie(received[1], *early)
+    second = kept[1] + received
     activated, spread, weight_term = middle_part(
-        1, bounds, across, weight, cotangent, kept[1], permute(kept[1], core_swap), pairs, early
+        1, bounds, across, weight, cotangent, second, permute(second, core_swap), pairs, early
     )
     total, weight_term = scatter_terms(plan, pairs, spread, weight_term)
     far_total = permute(total, y_pair)

time: 168 us -> 181 us (1.077)
  waiting for transfers between devices: 82.5 us -> 92.8 us
  starting transfers between devices: 56.6 us -> 59.8 us
    ppermute x39 -> x40, waiting for transfers between devices: 82.5 us -> 92.8 us  [permute(): return lax.ppermute(value, AXES, pairs)]
    ppermute x39 -> x40, starting transfers between devices: 56.6 us -> 59.8 us  [permute(): return lax.ppermute(value, AXES, pairs)]
  transfers between devices with their start and end apart: 39 -> 40, of which waited for: 21 -> 24; matrix products, arithmetic and copies ran while one was open for 1% -> 1% of each run, Pallas kernels for 8% -> 7%
where the time goes in v13:
time: 181 us; the launch traced here: 179 us
  waiting for transfers between devices  92.8 us (51%)
  starting transfers between devices  59.8 us (33%)
  Pallas kernels  20.8 us (11%)
  other arithmetic  2 us (1%)
  local copies, waits for them, and re-layouts  1.88 us (1%)
    ppermute x40, waiting for transfers between devices, permute(): return lax.ppermute(value, AXES, pairs)  92.8 us
    ppermute x40, starting transfers between devices, permute(): return lax.ppermute(value, AXES, pairs)  59.8 us
    pallas_call x3, Pallas kernels, forward_part(): pl.pallas_call(functools.partial(forward_kernel, which), name='forward_ti...  6.38 us
    pallas_call x2, Pallas kernels, middle_part(): pl.pallas_call(functools.partial(middle_kernel, which), name='middle_%d'...  4.51 us
    pallas_call x2, Pallas kernels, backward_part(): pl.pallas_call(functools.partial(backward_kernel, which), name='backward_...  4.48 us
  transfers between devices with their start and end apart: 40, of which 24 were waited for; matrix products, arithmetic and copies ran while one was open for 1% of the time, Pallas kernels for 7%

profile of v13, /device:TPU:0, one launch (start us, length us, event | category | flops | bytes accessed | tf_op | source)
XLA Modules:
  0.0 178.9 jit_solution(7689626504918005372)
XLA Ops:
  3.9 2.7 %collective-permute-start.1 = (f32[4,128,128]{2,1,0:T(8,128)S(1)}, f32[4,128,128]{2,1,0:T(8,128)S(1)}, u32[]{:S(2)}, u32[]{:S(2)}) collective-permute-start(f32[4,128,128]{2,1,0:T(8,128)S(1)} %get-tuple-element.115), channel_id=1, source_target_pairs={{0,8},{1,9},{2,10},{3,11},{4,12},{5,13},{6,14},{7,15},{8,0},{9,1},... | collective-permute-start | bytes 786440 | tf_op jit(solution)/shard_map/ppermute | solution.py:52
  8.1 3.0 %collective-permute-start.3 = (f32[4,128,128]{2,1,0:T(8,128)S(1)}, f32[4,128,128]{2,1,0:T(8,128)S(1)}, u32[]{:S(2)}, u32[]{:S(2)}) collective-permute-start(f32[4,128,128]{2,1,0:T(8,128)S(1)} %get-tuple-element.114), channel_id=1, source_target_pairs={{0,80},{1,81},{2,82},{3,83},{4,84},{5,85},{6,86},{7,87},{8,88},{9,... | collective-permute-start | bytes 786440 | tf_op jit(solution)/shard_map/ppermute | solution.py:52
  13.9 3.6 %collective-permute-done.3 = f32[4,128,128]{2,1,0:T(8,128)S(1)} collective-permute-done((f32[4,128,128]{2,1,0:T(8,128)S(1)}, f32[4,128,128]{2,1,0:T(8,128)S(1)}, u32[]{:S(2)}, u32[]{:S(2)}) %collective-permute-start.3) | collective-permute-done | bytes 262176 | tf_op jit(solution)/shard_map/ppermute | solution.py:52
  23.8 5.6 %collective-permute-done.4.rest_2_ = f32[8,128,128]{2,1,0:T(8,128)S(1)} collective-permute-done((f32[8,128,128]{2,1,0:T(8,128)S(1)}, f32[8,128,128]{2,1,0:T(8,128)S(1)}, u32[]{:S(2)}, u32[]{:S(2)}) %collective-permute-start.4) | collective-permute-done | bytes 524320 | tf_op jit(solution)/shard_map/ppermute | solution.py:52
  31.3 3.0 %collective-permute-start.7 = (f32[8,128,128]{2,1,0:T(8,128)S(1)}, f32[8,128,128]{2,1,0:T(8,128)S(1)}, u32[]{:S(2)}, u32[]{:S(2)}) collective-permute-start(f32[8,128,128]{2,1,0:T(8,128)S(1)} %collective-permute-done.4.rest_2_), channel_id=1, source_target_pairs={{0,3},{1,0},{2,1},{3,2},{4,7},{5,4},{6,5},{7,6},{8,11},{9,8},{10,9... | collective-permute-start | bytes 1572872 | tf_op jit(solution)/shard_map/ppermute | solution.py:52
  34.3 2.6 %pair_tiles.1.tiles_ref.rest_2_ = bf16[256,128,256]{2,1,0:T(8,128)(2,1)S(1)} custom-call(s32[1]{0:T(128)} %bitcast.34.count_ref, f32[256,128,128]{2,1,0:T(8,128)} %bitcast.41), custom_call_target="tpu_custom_call" | custom-call | flops 8800000000 | bytes 1048576 | tf_op jit(solution)/shard_map/pair_tiles/pallas_call | solution.py:123
  37.0 5.8 %collective-permute-done.5.rest_1_ = f32[8,128,128]{2,1,0:T(8,128)S(1)} collective-permute-done((f32[8,128,128]{2,1,0:T(8,128)S(1)}, f32[8,128,128]{2,1,0:T(8,128)S(1)}, u32[]{:S(2)}, u32[]{:S(2)}) %collective-permute-start.5) | collective-permute-done | bytes 524320 | tf_op jit(solution)/shard_map/ppermute | solution.py:52
  46.9 2.8 %forward_tiles_0.1.rest_6_ = f32[16,128,128]{2,1,0:T(8,128)S(1)} custom-call(s32[9]{0:T(128)S(1)} %compare_select_fusion.10.bounds_ref, s32[256]{0:T(256)S(1)} %get-tuple-element.50.order_ref, s32[256]{0:T(256)S(1)} %get-tuple-element.51.rows_ref, s32[256]{0:T(256)S(1)} %get-tuple-element.52.slots_ref, ...), custom_call_target="tpu_custom_call" | custom-call | flops 6600000000 | bytes 1048576 | tf_op jit(solution)/shard_map/forward_tiles_0/pallas_call | solution.py:263
  49.8 3.2 %collective-permute-start.16 = (f32[8,128,128]{2,1,0:T(8,128)S(1)}, f32[8,128,128]{2,1,0:T(8,128)S(1)}, u32[]{:S(2)}, u32[]{:S(2)}) collective-permute-start(f32[8,128,128]{2,1,0:T(8,128)S(1)} %collective-permute-done.5.rest_1_), channel_id=1, source_target_pairs={{0,3},{1,0},{2,1},{3,2},{4,7},{5,4},{6,5},{7,6},{8,11},{9,8},{10,9... | collective-permute-start | bytes 1572872 | tf_op jit(solution)/shard_map/ppermute | solution.py:52
  56.0 4.9 %collective-permute-done.17.rest_4_ = f32[8,128,128]{2,1,0:T(8,128)S(1)} collective-permute-done((f32[8,128,128]{2,1,0:T(8,128)S(1)}, f32[8,128,128]{2,1,0:T(8,128)S(1)}, u32[]{:S(2)}, u32[]{:S(2)}) %collective-permute-start.17) | collective-permute-done | bytes 524320 | tf_op jit(solution)/shard_map/ppermute | solution.py:52
  71.1 6.9 %collective-permute-done.21 = f32[4,128,128]{2,1,0:T(8,128)S(1)} collective-permute-done((f32[4,128,128]{2,1,0:T(8,128)S(1)}, f32[4,128,128]{2,1,0:T(8,128)S(1)}, u32[]{:S(2)}, u32[]{:S(2)}) %collective-permute-start.21) | collective-permute-done | bytes 262176 | tf_op jit(solution)/shard_map/ppermute | solution.py:52
  81.7 5.4 %collective-permute-done.19 = f32[4,128,128]{2,1,0:T(8,128)S(1)} collective-permute-done((f32[4,128,128]{2,1,0:T(8,128)S(1)}, f32[4,128,128]{2,1,0:T(8,128)S(1)}, u32[]{:S(2)}, u32[]{:S(2)}) %collective-permute-start.19) | collective-permute-done | bytes 262176 | tf_op jit(solution)/shard_map/ppermute | solution.py:52
  88.8 2.7 %middle_1.1 = (f32[128,2048]{1,0:T(8,128)}, bf16[16,128,256]{2,1,0:T(8,128)(2,1)S(1)}, f32[128,128]{1,0:T(8,128)S(1)}) custom-call(s32[9]{0:T(128)S(1)} %compare_select_fusion.10.bounds_ref, f32[128,128]{1,0:T(8,128)S(1)} %bitcast.37, f32[128,128]{1,0:T(8,128)S(1)} %copy-done.1, f32[128,2048]{1,0:T(8,128)S(1)} %copy-done, f32[4,128,128]{2,1,0:T(8,128)S(1)} %add.304.rest_0_, ...), custom_call_target="tpu_custom_call" | custom-call | flops 2200000000 | bytes 1048576 | tf_op jit(solution)/shard_map/middle_1/pallas_call | solution.py:364
  96.4 2.9 %backward_tiles_1.1 = (f32[16,128,128]{2,1,0:T(8,128)S(1)}, f32[17,128,128]{2,1,0:T(8,128)S(1)}, f32[16,128,128]{2,1,0:T(8,128)S(1)}, f32[16,128,128]{2,1,0:T(8,...) custom-call(s32[9]{0:T(128)S(1)} %compare_select_fusion.10.bounds_ref, ...), custom_call_target="tpu_custom_call" | custom-call | flops 8800000000 | bytes 1048576 | tf_op jit(solution)/shard_map/backward_tiles_1/pallas_call | solution.py:280
  99.3 10.6 %collective-permute-done.24 = f32[17,128,128]{2,1,0:T(8,128)S(1)} collective-permute-done((f32[17,128,128]{2,1,0:T(8,128)S(1)}, f32[17,128,128]{2,1,0:T(8,128)S(1)}, u32[]{:S(2)}, u32[]{:S(2)}) %collective-permute-start.24) | collective-permute-done | bytes 1114144 | tf_op jit(solution)/shard_map/ppermute | solution.py:52
  111.0 2.7 %collective-permute-start.29 = (f32[16,128,128]{2,1,0:T(8,128)S(1)}, f32[16,128,128]{2,1,0:T(8,128)S(1)}, u32[]{:S(2)}, u32[]{:S(2)}) collective-permute-start(f32[16,128,128]{2,1,0:T(8,128)S(1)} %get-tuple-element.102), channel_id=1, source_target_pairs={{0,3},{1,0},{2,1},{3,2},{4,7},{5,4},{6,5},{7,6},{8,11},{9,8},{10,9... | collective-permute-start | bytes 3145736 | tf_op jit(solution)/shard_map/ppermute | solution.py:52
  113.7 3.2 %collective-permute-start.27 = (f32[16,128,128]{2,1,0:T(8,128)S(1)}, f32[16,128,128]{2,1,0:T(8,128)S(1)}, u32[]{:S(2)}, u32[]{:S(2)}) collective-permute-start(f32[16,128,128]{2,1,0:T(8,128)S(1)} %get-tuple-element.103), channel_id=1, source_target_pairs={{0,3},{1,0},{2,1},{3,2},{4,7},{5,4},{6,5},{7,6},{8,11},{9,8},{10,9... | collective-permute-start | bytes 3145736 | tf_op jit(solution)/shard_map/ppermute | solution.py:52
  117.0 9.9 %collective-permute-done.28 = f32[17,128,128]{2,1,0:T(8,128)S(1)} collective-permute-done((f32[17,128,128]{2,1,0:T(8,128)S(1)}, f32[17,128,128]{2,1,0:T(8,128)S(1)}, u32[]{:S(2)}, u32[]{:S(2)}) %collective-permute-start.28) | collective-permute-done | bytes 1114144 | tf_op jit(solution)/shard_map/ppermute | solution.py:52
  127.8 3.8 %collective-permute-start.30 = (f32[5,128,128]{2,1,0:T(8,128)S(1)}, f32[5,128,128]{2,1,0:T(8,128)S(1)}, u32[]{:S(2)}, u32[]{:S(2)}) collective-permute-start(f32[5,128,128]{2,1,0:T(8,128)S(1)} %get-tuple-element.116), channel_id=1, source_target_pairs={{0,4},{1,5},{2,6},{3,7},{4,8},{5,9},{6,10},{7,11},{8,12},{9,13},{1... | collective-permute-start | bytes 983048 | tf_op jit(solution)/shard_map/ppermute | solution.py:52
  133.4 11.8 %collective-permute-done.25 = f32[16,128,128]{2,1,0:T(8,128)S(1)} collective-permute-done((f32[16,128,128]{2,1,0:T(8,128)S(1)}, f32[16,128,128]{2,1,0:T(8,128)S(1)}, u32[]{:S(2)}, u32[]{:S(2)}) %collective-permute-start.25) | collective-permute-done | bytes 1048608 | tf_op jit(solution)/shard_map/ppermute | solution.py:52
  145.4 4.1 %collective-permute-start.32 = (f32[5,128,128]{2,1,0:T(8,128)S(1)}, f32[5,128,128]{2,1,0:T(8,128)S(1)}, u32[]{:S(2)}, u32[]{:S(2)}) collective-permute-start(f32[5,128,128]{2,1,0:T(8,128)S(1)} %get-tuple-element.118), channel_id=1, source_target_pairs={{0,12},{1,13},{2,14},{3,15},{4,0},{5,1},{6,2},{7,3},{8,4},{9,5},{1... | collective-permute-start | bytes 983048 | tf_op jit(solution)/shard_map/ppermute | solution.py:52
  149.5 4.7 %collective-permute-done.32 = f32[5,128,128]{2,1,0:T(8,128)S(1)} collective-permute-done((f32[5,128,128]{2,1,0:T(8,128)S(1)}, f32[5,128,128]{2,1,0:T(8,128)S(1)}, u32[]{:S(2)}, u32[]{:S(2)}) %collective-permute-start.32) | collective-permute-done | bytes 327712 | tf_op jit(solution)/shard_map/ppermute | solution.py:52
  165.0 2.5 %collective-permute-done.36 = f32[4,128,128]{2,1,0:T(8,128)S(1)} collective-permute-done((f32[4,128,128]{2,1,0:T(8,128)S(1)}, f32[4,128,128]{2,1,0:T(8,128)S(1)}, u32[]{:S(2)}, u32[]{:S(2)}) %collective-permute-start.36) | collective-permute-done | bytes 262176 | tf_op jit(solution)/shard_map/ppermute | solution.py:52
  171.2 4.6 %collective-permute-done.38.across_ref = f32[4,128,128]{2,1,0:T(8,128)S(1)} collective-permute-done((f32[4,128,128]{2,1,0:T(8,128)S(1)}, f32[4,128,128]{2,1,0:T(8,128)S(1)}, u32[]{:S(2)}, u32[]{:S(2)}) %collective-permute-start.38) | collective-permute-done | bytes 262176 | tf_op jit(solution)/shard_map/ppermute | solution.py:52
  (110 shorter events, 64.2 us)
Async XLA Ops:
  2.3 11.4 %collective-permute-start.2 = (f32[4,128,128]{2,1,0:T(8,128)S(1)}, f32[4,128,128]{2,1,0:T(8,128)S(1)}, u32[]{:S(2)}, u32[]{:S(2)}) collective-permute-start(f32[4,128,128]{2,1,0:T(8,128)S(1)} %get-tuple-element.115), channel_id=1, source_target_pairs={{0,4},{1,5},{2,6},{3,7},{4,8},{5,9},{6,10},{7,11},{8,12},{9,13},{1... | collective-permute-start | bytes 786440 | tf_op jit(solution)/shard_map/ppermute | solution.py:52
  3.9 9.9 %collective-permute-start.1 = (f32[4,128,128]{2,1,0:T(8,128)S(1)}, f32[4,128,128]{2,1,0:T(8,128)S(1)}, u32[]{:S(2)}, u32[]{:S(2)}) collective-permute-start(f32[4,128,128]{2,1,0:T(8,128)S(1)} %get-tuple-element.115), channel_id=1, source_target_pairs={{0,8},{1,9},{2,10},{3,11},{4,12},{5,13},{6,14},{7,15},{8,0},{9,1},... | collective-permute-start | bytes 786440 | tf_op jit(solution)/shard_map/ppermute | solution.py:52
  17.4 12.0 %collective-permute-start.4 = (f32[8,128,128]{2,1,0:T(8,128)S(1)}, f32[8,128,128]{2,1,0:T(8,128)S(1)}, u32[]{:S(2)}, u32[]{:S(2)}) collective-permute-start(f32[8,128,128]{2,1,0:T(8,128)S(1)} %pad_maximum_fusion.3.rest_0_), channel_id=1, source_target_pairs={{0,3},{1,0},{2,1},{3,2},{4,7},{5,4},{6,5},{7,6},{8,11},{9,8},{10,9... | collective-permute-start | bytes 1572872 | tf_op jit(solution)/shard_map/ppermute | solution.py:52
  19.7 14.6 %collective-permute-start.8 = (f32[8,128,128]{2,1,0:T(8,128)S(1)}, f32[8,128,128]{2,1,0:T(8,128)S(1)}, u32[]{:S(2)}, u32[]{:S(2)}) collective-permute-start(f32[8,128,128]{2,1,0:T(8,128)S(1)} %pad_maximum_fusion.4.rest_1_), channel_id=1, source_target_pairs={{0,1},{1,2},{2,3},{3,0},{4,5},{5,6},{6,7},{7,4},{8,9},{9,10},{10,1... | collective-permute-start | bytes 1572872 | tf_op jit(solution)/shard_map/ppermute | solution.py:52
  19.7 11.6 %collective-permute-start.6 = (f32[4,128,128]{2,1,0:T(8,128)S(1)}, f32[4,128,128]{2,1,0:T(8,128)S(1)}, u32[]{:S(2)}, u32[]{:S(2)}) collective-permute-start(f32[4,128,128]{2,1,0:T(8,128)S(1)} %collective-permute-done.3), channel_id=1, source_target_pairs={{0,12},{1,13},{2,14},{3,15},{4,0},{5,1},{6,2},{7,3},{8,4},{9,5},{1... | collective-permute-start | bytes 786440 | tf_op jit(solution)/shard_map/ppermute | solution.py:52
  20.6 26.3 %collective-permute-start.15 = (f32[8,128,128]{2,1,0:T(8,128)S(1)}, f32[8,128,128]{2,1,0:T(8,128)S(1)}, u32[]{:S(2)}, u32[]{:S(2)}) collective-permute-start(f32[8,128,128]{2,1,0:T(8,128)S(1)} %pad_maximum_fusion.3.rest_0_), channel_id=1, source_target_pairs={{0,1},{1,2},{2,3},{3,0},{4,5},{5,6},{6,7},{7,4},{8,9},{9,10},{10,1... | collective-permute-start | bytes 1572872 | tf_op jit(solution)/shard_map/ppermute | solution.py:52
  21.7 25.2 %collective-permute-start.14 = (f32[8,128,128]{2,1,0:T(8,128)S(1)}, f32[8,128,128]{2,1,0:T(8,128)S(1)}, u32[]{:S(2)}, u32[]{:S(2)}) collective-permute-start(f32[8,128,128]{2,1,0:T(8,128)S(1)} %pad_maximum_fusion.4.rest_1_), channel_id=1, source_target_pairs={{0,3},{1,0},{2,1},{3,2},{4,7},{5,4},{6,5},{7,6},{8,11},{9,8},{10,9... | collective-permute-start | bytes 1572872 | tf_op jit(solution)/shard_map/ppermute | solution.py:52
  29.4 13.4 %collective-permute-start.5 = (f32[8,128,128]{2,1,0:T(8,128)S(1)}, f32[8,128,128]{2,1,0:T(8,128)S(1)}, u32[]{:S(2)}, u32[]{:S(2)}) collective-permute-start(f32[8,128,128]{2,1,0:T(8,128)S(1)} %pad_maximum_fusion.4.rest_1_), channel_id=1, source_target_pairs={{0,16},{1,17},{2,18},{3,19},{4,20},{5,21},{6,22},{7,23},{8,24},{9,... | collective-permute-start | bytes 1572872 | tf_op jit(solution)/shard_map/ppermute | solution.py:52
  31.3 11.4 %collective-permute-start.7 = (f32[8,128,128]{2,1,0:T(8,128)S(1)}, f32[8,128,128]{2,1,0:T(8,128)S(1)}, u32[]{:S(2)}, u32[]{:S(2)}) collective-permute-start(f32[8,128,128]{2,1,0:T(8,128)S(1)} %collective-permute-done.4.rest_2_), channel_id=1, source_target_pairs={{0,3},{1,0},{2,1},{3,2},{4,7},{5,4},{6,5},{7,6},{8,11},{9,8},{10,9... | collective-permute-start | bytes 1572872 | tf_op jit(solution)/shard_map/ppermute | solution.py:52
  34.3 10.4 %collective-permute-start.9 = (f32[8,128,128]{2,1,0:T(8,128)S(1)}, f32[8,128,128]{2,1,0:T(8,128)S(1)}, u32[]{:S(2)}, u32[]{:S(2)}) collective-permute-start(f32[8,128,128]{2,1,0:T(8,128)S(1)} %collective-permute-done.8.rest_5_), channel_id=1, source_target_pairs={{0,1},{1,2},{2,3},{3,0},{4,5},{5,6},{6,7},{7,4},{8,9},{9,10},{10,1... | collective-permute-start | bytes 1572872 | tf_op jit(solution)/shard_map/ppermute | solution.py:52
  44.8 10.5 %collective-permute-start.12 = (f32[8,128,128]{2,1,0:T(8,128)S(1)}, f32[8,128,128]{2,1,0:T(8,128)S(1)}, u32[]{:S(2)}, u32[]{:S(2)}) collective-permute-start(f32[8,128,128]{2,1,0:T(8,128)S(1)} %collective-permute-done.5.rest_1_), channel_id=1, source_target_pairs={{0,1},{1,2},{2,3},{3,0},{4,5},{5,6},{6,7},{7,4},{8,9},{9,10},{10,1... | collective-permute-start | bytes 1572872 | tf_op jit(solution)/shard_map/ppermute | solution.py:52
  49.7 11.2 %collective-permute-start.17 = (f32[8,128,128]{2,1,0:T(8,128)S(1)}, f32[8,128,128]{2,1,0:T(8,128)S(1)}, u32[]{:S(2)}, u32[]{:S(2)}) collective-permute-start(f32[8,128,128]{2,1,0:T(8,128)S(1)} %constant_dynamic-update-slice_fusion.rest_0_), channel_id=1, source_target_pairs={{0,1},{1,2},{2,3},{3,0},{4,5},{5,6},{6,7},{7,4},{8,9},{9,10},{10,1... | collective-permute-start | bytes 1572872 | tf_op jit(solution)/shard_map/ppermute | solution.py:52
  49.8 11.1 %collective-permute-start.16 = (f32[8,128,128]{2,1,0:T(8,128)S(1)}, f32[8,128,128]{2,1,0:T(8,128)S(1)}, u32[]{:S(2)}, u32[]{:S(2)}) collective-permute-start(f32[8,128,128]{2,1,0:T(8,128)S(1)} %collective-permute-done.5.rest_1_), channel_id=1, source_target_pairs={{0,3},{1,0},{2,1},{3,2},{4,7},{5,4},{6,5},{7,6},{8,11},{9,8},{10,9... | collective-permute-start | bytes 1572872 | tf_op jit(solution)/shard_map/ppermute | solution.py:52
  54.0 11.3 %collective-permute-start.11 = (f32[8,128,128]{2,1,0:T(8,128)S(1)}, f32[8,128,128]{2,1,0:T(8,128)S(1)}, u32[]{:S(2)}, u32[]{:S(2)}) collective-permute-start(f32[8,128,128]{2,1,0:T(8,128)S(1)} %collective-permute-done.10.rest_2_), channel_id=1, source_target_pairs={{0,3},{1,0},{2,1},{3,2},{4,7},{5,4},{6,5},{7,6},{8,11},{9,8},{10,9... | collective-permute-start | bytes 1572872 | tf_op jit(solution)/shard_map/ppermute | solution.py:52
  55.3 11.2 %collective-permute-start.13 = (f32[8,128,128]{2,1,0:T(8,128)S(1)}, f32[8,128,128]{2,1,0:T(8,128)S(1)}, u32[]{:S(2)}, u32[]{:S(2)}) collective-permute-start(f32[8,128,128]{2,1,0:T(8,128)S(1)} %collective-permute-done.12.rest_5_), channel_id=1, source_target_pairs={{0,1},{1,2},{2,3},{3,0},{4,5},{5,6},{6,7},{7,4},{8,9},{9,10},{10,1... | collective-permute-start | bytes 1572872 | tf_op jit(solution)/shard_map/ppermute | solution.py:52
  93.0 16.8 %collective-permute-start.24 = (f32[17,128,128]{2,1,0:T(8,128)S(1)}, f32[17,128,128]{2,1,0:T(8,128)S(1)}, u32[]{:S(2)}, u32[]{:S(2)}) collective-permute-start(f32[17,128,128]{2,1,0:T(8,128)S(1)} %get-tuple-element.85), channel_id=1, source_target_pairs={{0,1},{1,2},{2,3},{3,0},{4,5},{5,6},{6,7},{7,4},{8,9},{9,10},{10,1... | collective-permute-start | bytes 3342344 | tf_op jit(solution)/shard_map/ppermute | solution.py:52
  94.9 15.8 %collective-permute-start.26 = (f32[17,128,128]{2,1,0:T(8,128)S(1)}, f32[17,128,128]{2,1,0:T(8,128)S(1)}, u32[]{:S(2)}, u32[]{:S(2)}) collective-permute-start(f32[17,128,128]{2,1,0:T(8,128)S(1)} %get-tuple-element.87), channel_id=1, source_target_pairs={{0,3},{1,0},{2,1},{3,2},{4,7},{5,4},{6,5},{7,6},{8,11},{9,8},{10,9... | collective-permute-start | bytes 3342344 | tf_op jit(solution)/shard_map/ppermute | solution.py:52
  110.1 16.8 %collective-permute-start.28 = (f32[17,128,128]{2,1,0:T(8,128)S(1)}, f32[17,128,128]{2,1,0:T(8,128)S(1)}, u32[]{:S(2)}, u32[]{:S(2)}) collective-permute-start(f32[17,128,128]{2,1,0:T(8,128)S(1)} %get-tuple-element.105), channel_id=1, source_target_pairs={{0,1},{1,2},{2,3},{3,0},{4,5},{5,6},{6,7},{7,4},{8,9},{9,10},{10,1... | collective-permute-start | bytes 3342344 | tf_op jit(solution)/shard_map/ppermute | solution.py:52
  111.0 16.5 %collective-permute-start.29 = (f32[16,128,128]{2,1,0:T(8,128)S(1)}, f32[16,128,128]{2,1,0:T(8,128)S(1)}, u32[]{:S(2)}, u32[]{:S(2)}) collective-permute-start(f32[16,128,128]{2,1,0:T(8,128)S(1)} %get-tuple-element.102), channel_id=1, source_target_pairs={{0,3},{1,0},{2,1},{3,2},{4,7},{5,4},{6,5},{7,6},{8,11},{9,8},{10,9... | collective-permute-start | bytes 3145736 | tf_op jit(solution)/shard_map/ppermute | solution.py:52
  113.7 31.4 %collective-permute-start.25 = (f32[16,128,128]{2,1,0:T(8,128)S(1)}, f32[16,128,128]{2,1,0:T(8,128)S(1)}, u32[]{:S(2)}, u32[]{:S(2)}) collective-permute-start(f32[16,128,128]{2,1,0:T(8,128)S(1)} %get-tuple-element.107), channel_id=1, source_target_pairs={{0,1},{1,2},{2,3},{3,0},{4,5},{5,6},{6,7},{7,4},{8,9},{9,10},{10,1... | collective-permute-start | bytes 3145736 | tf_op jit(solution)/shard_map/ppermute | solution.py:52
  113.7 31.4 %collective-permute-start.27 = (f32[16,128,128]{2,1,0:T(8,128)S(1)}, f32[16,128,128]{2,1,0:T(8,128)S(1)}, u32[]{:S(2)}, u32[]{:S(2)}) collective-permute-start(f32[16,128,128]{2,1,0:T(8,128)S(1)} %get-tuple-element.103), channel_id=1, source_target_pairs={{0,3},{1,0},{2,1},{3,2},{4,7},{5,4},{6,5},{7,6},{8,11},{9,8},{10,9... | collective-permute-start | bytes 3145736 | tf_op jit(solution)/shard_map/ppermute | solution.py:52
  127.8 21.6 %collective-permute-start.30 = (f32[5,128,128]{2,1,0:T(8,128)S(1)}, f32[5,128,128]{2,1,0:T(8,128)S(1)}, u32[]{:S(2)}, u32[]{:S(2)}) collective-permute-start(f32[5,128,128]{2,1,0:T(8,128)S(1)} %get-tuple-element.116), channel_id=1, source_target_pairs={{0,4},{1,5},{2,6},{3,7},{4,8},{5,9},{6,10},{7,11},{8,12},{9,13},{1... | collective-permute-start | bytes 983048 | tf_op jit(solution)/shard_map/ppermute | solution.py:52
  131.6 17.8 %collective-permute-start.31 = (f32[5,128,128]{2,1,0:T(8,128)S(1)}, f32[5,128,128]{2,1,0:T(8,128)S(1)}, u32[]{:S(2)}, u32[]{:S(2)}) collective-permute-start(f32[5,128,128]{2,1,0:T(8,128)S(1)} %get-tuple-element.117), channel_id=1, source_target_pairs={{0,8},{1,9},{2,10},{3,11},{4,12},{5,13},{6,14},{7,15},{8,0},{9,1},... | collective-permute-start | bytes 983048 | tf_op jit(solution)/shard_map/ppermute | solution.py:52
  155.0 14.3 %collective-permute-start.33 = (f32[5,128,128]{2,1,0:T(8,128)S(1)}, f32[5,128,128]{2,1,0:T(8,128)S(1)}, u32[]{:S(2)}, u32[]{:S(2)}) collective-permute-start(f32[5,128,128]{2,1,0:T(8,128)S(1)} %pad_maximum_fusion.5), channel_id=1, source_target_pairs={{0,16},{1,17},{2,18},{3,19},{4,20},{5,21},{6,22},{7,23},{8,24},{9,... | collective-permute-start | bytes 983048 | tf_op jit(solution)/shard_map/ppermute | solution.py:52
  (20 other events, 142.2 us)

commit v14 on v12

--- a/solution.py
+++ b/solution.py
@@ -543,12 +543,12 @@
     pairs = pair_tiles(count, tile_collection)
     near = [first, second, one_first, one_second, three_first, three_second]
     far = [permute(one_first, v_down), permute(three_second, v_up)]
-    second_far, partner_one, *far = tie(second_far, partner_one, *far)
     first, second = jnp.concatenate([partner, partner_one], axis=0), second_far
     one_first, three_second = permute(first, v_down), permute(second, v_up)
+    first, second, *far = tie(first, second, *far)
+    one_second, three_first = permute(second, v_down), permute(first, v_up)
     partial = forward_part(0, plan[:4], pairs, near + far, None, nrow)
-    first, second, partial = tie(first, second, partial[0])
-    one_second, three_first = permute(second, v_down), permute(first, v_up)
+    one_first, three_second, partial = tie(one_first, three_second, partial[0])
     apart = [first, second, one_first, one_second, three_first, three_second]
     far = [permute(one_first, v_down), permute(three_second, v_up)]
     partial = forward_part(1, plan[:4], pairs, apart, partial, nrow)

time: 168 us -> 164 us (0.976)
  Pallas kernels: 36.1 us -> 20.8 us
  starting transfers between devices: 46.2 us -> 60.4 us
  waiting for transfers between devices: 78.5 us -> 75.6 us
    ppermute x39, starting transfers between devices: 46.2 us -> 60.4 us  [permute(): return lax.ppermute(value, AXES, pairs)]
    pallas_call x2, Pallas kernels: 10.5 us -> 4.48 us  [backward_part(): pl.pallas_call(functools.partial(backward_kernel, which), name='backward_...]
    pallas_call x3, Pallas kernels: 11.8 us -> 6.37 us  [forward_part(): pl.pallas_call(functools.partial(forward_kernel, which), name='forward_ti...]
    pallas_call x1, Pallas kernels: 6.48 us -> 2.63 us  [pair_tiles(): pl.pallas_call(pair_kernel, name='pair_tiles', out_shape=pltpu.VMEM((SLOT...]
    ppermute x39, waiting for transfers between devices: 78.5 us -> 75.6 us  [permute(): return lax.ppermute(value, AXES, pairs)]
  transfers between devices with their start and end apart: 39 -> 39, of which waited for: 22 -> 24; matrix products, arithmetic and copies ran while one was open for 1% -> 1% of each run, Pallas kernels for 16% -> 8%
where the time goes in v14:
time: 164 us; the launch traced here: 162 us
  waiting for transfers between devices  75.6 us (46%)
  starting transfers between devices  60.4 us (37%)
  Pallas kernels  20.8 us (13%)
  other arithmetic  2.08 us (1%)
  local copies, waits for them, and re-layouts  1.83 us (1%)
  between operations  1.73 us (1%)
    ppermute x39, waiting for transfers between devices, permute(): return lax.ppermute(value, AXES, pairs)  75.6 us
    ppermute x39, starting transfers between devices, permute(): return lax.ppermute(value, AXES, pairs)  60.4 us
    pallas_call x3, Pallas kernels, forward_part(): pl.pallas_call(functools.partial(forward_kernel, which), name='forward_ti...  6.37 us
    pallas_call x2, Pallas kernels, middle_part(): pl.pallas_call(functools.partial(middle_kernel, which), name='middle_%d'...  4.53 us
    pallas_call x2, Pallas kernels, backward_part(): pl.pallas_call(functools.partial(backward_kernel, which), name='backward_...  4.48 us
  transfers between devices with their start and end apart: 39, of which 24 were waited for; matrix products, arithmetic and copies ran while one was open for 1% of the time, Pallas kernels for 8%

profile of v14, /device:TPU:0, one launch (start us, length us, event | category | flops | bytes accessed | tf_op | source)
XLA Modules:
  0.0 162.4 jit_solution(13275989618273698493)
XLA Ops:
  8.1 3.0 %collective-permute-start.3 = (f32[4,128,128]{2,1,0:T(8,128)S(1)}, f32[4,128,128]{2,1,0:T(8,128)S(1)}, u32[]{:S(2)}, u32[]{:S(2)}) collective-permute-start(f32[4,128,128]{2,1,0:T(8,128)S(1)} %get-tuple-element.112), channel_id=1, source_target_pairs={{0,80},{1,81},{2,82},{3,83},{4,84},{5,85},{6,86},{7,87},{8,88},{9,... | collective-permute-start | bytes 786440 | tf_op jit(solution)/shard_map/ppermute | solution.py:52
  13.9 3.6 %collective-permute-done.3 = f32[4,128,128]{2,1,0:T(8,128)S(1)} collective-permute-done((f32[4,128,128]{2,1,0:T(8,128)S(1)}, f32[4,128,128]{2,1,0:T(8,128)S(1)}, u32[]{:S(2)}, u32[]{:S(2)}) %collective-permute-start.3) | collective-permute-done | bytes 262176 | tf_op jit(solution)/shard_map/ppermute | solution.py:52
  31.0 2.9 %collective-permute-done.7.rest_1_ = f32[8,128,128]{2,1,0:T(8,128)S(1)} collective-permute-done((f32[8,128,128]{2,1,0:T(8,128)S(1)}, f32[8,128,128]{2,1,0:T(8,128)S(1)}, u32[]{:S(2)}, u32[]{:S(2)}) %collective-permute-start.7) | collective-permute-done | bytes 524320 | tf_op jit(solution)/shard_map/ppermute | solution.py:52
  40.7 3.5 %collective-permute-start.6 = (f32[8,128,128]{2,1,0:T(8,128)S(1)}, f32[8,128,128]{2,1,0:T(8,128)S(1)}, u32[]{:S(2)}, u32[]{:S(2)}) collective-permute-start(f32[8,128,128]{2,1,0:T(8,128)S(1)} %constant_dynamic-update-slice_fusion.rest_0_), channel_id=1, source_target_pairs={{0,3},{1,0},{2,1},{3,2},{4,7},{5,4},{6,5},{7,6},{8,11},{9,8},{10,9... | collective-permute-start | bytes 1572872 | tf_op jit(solution)/shard_map/ppermute | solution.py:52
  44.5 3.1 %collective-permute-start.16 = (f32[8,128,128]{2,1,0:T(8,128)S(1)}, f32[8,128,128]{2,1,0:T(8,128)S(1)}, u32[]{:S(2)}, u32[]{:S(2)}) collective-permute-start(f32[8,128,128]{2,1,0:T(8,128)S(1)} %collective-permute-done.7.rest_1_), channel_id=1, source_target_pairs={{0,3},{1,0},{2,1},{3,2},{4,7},{5,4},{6,5},{7,6},{8,11},{9,8},{10,9... | collective-permute-start | bytes 1572872 | tf_op jit(solution)/shard_map/ppermute | solution.py:52
  50.9 3.7 %collective-permute-start.14 = (f32[8,128,128]{2,1,0:T(8,128)S(1)}, f32[8,128,128]{2,1,0:T(8,128)S(1)}, u32[]{:S(2)}, u32[]{:S(2)}) collective-permute-start(f32[8,128,128]{2,1,0:T(8,128)S(1)} %collective-permute-done.6.rest_2_), channel_id=1, source_target_pairs={{0,3},{1,0},{2,1},{3,2},{4,7},{5,4},{6,5},{7,6},{8,11},{9,8},{10,9... | collective-permute-start | bytes 1572872 | tf_op jit(solution)/shard_map/ppermute | solution.py:52
  58.7 3.4 %collective-permute-done.14.rest_0_ = f32[8,128,128]{2,1,0:T(8,128)S(1)} collective-permute-done((f32[8,128,128]{2,1,0:T(8,128)S(1)}, f32[8,128,128]{2,1,0:T(8,128)S(1)}, u32[]{:S(2)}, u32[]{:S(2)}) %collective-permute-start.14) | collective-permute-done | bytes 524320 | tf_op jit(solution)/shard_map/ppermute | solution.py:52
  62.1 2.8 %collective-permute-done.15.rest_1_ = f32[8,128,128]{2,1,0:T(8,128)S(1)} collective-permute-done((f32[8,128,128]{2,1,0:T(8,128)S(1)}, f32[8,128,128]{2,1,0:T(8,128)S(1)}, u32[]{:S(2)}, u32[]{:S(2)}) %collective-permute-start.15) | collective-permute-done | bytes 524320 | tf_op jit(solution)/shard_map/ppermute | solution.py:52
  70.7 6.5 %collective-permute-done.22 = f32[4,128,128]{2,1,0:T(8,128)S(1)} collective-permute-done((f32[4,128,128]{2,1,0:T(8,128)S(1)}, f32[4,128,128]{2,1,0:T(8,128)S(1)}, u32[]{:S(2)}, u32[]{:S(2)}) %collective-permute-start.22) | collective-permute-done | bytes 262176 | tf_op jit(solution)/shard_map/ppermute | solution.py:52
  77.4 5.0 %collective-permute-done.19 = f32[4,128,128]{2,1,0:T(8,128)S(1)} collective-permute-done((f32[4,128,128]{2,1,0:T(8,128)S(1)}, f32[4,128,128]{2,1,0:T(8,128)S(1)}, u32[]{:S(2)}, u32[]{:S(2)}) %collective-permute-start.19) | collective-permute-done | bytes 262176 | tf_op jit(solution)/shard_map/ppermute | solution.py:52
  88.8 3.2 %collective-permute-start.26 = (f32[17,128,128]{2,1,0:T(8,128)S(1)}, f32[17,128,128]{2,1,0:T(8,128)S(1)}, u32[]{:S(2)}, u32[]{:S(2)}) collective-permute-start(f32[17,128,128]{2,1,0:T(8,128)S(1)} %get-tuple-element.83), channel_id=1, source_target_pairs={{0,3},{1,0},{2,1},{3,2},{4,7},{5,4},{6,5},{7,6},{8,11},{9,8},{10,9... | collective-permute-start | bytes 3342344 | tf_op jit(solution)/shard_map/ppermute | solution.py:52
  92.0 2.9 %backward_tiles_1.1 = (f32[16,128,128]{2,1,0:T(8,128)S(1)}, f32[17,128,128]{2,1,0:T(8,128)S(1)}, f32[16,128,128]{2,1,0:T(8,128)S(1)}, f32[16,128,128]{2,1,0:T(8,...) custom-call(s32[9]{0:T(128)S(1)} %compare_select_fusion.10.bounds_ref, ...), custom_call_target="tpu_custom_call" | custom-call | flops 8800000000 | bytes 1048576 | tf_op jit(solution)/shard_map/backward_tiles_1/pallas_call | solution.py:280
  94.9 10.6 %collective-permute-done.24 = f32[17,128,128]{2,1,0:T(8,128)S(1)} collective-permute-done((f32[17,128,128]{2,1,0:T(8,128)S(1)}, f32[17,128,128]{2,1,0:T(8,128)S(1)}, u32[]{:S(2)}, u32[]{:S(2)}) %collective-permute-start.24) | collective-permute-done | bytes 1114144 | tf_op jit(solution)/shard_map/ppermute | solution.py:52
  106.1 3.3 %collective-permute-start.29 = (f32[16,128,128]{2,1,0:T(8,128)S(1)}, f32[16,128,128]{2,1,0:T(8,128)S(1)}, u32[]{:S(2)}, u32[]{:S(2)}) collective-permute-start(f32[16,128,128]{2,1,0:T(8,128)S(1)} %get-tuple-element.105), channel_id=1, source_target_pairs={{0,3},{1,0},{2,1},{3,2},{4,7},{5,4},{6,5},{7,6},{8,11},{9,8},{10,9... | collective-permute-start | bytes 3145736 | tf_op jit(solution)/shard_map/ppermute | solution.py:52
  109.4 3.2 %collective-permute-start.27 = (f32[16,128,128]{2,1,0:T(8,128)S(1)}, f32[16,128,128]{2,1,0:T(8,128)S(1)}, u32[]{:S(2)}, u32[]{:S(2)}) collective-permute-start(f32[16,128,128]{2,1,0:T(8,128)S(1)} %get-tuple-element.104), channel_id=1, source_target_pairs={{0,3},{1,0},{2,1},{3,2},{4,7},{5,4},{6,5},{7,6},{8,11},{9,8},{10,9... | collective-permute-start | bytes 3145736 | tf_op jit(solution)/shard_map/ppermute | solution.py:52
  112.6 9.9 %collective-permute-done.28 = f32[17,128,128]{2,1,0:T(8,128)S(1)} collective-permute-done((f32[17,128,128]{2,1,0:T(8,128)S(1)}, f32[17,128,128]{2,1,0:T(8,128)S(1)}, u32[]{:S(2)}, u32[]{:S(2)}) %collective-permute-start.28) | collective-permute-done | bytes 1114144 | tf_op jit(solution)/shard_map/ppermute | solution.py:52
  123.4 3.3 %collective-permute-start.31 = (f32[9,128,128]{2,1,0:T(8,128)S(1)}, f32[9,128,128]{2,1,0:T(8,128)S(1)}, u32[]{:S(2)}, u32[]{:S(2)}) collective-permute-start(f32[9,128,128]{2,1,0:T(8,128)S(1)} %pad_maximum_fusion), channel_id=1, source_target_pairs={{0,16},{1,17},{2,18},{3,19},{4,20},{5,21},{6,22},{7,23},{8,24},{9,... | collective-permute-start | bytes 1769480 | tf_op jit(solution)/shard_map/ppermute | solution.py:52
  126.8 4.2 %collective-permute-start.30 = (f32[4,128,128]{2,1,0:T(8,128)S(1)}, f32[4,128,128]{2,1,0:T(8,128)S(1)}, u32[]{:S(2)}, u32[]{:S(2)}) collective-permute-start(f32[4,128,128]{2,1,0:T(8,128)S(1)} %get-tuple-element.111), channel_id=1, source_target_pairs={{0,8},{1,9},{2,10},{3,11},{4,12},{5,13},{6,14},{7,15},{8,0},{9,1},... | collective-permute-start | bytes 786440 | tf_op jit(solution)/shard_map/ppermute | solution.py:52
  131.0 5.6 %collective-permute-done.25 = f32[16,128,128]{2,1,0:T(8,128)S(1)} collective-permute-done((f32[16,128,128]{2,1,0:T(8,128)S(1)}, f32[16,128,128]{2,1,0:T(8,128)S(1)}, u32[]{:S(2)}, u32[]{:S(2)}) %collective-permute-start.25) | collective-permute-done | bytes 1048608 | tf_op jit(solution)/shard_map/ppermute | solution.py:52
  136.8 2.9 %collective-permute-done.31 = f32[9,128,128]{2,1,0:T(8,128)S(1)} collective-permute-done((f32[9,128,128]{2,1,0:T(8,128)S(1)}, f32[9,128,128]{2,1,0:T(8,128)S(1)}, u32[]{:S(2)}, u32[]{:S(2)}) %collective-permute-start.31) | collective-permute-done | bytes 589856 | tf_op jit(solution)/shard_map/ppermute | solution.py:52
  140.2 3.2 %collective-permute-start.34 = (f32[5,128,128]{2,1,0:T(8,128)S(1)}, f32[5,128,128]{2,1,0:T(8,128)S(1)}, u32[]{:S(2)}, u32[]{:S(2)}) collective-permute-start(f32[5,128,128]{2,1,0:T(8,128)S(1)} %get-tuple-element.115), channel_id=1, source_target_pairs={{0,8},{1,9},{2,10},{3,11},{4,12},{5,13},{6,14},{7,15},{8,0},{9,1},... | collective-permute-start | bytes 983048 | tf_op jit(solution)/shard_map/ppermute | solution.py:52
  144.2 3.2 %collective-permute-start.32 = (f32[4,128,128]{2,1,0:T(8,128)S(1)}, f32[4,128,128]{2,1,0:T(8,128)S(1)}, u32[]{:S(2)}, u32[]{:S(2)}) collective-permute-start(f32[4,128,128]{2,1,0:T(8,128)S(1)} %slice_add_fusion.10), channel_id=1, source_target_pairs={{0,16},{1,17},{2,18},{3,19},{4,20},{5,21},{6,22},{7,23},{8,24},{9,... | collective-permute-start | bytes 786440 | tf_op jit(solution)/shard_map/ppermute | solution.py:52
  147.4 4.6 %collective-permute-done.32 = f32[4,128,128]{2,1,0:T(8,128)S(1)} collective-permute-done((f32[4,128,128]{2,1,0:T(8,128)S(1)}, f32[4,128,128]{2,1,0:T(8,128)S(1)}, u32[]{:S(2)}, u32[]{:S(2)}) %collective-permute-start.32) | collective-permute-done | bytes 262176 | tf_op jit(solution)/shard_map/ppermute | solution.py:52
  154.7 4.5 %collective-permute-done.37.across_ref = f32[4,128,128]{2,1,0:T(8,128)S(1)} collective-permute-done((f32[4,128,128]{2,1,0:T(8,128)S(1)}, f32[4,128,128]{2,1,0:T(8,128)S(1)}, u32[]{:S(2)}, u32[]{:S(2)}) %collective-permute-start.37) | collective-permute-done | bytes 262176 | tf_op jit(solution)/shard_map/ppermute | solution.py:52
  (108 shorter events, 58.3 us)
Async XLA Ops:
  2.3 11.4 %collective-permute-start.2 = (f32[4,128,128]{2,1,0:T(8,128)S(1)}, f32[4,128,128]{2,1,0:T(8,128)S(1)}, u32[]{:S(2)}, u32[]{:S(2)}) collective-permute-start(f32[4,128,128]{2,1,0:T(8,128)S(1)} %get-tuple-element.113), channel_id=1, source_target_pairs={{0,4},{1,5},{2,6},{3,7},{4,8},{5,9},{6,10},{7,11},{8,12},{9,13},{1... | collective-permute-start | bytes 786440 | tf_op jit(solution)/shard_map/ppermute | solution.py:52
  19.7 10.4 %collective-permute-start.11 = (f32[8,128,128]{2,1,0:T(8,128)S(1)}, f32[8,128,128]{2,1,0:T(8,128)S(1)}, u32[]{:S(2)}, u32[]{:S(2)}) collective-permute-start(f32[8,128,128]{2,1,0:T(8,128)S(1)} %pad_maximum_fusion.5.rest_1_), channel_id=1, source_target_pairs={{0,1},{1,2},{2,3},{3,0},{4,5},{5,6},{6,7},{7,4},{8,9},{9,10},{10,1... | collective-permute-start | bytes 1572872 | tf_op jit(solution)/shard_map/ppermute | solution.py:52
  19.7 14.2 %collective-permute-start.7 = (f32[8,128,128]{2,1,0:T(8,128)S(1)}, f32[8,128,128]{2,1,0:T(8,128)S(1)}, u32[]{:S(2)}, u32[]{:S(2)}) collective-permute-start(f32[8,128,128]{2,1,0:T(8,128)S(1)} %pad_maximum_fusion.5.rest_1_), channel_id=1, source_target_pairs={{0,16},{1,17},{2,18},{3,19},{4,20},{5,21},{6,22},{7,23},{8,24},{9,... | collective-permute-start | bytes 1572872 | tf_op jit(solution)/shard_map/ppermute | solution.py:52
  21.7 22.8 %collective-permute-start.10 = (f32[8,128,128]{2,1,0:T(8,128)S(1)}, f32[8,128,128]{2,1,0:T(8,128)S(1)}, u32[]{:S(2)}, u32[]{:S(2)}) collective-permute-start(f32[8,128,128]{2,1,0:T(8,128)S(1)} %pad_maximum_fusion.4.rest_0_), channel_id=1, source_target_pairs={{0,1},{1,2},{2,3},{3,0},{4,5},{5,6},{6,7},{7,4},{8,9},{9,10},{10,1... | collective-permute-start | bytes 1572872 | tf_op jit(solution)/shard_map/ppermute | solution.py:52
  22.4 25.2 %collective-permute-start.9 = (f32[8,128,128]{2,1,0:T(8,128)S(1)}, f32[8,128,128]{2,1,0:T(8,128)S(1)}, u32[]{:S(2)}, u32[]{:S(2)}) collective-permute-start(f32[8,128,128]{2,1,0:T(8,128)S(1)} %pad_maximum_fusion.5.rest_1_), channel_id=1, source_target_pairs={{0,3},{1,0},{2,1},{3,2},{4,7},{5,4},{6,5},{7,6},{8,11},{9,8},{10,9... | collective-permute-start | bytes 1572872 | tf_op jit(solution)/shard_map/ppermute | solution.py:52
  26.9 11.0 %collective-permute-start.5 = (f32[4,128,128]{2,1,0:T(8,128)S(1)}, f32[4,128,128]{2,1,0:T(8,128)S(1)}, u32[]{:S(2)}, u32[]{:S(2)}) collective-permute-start(f32[4,128,128]{2,1,0:T(8,128)S(1)} %collective-permute-done.3), channel_id=1, source_target_pairs={{0,12},{1,13},{2,14},{3,15},{4,0},{5,1},{6,2},{7,3},{8,4},{9,5},{1... | collective-permute-start | bytes 786440 | tf_op jit(solution)/shard_map/ppermute | solution.py:52
  30.1 10.5 %collective-permute-start.12 = (f32[8,128,128]{2,1,0:T(8,128)S(1)}, f32[8,128,128]{2,1,0:T(8,128)S(1)}, u32[]{:S(2)}, u32[]{:S(2)}) collective-permute-start(f32[8,128,128]{2,1,0:T(8,128)S(1)} %collective-permute-done.4.rest_2_), channel_id=1, source_target_pairs={{0,3},{1,0},{2,1},{3,2},{4,7},{5,4},{6,5},{7,6},{8,11},{9,8},{10,9... | collective-permute-start | bytes 1572872 | tf_op jit(solution)/shard_map/ppermute | solution.py:52
  33.9 10.4 %collective-permute-start.13 = (f32[8,128,128]{2,1,0:T(8,128)S(1)}, f32[8,128,128]{2,1,0:T(8,128)S(1)}, u32[]{:S(2)}, u32[]{:S(2)}) collective-permute-start(f32[8,128,128]{2,1,0:T(8,128)S(1)} %collective-permute-done.11.rest_5_), channel_id=1, source_target_pairs={{0,1},{1,2},{2,3},{3,0},{4,5},{5,6},{6,7},{7,4},{8,9},{9,10},{10,1... | collective-permute-start | bytes 1572872 | tf_op jit(solution)/shard_map/ppermute | solution.py:52
  38.0 12.4 %collective-permute-start.8 = (f32[8,128,128]{2,1,0:T(8,128)S(1)}, f32[8,128,128]{2,1,0:T(8,128)S(1)}, u32[]{:S(2)}, u32[]{:S(2)}) collective-permute-start(f32[8,128,128]{2,1,0:T(8,128)S(1)} %collective-permute-done.7.rest_1_), channel_id=1, source_target_pairs={{0,1},{1,2},{2,3},{3,0},{4,5},{5,6},{6,7},{7,4},{8,9},{9,10},{10,1... | collective-permute-start | bytes 1572872 | tf_op jit(solution)/shard_map/ppermute | solution.py:52
  40.7 10.2 %collective-permute-start.6 = (f32[8,128,128]{2,1,0:T(8,128)S(1)}, f32[8,128,128]{2,1,0:T(8,128)S(1)}, u32[]{:S(2)}, u32[]{:S(2)}) collective-permute-start(f32[8,128,128]{2,1,0:T(8,128)S(1)} %constant_dynamic-update-slice_fusion.rest_0_), channel_id=1, source_target_pairs={{0,3},{1,0},{2,1},{3,2},{4,7},{5,4},{6,5},{7,6},{8,11},{9,8},{10,9... | collective-permute-start | bytes 1572872 | tf_op jit(solution)/shard_map/ppermute | solution.py:52
  44.3 11.2 %collective-permute-start.17 = (f32[8,128,128]{2,1,0:T(8,128)S(1)}, f32[8,128,128]{2,1,0:T(8,128)S(1)}, u32[]{:S(2)}, u32[]{:S(2)}) collective-permute-start(f32[8,128,128]{2,1,0:T(8,128)S(1)} %constant_dynamic-update-slice_fusion.rest_0_), channel_id=1, source_target_pairs={{0,1},{1,2},{2,3},{3,0},{4,5},{5,6},{6,7},{7,4},{8,9},{9,10},{10,1... | collective-permute-start | bytes 1572872 | tf_op jit(solution)/shard_map/ppermute | solution.py:52
  44.5 12.0 %collective-permute-start.16 = (f32[8,128,128]{2,1,0:T(8,128)S(1)}, f32[8,128,128]{2,1,0:T(8,128)S(1)}, u32[]{:S(2)}, u32[]{:S(2)}) collective-permute-start(f32[8,128,128]{2,1,0:T(8,128)S(1)} %collective-permute-done.7.rest_1_), channel_id=1, source_target_pairs={{0,3},{1,0},{2,1},{3,2},{4,7},{5,4},{6,5},{7,6},{8,11},{9,8},{10,9... | collective-permute-start | bytes 1572872 | tf_op jit(solution)/shard_map/ppermute | solution.py:52
  50.9 11.2 %collective-permute-start.14 = (f32[8,128,128]{2,1,0:T(8,128)S(1)}, f32[8,128,128]{2,1,0:T(8,128)S(1)}, u32[]{:S(2)}, u32[]{:S(2)}) collective-permute-start(f32[8,128,128]{2,1,0:T(8,128)S(1)} %collective-permute-done.6.rest_2_), channel_id=1, source_target_pairs={{0,3},{1,0},{2,1},{3,2},{4,7},{5,4},{6,5},{7,6},{8,11},{9,8},{10,9... | collective-permute-start | bytes 1572872 | tf_op jit(solution)/shard_map/ppermute | solution.py:52
  54.5 10.4 %collective-permute-start.15 = (f32[8,128,128]{2,1,0:T(8,128)S(1)}, f32[8,128,128]{2,1,0:T(8,128)S(1)}, u32[]{:S(2)}, u32[]{:S(2)}) collective-permute-start(f32[8,128,128]{2,1,0:T(8,128)S(1)} %collective-permute-done.8.rest_5_), channel_id=1, source_target_pairs={{0,1},{1,2},{2,3},{3,0},{4,5},{5,6},{6,7},{7,4},{8,9},{9,10},{10,1... | collective-permute-start | bytes 1572872 | tf_op jit(solution)/shard_map/ppermute | solution.py:52
  70.2 12.2 %collective-permute-start.19 = (f32[4,128,128]{2,1,0:T(8,128)S(1)}, f32[4,128,128]{2,1,0:T(8,128)S(1)}, u32[]{:S(2)}, u32[]{:S(2)}) collective-permute-start(f32[4,128,128]{2,1,0:T(8,128)S(1)} %add.301), channel_id=1, source_target_pairs={{0,64},{1,65},{2,66},{3,67},{4,68},{5,69},{6,70},{7,71},{8,72},{9,... | collective-permute-start | bytes 786440 | tf_op jit(solution)/shard_map/ppermute | solution.py:52
  88.7 16.8 %collective-permute-start.24 = (f32[17,128,128]{2,1,0:T(8,128)S(1)}, f32[17,128,128]{2,1,0:T(8,128)S(1)}, u32[]{:S(2)}, u32[]{:S(2)}) collective-permute-start(f32[17,128,128]{2,1,0:T(8,128)S(1)} %get-tuple-element.81), channel_id=1, source_target_pairs={{0,1},{1,2},{2,3},{3,0},{4,5},{5,6},{6,7},{7,4},{8,9},{9,10},{10,1... | collective-permute-start | bytes 3342344 | tf_op jit(solution)/shard_map/ppermute | solution.py:52
  88.8 17.1 %collective-permute-start.26 = (f32[17,128,128]{2,1,0:T(8,128)S(1)}, f32[17,128,128]{2,1,0:T(8,128)S(1)}, u32[]{:S(2)}, u32[]{:S(2)}) collective-permute-start(f32[17,128,128]{2,1,0:T(8,128)S(1)} %get-tuple-element.83), channel_id=1, source_target_pairs={{0,3},{1,0},{2,1},{3,2},{4,7},{5,4},{6,5},{7,6},{8,11},{9,8},{10,9... | collective-permute-start | bytes 3342344 | tf_op jit(solution)/shard_map/ppermute | solution.py:52
  105.7 16.8 %collective-permute-start.28 = (f32[17,128,128]{2,1,0:T(8,128)S(1)}, f32[17,128,128]{2,1,0:T(8,128)S(1)}, u32[]{:S(2)}, u32[]{:S(2)}) collective-permute-start(f32[17,128,128]{2,1,0:T(8,128)S(1)} %get-tuple-element.107), channel_id=1, source_target_pairs={{0,1},{1,2},{2,3},{3,0},{4,5},{5,6},{6,7},{7,4},{8,9},{9,10},{10,1... | collective-permute-start | bytes 3342344 | tf_op jit(solution)/shard_map/ppermute | solution.py:52
  106.1 17.0 %collective-permute-start.29 = (f32[16,128,128]{2,1,0:T(8,128)S(1)}, f32[16,128,128]{2,1,0:T(8,128)S(1)}, u32[]{:S(2)}, u32[]{:S(2)}) collective-permute-start(f32[16,128,128]{2,1,0:T(8,128)S(1)} %get-tuple-element.105), channel_id=1, source_target_pairs={{0,3},{1,0},{2,1},{3,2},{4,7},{5,4},{6,5},{7,6},{8,11},{9,8},{10,9... | collective-permute-start | bytes 3145736 | tf_op jit(solution)/shard_map/ppermute | solution.py:52
  109.4 27.2 %collective-permute-start.25 = (f32[16,128,128]{2,1,0:T(8,128)S(1)}, f32[16,128,128]{2,1,0:T(8,128)S(1)}, u32[]{:S(2)}, u32[]{:S(2)}) collective-permute-start(f32[16,128,128]{2,1,0:T(8,128)S(1)} %get-tuple-element.102), channel_id=1, source_target_pairs={{0,1},{1,2},{2,3},{3,0},{4,5},{5,6},{6,7},{7,4},{8,9},{9,10},{10,1... | collective-permute-start | bytes 3145736 | tf_op jit(solution)/shard_map/ppermute | solution.py:52
  109.4 27.2 %collective-permute-start.27 = (f32[16,128,128]{2,1,0:T(8,128)S(1)}, f32[16,128,128]{2,1,0:T(8,128)S(1)}, u32[]{:S(2)}, u32[]{:S(2)}) collective-permute-start(f32[16,128,128]{2,1,0:T(8,128)S(1)} %get-tuple-element.104), channel_id=1, source_target_pairs={{0,3},{1,0},{2,1},{3,2},{4,7},{5,4},{6,5},{7,6},{8,11},{9,8},{10,9... | collective-permute-start | bytes 3145736 | tf_op jit(solution)/shard_map/ppermute | solution.py:52
  123.4 16.3 %collective-permute-start.31 = (f32[9,128,128]{2,1,0:T(8,128)S(1)}, f32[9,128,128]{2,1,0:T(8,128)S(1)}, u32[]{:S(2)}, u32[]{:S(2)}) collective-permute-start(f32[9,128,128]{2,1,0:T(8,128)S(1)} %pad_maximum_fusion), channel_id=1, source_target_pairs={{0,16},{1,17},{2,18},{3,19},{4,20},{5,21},{6,22},{7,23},{8,24},{9,... | collective-permute-start | bytes 1769480 | tf_op jit(solution)/shard_map/ppermute | solution.py:52
  139.9 12.1 %collective-permute-start.33 = (f32[5,128,128]{2,1,0:T(8,128)S(1)}, f32[5,128,128]{2,1,0:T(8,128)S(1)}, u32[]{:S(2)}, u32[]{:S(2)}) collective-permute-start(f32[5,128,128]{2,1,0:T(8,128)S(1)} %get-tuple-element.114), channel_id=1, source_target_pairs={{0,4},{1,5},{2,6},{3,7},{4,8},{5,9},{6,10},{7,11},{8,12},{9,13},{1... | collective-permute-start | bytes 983048 | tf_op jit(solution)/shard_map/ppermute | solution.py:52
  140.2 11.8 %collective-permute-start.34 = (f32[5,128,128]{2,1,0:T(8,128)S(1)}, f32[5,128,128]{2,1,0:T(8,128)S(1)}, u32[]{:S(2)}, u32[]{:S(2)}) collective-permute-start(f32[5,128,128]{2,1,0:T(8,128)S(1)} %get-tuple-element.115), channel_id=1, source_target_pairs={{0,8},{1,9},{2,10},{3,11},{4,12},{5,13},{6,14},{7,15},{8,0},{9,1},... | collective-permute-start | bytes 983048 | tf_op jit(solution)/shard_map/ppermute | solution.py:52
  (19 other events, 139.4 us)

commit v15 on v14

--- a/solution.py
+++ b/solution.py
@@ -508,16 +508,15 @@
     weight_term = ring_sum(1, plan[0], (weight_term, down[PER], one[PER], up[PER]))
     apart = zero + one[:PER] + three
     apart_two = permute(apart[8:12], u_far)
-    apart_far = permute(
-        jnp.concatenate([apart[4:8], apart[12:16], weight_term[None]], axis=0), y_far
-    )
-    last, apart_far = tie(apart[:4] + apart_two, apart_far)
+    far_one = permute(with_tile(apart[4:8], weight_term), y_far)
+    far_three = permute(apart[12:16], y_far)
+    last, far_three = tie(apart[:4] + apart_two, far_three)
     last = permute(last, y_far)
-    weight_term = weight_term + apart_far[8]
+    weight_term = weight_term + far_one[4]
     total = own + own_one + own_three
     two = permute(with_tile(total[8:12], weight_term), u_far)
-    one = permute(with_tile(total[4:8] + apart_far[:4], weight_term), u_up)
-    three = permute(with_tile(total[12:16] + apart_far[4:8], weight_term), u_down)
+    one = permute(with_tile(total[4:8] + far_one[:4], weight_term), u_up)
+    three = permute(with_tile(total[12:16] + far_three, weight_term), u_down)
     weight_term = ring_sum(0, plan[0], (weight_term, three[4], two[4], one[4]))
     return total[:4] + last + one[:4] + two[:4] + three[:4], weight_term
 

time: 164 us -> 169 us (1.030)
  Pallas kernels: 20.8 us -> 25.2 us
    pallas_call x2, Pallas kernels: 4.48 us -> 6.33 us  [backward_part(): pl.pallas_call(functools.partial(backward_kernel, which), name='backward_...]
    ppermute x39 -> x40, starting transfers between devices: 60.4 us -> 61.3 us  [permute(): return lax.ppermute(value, AXES, pairs)]
    ppermute x39 -> x40, waiting for transfers between devices: 75.6 us -> 75.7 us  [permute(): return lax.ppermute(value, AXES, pairs)]
  transfers between devices with their start and end apart: 39 -> 40, of which waited for: 24 -> 24; matrix products, arithmetic and copies ran while one was open for 1% -> 1% of each run, Pallas kernels for 8% -> 10%
where the time goes in v15:
time: 169 us; the launch traced here: 168 us
  waiting for transfers between devices  75.7 us (45%)
  starting transfers between devices  61.3 us (36%)
  Pallas kernels  25.2 us (15%)
  other arithmetic  2.07 us (1%)
  local copies, waits for them, and re-layouts  1.83 us (1%)
  between operations  1.76 us (1%)
    ppermute x40, waiting for transfers between devices, permute(): return lax.ppermute(value, AXES, pairs)  75.7 us
    ppermute x40, starting transfers between devices, permute(): return lax.ppermute(value, AXES, pairs)  61.3 us
    pallas_call x3, Pallas kernels, forward_part(): pl.pallas_call(functools.partial(forward_kernel, which), name='forward_ti...  7.73 us
    pallas_call x2, Pallas kernels, backward_part(): pl.pallas_call(functools.partial(backward_kernel, which), name='backward_...  6.33 us
    pallas_call x2, Pallas kernels, middle_part(): pl.pallas_call(functools.partial(middle_kernel, which), name='middle_%d'...  4.52 us
    pallas_call x1, Pallas kernels, pair_tiles(): pl.pallas_call(pair_kernel, name='pair_tiles', out_shape=pltpu.VMEM((SLOT...  3.87 us
  transfers between devices with their start and end apart: 40, of which 24 were waited for; matrix products, arithmetic and copies ran while one was open for 1% of the time, Pallas kernels for 10%

profile of v15, /device:TPU:0, one launch (start us, length us, event | category | flops | bytes accessed | tf_op | source)
XLA Modules:
  0.0 167.9 jit_solution(12493215740129083520)
XLA Ops:
  3.9 2.7 %collective-permute-start.1 = (f32[4,128,128]{2,1,0:T(8,128)S(1)}, f32[4,128,128]{2,1,0:T(8,128)S(1)}, u32[]{:S(2)}, u32[]{:S(2)}) collective-permute-start(f32[4,128,128]{2,1,0:T(8,128)S(1)} %get-tuple-element.113), channel_id=1, source_target_pairs={{0,8},{1,9},{2,10},{3,11},{4,12},{5,13},{6,14},{7,15},{8,0},{9,1},... | collective-permute-start | bytes 786440 | tf_op jit(solution)/shard_map/ppermute | solution.py:52
  8.1 3.0 %collective-permute-start.3 = (f32[4,128,128]{2,1,0:T(8,128)S(1)}, f32[4,128,128]{2,1,0:T(8,128)S(1)}, u32[]{:S(2)}, u32[]{:S(2)}) collective-permute-start(f32[4,128,128]{2,1,0:T(8,128)S(1)} %get-tuple-element.112), channel_id=1, source_target_pairs={{0,80},{1,81},{2,82},{3,83},{4,84},{5,85},{6,86},{7,87},{8,88},{9,... | collective-permute-start | bytes 786440 | tf_op jit(solution)/shard_map/ppermute | solution.py:52
  13.9 3.6 %collective-permute-done.3 = f32[4,128,128]{2,1,0:T(8,128)S(1)} collective-permute-done((f32[4,128,128]{2,1,0:T(8,128)S(1)}, f32[4,128,128]{2,1,0:T(8,128)S(1)}, u32[]{:S(2)}, u32[]{:S(2)}) %collective-permute-start.3) | collective-permute-done | bytes 262176 | tf_op jit(solution)/shard_map/ppermute | solution.py:52
  27.3 2.8 %collective-permute-done.11.rest_5_ = f32[8,128,128]{2,1,0:T(8,128)S(1)} collective-permute-done((f32[8,128,128]{2,1,0:T(8,128)S(1)}, f32[8,128,128]{2,1,0:T(8,128)S(1)}, u32[]{:S(2)}, u32[]{:S(2)}) %collective-permute-start.11) | collective-permute-done | bytes 524320 | tf_op jit(solution)/shard_map/ppermute | solution.py:52
  31.0 2.9 %collective-permute-done.7.rest_1_ = f32[8,128,128]{2,1,0:T(8,128)S(1)} collective-permute-done((f32[8,128,128]{2,1,0:T(8,128)S(1)}, f32[8,128,128]{2,1,0:T(8,128)S(1)}, u32[]{:S(2)}, u32[]{:S(2)}) %collective-permute-start.7) | collective-permute-done | bytes 524320 | tf_op jit(solution)/shard_map/ppermute | solution.py:52
  35.3 3.9 %pair_tiles.1.tiles_ref.rest_2_ = bf16[256,128,256]{2,1,0:T(8,128)(2,1)S(1)} custom-call(s32[1]{0:T(128)} %bitcast.34.count_ref, f32[256,128,128]{2,1,0:T(8,128)} %bitcast.41), custom_call_target="tpu_custom_call" | custom-call | flops 8800000000 | bytes 1048576 | tf_op jit(solution)/shard_map/pair_tiles/pallas_call | solution.py:123
  44.5 3.1 %collective-permute-start.16 = (f32[8,128,128]{2,1,0:T(8,128)S(1)}, f32[8,128,128]{2,1,0:T(8,128)S(1)}, u32[]{:S(2)}, u32[]{:S(2)}) collective-permute-start(f32[8,128,128]{2,1,0:T(8,128)S(1)} %collective-permute-done.7.rest_1_), channel_id=1, source_target_pairs={{0,3},{1,0},{2,1},{3,2},{4,7},{5,4},{6,5},{7,6},{8,11},{9,8},{10,9... | collective-permute-start | bytes 1572872 | tf_op jit(solution)/shard_map/ppermute | solution.py:52
  47.6 3.3 %forward_tiles_0.1.rest_6_ = f32[16,128,128]{2,1,0:T(8,128)S(1)} custom-call(s32[9]{0:T(128)S(1)} %compare_select_fusion.10.bounds_ref, s32[256]{0:T(256)S(1)} %get-tuple-element.49.order_ref, s32[256]{0:T(256)S(1)} %get-tuple-element.50.rows_ref, s32[256]{0:T(256)S(1)} %get-tuple-element.51.slots_ref, ...), custom_call_target="tpu_custom_call" | custom-call | flops 6600000000 | bytes 1048576 | tf_op jit(solution)/shard_map/forward_tiles_0/pallas_call | solution.py:263
  51.2 3.4 %collective-permute-start.14 = (f32[8,128,128]{2,1,0:T(8,128)S(1)}, f32[8,128,128]{2,1,0:T(8,128)S(1)}, u32[]{:S(2)}, u32[]{:S(2)}) collective-permute-start(f32[8,128,128]{2,1,0:T(8,128)S(1)} %collective-permute-done.6.rest_2_), channel_id=1, source_target_pairs={{0,3},{1,0},{2,1},{3,2},{4,7},{5,4},{6,5},{7,6},{8,11},{9,8},{10,9... | collective-permute-start | bytes 1572872 | tf_op jit(solution)/shard_map/ppermute | solution.py:52
  56.8 3.1 %forward_tiles_1.1.rest_2_ = f32[16,128,128]{2,1,0:T(8,128)S(1)} custom-call(s32[9]{0:T(128)S(1)} %compare_select_fusion.10.bounds_ref, s32[256]{0:T(256)S(1)} %get-tuple-element.49.order_ref, s32[256]{0:T(256)S(1)} %get-tuple-element.50.rows_ref, s32[256]{0:T(256)S(1)} %get-tuple-element.51.slots_ref, ...), custom_call_target="tpu_custom_call" | custom-call | flops 5500000256 | bytes 1048576 | tf_op jit(solution)/shard_map/forward_tiles_1/pallas_call | solution.py:263
  71.2 6.5 %collective-permute-done.22 = f32[4,128,128]{2,1,0:T(8,128)S(1)} collective-permute-done((f32[4,128,128]{2,1,0:T(8,128)S(1)}, f32[4,128,128]{2,1,0:T(8,128)S(1)}, u32[]{:S(2)}, u32[]{:S(2)}) %collective-permute-start.22) | collective-permute-done | bytes 262176 | tf_op jit(solution)/shard_map/ppermute | solution.py:52
  77.8 5.0 %collective-permute-done.19 = f32[4,128,128]{2,1,0:T(8,128)S(1)} collective-permute-done((f32[4,128,128]{2,1,0:T(8,128)S(1)}, f32[4,128,128]{2,1,0:T(8,128)S(1)}, u32[]{:S(2)}, u32[]{:S(2)}) %collective-permute-start.19) | collective-permute-done | bytes 262176 | tf_op jit(solution)/shard_map/ppermute | solution.py:52
  84.8 2.7 %middle_1.1 = (f32[128,2048]{1,0:T(8,128)}, bf16[16,128,256]{2,1,0:T(8,128)(2,1)S(1)}, f32[128,128]{1,0:T(8,128)S(1)}) custom-call(s32[9]{0:T(128)S(1)} %compare_select_fusion.10.bounds_ref, f32[128,128]{1,0:T(8,128)S(1)} %bitcast.37, f32[128,128]{1,0:T(8,128)S(1)} %copy-done.1, f32[128,2048]{1,0:T(8,128)S(1)} %copy-done, f32[4,128,128]{2,1,0:T(8,128)S(1)} %add.302.rest_0_, ...), custom_call_target="tpu_custom_call" | custom-call | flops 2200000000 | bytes 1048576 | tf_op jit(solution)/shard_map/middle_1/pallas_call | solution.py:364
  89.7 3.2 %collective-permute-start.26 = (f32[17,128,128]{2,1,0:T(8,128)S(1)}, f32[17,128,128]{2,1,0:T(8,128)S(1)}, u32[]{:S(2)}, u32[]{:S(2)}) collective-permute-start(f32[17,128,128]{2,1,0:T(8,128)S(1)} %get-tuple-element.83), channel_id=1, source_target_pairs={{0,3},{1,0},{2,1},{3,2},{4,7},{5,4},{6,5},{7,6},{8,11},{9,8},{10,9... | collective-permute-start | bytes 3342344 | tf_op jit(solution)/shard_map/ppermute | solution.py:52
  92.9 4.3 %backward_tiles_1.1 = (f32[16,128,128]{2,1,0:T(8,128)S(1)}, f32[17,128,128]{2,1,0:T(8,128)S(1)}, f32[16,128,128]{2,1,0:T(8,128)S(1)}, f32[16,128,128]{2,1,0:T(8,...) custom-call(s32[9]{0:T(128)S(1)} %compare_select_fusion.10.bounds_ref, ...), custom_call_target="tpu_custom_call" | custom-call | flops 8800000000 | bytes 1048576 | tf_op jit(solution)/shard_map/backward_tiles_1/pallas_call | solution.py:280
  97.2 9.2 %collective-permute-done.24 = f32[17,128,128]{2,1,0:T(8,128)S(1)} collective-permute-done((f32[17,128,128]{2,1,0:T(8,128)S(1)}, f32[17,128,128]{2,1,0:T(8,128)S(1)}, u32[]{:S(2)}, u32[]{:S(2)}) %collective-permute-start.24) | collective-permute-done | bytes 1114144 | tf_op jit(solution)/shard_map/ppermute | solution.py:52
  107.0 3.3 %collective-permute-start.29 = (f32[16,128,128]{2,1,0:T(8,128)S(1)}, f32[16,128,128]{2,1,0:T(8,128)S(1)}, u32[]{:S(2)}, u32[]{:S(2)}) collective-permute-start(f32[16,128,128]{2,1,0:T(8,128)S(1)} %get-tuple-element.103), channel_id=1, source_target_pairs={{0,3},{1,0},{2,1},{3,2},{4,7},{5,4},{6,5},{7,6},{8,11},{9,8},{10,9... | collective-permute-start | bytes 3145736 | tf_op jit(solution)/shard_map/ppermute | solution.py:52
  110.3 3.2 %collective-permute-start.27 = (f32[16,128,128]{2,1,0:T(8,128)S(1)}, f32[16,128,128]{2,1,0:T(8,128)S(1)}, u32[]{:S(2)}, u32[]{:S(2)}) collective-permute-start(f32[16,128,128]{2,1,0:T(8,128)S(1)} %get-tuple-element.102), channel_id=1, source_target_pairs={{0,3},{1,0},{2,1},{3,2},{4,7},{5,4},{6,5},{7,6},{8,11},{9,8},{10,9... | collective-permute-start | bytes 3145736 | tf_op jit(solution)/shard_map/ppermute | solution.py:52
  113.5 9.1 %collective-permute-done.29 = f32[16,128,128]{2,1,0:T(8,128)S(1)} collective-permute-done((f32[16,128,128]{2,1,0:T(8,128)S(1)}, f32[16,128,128]{2,1,0:T(8,128)S(1)}, u32[]{:S(2)}, u32[]{:S(2)}) %collective-permute-start.29) | collective-permute-done | bytes 1048608 | tf_op jit(solution)/shard_map/ppermute | solution.py:52
  129.2 3.5 %collective-permute-start.33 = (f32[5,128,128]{2,1,0:T(8,128)S(1)}, f32[5,128,128]{2,1,0:T(8,128)S(1)}, u32[]{:S(2)}, u32[]{:S(2)}) collective-permute-start(f32[5,128,128]{2,1,0:T(8,128)S(1)} %pad_maximum_fusion.5), channel_id=1, source_target_pairs={{0,16},{1,17},{2,18},{3,19},{4,20},{5,21},{6,22},{7,23},{8,24},{9,... | collective-permute-start | bytes 983048 | tf_op jit(solution)/shard_map/ppermute | solution.py:52
  132.8 4.7 %collective-permute-done.25 = f32[16,128,128]{2,1,0:T(8,128)S(1)} collective-permute-done((f32[16,128,128]{2,1,0:T(8,128)S(1)}, f32[16,128,128]{2,1,0:T(8,128)S(1)}, u32[]{:S(2)}, u32[]{:S(2)}) %collective-permute-start.25) | collective-permute-done | bytes 1048608 | tf_op jit(solution)/shard_map/ppermute | solution.py:52
  140.1 3.2 %collective-permute-start.34 = (f32[5,128,128]{2,1,0:T(8,128)S(1)}, f32[5,128,128]{2,1,0:T(8,128)S(1)}, u32[]{:S(2)}, u32[]{:S(2)}) collective-permute-start(f32[5,128,128]{2,1,0:T(8,128)S(1)} %get-tuple-element.114), channel_id=1, source_target_pairs={{0,4},{1,5},{2,6},{3,7},{4,8},{5,9},{6,10},{7,11},{8,12},{9,13},{1... | collective-permute-start | bytes 983048 | tf_op jit(solution)/shard_map/ppermute | solution.py:52
  148.5 9.7 %collective-permute-done.32 = f32[4,128,128]{2,1,0:T(8,128)S(1)} collective-permute-done((f32[4,128,128]{2,1,0:T(8,128)S(1)}, f32[4,128,128]{2,1,0:T(8,128)S(1)}, u32[]{:S(2)}, u32[]{:S(2)}) %collective-permute-start.32) | collective-permute-done | bytes 262176 | tf_op jit(solution)/shard_map/ppermute | solution.py:52
  159.1 5.6 %collective-permute-done.38.across_ref = f32[4,128,128]{2,1,0:T(8,128)S(1)} collective-permute-done((f32[4,128,128]{2,1,0:T(8,128)S(1)}, f32[4,128,128]{2,1,0:T(8,128)S(1)}, u32[]{:S(2)}, u32[]{:S(2)}) %collective-permute-start.38) | collective-permute-done | bytes 262176 | tf_op jit(solution)/shard_map/ppermute | solution.py:52
  (110 shorter events, 61.1 us)
Async XLA Ops:
  2.3 11.4 %collective-permute-start.2 = (f32[4,128,128]{2,1,0:T(8,128)S(1)}, f32[4,128,128]{2,1,0:T(8,128)S(1)}, u32[]{:S(2)}, u32[]{:S(2)}) collective-permute-start(f32[4,128,128]{2,1,0:T(8,128)S(1)} %get-tuple-element.113), channel_id=1, source_target_pairs={{0,4},{1,5},{2,6},{3,7},{4,8},{5,9},{6,10},{7,11},{8,12},{9,13},{1... | collective-permute-start | bytes 786440 | tf_op jit(solution)/shard_map/ppermute | solution.py:52
  19.7 10.4 %collective-permute-start.11 = (f32[8,128,128]{2,1,0:T(8,128)S(1)}, f32[8,128,128]{2,1,0:T(8,128)S(1)}, u32[]{:S(2)}, u32[]{:S(2)}) collective-permute-start(f32[8,128,128]{2,1,0:T(8,128)S(1)} %pad_maximum_fusion.4.rest_1_), channel_id=1, source_target_pairs={{0,1},{1,2},{2,3},{3,0},{4,5},{5,6},{6,7},{7,4},{8,9},{9,10},{10,1... | collective-permute-start | bytes 1572872 | tf_op jit(solution)/shard_map/ppermute | solution.py:52
  19.7 14.2 %collective-permute-start.7 = (f32[8,128,128]{2,1,0:T(8,128)S(1)}, f32[8,128,128]{2,1,0:T(8,128)S(1)}, u32[]{:S(2)}, u32[]{:S(2)}) collective-permute-start(f32[8,128,128]{2,1,0:T(8,128)S(1)} %pad_maximum_fusion.4.rest_1_), channel_id=1, source_target_pairs={{0,16},{1,17},{2,18},{3,19},{4,20},{5,21},{6,22},{7,23},{8,24},{9,... | collective-permute-start | bytes 1572872 | tf_op jit(solution)/shard_map/ppermute | solution.py:52
  21.7 22.8 %collective-permute-start.10 = (f32[8,128,128]{2,1,0:T(8,128)S(1)}, f32[8,128,128]{2,1,0:T(8,128)S(1)}, u32[]{:S(2)}, u32[]{:S(2)}) collective-permute-start(f32[8,128,128]{2,1,0:T(8,128)S(1)} %pad_maximum_fusion.3.rest_0_), channel_id=1, source_target_pairs={{0,1},{1,2},{2,3},{3,0},{4,5},{5,6},{6,7},{7,4},{8,9},{9,10},{10,1... | collective-permute-start | bytes 1572872 | tf_op jit(solution)/shard_map/ppermute | solution.py:52
  22.4 25.2 %collective-permute-start.9 = (f32[8,128,128]{2,1,0:T(8,128)S(1)}, f32[8,128,128]{2,1,0:T(8,128)S(1)}, u32[]{:S(2)}, u32[]{:S(2)}) collective-permute-start(f32[8,128,128]{2,1,0:T(8,128)S(1)} %pad_maximum_fusion.4.rest_1_), channel_id=1, source_target_pairs={{0,3},{1,0},{2,1},{3,2},{4,7},{5,4},{6,5},{7,6},{8,11},{9,8},{10,9... | collective-permute-start | bytes 1572872 | tf_op jit(solution)/shard_map/ppermute | solution.py:52
  26.9 12.3 %collective-permute-start.5 = (f32[4,128,128]{2,1,0:T(8,128)S(1)}, f32[4,128,128]{2,1,0:T(8,128)S(1)}, u32[]{:S(2)}, u32[]{:S(2)}) collective-permute-start(f32[4,128,128]{2,1,0:T(8,128)S(1)} %collective-permute-done.3), channel_id=1, source_target_pairs={{0,12},{1,13},{2,14},{3,15},{4,0},{5,1},{6,2},{7,3},{8,4},{9,5},{1... | collective-permute-start | bytes 786440 | tf_op jit(solution)/shard_map/ppermute | solution.py:52
  30.1 11.8 %collective-permute-start.12 = (f32[8,128,128]{2,1,0:T(8,128)S(1)}, f32[8,128,128]{2,1,0:T(8,128)S(1)}, u32[]{:S(2)}, u32[]{:S(2)}) collective-permute-start(f32[8,128,128]{2,1,0:T(8,128)S(1)} %collective-permute-done.4.rest_2_), channel_id=1, source_target_pairs={{0,3},{1,0},{2,1},{3,2},{4,7},{5,4},{6,5},{7,6},{8,11},{9,8},{10,9... | collective-permute-start | bytes 1572872 | tf_op jit(solution)/shard_map/ppermute | solution.py:52
  39.2 11.7 %collective-permute-start.8 = (f32[8,128,128]{2,1,0:T(8,128)S(1)}, f32[8,128,128]{2,1,0:T(8,128)S(1)}, u32[]{:S(2)}, u32[]{:S(2)}) collective-permute-start(f32[8,128,128]{2,1,0:T(8,128)S(1)} %collective-permute-done.7.rest_1_), channel_id=1, source_target_pairs={{0,1},{1,2},{2,3},{3,0},{4,5},{5,6},{6,7},{7,4},{8,9},{9,10},{10,1... | collective-permute-start | bytes 1572872 | tf_op jit(solution)/shard_map/ppermute | solution.py:52
  44.3 12.2 %collective-permute-start.17 = (f32[8,128,128]{2,1,0:T(8,128)S(1)}, f32[8,128,128]{2,1,0:T(8,128)S(1)}, u32[]{:S(2)}, u32[]{:S(2)}) collective-permute-start(f32[8,128,128]{2,1,0:T(8,128)S(1)} %constant_dynamic-update-slice_fusion.rest_0_), channel_id=1, source_target_pairs={{0,1},{1,2},{2,3},{3,0},{4,5},{5,6},{6,7},{7,4},{8,9},{9,10},{10,1... | collective-permute-start | bytes 1572872 | tf_op jit(solution)/shard_map/ppermute | solution.py:52
  44.5 12.3 %collective-permute-start.16 = (f32[8,128,128]{2,1,0:T(8,128)S(1)}, f32[8,128,128]{2,1,0:T(8,128)S(1)}, u32[]{:S(2)}, u32[]{:S(2)}) collective-permute-start(f32[8,128,128]{2,1,0:T(8,128)S(1)} %collective-permute-done.7.rest_1_), channel_id=1, source_target_pairs={{0,3},{1,0},{2,1},{3,2},{4,7},{5,4},{6,5},{7,6},{8,11},{9,8},{10,9... | collective-permute-start | bytes 1572872 | tf_op jit(solution)/shard_map/ppermute | solution.py:52
  51.2 11.2 %collective-permute-start.14 = (f32[8,128,128]{2,1,0:T(8,128)S(1)}, f32[8,128,128]{2,1,0:T(8,128)S(1)}, u32[]{:S(2)}, u32[]{:S(2)}) collective-permute-start(f32[8,128,128]{2,1,0:T(8,128)S(1)} %collective-permute-done.6.rest_2_), channel_id=1, source_target_pairs={{0,3},{1,0},{2,1},{3,2},{4,7},{5,4},{6,5},{7,6},{8,11},{9,8},{10,9... | collective-permute-start | bytes 1572872 | tf_op jit(solution)/shard_map/ppermute | solution.py:52
  70.7 12.2 %collective-permute-start.19 = (f32[4,128,128]{2,1,0:T(8,128)S(1)}, f32[4,128,128]{2,1,0:T(8,128)S(1)}, u32[]{:S(2)}, u32[]{:S(2)}) collective-permute-start(f32[4,128,128]{2,1,0:T(8,128)S(1)} %add.301), channel_id=1, source_target_pairs={{0,64},{1,65},{2,66},{3,67},{4,68},{5,69},{6,70},{7,71},{8,72},{9,... | collective-permute-start | bytes 786440 | tf_op jit(solution)/shard_map/ppermute | solution.py:52
  89.6 16.8 %collective-permute-start.24 = (f32[17,128,128]{2,1,0:T(8,128)S(1)}, f32[17,128,128]{2,1,0:T(8,128)S(1)}, u32[]{:S(2)}, u32[]{:S(2)}) collective-permute-start(f32[17,128,128]{2,1,0:T(8,128)S(1)} %get-tuple-element.81), channel_id=1, source_target_pairs={{0,1},{1,2},{2,3},{3,0},{4,5},{5,6},{6,7},{7,4},{8,9},{9,10},{10,1... | collective-permute-start | bytes 3342344 | tf_op jit(solution)/shard_map/ppermute | solution.py:52
  89.7 17.1 %collective-permute-start.26 = (f32[17,128,128]{2,1,0:T(8,128)S(1)}, f32[17,128,128]{2,1,0:T(8,128)S(1)}, u32[]{:S(2)}, u32[]{:S(2)}) collective-permute-start(f32[17,128,128]{2,1,0:T(8,128)S(1)} %get-tuple-element.83), channel_id=1, source_target_pairs={{0,3},{1,0},{2,1},{3,2},{4,7},{5,4},{6,5},{7,6},{8,11},{9,8},{10,9... | collective-permute-start | bytes 3342344 | tf_op jit(solution)/shard_map/ppermute | solution.py:52
  106.6 16.8 %collective-permute-start.28 = (f32[17,128,128]{2,1,0:T(8,128)S(1)}, f32[17,128,128]{2,1,0:T(8,128)S(1)}, u32[]{:S(2)}, u32[]{:S(2)}) collective-permute-start(f32[17,128,128]{2,1,0:T(8,128)S(1)} %get-tuple-element.105), channel_id=1, source_target_pairs={{0,1},{1,2},{2,3},{3,0},{4,5},{5,6},{6,7},{7,4},{8,9},{9,10},{10,1... | collective-permute-start | bytes 3342344 | tf_op jit(solution)/shard_map/ppermute | solution.py:52
  107.0 15.6 %collective-permute-start.29 = (f32[16,128,128]{2,1,0:T(8,128)S(1)}, f32[16,128,128]{2,1,0:T(8,128)S(1)}, u32[]{:S(2)}, u32[]{:S(2)}) collective-permute-start(f32[16,128,128]{2,1,0:T(8,128)S(1)} %get-tuple-element.103), channel_id=1, source_target_pairs={{0,3},{1,0},{2,1},{3,2},{4,7},{5,4},{6,5},{7,6},{8,11},{9,8},{10,9... | collective-permute-start | bytes 3145736 | tf_op jit(solution)/shard_map/ppermute | solution.py:52
  110.3 27.2 %collective-permute-start.25 = (f32[16,128,128]{2,1,0:T(8,128)S(1)}, f32[16,128,128]{2,1,0:T(8,128)S(1)}, u32[]{:S(2)}, u32[]{:S(2)}) collective-permute-start(f32[16,128,128]{2,1,0:T(8,128)S(1)} %get-tuple-element.100), channel_id=1, source_target_pairs={{0,1},{1,2},{2,3},{3,0},{4,5},{5,6},{6,7},{7,4},{8,9},{9,10},{10,1... | collective-permute-start | bytes 3145736 | tf_op jit(solution)/shard_map/ppermute | solution.py:52
  110.3 27.2 %collective-permute-start.27 = (f32[16,128,128]{2,1,0:T(8,128)S(1)}, f32[16,128,128]{2,1,0:T(8,128)S(1)}, u32[]{:S(2)}, u32[]{:S(2)}) collective-permute-start(f32[16,128,128]{2,1,0:T(8,128)S(1)} %get-tuple-element.102), channel_id=1, source_target_pairs={{0,3},{1,0},{2,1},{3,2},{4,7},{5,4},{6,5},{7,6},{8,11},{9,8},{10,9... | collective-permute-start | bytes 3145736 | tf_op jit(solution)/shard_map/ppermute | solution.py:52
  123.7 14.1 %collective-permute-start.31 = (f32[4,128,128]{2,1,0:T(8,128)S(1)}, f32[4,128,128]{2,1,0:T(8,128)S(1)}, u32[]{:S(2)}, u32[]{:S(2)}) collective-permute-start(f32[4,128,128]{2,1,0:T(8,128)S(1)} %get-tuple-element.109), channel_id=1, source_target_pairs={{0,16},{1,17},{2,18},{3,19},{4,20},{5,21},{6,22},{7,23},{8,24},{9,... | collective-permute-start | bytes 786440 | tf_op jit(solution)/shard_map/ppermute | solution.py:52
  126.1 11.6 %collective-permute-start.30 = (f32[4,128,128]{2,1,0:T(8,128)S(1)}, f32[4,128,128]{2,1,0:T(8,128)S(1)}, u32[]{:S(2)}, u32[]{:S(2)}) collective-permute-start(f32[4,128,128]{2,1,0:T(8,128)S(1)} %get-tuple-element.111), channel_id=1, source_target_pairs={{0,8},{1,9},{2,10},{3,11},{4,12},{5,13},{6,14},{7,15},{8,0},{9,1},... | collective-permute-start | bytes 786440 | tf_op jit(solution)/shard_map/ppermute | solution.py:52
  129.2 10.7 %collective-permute-start.33 = (f32[5,128,128]{2,1,0:T(8,128)S(1)}, f32[5,128,128]{2,1,0:T(8,128)S(1)}, u32[]{:S(2)}, u32[]{:S(2)}) collective-permute-start(f32[5,128,128]{2,1,0:T(8,128)S(1)} %pad_maximum_fusion.5), channel_id=1, source_target_pairs={{0,16},{1,17},{2,18},{3,19},{4,20},{5,21},{6,22},{7,23},{8,24},{9,... | collective-permute-start | bytes 983048 | tf_op jit(solution)/shard_map/ppermute | solution.py:52
  140.1 18.0 %collective-permute-start.34 = (f32[5,128,128]{2,1,0:T(8,128)S(1)}, f32[5,128,128]{2,1,0:T(8,128)S(1)}, u32[]{:S(2)}, u32[]{:S(2)}) collective-permute-start(f32[5,128,128]{2,1,0:T(8,128)S(1)} %get-tuple-element.114), channel_id=1, source_target_pairs={{0,4},{1,5},{2,6},{3,7},{4,8},{5,9},{6,10},{7,11},{8,12},{9,13},{1... | collective-permute-start | bytes 983048 | tf_op jit(solution)/shard_map/ppermute | solution.py:52
  143.3 14.9 %collective-permute-start.35 = (f32[5,128,128]{2,1,0:T(8,128)S(1)}, f32[5,128,128]{2,1,0:T(8,128)S(1)}, u32[]{:S(2)}, u32[]{:S(2)}) collective-permute-start(f32[5,128,128]{2,1,0:T(8,128)S(1)} %get-tuple-element.115), channel_id=1, source_target_pairs={{0,8},{1,9},{2,10},{3,11},{4,12},{5,13},{6,14},{7,15},{8,0},{9,1},... | collective-permute-start | bytes 983048 | tf_op jit(solution)/shard_map/ppermute | solution.py:52
  145.9 12.3 %collective-permute-start.36 = (f32[5,128,128]{2,1,0:T(8,128)S(1)}, f32[5,128,128]{2,1,0:T(8,128)S(1)}, u32[]{:S(2)}, u32[]{:S(2)}) collective-permute-start(f32[5,128,128]{2,1,0:T(8,128)S(1)} %get-tuple-element.116), channel_id=1, source_target_pairs={{0,12},{1,13},{2,14},{3,15},{4,0},{5,1},{6,2},{7,3},{8,4},{9,5},{1... | collective-permute-start | bytes 983048 | tf_op jit(solution)/shard_map/ppermute | solution.py:52
  (20 other events, 153.9 us)

commit v16 on v15

--- a/solution.py
+++ b/solution.py
@@ -517,8 +517,9 @@
     two = permute(with_tile(total[8:12], weight_term), u_far)
     one = permute(with_tile(total[4:8] + far_one[:4], weight_term), u_up)
     three = permute(with_tile(total[12:16] + far_three, weight_term), u_down)
+    base, one = tie(total[:4] + last, one)
     weight_term = ring_sum(0, plan[0], (weight_term, three[4], two[4], one[4]))
-    return total[:4] + last + one[:4] + two[:4] + three[:4], weight_term
+    return base + one[:4] + two[:4] + three[:4], weight_term
 
 
 def per_device(features, weight, cotangent, tiles, tile_rows, tile_cols, counts):

time: 169 us -> 170 us (level)
  transfers between devices with their start and end apart: 40 -> 40, of which waited for: 24 -> 26; matrix products, arithmetic and copies ran while one was open for 1% -> 1% of each run, Pallas kernels for 10% -> 11%
where the time goes in v16:
time: 170 us; the launch traced here: 169 us
  waiting for transfers between devices  76.9 us (45%)
  starting transfers between devices  60.7 us (36%)
  Pallas kernels  25.7 us (15%)
  other arithmetic  2.08 us (1%)
  local copies, waits for them, and re-layouts  1.83 us (1%)
  between operations  1.72 us (1%)
    ppermute x40, waiting for transfers between devices, permute(): return lax.ppermute(value, AXES, pairs)  76.9 us
    ppermute x40, starting transfers between devices, permute(): return lax.ppermute(value, AXES, pairs)  60.7 us
    pallas_call x3, Pallas kernels, forward_part(): pl.pallas_call(functools.partial(forward_kernel, which), name='forward_ti...  7.73 us
    pallas_call x2, Pallas kernels, backward_part(): pl.pallas_call(functools.partial(backward_kernel, which), name='backward_...  6.78 us
    pallas_call x2, Pallas kernels, middle_part(): pl.pallas_call(functools.partial(middle_kernel, which), name='middle_%d'...  4.52 us
    pallas_call x1, Pallas kernels, pair_tiles(): pl.pallas_call(pair_kernel, name='pair_tiles', out_shape=pltpu.VMEM((SLOT...  3.87 us
  transfers between devices with their start and end apart: 40, of which 26 were waited for; matrix products, arithmetic and copies ran while one was open for 1% of the time, Pallas kernels for 11%

profile of v16, /device:TPU:0, one launch (start us, length us, event | category | flops | bytes accessed | tf_op | source)
XLA Modules:
  0.0 168.9 jit_solution(17094384083500197457)
XLA Ops:
  8.1 3.0 %collective-permute-start.3 = (f32[4,128,128]{2,1,0:T(8,128)S(1)}, f32[4,128,128]{2,1,0:T(8,128)S(1)}, u32[]{:S(2)}, u32[]{:S(2)}) collective-permute-start(f32[4,128,128]{2,1,0:T(8,128)S(1)} %get-tuple-element.117), channel_id=1, source_target_pairs={{0,80},{1,81},{2,82},{3,83},{4,84},{5,85},{6,86},{7,87},{8,88},{9,... | collective-permute-start | bytes 786440 | tf_op jit(solution)/shard_map/ppermute | solution.py:52
  13.9 3.6 %collective-permute-done.3 = f32[4,128,128]{2,1,0:T(8,128)S(1)} collective-permute-done((f32[4,128,128]{2,1,0:T(8,128)S(1)}, f32[4,128,128]{2,1,0:T(8,128)S(1)}, u32[]{:S(2)}, u32[]{:S(2)}) %collective-permute-start.3) | collective-permute-done | bytes 262176 | tf_op jit(solution)/shard_map/ppermute | solution.py:52
  31.0 2.9 %collective-permute-done.7.rest_1_ = f32[8,128,128]{2,1,0:T(8,128)S(1)} collective-permute-done((f32[8,128,128]{2,1,0:T(8,128)S(1)}, f32[8,128,128]{2,1,0:T(8,128)S(1)}, u32[]{:S(2)}, u32[]{:S(2)}) %collective-permute-start.7) | collective-permute-done | bytes 524320 | tf_op jit(solution)/shard_map/ppermute | solution.py:52
  35.3 3.9 %pair_tiles.1.tiles_ref.rest_2_ = bf16[256,128,256]{2,1,0:T(8,128)(2,1)S(1)} custom-call(s32[1]{0:T(128)} %bitcast.34.count_ref, f32[256,128,128]{2,1,0:T(8,128)} %bitcast.41), custom_call_target="tpu_custom_call" | custom-call | flops 8800000000 | bytes 1048576 | tf_op jit(solution)/shard_map/pair_tiles/pallas_call | solution.py:123
  44.5 3.1 %collective-permute-start.16 = (f32[8,128,128]{2,1,0:T(8,128)S(1)}, f32[8,128,128]{2,1,0:T(8,128)S(1)}, u32[]{:S(2)}, u32[]{:S(2)}) collective-permute-start(f32[8,128,128]{2,1,0:T(8,128)S(1)} %collective-permute-done.7.rest_1_), channel_id=1, source_target_pairs={{0,3},{1,0},{2,1},{3,2},{4,7},{5,4},{6,5},{7,6},{8,11},{9,8},{10,9... | collective-permute-start | bytes 1572872 | tf_op jit(solution)/shard_map/ppermute | solution.py:52
  47.6 3.3 %forward_tiles_0.1.rest_6_ = f32[16,128,128]{2,1,0:T(8,128)S(1)} custom-call(s32[9]{0:T(128)S(1)} %compare_select_fusion.10.bounds_ref, s32[256]{0:T(256)S(1)} %get-tuple-element.51.order_ref, s32[256]{0:T(256)S(1)} %get-tuple-element.52.rows_ref, s32[256]{0:T(256)S(1)} %get-tuple-element.53.slots_ref, ...), custom_call_target="tpu_custom_call" | custom-call | flops 6600000000 | bytes 1048576 | tf_op jit(solution)/shard_map/forward_tiles_0/pallas_call | solution.py:263
  51.2 3.4 %collective-permute-start.14 = (f32[8,128,128]{2,1,0:T(8,128)S(1)}, f32[8,128,128]{2,1,0:T(8,128)S(1)}, u32[]{:S(2)}, u32[]{:S(2)}) collective-permute-start(f32[8,128,128]{2,1,0:T(8,128)S(1)} %collective-permute-done.6.rest_2_), channel_id=1, source_target_pairs={{0,3},{1,0},{2,1},{3,2},{4,7},{5,4},{6,5},{7,6},{8,11},{9,8},{10,9... | collective-permute-start | bytes 1572872 | tf_op jit(solution)/shard_map/ppermute | solution.py:52
  56.8 3.1 %forward_tiles_1.1.rest_2_ = f32[16,128,128]{2,1,0:T(8,128)S(1)} custom-call(s32[9]{0:T(128)S(1)} %compare_select_fusion.10.bounds_ref, s32[256]{0:T(256)S(1)} %get-tuple-element.51.order_ref, s32[256]{0:T(256)S(1)} %get-tuple-element.52.rows_ref, s32[256]{0:T(256)S(1)} %get-tuple-element.53.slots_ref, ...), custom_call_target="tpu_custom_call" | custom-call | flops 5500000256 | bytes 1048576 | tf_op jit(solution)/shard_map/forward_tiles_1/pallas_call | solution.py:263
  71.2 6.5 %collective-permute-done.22 = f32[4,128,128]{2,1,0:T(8,128)S(1)} collective-permute-done((f32[4,128,128]{2,1,0:T(8,128)S(1)}, f32[4,128,128]{2,1,0:T(8,128)S(1)}, u32[]{:S(2)}, u32[]{:S(2)}) %collective-permute-start.22) | collective-permute-done | bytes 262176 | tf_op jit(solution)/shard_map/ppermute | solution.py:52
  77.8 5.0 %collective-permute-done.19 = f32[4,128,128]{2,1,0:T(8,128)S(1)} collective-permute-done((f32[4,128,128]{2,1,0:T(8,128)S(1)}, f32[4,128,128]{2,1,0:T(8,128)S(1)}, u32[]{:S(2)}, u32[]{:S(2)}) %collective-permute-start.19) | collective-permute-done | bytes 262176 | tf_op jit(solution)/shard_map/ppermute | solution.py:52
  89.9 3.0 %collective-permute-start.26 = (f32[17,128,128]{2,1,0:T(8,128)S(1)}, f32[17,128,128]{2,1,0:T(8,128)S(1)}, u32[]{:S(2)}, u32[]{:S(2)}) collective-permute-start(f32[17,128,128]{2,1,0:T(8,128)S(1)} %get-tuple-element.85), channel_id=1, source_target_pairs={{0,3},{1,0},{2,1},{3,2},{4,7},{5,4},{6,5},{7,6},{8,11},{9,8},{10,9... | collective-permute-start | bytes 3342344 | tf_op jit(solution)/shard_map/ppermute | solution.py:52
  92.9 4.8 %backward_tiles_1.1 = (f32[16,128,128]{2,1,0:T(8,128)S(1)}, f32[17,128,128]{2,1,0:T(8,128)S(1)}, f32[16,128,128]{2,1,0:T(8,128)S(1)}, f32[16,128,128]{2,1,0:T(8,...) custom-call(s32[9]{0:T(128)S(1)} %compare_select_fusion.10.bounds_ref, ...), custom_call_target="tpu_custom_call" | custom-call | flops 8800000000 | bytes 1048576 | tf_op jit(solution)/shard_map/backward_tiles_1/pallas_call | solution.py:280
  97.7 8.7 %collective-permute-done.24 = f32[17,128,128]{2,1,0:T(8,128)S(1)} collective-permute-done((f32[17,128,128]{2,1,0:T(8,128)S(1)}, f32[17,128,128]{2,1,0:T(8,128)S(1)}, u32[]{:S(2)}, u32[]{:S(2)}) %collective-permute-start.24) | collective-permute-done | bytes 1114144 | tf_op jit(solution)/shard_map/ppermute | solution.py:52
  107.0 3.3 %collective-permute-start.29 = (f32[16,128,128]{2,1,0:T(8,128)S(1)}, f32[16,128,128]{2,1,0:T(8,128)S(1)}, u32[]{:S(2)}, u32[]{:S(2)}) collective-permute-start(f32[16,128,128]{2,1,0:T(8,128)S(1)} %get-tuple-element.107), channel_id=1, source_target_pairs={{0,3},{1,0},{2,1},{3,2},{4,7},{5,4},{6,5},{7,6},{8,11},{9,8},{10,9... | collective-permute-start | bytes 3145736 | tf_op jit(solution)/shard_map/ppermute | solution.py:52
  110.3 3.2 %collective-permute-start.27 = (f32[16,128,128]{2,1,0:T(8,128)S(1)}, f32[16,128,128]{2,1,0:T(8,128)S(1)}, u32[]{:S(2)}, u32[]{:S(2)}) collective-permute-start(f32[16,128,128]{2,1,0:T(8,128)S(1)} %get-tuple-element.106), channel_id=1, source_target_pairs={{0,3},{1,0},{2,1},{3,2},{4,7},{5,4},{6,5},{7,6},{8,11},{9,8},{10,9... | collective-permute-start | bytes 3145736 | tf_op jit(solution)/shard_map/ppermute | solution.py:52
  113.5 9.1 %collective-permute-done.29 = f32[16,128,128]{2,1,0:T(8,128)S(1)} collective-permute-done((f32[16,128,128]{2,1,0:T(8,128)S(1)}, f32[16,128,128]{2,1,0:T(8,128)S(1)}, u32[]{:S(2)}, u32[]{:S(2)}) %collective-permute-start.29) | collective-permute-done | bytes 1048608 | tf_op jit(solution)/shard_map/ppermute | solution.py:52
  123.7 3.9 %collective-permute-start.31 = (f32[4,128,128]{2,1,0:T(8,128)S(1)}, f32[4,128,128]{2,1,0:T(8,128)S(1)}, u32[]{:S(2)}, u32[]{:S(2)}) collective-permute-start(f32[4,128,128]{2,1,0:T(8,128)S(1)} %get-tuple-element.114), channel_id=1, source_target_pairs={{0,16},{1,17},{2,18},{3,19},{4,20},{5,21},{6,22},{7,23},{8,24},{9,... | collective-permute-start | bytes 786440 | tf_op jit(solution)/shard_map/ppermute | solution.py:52
  128.3 3.5 %collective-permute-start.33 = (f32[5,128,128]{2,1,0:T(8,128)S(1)}, f32[5,128,128]{2,1,0:T(8,128)S(1)}, u32[]{:S(2)}, u32[]{:S(2)}) collective-permute-start(f32[5,128,128]{2,1,0:T(8,128)S(1)} %pad_maximum_fusion.5), channel_id=1, source_target_pairs={{0,16},{1,17},{2,18},{3,19},{4,20},{5,21},{6,22},{7,23},{8,24},{9,... | collective-permute-start | bytes 983048 | tf_op jit(solution)/shard_map/ppermute | solution.py:52
  131.8 3.8 %collective-permute-done.30 = f32[4,128,128]{2,1,0:T(8,128)S(1)} collective-permute-done((f32[4,128,128]{2,1,0:T(8,128)S(1)}, f32[4,128,128]{2,1,0:T(8,128)S(1)}, u32[]{:S(2)}, u32[]{:S(2)}) %collective-permute-start.30) | collective-permute-done | bytes 262176 | tf_op jit(solution)/shard_map/ppermute | solution.py:52
  141.4 4.5 %collective-permute-done.32 = f32[4,128,128]{2,1,0:T(8,128)S(1)} collective-permute-done((f32[4,128,128]{2,1,0:T(8,128)S(1)}, f32[4,128,128]{2,1,0:T(8,128)S(1)}, u32[]{:S(2)}, u32[]{:S(2)}) %collective-permute-start.32) | collective-permute-done | bytes 262176 | tf_op jit(solution)/shard_map/ppermute | solution.py:52
  146.3 4.0 %collective-permute-start.35 = (f32[5,128,128]{2,1,0:T(8,128)S(1)}, f32[5,128,128]{2,1,0:T(8,128)S(1)}, u32[]{:S(2)}, u32[]{:S(2)}) collective-permute-start(f32[5,128,128]{2,1,0:T(8,128)S(1)} %get-tuple-element.120), channel_id=1, source_target_pairs={{0,8},{1,9},{2,10},{3,11},{4,12},{5,13},{6,14},{7,15},{8,0},{9,1},... | collective-permute-start | bytes 983048 | tf_op jit(solution)/shard_map/ppermute | solution.py:52
  150.9 3.7 %collective-permute-done.34 = f32[5,128,128]{2,1,0:T(8,128)S(1)} collective-permute-done((f32[5,128,128]{2,1,0:T(8,128)S(1)}, f32[5,128,128]{2,1,0:T(8,128)S(1)}, u32[]{:S(2)}, u32[]{:S(2)}) %collective-permute-start.34) | collective-permute-done | bytes 327712 | tf_op jit(solution)/shard_map/ppermute | solution.py:52
  154.6 4.3 %collective-permute-done.35 = f32[5,128,128]{2,1,0:T(8,128)S(1)} collective-permute-done((f32[5,128,128]{2,1,0:T(8,128)S(1)}, f32[5,128,128]{2,1,0:T(8,128)S(1)}, u32[]{:S(2)}, u32[]{:S(2)}) %collective-permute-start.35) | collective-permute-done | bytes 327712 | tf_op jit(solution)/shard_map/ppermute | solution.py:52
  161.1 4.7 %collective-permute-done.38.across_ref = f32[4,128,128]{2,1,0:T(8,128)S(1)} collective-permute-done((f32[4,128,128]{2,1,0:T(8,128)S(1)}, f32[4,128,128]{2,1,0:T(8,128)S(1)}, u32[]{:S(2)}, u32[]{:S(2)}) %collective-permute-start.38) | collective-permute-done | bytes 262176 | tf_op jit(solution)/shard_map/ppermute | solution.py:52
  (110 shorter events, 64.9 us)
Async XLA Ops:
  2.3 11.4 %collective-permute-start.2 = (f32[4,128,128]{2,1,0:T(8,128)S(1)}, f32[4,128,128]{2,1,0:T(8,128)S(1)}, u32[]{:S(2)}, u32[]{:S(2)}) collective-permute-start(f32[4,128,128]{2,1,0:T(8,128)S(1)} %get-tuple-element.118), channel_id=1, source_target_pairs={{0,4},{1,5},{2,6},{3,7},{4,8},{5,9},{6,10},{7,11},{8,12},{9,13},{1... | collective-permute-start | bytes 786440 | tf_op jit(solution)/shard_map/ppermute | solution.py:52
  19.7 10.4 %collective-permute-start.11 = (f32[8,128,128]{2,1,0:T(8,128)S(1)}, f32[8,128,128]{2,1,0:T(8,128)S(1)}, u32[]{:S(2)}, u32[]{:S(2)}) collective-permute-start(f32[8,128,128]{2,1,0:T(8,128)S(1)} %pad_maximum_fusion.4.rest_1_), channel_id=1, source_target_pairs={{0,1},{1,2},{2,3},{3,0},{4,5},{5,6},{6,7},{7,4},{8,9},{9,10},{10,1... | collective-permute-start | bytes 1572872 | tf_op jit(solution)/shard_map/ppermute | solution.py:52
  19.7 14.2 %collective-permute-start.7 = (f32[8,128,128]{2,1,0:T(8,128)S(1)}, f32[8,128,128]{2,1,0:T(8,128)S(1)}, u32[]{:S(2)}, u32[]{:S(2)}) collective-permute-start(f32[8,128,128]{2,1,0:T(8,128)S(1)} %pad_maximum_fusion.4.rest_1_), channel_id=1, source_target_pairs={{0,16},{1,17},{2,18},{3,19},{4,20},{5,21},{6,22},{7,23},{8,24},{9,... | collective-permute-start | bytes 1572872 | tf_op jit(solution)/shard_map/ppermute | solution.py:52
  21.7 22.8 %collective-permute-start.10 = (f32[8,128,128]{2,1,0:T(8,128)S(1)}, f32[8,128,128]{2,1,0:T(8,128)S(1)}, u32[]{:S(2)}, u32[]{:S(2)}) collective-permute-start(f32[8,128,128]{2,1,0:T(8,128)S(1)} %pad_maximum_fusion.3.rest_0_), channel_id=1, source_target_pairs={{0,1},{1,2},{2,3},{3,0},{4,5},{5,6},{6,7},{7,4},{8,9},{9,10},{10,1... | collective-permute-start | bytes 1572872 | tf_op jit(solution)/shard_map/ppermute | solution.py:52
  22.4 25.2 %collective-permute-start.9 = (f32[8,128,128]{2,1,0:T(8,128)S(1)}, f32[8,128,128]{2,1,0:T(8,128)S(1)}, u32[]{:S(2)}, u32[]{:S(2)}) collective-permute-start(f32[8,128,128]{2,1,0:T(8,128)S(1)} %pad_maximum_fusion.4.rest_1_), channel_id=1, source_target_pairs={{0,3},{1,0},{2,1},{3,2},{4,7},{5,4},{6,5},{7,6},{8,11},{9,8},{10,9... | collective-permute-start | bytes 1572872 | tf_op jit(solution)/shard_map/ppermute | solution.py:52
  26.9 12.3 %collective-permute-start.5 = (f32[4,128,128]{2,1,0:T(8,128)S(1)}, f32[4,128,128]{2,1,0:T(8,128)S(1)}, u32[]{:S(2)}, u32[]{:S(2)}) collective-permute-start(f32[4,128,128]{2,1,0:T(8,128)S(1)} %collective-permute-done.3), channel_id=1, source_target_pairs={{0,12},{1,13},{2,14},{3,15},{4,0},{5,1},{6,2},{7,3},{8,4},{9,5},{1... | collective-permute-start | bytes 786440 | tf_op jit(solution)/shard_map/ppermute | solution.py:52
  30.1 11.8 %collective-permute-start.12 = (f32[8,128,128]{2,1,0:T(8,128)S(1)}, f32[8,128,128]{2,1,0:T(8,128)S(1)}, u32[]{:S(2)}, u32[]{:S(2)}) collective-permute-start(f32[8,128,128]{2,1,0:T(8,128)S(1)} %collective-permute-done.4.rest_2_), channel_id=1, source_target_pairs={{0,3},{1,0},{2,1},{3,2},{4,7},{5,4},{6,5},{7,6},{8,11},{9,8},{10,9... | collective-permute-start | bytes 1572872 | tf_op jit(solution)/shard_map/ppermute | solution.py:52
  33.9 10.4 %collective-permute-start.13 = (f32[8,128,128]{2,1,0:T(8,128)S(1)}, f32[8,128,128]{2,1,0:T(8,128)S(1)}, u32[]{:S(2)}, u32[]{:S(2)}) collective-permute-start(f32[8,128,128]{2,1,0:T(8,128)S(1)} %collective-permute-done.11.rest_5_), channel_id=1, source_target_pairs={{0,1},{1,2},{2,3},{3,0},{4,5},{5,6},{6,7},{7,4},{8,9},{9,10},{10,1... | collective-permute-start | bytes 1572872 | tf_op jit(solution)/shard_map/ppermute | solution.py:52
  39.2 11.6 %collective-permute-start.8 = (f32[8,128,128]{2,1,0:T(8,128)S(1)}, f32[8,128,128]{2,1,0:T(8,128)S(1)}, u32[]{:S(2)}, u32[]{:S(2)}) collective-permute-start(f32[8,128,128]{2,1,0:T(8,128)S(1)} %collective-permute-done.7.rest_1_), channel_id=1, source_target_pairs={{0,1},{1,2},{2,3},{3,0},{4,5},{5,6},{6,7},{7,4},{8,9},{9,10},{10,1... | collective-permute-start | bytes 1572872 | tf_op jit(solution)/shard_map/ppermute | solution.py:52
  44.3 11.2 %collective-permute-start.17 = (f32[8,128,128]{2,1,0:T(8,128)S(1)}, f32[8,128,128]{2,1,0:T(8,128)S(1)}, u32[]{:S(2)}, u32[]{:S(2)}) collective-permute-start(f32[8,128,128]{2,1,0:T(8,128)S(1)} %constant_dynamic-update-slice_fusion.rest_0_), channel_id=1, source_target_pairs={{0,1},{1,2},{2,3},{3,0},{4,5},{5,6},{6,7},{7,4},{8,9},{9,10},{10,1... | collective-permute-start | bytes 1572872 | tf_op jit(solution)/shard_map/ppermute | solution.py:52
  44.5 12.3 %collective-permute-start.16 = (f32[8,128,128]{2,1,0:T(8,128)S(1)}, f32[8,128,128]{2,1,0:T(8,128)S(1)}, u32[]{:S(2)}, u32[]{:S(2)}) collective-permute-start(f32[8,128,128]{2,1,0:T(8,128)S(1)} %collective-permute-done.7.rest_1_), channel_id=1, source_target_pairs={{0,3},{1,0},{2,1},{3,2},{4,7},{5,4},{6,5},{7,6},{8,11},{9,8},{10,9... | collective-permute-start | bytes 1572872 | tf_op jit(solution)/shard_map/ppermute | solution.py:52
  51.2 11.2 %collective-permute-start.14 = (f32[8,128,128]{2,1,0:T(8,128)S(1)}, f32[8,128,128]{2,1,0:T(8,128)S(1)}, u32[]{:S(2)}, u32[]{:S(2)}) collective-permute-start(f32[8,128,128]{2,1,0:T(8,128)S(1)} %collective-permute-done.6.rest_2_), channel_id=1, source_target_pairs={{0,3},{1,0},{2,1},{3,2},{4,7},{5,4},{6,5},{7,6},{8,11},{9,8},{10,9... | collective-permute-start | bytes 1572872 | tf_op jit(solution)/shard_map/ppermute | solution.py:52
  54.5 10.4 %collective-permute-start.15 = (f32[8,128,128]{2,1,0:T(8,128)S(1)}, f32[8,128,128]{2,1,0:T(8,128)S(1)}, u32[]{:S(2)}, u32[]{:S(2)}) collective-permute-start(f32[8,128,128]{2,1,0:T(8,128)S(1)} %collective-permute-done.8.rest_5_), channel_id=1, source_target_pairs={{0,1},{1,2},{2,3},{3,0},{4,5},{5,6},{6,7},{7,4},{8,9},{9,10},{10,1... | collective-permute-start | bytes 1572872 | tf_op jit(solution)/shard_map/ppermute | solution.py:52
  70.7 12.2 %collective-permute-start.19 = (f32[4,128,128]{2,1,0:T(8,128)S(1)}, f32[4,128,128]{2,1,0:T(8,128)S(1)}, u32[]{:S(2)}, u32[]{:S(2)}) collective-permute-start(f32[4,128,128]{2,1,0:T(8,128)S(1)} %add.301), channel_id=1, source_target_pairs={{0,64},{1,65},{2,66},{3,67},{4,68},{5,69},{6,70},{7,71},{8,72},{9,... | collective-permute-start | bytes 786440 | tf_op jit(solution)/shard_map/ppermute | solution.py:52
  89.6 16.8 %collective-permute-start.24 = (f32[17,128,128]{2,1,0:T(8,128)S(1)}, f32[17,128,128]{2,1,0:T(8,128)S(1)}, u32[]{:S(2)}, u32[]{:S(2)}) collective-permute-start(f32[17,128,128]{2,1,0:T(8,128)S(1)} %get-tuple-element.83), channel_id=1, source_target_pairs={{0,1},{1,2},{2,3},{3,0},{4,5},{5,6},{6,7},{7,4},{8,9},{9,10},{10,1... | collective-permute-start | bytes 3342344 | tf_op jit(solution)/shard_map/ppermute | solution.py:52
  89.9 16.8 %collective-permute-start.26 = (f32[17,128,128]{2,1,0:T(8,128)S(1)}, f32[17,128,128]{2,1,0:T(8,128)S(1)}, u32[]{:S(2)}, u32[]{:S(2)}) collective-permute-start(f32[17,128,128]{2,1,0:T(8,128)S(1)} %get-tuple-element.85), channel_id=1, source_target_pairs={{0,3},{1,0},{2,1},{3,2},{4,7},{5,4},{6,5},{7,6},{8,11},{9,8},{10,9... | collective-permute-start | bytes 3342344 | tf_op jit(solution)/shard_map/ppermute | solution.py:52
  106.6 16.8 %collective-permute-start.28 = (f32[17,128,128]{2,1,0:T(8,128)S(1)}, f32[17,128,128]{2,1,0:T(8,128)S(1)}, u32[]{:S(2)}, u32[]{:S(2)}) collective-permute-start(f32[17,128,128]{2,1,0:T(8,128)S(1)} %get-tuple-element.109), channel_id=1, source_target_pairs={{0,1},{1,2},{2,3},{3,0},{4,5},{5,6},{6,7},{7,4},{8,9},{9,10},{10,1... | collective-permute-start | bytes 3342344 | tf_op jit(solution)/shard_map/ppermute | solution.py:52
  107.0 15.6 %collective-permute-start.29 = (f32[16,128,128]{2,1,0:T(8,128)S(1)}, f32[16,128,128]{2,1,0:T(8,128)S(1)}, u32[]{:S(2)}, u32[]{:S(2)}) collective-permute-start(f32[16,128,128]{2,1,0:T(8,128)S(1)} %get-tuple-element.107), channel_id=1, source_target_pairs={{0,3},{1,0},{2,1},{3,2},{4,7},{5,4},{6,5},{7,6},{8,11},{9,8},{10,9... | collective-permute-start | bytes 3145736 | tf_op jit(solution)/shard_map/ppermute | solution.py:52
  110.3 28.2 %collective-permute-start.25 = (f32[16,128,128]{2,1,0:T(8,128)S(1)}, f32[16,128,128]{2,1,0:T(8,128)S(1)}, u32[]{:S(2)}, u32[]{:S(2)}) collective-permute-start(f32[16,128,128]{2,1,0:T(8,128)S(1)} %get-tuple-element.104), channel_id=1, source_target_pairs={{0,1},{1,2},{2,3},{3,0},{4,5},{5,6},{6,7},{7,4},{8,9},{9,10},{10,1... | collective-permute-start | bytes 3145736 | tf_op jit(solution)/shard_map/ppermute | solution.py:52
  110.3 28.2 %collective-permute-start.27 = (f32[16,128,128]{2,1,0:T(8,128)S(1)}, f32[16,128,128]{2,1,0:T(8,128)S(1)}, u32[]{:S(2)}, u32[]{:S(2)}) collective-permute-start(f32[16,128,128]{2,1,0:T(8,128)S(1)} %get-tuple-element.106), channel_id=1, source_target_pairs={{0,3},{1,0},{2,1},{3,2},{4,7},{5,4},{6,5},{7,6},{8,11},{9,8},{10,9... | collective-permute-start | bytes 3145736 | tf_op jit(solution)/shard_map/ppermute | solution.py:52
  123.7 12.0 %collective-permute-start.31 = (f32[4,128,128]{2,1,0:T(8,128)S(1)}, f32[4,128,128]{2,1,0:T(8,128)S(1)}, u32[]{:S(2)}, u32[]{:S(2)}) collective-permute-start(f32[4,128,128]{2,1,0:T(8,128)S(1)} %get-tuple-element.114), channel_id=1, source_target_pairs={{0,16},{1,17},{2,18},{3,19},{4,20},{5,21},{6,22},{7,23},{8,24},{9,... | collective-permute-start | bytes 786440 | tf_op jit(solution)/shard_map/ppermute | solution.py:52
  128.3 13.1 %collective-permute-start.33 = (f32[5,128,128]{2,1,0:T(8,128)S(1)}, f32[5,128,128]{2,1,0:T(8,128)S(1)}, u32[]{:S(2)}, u32[]{:S(2)}) collective-permute-start(f32[5,128,128]{2,1,0:T(8,128)S(1)} %pad_maximum_fusion.5), channel_id=1, source_target_pairs={{0,16},{1,17},{2,18},{3,19},{4,20},{5,21},{6,22},{7,23},{8,24},{9,... | collective-permute-start | bytes 983048 | tf_op jit(solution)/shard_map/ppermute | solution.py:52
  135.7 10.3 %collective-permute-start.32 = (f32[4,128,128]{2,1,0:T(8,128)S(1)}, f32[4,128,128]{2,1,0:T(8,128)S(1)}, u32[]{:S(2)}, u32[]{:S(2)}) collective-permute-start(f32[4,128,128]{2,1,0:T(8,128)S(1)} %slice_add_fusion.9), channel_id=1, source_target_pairs={{0,16},{1,17},{2,18},{3,19},{4,20},{5,21},{6,22},{7,23},{8,24},{9,... | collective-permute-start | bytes 786440 | tf_op jit(solution)/shard_map/ppermute | solution.py:52
  146.3 12.6 %collective-permute-start.35 = (f32[5,128,128]{2,1,0:T(8,128)S(1)}, f32[5,128,128]{2,1,0:T(8,128)S(1)}, u32[]{:S(2)}, u32[]{:S(2)}) collective-permute-start(f32[5,128,128]{2,1,0:T(8,128)S(1)} %get-tuple-element.120), channel_id=1, source_target_pairs={{0,8},{1,9},{2,10},{3,11},{4,12},{5,13},{6,14},{7,15},{8,0},{9,1},... | collective-permute-start | bytes 983048 | tf_op jit(solution)/shard_map/ppermute | solution.py:52
  (20 other events, 147.8 us)

commit v17 on v15

--- a/solution.py
+++ b/solution.py
@@ -511,7 +511,8 @@
     far_one = permute(with_tile(apart[4:8], weight_term), y_far)
     far_three = permute(apart[12:16], y_far)
     last, far_three = tie(apart[:4] + apart_two, far_three)
-    last = permute(last, y_far)
+    filler = apart[:2]
+    last = permute(jnp.concatenate([last, filler], axis=0), y_far)[:4]
     weight_term = weight_term + far_one[4]
     total = own + own_one + own_three
     two = permute(with_tile(total[8:12], weight_term), u_far)

time: 169 us -> 178 us (1.053)
  waiting for transfers between devices: 75.7 us -> 85.2 us
  starting transfers between devices: 61.3 us -> 59.4 us
    ppermute x40, waiting for transfers between devices: 75.7 us -> 85.2 us  [permute(): return lax.ppermute(value, AXES, pairs)]
    ppermute x40, starting transfers between devices: 61.3 us -> 59.4 us  [permute(): return lax.ppermute(value, AXES, pairs)]
  transfers between devices with their start and end apart: 40 -> 40, of which waited for: 24 -> 26; matrix products, arithmetic and copies ran while one was open for 1% -> 1% of each run, Pallas kernels for 10% -> 10%
where the time goes in v17:
time: 178 us; the launch traced here: 176 us
  waiting for transfers between devices  85.2 us (48%)
  starting transfers between devices  59.4 us (33%)
  Pallas kernels  25.7 us (14%)
  other arithmetic  2.11 us (1%)
  local copies, waits for them, and re-layouts  1.84 us (1%)
    ppermute x40, waiting for transfers between devices, permute(): return lax.ppermute(value, AXES, pairs)  85.2 us
    ppermute x40, starting transfers between devices, permute(): return lax.ppermute(value, AXES, pairs)  59.4 us
    pallas_call x3, Pallas kernels, forward_part(): pl.pallas_call(functools.partial(forward_kernel, which), name='forward_ti...  7.74 us
    pallas_call x2, Pallas kernels, backward_part(): pl.pallas_call(functools.partial(backward_kernel, which), name='backward_...  6.78 us
    pallas_call x2, Pallas kernels, middle_part(): pl.pallas_call(functools.partial(middle_kernel, which), name='middle_%d'...  4.52 us
    pallas_call x1, Pallas kernels, pair_tiles(): pl.pallas_call(pair_kernel, name='pair_tiles', out_shape=pltpu.VMEM((SLOT...  3.87 us
  transfers between devices with their start and end apart: 40, of which 26 were waited for; matrix products, arithmetic and copies ran while one was open for 1% of the time, Pallas kernels for 10%

profile of v17, /device:TPU:0, one launch (start us, length us, event | category | flops | bytes accessed | tf_op | source)
XLA Modules:
  0.0 176.0 jit_solution(9896198172983564760)
XLA Ops:
  8.1 3.0 %collective-permute-start.3 = (f32[4,128,128]{2,1,0:T(8,128)S(1)}, f32[4,128,128]{2,1,0:T(8,128)S(1)}, u32[]{:S(2)}, u32[]{:S(2)}) collective-permute-start(f32[4,128,128]{2,1,0:T(8,128)S(1)} %get-tuple-element.112), channel_id=1, source_target_pairs={{0,80},{1,81},{2,82},{3,83},{4,84},{5,85},{6,86},{7,87},{8,88},{9,... | collective-permute-start | bytes 786440 | tf_op jit(solution)/shard_map/ppermute | solution.py:52
  13.9 3.6 %collective-permute-done.3 = f32[4,128,128]{2,1,0:T(8,128)S(1)} collective-permute-done((f32[4,128,128]{2,1,0:T(8,128)S(1)}, f32[4,128,128]{2,1,0:T(8,128)S(1)}, u32[]{:S(2)}, u32[]{:S(2)}) %collective-permute-start.3) | collective-permute-done | bytes 262176 | tf_op jit(solution)/shard_map/ppermute | solution.py:52
  35.3 3.9 %pair_tiles.1.tiles_ref.rest_2_ = bf16[256,128,256]{2,1,0:T(8,128)(2,1)S(1)} custom-call(s32[1]{0:T(128)} %bitcast.34.count_ref, f32[256,128,128]{2,1,0:T(8,128)} %bitcast.41), custom_call_target="tpu_custom_call" | custom-call | flops 8800000000 | bytes 1048576 | tf_op jit(solution)/shard_map/pair_tiles/pallas_call | solution.py:123
  40.7 3.5 %collective-permute-start.6 = (f32[8,128,128]{2,1,0:T(8,128)S(1)}, f32[8,128,128]{2,1,0:T(8,128)S(1)}, u32[]{:S(2)}, u32[]{:S(2)}) collective-permute-start(f32[8,128,128]{2,1,0:T(8,128)S(1)} %constant_dynamic-update-slice_fusion.rest_0_), channel_id=1, source_target_pairs={{0,3},{1,0},{2,1},{3,2},{4,7},{5,4},{6,5},{7,6},{8,11},{9,8},{10,9... | collective-permute-start | bytes 1572872 | tf_op jit(solution)/shard_map/ppermute | solution.py:52
  44.5 3.1 %collective-permute-start.16 = (f32[8,128,128]{2,1,0:T(8,128)S(1)}, f32[8,128,128]{2,1,0:T(8,128)S(1)}, u32[]{:S(2)}, u32[]{:S(2)}) collective-permute-start(f32[8,128,128]{2,1,0:T(8,128)S(1)} %collective-permute-done.7.rest_1_), channel_id=1, source_target_pairs={{0,3},{1,0},{2,1},{3,2},{4,7},{5,4},{6,5},{7,6},{8,11},{9,8},{10,9... | collective-permute-start | bytes 1572872 | tf_op jit(solution)/shard_map/ppermute | solution.py:52
  47.6 3.3 %forward_tiles_0.1.rest_6_ = f32[16,128,128]{2,1,0:T(8,128)S(1)} custom-call(s32[9]{0:T(128)S(1)} %compare_select_fusion.10.bounds_ref, s32[256]{0:T(256)S(1)} %get-tuple-element.49.order_ref, s32[256]{0:T(256)S(1)} %get-tuple-element.50.rows_ref, s32[256]{0:T(256)S(1)} %get-tuple-element.51.slots_ref, ...), custom_call_target="tpu_custom_call" | custom-call | flops 6600000000 | bytes 1048576 | tf_op jit(solution)/shard_map/forward_tiles_0/pallas_call | solution.py:263
  50.9 3.6 %collective-permute-start.14 = (f32[8,128,128]{2,1,0:T(8,128)S(1)}, f32[8,128,128]{2,1,0:T(8,128)S(1)}, u32[]{:S(2)}, u32[]{:S(2)}) collective-permute-start(f32[8,128,128]{2,1,0:T(8,128)S(1)} %collective-permute-done.6.rest_2_), channel_id=1, source_target_pairs={{0,3},{1,0},{2,1},{3,2},{4,7},{5,4},{6,5},{7,6},{8,11},{9,8},{10,9... | collective-permute-start | bytes 1572872 | tf_op jit(solution)/shard_map/ppermute | solution.py:52
  56.5 3.1 %forward_tiles_1.1.rest_2_ = f32[16,128,128]{2,1,0:T(8,128)S(1)} custom-call(s32[9]{0:T(128)S(1)} %compare_select_fusion.10.bounds_ref, s32[256]{0:T(256)S(1)} %get-tuple-element.49.order_ref, s32[256]{0:T(256)S(1)} %get-tuple-element.50.rows_ref, s32[256]{0:T(256)S(1)} %get-tuple-element.51.slots_ref, ...), custom_call_target="tpu_custom_call" | custom-call | flops 5500000256 | bytes 1048576 | tf_op jit(solution)/shard_map/forward_tiles_1/pallas_call | solution.py:263
  70.4 6.8 %collective-permute-done.22 = f32[4,128,128]{2,1,0:T(8,128)S(1)} collective-permute-done((f32[4,128,128]{2,1,0:T(8,128)S(1)}, f32[4,128,128]{2,1,0:T(8,128)S(1)}, u32[]{:S(2)}, u32[]{:S(2)}) %collective-permute-start.22) | collective-permute-done | bytes 262176 | tf_op jit(solution)/shard_map/ppermute | solution.py:52
  77.3 4.7 %collective-permute-done.19 = f32[4,128,128]{2,1,0:T(8,128)S(1)} collective-permute-done((f32[4,128,128]{2,1,0:T(8,128)S(1)}, f32[4,128,128]{2,1,0:T(8,128)S(1)}, u32[]{:S(2)}, u32[]{:S(2)}) %collective-permute-start.19) | collective-permute-done | bytes 262176 | tf_op jit(solution)/shard_map/ppermute | solution.py:52
  88.8 3.2 %collective-permute-start.26 = (f32[17,128,128]{2,1,0:T(8,128)S(1)}, f32[17,128,128]{2,1,0:T(8,128)S(1)}, u32[]{:S(2)}, u32[]{:S(2)}) collective-permute-start(f32[17,128,128]{2,1,0:T(8,128)S(1)} %get-tuple-element.83), channel_id=1, source_target_pairs={{0,3},{1,0},{2,1},{3,2},{4,7},{5,4},{6,5},{7,6},{8,11},{9,8},{10,9... | collective-permute-start | bytes 3342344 | tf_op jit(solution)/shard_map/ppermute | solution.py:52
  92.0 4.8 %backward_tiles_1.1 = (f32[16,128,128]{2,1,0:T(8,128)S(1)}, f32[17,128,128]{2,1,0:T(8,128)S(1)}, f32[16,128,128]{2,1,0:T(8,128)S(1)}, f32[16,128,128]{2,1,0:T(8,...) custom-call(s32[9]{0:T(128)S(1)} %compare_select_fusion.10.bounds_ref, ...), custom_call_target="tpu_custom_call" | custom-call | flops 8800000000 | bytes 1048576 | tf_op jit(solution)/shard_map/backward_tiles_1/pallas_call | solution.py:280
  96.8 8.7 %collective-permute-done.24 = f32[17,128,128]{2,1,0:T(8,128)S(1)} collective-permute-done((f32[17,128,128]{2,1,0:T(8,128)S(1)}, f32[17,128,128]{2,1,0:T(8,128)S(1)}, u32[]{:S(2)}, u32[]{:S(2)}) %collective-permute-start.24) | collective-permute-done | bytes 1114144 | tf_op jit(solution)/shard_map/ppermute | solution.py:52
  106.1 3.3 %collective-permute-start.27 = (f32[16,128,128]{2,1,0:T(8,128)S(1)}, f32[16,128,128]{2,1,0:T(8,128)S(1)}, u32[]{:S(2)}, u32[]{:S(2)}) collective-permute-start(f32[16,128,128]{2,1,0:T(8,128)S(1)} %get-tuple-element.102), channel_id=1, source_target_pairs={{0,3},{1,0},{2,1},{3,2},{4,7},{5,4},{6,5},{7,6},{8,11},{9,8},{10,9... | collective-permute-start | bytes 3145736 | tf_op jit(solution)/shard_map/ppermute | solution.py:52
  109.5 3.2 %collective-permute-start.29 = (f32[16,128,128]{2,1,0:T(8,128)S(1)}, f32[16,128,128]{2,1,0:T(8,128)S(1)}, u32[]{:S(2)}, u32[]{:S(2)}) collective-permute-start(f32[16,128,128]{2,1,0:T(8,128)S(1)} %get-tuple-element.103), channel_id=1, source_target_pairs={{0,3},{1,0},{2,1},{3,2},{4,7},{5,4},{6,5},{7,6},{8,11},{9,8},{10,9... | collective-permute-start | bytes 3145736 | tf_op jit(solution)/shard_map/ppermute | solution.py:52
  112.7 9.1 %collective-permute-done.25 = f32[16,128,128]{2,1,0:T(8,128)S(1)} collective-permute-done((f32[16,128,128]{2,1,0:T(8,128)S(1)}, f32[16,128,128]{2,1,0:T(8,128)S(1)}, u32[]{:S(2)}, u32[]{:S(2)}) %collective-permute-start.25) | collective-permute-done | bytes 1048608 | tf_op jit(solution)/shard_map/ppermute | solution.py:52
  122.1 10.9 %collective-permute-done.29 = f32[16,128,128]{2,1,0:T(8,128)S(1)} collective-permute-done((f32[16,128,128]{2,1,0:T(8,128)S(1)}, f32[16,128,128]{2,1,0:T(8,128)S(1)}, u32[]{:S(2)}, u32[]{:S(2)}) %collective-permute-start.29) | collective-permute-done | bytes 1048608 | tf_op jit(solution)/shard_map/ppermute | solution.py:52
  134.1 3.3 %collective-permute-start.31 = (f32[4,128,128]{2,1,0:T(8,128)S(1)}, f32[4,128,128]{2,1,0:T(8,128)S(1)}, u32[]{:S(2)}, u32[]{:S(2)}) collective-permute-start(f32[4,128,128]{2,1,0:T(8,128)S(1)} %get-tuple-element.109), channel_id=1, source_target_pairs={{0,16},{1,17},{2,18},{3,19},{4,20},{5,21},{6,22},{7,23},{8,24},{9,... | collective-permute-start | bytes 786440 | tf_op jit(solution)/shard_map/ppermute | solution.py:52
  137.3 3.8 %collective-permute-start.30 = (f32[4,128,128]{2,1,0:T(8,128)S(1)}, f32[4,128,128]{2,1,0:T(8,128)S(1)}, u32[]{:S(2)}, u32[]{:S(2)}) collective-permute-start(f32[4,128,128]{2,1,0:T(8,128)S(1)} %get-tuple-element.111), channel_id=1, source_target_pairs={{0,8},{1,9},{2,10},{3,11},{4,12},{5,13},{6,14},{7,15},{8,0},{9,1},... | collective-permute-start | bytes 786440 | tf_op jit(solution)/shard_map/ppermute | solution.py:52
  141.9 3.5 %collective-permute-done.30 = f32[4,128,128]{2,1,0:T(8,128)S(1)} collective-permute-done((f32[4,128,128]{2,1,0:T(8,128)S(1)}, f32[4,128,128]{2,1,0:T(8,128)S(1)}, u32[]{:S(2)}, u32[]{:S(2)}) %collective-permute-start.30) | collective-permute-done | bytes 262176 | tf_op jit(solution)/shard_map/ppermute | solution.py:52
  148.1 5.0 %collective-permute-done.33 = f32[5,128,128]{2,1,0:T(8,128)S(1)} collective-permute-done((f32[5,128,128]{2,1,0:T(8,128)S(1)}, f32[5,128,128]{2,1,0:T(8,128)S(1)}, u32[]{:S(2)}, u32[]{:S(2)}) %collective-permute-start.33) | collective-permute-done | bytes 327712 | tf_op jit(solution)/shard_map/ppermute | solution.py:52
  158.1 3.6 %collective-permute-done.34 = f32[5,128,128]{2,1,0:T(8,128)S(1)} collective-permute-done((f32[5,128,128]{2,1,0:T(8,128)S(1)}, f32[5,128,128]{2,1,0:T(8,128)S(1)}, u32[]{:S(2)}, u32[]{:S(2)}) %collective-permute-start.34) | collective-permute-done | bytes 327712 | tf_op jit(solution)/shard_map/ppermute | solution.py:52
  161.7 3.8 %collective-permute-done.35 = f32[5,128,128]{2,1,0:T(8,128)S(1)} collective-permute-done((f32[5,128,128]{2,1,0:T(8,128)S(1)}, f32[5,128,128]{2,1,0:T(8,128)S(1)}, u32[]{:S(2)}, u32[]{:S(2)}) %collective-permute-start.35) | collective-permute-done | bytes 327712 | tf_op jit(solution)/shard_map/ppermute | solution.py:52
  169.2 3.6 %collective-permute-done.38.across_ref = f32[4,128,128]{2,1,0:T(8,128)S(1)} collective-permute-done((f32[4,128,128]{2,1,0:T(8,128)S(1)}, f32[4,128,128]{2,1,0:T(8,128)S(1)}, u32[]{:S(2)}, u32[]{:S(2)}) %collective-permute-start.38) | collective-permute-done | bytes 262176 | tf_op jit(solution)/shard_map/ppermute | solution.py:52
  (112 shorter events, 65.9 us)
Async XLA Ops:
  2.3 11.4 %collective-permute-start.2 = (f32[4,128,128]{2,1,0:T(8,128)S(1)}, f32[4,128,128]{2,1,0:T(8,128)S(1)}, u32[]{:S(2)}, u32[]{:S(2)}) collective-permute-start(f32[4,128,128]{2,1,0:T(8,128)S(1)} %get-tuple-element.113), channel_id=1, source_target_pairs={{0,4},{1,5},{2,6},{3,7},{4,8},{5,9},{6,10},{7,11},{8,12},{9,13},{1... | collective-permute-start | bytes 786440 | tf_op jit(solution)/shard_map/ppermute | solution.py:52
  19.7 10.4 %collective-permute-start.11 = (f32[8,128,128]{2,1,0:T(8,128)S(1)}, f32[8,128,128]{2,1,0:T(8,128)S(1)}, u32[]{:S(2)}, u32[]{:S(2)}) collective-permute-start(f32[8,128,128]{2,1,0:T(8,128)S(1)} %pad_maximum_fusion.4.rest_1_), channel_id=1, source_target_pairs={{0,1},{1,2},{2,3},{3,0},{4,5},{5,6},{6,7},{7,4},{8,9},{9,10},{10,1... | collective-permute-start | bytes 1572872 | tf_op jit(solution)/shard_map/ppermute | solution.py:52
  19.7 14.2 %collective-permute-start.7 = (f32[8,128,128]{2,1,0:T(8,128)S(1)}, f32[8,128,128]{2,1,0:T(8,128)S(1)}, u32[]{:S(2)}, u32[]{:S(2)}) collective-permute-start(f32[8,128,128]{2,1,0:T(8,128)S(1)} %pad_maximum_fusion.4.rest_1_), channel_id=1, source_target_pairs={{0,16},{1,17},{2,18},{3,19},{4,20},{5,21},{6,22},{7,23},{8,24},{9,... | collective-permute-start | bytes 1572872 | tf_op jit(solution)/shard_map/ppermute | solution.py:52
  21.7 22.8 %collective-permute-start.10 = (f32[8,128,128]{2,1,0:T(8,128)S(1)}, f32[8,128,128]{2,1,0:T(8,128)S(1)}, u32[]{:S(2)}, u32[]{:S(2)}) collective-permute-start(f32[8,128,128]{2,1,0:T(8,128)S(1)} %pad_maximum_fusion.3.rest_0_), channel_id=1, source_target_pairs={{0,1},{1,2},{2,3},{3,0},{4,5},{5,6},{6,7},{7,4},{8,9},{9,10},{10,1... | collective-permute-start | bytes 1572872 | tf_op jit(solution)/shard_map/ppermute | solution.py:52
  22.4 25.2 %collective-permute-start.9 = (f32[8,128,128]{2,1,0:T(8,128)S(1)}, f32[8,128,128]{2,1,0:T(8,128)S(1)}, u32[]{:S(2)}, u32[]{:S(2)}) collective-permute-start(f32[8,128,128]{2,1,0:T(8,128)S(1)} %pad_maximum_fusion.4.rest_1_), channel_id=1, source_target_pairs={{0,3},{1,0},{2,1},{3,2},{4,7},{5,4},{6,5},{7,6},{8,11},{9,8},{10,9... | collective-permute-start | bytes 1572872 | tf_op jit(solution)/shard_map/ppermute | solution.py:52
  26.9 12.3 %collective-permute-start.5 = (f32[4,128,128]{2,1,0:T(8,128)S(1)}, f32[4,128,128]{2,1,0:T(8,128)S(1)}, u32[]{:S(2)}, u32[]{:S(2)}) collective-permute-start(f32[4,128,128]{2,1,0:T(8,128)S(1)} %collective-permute-done.3), channel_id=1, source_target_pairs={{0,12},{1,13},{2,14},{3,15},{4,0},{5,1},{6,2},{7,3},{8,4},{9,5},{1... | collective-permute-start | bytes 786440 | tf_op jit(solution)/shard_map/ppermute | solution.py:52
  30.1 10.5 %collective-permute-start.12 = (f32[8,128,128]{2,1,0:T(8,128)S(1)}, f32[8,128,128]{2,1,0:T(8,128)S(1)}, u32[]{:S(2)}, u32[]{:S(2)}) collective-permute-start(f32[8,128,128]{2,1,0:T(8,128)S(1)} %collective-permute-done.4.rest_2_), channel_id=1, source_target_pairs={{0,3},{1,0},{2,1},{3,2},{4,7},{5,4},{6,5},{7,6},{8,11},{9,8},{10,9... | collective-permute-start | bytes 1572872 | tf_op jit(solution)/shard_map/ppermute | solution.py:52
  33.9 10.4 %collective-permute-start.13 = (f32[8,128,128]{2,1,0:T(8,128)S(1)}, f32[8,128,128]{2,1,0:T(8,128)S(1)}, u32[]{:S(2)}, u32[]{:S(2)}) collective-permute-start(f32[8,128,128]{2,1,0:T(8,128)S(1)} %collective-permute-done.11.rest_5_), channel_id=1, source_target_pairs={{0,1},{1,2},{2,3},{3,0},{4,5},{5,6},{6,7},{7,4},{8,9},{9,10},{10,1... | collective-permute-start | bytes 1572872 | tf_op jit(solution)/shard_map/ppermute | solution.py:52
  39.2 11.7 %collective-permute-start.8 = (f32[8,128,128]{2,1,0:T(8,128)S(1)}, f32[8,128,128]{2,1,0:T(8,128)S(1)}, u32[]{:S(2)}, u32[]{:S(2)}) collective-permute-start(f32[8,128,128]{2,1,0:T(8,128)S(1)} %collective-permute-done.7.rest_1_), channel_id=1, source_target_pairs={{0,1},{1,2},{2,3},{3,0},{4,5},{5,6},{6,7},{7,4},{8,9},{9,10},{10,1... | collective-permute-start | bytes 1572872 | tf_op jit(solution)/shard_map/ppermute | solution.py:52
  40.7 10.3 %collective-permute-start.6 = (f32[8,128,128]{2,1,0:T(8,128)S(1)}, f32[8,128,128]{2,1,0:T(8,128)S(1)}, u32[]{:S(2)}, u32[]{:S(2)}) collective-permute-start(f32[8,128,128]{2,1,0:T(8,128)S(1)} %constant_dynamic-update-slice_fusion.rest_0_), channel_id=1, source_target_pairs={{0,3},{1,0},{2,1},{3,2},{4,7},{5,4},{6,5},{7,6},{8,11},{9,8},{10,9... | collective-permute-start | bytes 1572872 | tf_op jit(solution)/shard_map/ppermute | solution.py:52
  44.3 12.2 %collective-permute-start.17 = (f32[8,128,128]{2,1,0:T(8,128)S(1)}, f32[8,128,128]{2,1,0:T(8,128)S(1)}, u32[]{:S(2)}, u32[]{:S(2)}) collective-permute-start(f32[8,128,128]{2,1,0:T(8,128)S(1)} %constant_dynamic-update-slice_fusion.rest_0_), channel_id=1, source_target_pairs={{0,1},{1,2},{2,3},{3,0},{4,5},{5,6},{6,7},{7,4},{8,9},{9,10},{10,1... | collective-permute-start | bytes 1572872 | tf_op jit(solution)/shard_map/ppermute | solution.py:52
  44.5 12.1 %collective-permute-start.16 = (f32[8,128,128]{2,1,0:T(8,128)S(1)}, f32[8,128,128]{2,1,0:T(8,128)S(1)}, u32[]{:S(2)}, u32[]{:S(2)}) collective-permute-start(f32[8,128,128]{2,1,0:T(8,128)S(1)} %collective-permute-done.7.rest_1_), channel_id=1, source_target_pairs={{0,3},{1,0},{2,1},{3,2},{4,7},{5,4},{6,5},{7,6},{8,11},{9,8},{10,9... | collective-permute-start | bytes 1572872 | tf_op jit(solution)/shard_map/ppermute | solution.py:52
  50.9 11.2 %collective-permute-start.14 = (f32[8,128,128]{2,1,0:T(8,128)S(1)}, f32[8,128,128]{2,1,0:T(8,128)S(1)}, u32[]{:S(2)}, u32[]{:S(2)}) collective-permute-start(f32[8,128,128]{2,1,0:T(8,128)S(1)} %collective-permute-done.6.rest_2_), channel_id=1, source_target_pairs={{0,3},{1,0},{2,1},{3,2},{4,7},{5,4},{6,5},{7,6},{8,11},{9,8},{10,9... | collective-permute-start | bytes 1572872 | tf_op jit(solution)/shard_map/ppermute | solution.py:52
  54.5 10.4 %collective-permute-start.15 = (f32[8,128,128]{2,1,0:T(8,128)S(1)}, f32[8,128,128]{2,1,0:T(8,128)S(1)}, u32[]{:S(2)}, u32[]{:S(2)}) collective-permute-start(f32[8,128,128]{2,1,0:T(8,128)S(1)} %collective-permute-done.8.rest_5_), channel_id=1, source_target_pairs={{0,1},{1,2},{2,3},{3,0},{4,5},{5,6},{6,7},{7,4},{8,9},{9,10},{10,1... | collective-permute-start | bytes 1572872 | tf_op jit(solution)/shard_map/ppermute | solution.py:52
  68.4 13.6 %collective-permute-start.19 = (f32[4,128,128]{2,1,0:T(8,128)S(1)}, f32[4,128,128]{2,1,0:T(8,128)S(1)}, u32[]{:S(2)}, u32[]{:S(2)}) collective-permute-start(f32[4,128,128]{2,1,0:T(8,128)S(1)} %add.301), channel_id=1, source_target_pairs={{0,64},{1,65},{2,66},{3,67},{4,68},{5,69},{6,70},{7,71},{8,72},{9,... | collective-permute-start | bytes 786440 | tf_op jit(solution)/shard_map/ppermute | solution.py:52
  88.7 16.8 %collective-permute-start.24 = (f32[17,128,128]{2,1,0:T(8,128)S(1)}, f32[17,128,128]{2,1,0:T(8,128)S(1)}, u32[]{:S(2)}, u32[]{:S(2)}) collective-permute-start(f32[17,128,128]{2,1,0:T(8,128)S(1)} %get-tuple-element.81), channel_id=1, source_target_pairs={{0,1},{1,2},{2,3},{3,0},{4,5},{5,6},{6,7},{7,4},{8,9},{9,10},{10,1... | collective-permute-start | bytes 3342344 | tf_op jit(solution)/shard_map/ppermute | solution.py:52
  88.8 17.0 %collective-permute-start.26 = (f32[17,128,128]{2,1,0:T(8,128)S(1)}, f32[17,128,128]{2,1,0:T(8,128)S(1)}, u32[]{:S(2)}, u32[]{:S(2)}) collective-permute-start(f32[17,128,128]{2,1,0:T(8,128)S(1)} %get-tuple-element.83), channel_id=1, source_target_pairs={{0,3},{1,0},{2,1},{3,2},{4,7},{5,4},{6,5},{7,6},{8,11},{9,8},{10,9... | collective-permute-start | bytes 3342344 | tf_op jit(solution)/shard_map/ppermute | solution.py:52
  105.8 16.1 %collective-permute-start.25 = (f32[16,128,128]{2,1,0:T(8,128)S(1)}, f32[16,128,128]{2,1,0:T(8,128)S(1)}, u32[]{:S(2)}, u32[]{:S(2)}) collective-permute-start(f32[16,128,128]{2,1,0:T(8,128)S(1)} %get-tuple-element.100), channel_id=1, source_target_pairs={{0,1},{1,2},{2,3},{3,0},{4,5},{5,6},{6,7},{7,4},{8,9},{9,10},{10,1... | collective-permute-start | bytes 3145736 | tf_op jit(solution)/shard_map/ppermute | solution.py:52
  106.1 15.7 %collective-permute-start.27 = (f32[16,128,128]{2,1,0:T(8,128)S(1)}, f32[16,128,128]{2,1,0:T(8,128)S(1)}, u32[]{:S(2)}, u32[]{:S(2)}) collective-permute-start(f32[16,128,128]{2,1,0:T(8,128)S(1)} %get-tuple-element.102), channel_id=1, source_target_pairs={{0,3},{1,0},{2,1},{3,2},{4,7},{5,4},{6,5},{7,6},{8,11},{9,8},{10,9... | collective-permute-start | bytes 3145736 | tf_op jit(solution)/shard_map/ppermute | solution.py:52
  109.4 24.4 %collective-permute-start.28 = (f32[17,128,128]{2,1,0:T(8,128)S(1)}, f32[17,128,128]{2,1,0:T(8,128)S(1)}, u32[]{:S(2)}, u32[]{:S(2)}) collective-permute-start(f32[17,128,128]{2,1,0:T(8,128)S(1)} %get-tuple-element.105), channel_id=1, source_target_pairs={{0,1},{1,2},{2,3},{3,0},{4,5},{5,6},{6,7},{7,4},{8,9},{9,10},{10,1... | collective-permute-start | bytes 3342344 | tf_op jit(solution)/shard_map/ppermute | solution.py:52
  109.5 23.5 %collective-permute-start.29 = (f32[16,128,128]{2,1,0:T(8,128)S(1)}, f32[16,128,128]{2,1,0:T(8,128)S(1)}, u32[]{:S(2)}, u32[]{:S(2)}) collective-permute-start(f32[16,128,128]{2,1,0:T(8,128)S(1)} %get-tuple-element.103), channel_id=1, source_target_pairs={{0,3},{1,0},{2,1},{3,2},{4,7},{5,4},{6,5},{7,6},{8,11},{9,8},{10,9... | collective-permute-start | bytes 3145736 | tf_op jit(solution)/shard_map/ppermute | solution.py:52
  134.1 11.4 %collective-permute-start.31 = (f32[4,128,128]{2,1,0:T(8,128)S(1)}, f32[4,128,128]{2,1,0:T(8,128)S(1)}, u32[]{:S(2)}, u32[]{:S(2)}) collective-permute-start(f32[4,128,128]{2,1,0:T(8,128)S(1)} %get-tuple-element.109), channel_id=1, source_target_pairs={{0,16},{1,17},{2,18},{3,19},{4,20},{5,21},{6,22},{7,23},{8,24},{9,... | collective-permute-start | bytes 786440 | tf_op jit(solution)/shard_map/ppermute | solution.py:52
  141.7 11.4 %collective-permute-start.33 = (f32[5,128,128]{2,1,0:T(8,128)S(1)}, f32[5,128,128]{2,1,0:T(8,128)S(1)}, u32[]{:S(2)}, u32[]{:S(2)}) collective-permute-start(f32[5,128,128]{2,1,0:T(8,128)S(1)} %pad_maximum_fusion.6), channel_id=1, source_target_pairs={{0,16},{1,17},{2,18},{3,19},{4,20},{5,21},{6,22},{7,23},{8,24},{9,... | collective-permute-start | bytes 983048 | tf_op jit(solution)/shard_map/ppermute | solution.py:52
  145.5 20.6 %collective-permute-start.32 = (f32[6,128,128]{2,1,0:T(8,128)S(1)}, f32[6,128,128]{2,1,0:T(8,128)S(1)}, u32[]{:S(2)}, u32[]{:S(2)}) collective-permute-start(f32[6,128,128]{2,1,0:T(8,128)S(1)} %pad_maximum_fusion.5), channel_id=1, source_target_pairs={{0,16},{1,17},{2,18},{3,19},{4,20},{5,21},{6,22},{7,23},{8,24},{9,... | collective-permute-start | bytes 1179656 | tf_op jit(solution)/shard_map/ppermute | solution.py:52
  (20 other events, 146.4 us)

commit v18 on v14

--- a/solution.py
+++ b/solution.py
@@ -538,8 +538,8 @@
     one_first, three_second = permute(first, v_down), permute(second, v_up)
     second_far = permute(second, y_far)
     one_second, three_first = permute(second, v_down), permute(first, v_up)
-    count, one_first, partner = tie(count, one_first, partner)
     partner_one = permute(partner, u_down)
+    count, one_first, partner_one = tie(count, one_first, partner_one)
     pairs = pair_tiles(count, tile_collection)
     near = [first, second, one_first, one_second, three_first, three_second]
     far = [permute(one_first, v_down), permute(three_second, v_up)]

time: 164 us -> 165 us (level)
  waiting for transfers between devices: 75.6 us -> 83.6 us
  starting transfers between devices: 60.4 us -> 54.1 us
    ppermute x39, waiting for transfers between devices: 75.6 us -> 83.6 us  [permute(): return lax.ppermute(value, AXES, pairs)]
    ppermute x39, starting transfers between devices: 60.4 us -> 54.1 us  [permute(): return lax.ppermute(value, AXES, pairs)]
  transfers between devices with their start and end apart: 39 -> 39, of which waited for: 24 -> 23; matrix products, arithmetic and copies ran while one was open for 1% -> 1% of each run, Pallas kernels for 8% -> 9%
where the time goes in v18:
time: 165 us
  waiting for transfers between devices  83.6 us (51%)
  starting transfers between devices  54.1 us (33%)
  Pallas kernels  21.3 us (13%)
  other arithmetic  2.08 us (1%)
  local copies, waits for them, and re-layouts  1.83 us (1%)
  between operations  1.71 us (1%)
    ppermute x39, waiting for transfers between devices, permute(): return lax.ppermute(value, AXES, pairs)  83.6 us
    ppermute x39, starting transfers between devices, permute(): return lax.ppermute(value, AXES, pairs)  54.1 us
    pallas_call x3, Pallas kernels, forward_part(): pl.pallas_call(functools.partial(forward_kernel, which), name='forward_ti...  6.39 us
    pallas_call x2, Pallas kernels, backward_part(): pl.pallas_call(functools.partial(backward_kernel, which), name='backward_...  4.94 us
    pallas_call x2, Pallas kernels, middle_part(): pl.pallas_call(functools.partial(middle_kernel, which), name='middle_%d'...  4.53 us
  transfers between devices with their start and end apart: 39, of which 23 were waited for; matrix products, arithmetic and copies ran while one was open for 1% of the time, Pallas kernels for 9%

profile of v18, /device:TPU:0, one launch (start us, length us, event | category | flops | bytes accessed | tf_op | source)
XLA Modules:
  0.0 164.6 jit_solution(774183872373964128)
XLA Ops:
  3.9 2.7 %collective-permute-start.1 = (f32[4,128,128]{2,1,0:T(8,128)S(1)}, f32[4,128,128]{2,1,0:T(8,128)S(1)}, u32[]{:S(2)}, u32[]{:S(2)}) collective-permute-start(f32[4,128,128]{2,1,0:T(8,128)S(1)} %get-tuple-element.113), channel_id=1, source_target_pairs={{0,8},{1,9},{2,10},{3,11},{4,12},{5,13},{6,14},{7,15},{8,0},{9,1},... | collective-permute-start | bytes 786440 | tf_op jit(solution)/shard_map/ppermute | solution.py:52
  8.1 3.0 %collective-permute-start.3 = (f32[4,128,128]{2,1,0:T(8,128)S(1)}, f32[4,128,128]{2,1,0:T(8,128)S(1)}, u32[]{:S(2)}, u32[]{:S(2)}) collective-permute-start(f32[4,128,128]{2,1,0:T(8,128)S(1)} %get-tuple-element.112), channel_id=1, source_target_pairs={{0,80},{1,81},{2,82},{3,83},{4,84},{5,85},{6,86},{7,87},{8,88},{9,... | collective-permute-start | bytes 786440 | tf_op jit(solution)/shard_map/ppermute | solution.py:52
  13.9 3.6 %collective-permute-done.3 = f32[4,128,128]{2,1,0:T(8,128)S(1)} collective-permute-done((f32[4,128,128]{2,1,0:T(8,128)S(1)}, f32[4,128,128]{2,1,0:T(8,128)S(1)}, u32[]{:S(2)}, u32[]{:S(2)}) %collective-permute-start.3) | collective-permute-done | bytes 262176 | tf_op jit(solution)/shard_map/ppermute | solution.py:52
  23.8 5.1 %collective-permute-done.5 = f32[4,128,128]{2,1,0:T(8,128)S(1)} collective-permute-done((f32[4,128,128]{2,1,0:T(8,128)S(1)}, f32[4,128,128]{2,1,0:T(8,128)S(1)}, u32[]{:S(2)}, u32[]{:S(2)}) %collective-permute-start.5) | collective-permute-done | bytes 262176 | tf_op jit(solution)/shard_map/ppermute | solution.py:52
  31.0 3.2 %collective-permute-start.12 = (f32[8,128,128]{2,1,0:T(8,128)S(1)}, f32[8,128,128]{2,1,0:T(8,128)S(1)}, u32[]{:S(2)}, u32[]{:S(2)}) collective-permute-start(f32[8,128,128]{2,1,0:T(8,128)S(1)} %collective-permute-done.4.rest_2_), channel_id=1, source_target_pairs={{0,3},{1,0},{2,1},{3,2},{4,7},{5,4},{6,5},{7,6},{8,11},{9,8},{10,9... | collective-permute-start | bytes 1572872 | tf_op jit(solution)/shard_map/ppermute | solution.py:52
  34.2 2.6 %pair_tiles.1.tiles_ref.rest_2_ = bf16[256,128,256]{2,1,0:T(8,128)(2,1)S(1)} custom-call(s32[1]{0:T(128)} %bitcast.32.count_ref, f32[256,128,128]{2,1,0:T(8,128)} %bitcast.39), custom_call_target="tpu_custom_call" | custom-call | flops 8800000000 | bytes 1048576 | tf_op jit(solution)/shard_map/pair_tiles/pallas_call | solution.py:123
  36.9 5.3 %collective-permute-done.7.rest_1_ = f32[8,128,128]{2,1,0:T(8,128)S(1)} collective-permute-done((f32[8,128,128]{2,1,0:T(8,128)S(1)}, f32[8,128,128]{2,1,0:T(8,128)S(1)}, u32[]{:S(2)}, u32[]{:S(2)}) %collective-permute-start.7) | collective-permute-done | bytes 524320 | tf_op jit(solution)/shard_map/ppermute | solution.py:52
  47.9 2.8 %forward_tiles_0.1.rest_6_ = f32[16,128,128]{2,1,0:T(8,128)S(1)} custom-call(s32[9]{0:T(128)S(1)} %compare_select_fusion.10.bounds_ref, s32[256]{0:T(256)S(1)} %get-tuple-element.49.order_ref, s32[256]{0:T(256)S(1)} %get-tuple-element.50.rows_ref, s32[256]{0:T(256)S(1)} %get-tuple-element.51.slots_ref, ...), custom_call_target="tpu_custom_call" | custom-call | flops 6600000000 | bytes 1048576 | tf_op jit(solution)/shard_map/forward_tiles_0/pallas_call | solution.py:263
  55.6 3.6 %collective-permute-done.17.rest_4_ = f32[8,128,128]{2,1,0:T(8,128)S(1)} collective-permute-done((f32[8,128,128]{2,1,0:T(8,128)S(1)}, f32[8,128,128]{2,1,0:T(8,128)S(1)}, u32[]{:S(2)}, u32[]{:S(2)}) %collective-permute-start.17) | collective-permute-done | bytes 524320 | tf_op jit(solution)/shard_map/ppermute | solution.py:52
  70.2 6.8 %collective-permute-done.22 = f32[4,128,128]{2,1,0:T(8,128)S(1)} collective-permute-done((f32[4,128,128]{2,1,0:T(8,128)S(1)}, f32[4,128,128]{2,1,0:T(8,128)S(1)}, u32[]{:S(2)}, u32[]{:S(2)}) %collective-permute-start.22) | collective-permute-done | bytes 262176 | tf_op jit(solution)/shard_map/ppermute | solution.py:52
  77.2 4.7 %collective-permute-done.19 = f32[4,128,128]{2,1,0:T(8,128)S(1)} collective-permute-done((f32[4,128,128]{2,1,0:T(8,128)S(1)}, f32[4,128,128]{2,1,0:T(8,128)S(1)}, u32[]{:S(2)}, u32[]{:S(2)}) %collective-permute-start.19) | collective-permute-done | bytes 262176 | tf_op jit(solution)/shard_map/ppermute | solution.py:52
  83.9 2.7 %middle_1.1 = (f32[128,2048]{1,0:T(8,128)}, bf16[16,128,256]{2,1,0:T(8,128)(2,1)S(1)}, f32[128,128]{1,0:T(8,128)S(1)}) custom-call(s32[9]{0:T(128)S(1)} %compare_select_fusion.10.bounds_ref, f32[128,128]{1,0:T(8,128)S(1)} %bitcast.35, f32[128,128]{1,0:T(8,128)S(1)} %copy-done.1, f32[128,2048]{1,0:T(8,128)S(1)} %copy-done, f32[4,128,128]{2,1,0:T(8,128)S(1)} %add.302.rest_0_, ...), custom_call_target="tpu_custom_call" | custom-call | flops 2200000000 | bytes 1048576 | tf_op jit(solution)/shard_map/middle_1/pallas_call | solution.py:364
  88.8 2.6 %collective-permute-start.26 = (f32[17,128,128]{2,1,0:T(8,128)S(1)}, f32[17,128,128]{2,1,0:T(8,128)S(1)}, u32[]{:S(2)}, u32[]{:S(2)}) collective-permute-start(f32[17,128,128]{2,1,0:T(8,128)S(1)} %get-tuple-element.83), channel_id=1, source_target_pairs={{0,3},{1,0},{2,1},{3,2},{4,7},{5,4},{6,5},{7,6},{8,11},{9,8},{10,9... | collective-permute-start | bytes 3342344 | tf_op jit(solution)/shard_map/ppermute | solution.py:52
  91.4 3.4 %backward_tiles_1.1 = (f32[16,128,128]{2,1,0:T(8,128)S(1)}, f32[17,128,128]{2,1,0:T(8,128)S(1)}, f32[16,128,128]{2,1,0:T(8,128)S(1)}, f32[16,128,128]{2,1,0:T(8,...) custom-call(s32[9]{0:T(128)S(1)} %compare_select_fusion.10.bounds_ref, ...), custom_call_target="tpu_custom_call" | custom-call | flops 8800000000 | bytes 1048576 | tf_op jit(solution)/shard_map/backward_tiles_1/pallas_call | solution.py:280
  94.8 10.1 %collective-permute-done.24 = f32[17,128,128]{2,1,0:T(8,128)S(1)} collective-permute-done((f32[17,128,128]{2,1,0:T(8,128)S(1)}, f32[17,128,128]{2,1,0:T(8,128)S(1)}, u32[]{:S(2)}, u32[]{:S(2)}) %collective-permute-start.24) | collective-permute-done | bytes 1114144 | tf_op jit(solution)/shard_map/ppermute | solution.py:52
  105.5 3.3 %collective-permute-start.29 = (f32[16,128,128]{2,1,0:T(8,128)S(1)}, f32[16,128,128]{2,1,0:T(8,128)S(1)}, u32[]{:S(2)}, u32[]{:S(2)}) collective-permute-start(f32[16,128,128]{2,1,0:T(8,128)S(1)} %get-tuple-element.105), channel_id=1, source_target_pairs={{0,3},{1,0},{2,1},{3,2},{4,7},{5,4},{6,5},{7,6},{8,11},{9,8},{10,9... | collective-permute-start | bytes 3145736 | tf_op jit(solution)/shard_map/ppermute | solution.py:52
  108.8 3.2 %collective-permute-start.27 = (f32[16,128,128]{2,1,0:T(8,128)S(1)}, f32[16,128,128]{2,1,0:T(8,128)S(1)}, u32[]{:S(2)}, u32[]{:S(2)}) collective-permute-start(f32[16,128,128]{2,1,0:T(8,128)S(1)} %get-tuple-element.104), channel_id=1, source_target_pairs={{0,3},{1,0},{2,1},{3,2},{4,7},{5,4},{6,5},{7,6},{8,11},{9,8},{10,9... | collective-permute-start | bytes 3145736 | tf_op jit(solution)/shard_map/ppermute | solution.py:52
  112.1 9.9 %collective-permute-done.28 = f32[17,128,128]{2,1,0:T(8,128)S(1)} collective-permute-done((f32[17,128,128]{2,1,0:T(8,128)S(1)}, f32[17,128,128]{2,1,0:T(8,128)S(1)}, u32[]{:S(2)}, u32[]{:S(2)}) %collective-permute-start.28) | collective-permute-done | bytes 1114144 | tf_op jit(solution)/shard_map/ppermute | solution.py:52
  122.9 4.3 %collective-permute-start.31 = (f32[9,128,128]{2,1,0:T(8,128)S(1)}, f32[9,128,128]{2,1,0:T(8,128)S(1)}, u32[]{:S(2)}, u32[]{:S(2)}) collective-permute-start(f32[9,128,128]{2,1,0:T(8,128)S(1)} %pad_maximum_fusion), channel_id=1, source_target_pairs={{0,16},{1,17},{2,18},{3,19},{4,20},{5,21},{6,22},{7,23},{8,24},{9,... | collective-permute-start | bytes 1769480 | tf_op jit(solution)/shard_map/ppermute | solution.py:52
  128.6 7.4 %collective-permute-done.25 = f32[16,128,128]{2,1,0:T(8,128)S(1)} collective-permute-done((f32[16,128,128]{2,1,0:T(8,128)S(1)}, f32[16,128,128]{2,1,0:T(8,128)S(1)}, u32[]{:S(2)}, u32[]{:S(2)}) %collective-permute-start.25) | collective-permute-done | bytes 1048608 | tf_op jit(solution)/shard_map/ppermute | solution.py:52
  137.9 3.2 %collective-permute-done.31 = f32[9,128,128]{2,1,0:T(8,128)S(1)} collective-permute-done((f32[9,128,128]{2,1,0:T(8,128)S(1)}, f32[9,128,128]{2,1,0:T(8,128)S(1)}, u32[]{:S(2)}, u32[]{:S(2)}) %collective-permute-start.31) | collective-permute-done | bytes 589856 | tf_op jit(solution)/shard_map/ppermute | solution.py:52
  141.4 3.9 %collective-permute-start.34 = (f32[5,128,128]{2,1,0:T(8,128)S(1)}, f32[5,128,128]{2,1,0:T(8,128)S(1)}, u32[]{:S(2)}, u32[]{:S(2)}) collective-permute-start(f32[5,128,128]{2,1,0:T(8,128)S(1)} %get-tuple-element.115), channel_id=1, source_target_pairs={{0,8},{1,9},{2,10},{3,11},{4,12},{5,13},{6,14},{7,15},{8,0},{9,1},... | collective-permute-start | bytes 983048 | tf_op jit(solution)/shard_map/ppermute | solution.py:52
  147.1 6.8 %collective-permute-done.32 = f32[4,128,128]{2,1,0:T(8,128)S(1)} collective-permute-done((f32[4,128,128]{2,1,0:T(8,128)S(1)}, f32[4,128,128]{2,1,0:T(8,128)S(1)}, u32[]{:S(2)}, u32[]{:S(2)}) %collective-permute-start.32) | collective-permute-done | bytes 262176 | tf_op jit(solution)/shard_map/ppermute | solution.py:52
  156.6 4.9 %collective-permute-done.37.across_ref = f32[4,128,128]{2,1,0:T(8,128)S(1)} collective-permute-done((f32[4,128,128]{2,1,0:T(8,128)S(1)}, f32[4,128,128]{2,1,0:T(8,128)S(1)}, u32[]{:S(2)}, u32[]{:S(2)}) %collective-permute-start.37) | collective-permute-done | bytes 262176 | tf_op jit(solution)/shard_map/ppermute | solution.py:52
  (108 shorter events, 53.8 us)
Async XLA Ops:
  2.3 11.4 %collective-permute-start.2 = (f32[4,128,128]{2,1,0:T(8,128)S(1)}, f32[4,128,128]{2,1,0:T(8,128)S(1)}, u32[]{:S(2)}, u32[]{:S(2)}) collective-permute-start(f32[4,128,128]{2,1,0:T(8,128)S(1)} %get-tuple-element.113), channel_id=1, source_target_pairs={{0,4},{1,5},{2,6},{3,7},{4,8},{5,9},{6,10},{7,11},{8,12},{9,13},{1... | collective-permute-start | bytes 786440 | tf_op jit(solution)/shard_map/ppermute | solution.py:52
  3.9 9.9 %collective-permute-start.1 = (f32[4,128,128]{2,1,0:T(8,128)S(1)}, f32[4,128,128]{2,1,0:T(8,128)S(1)}, u32[]{:S(2)}, u32[]{:S(2)}) collective-permute-start(f32[4,128,128]{2,1,0:T(8,128)S(1)} %get-tuple-element.113), channel_id=1, source_target_pairs={{0,8},{1,9},{2,10},{3,11},{4,12},{5,13},{6,14},{7,15},{8,0},{9,1},... | collective-permute-start | bytes 786440 | tf_op jit(solution)/shard_map/ppermute | solution.py:52
  17.4 13.6 %collective-permute-start.4 = (f32[8,128,128]{2,1,0:T(8,128)S(1)}, f32[8,128,128]{2,1,0:T(8,128)S(1)}, u32[]{:S(2)}, u32[]{:S(2)}) collective-permute-start(f32[8,128,128]{2,1,0:T(8,128)S(1)} %pad_maximum_fusion.4.rest_0_), channel_id=1, source_target_pairs={{0,3},{1,0},{2,1},{3,2},{4,7},{5,4},{6,5},{7,6},{8,11},{9,8},{10,9... | collective-permute-start | bytes 1572872 | tf_op jit(solution)/shard_map/ppermute | solution.py:52
  19.7 14.5 %collective-permute-start.11 = (f32[8,128,128]{2,1,0:T(8,128)S(1)}, f32[8,128,128]{2,1,0:T(8,128)S(1)}, u32[]{:S(2)}, u32[]{:S(2)}) collective-permute-start(f32[8,128,128]{2,1,0:T(8,128)S(1)} %pad_maximum_fusion.5.rest_1_), channel_id=1, source_target_pairs={{0,1},{1,2},{2,3},{3,0},{4,5},{5,6},{6,7},{7,4},{8,9},{9,10},{10,1... | collective-permute-start | bytes 1572872 | tf_op jit(solution)/shard_map/ppermute | solution.py:52
  20.6 25.0 %collective-permute-start.10 = (f32[8,128,128]{2,1,0:T(8,128)S(1)}, f32[8,128,128]{2,1,0:T(8,128)S(1)}, u32[]{:S(2)}, u32[]{:S(2)}) collective-permute-start(f32[8,128,128]{2,1,0:T(8,128)S(1)} %pad_maximum_fusion.4.rest_0_), channel_id=1, source_target_pairs={{0,1},{1,2},{2,3},{3,0},{4,5},{5,6},{6,7},{7,4},{8,9},{9,10},{10,1... | collective-permute-start | bytes 1572872 | tf_op jit(solution)/shard_map/ppermute | solution.py:52
  21.7 26.2 %collective-permute-start.9 = (f32[8,128,128]{2,1,0:T(8,128)S(1)}, f32[8,128,128]{2,1,0:T(8,128)S(1)}, u32[]{:S(2)}, u32[]{:S(2)}) collective-permute-start(f32[8,128,128]{2,1,0:T(8,128)S(1)} %pad_maximum_fusion.5.rest_1_), channel_id=1, source_target_pairs={{0,3},{1,0},{2,1},{3,2},{4,7},{5,4},{6,5},{7,6},{8,11},{9,8},{10,9... | collective-permute-start | bytes 1572872 | tf_op jit(solution)/shard_map/ppermute | solution.py:52
  29.0 13.3 %collective-permute-start.7 = (f32[8,128,128]{2,1,0:T(8,128)S(1)}, f32[8,128,128]{2,1,0:T(8,128)S(1)}, u32[]{:S(2)}, u32[]{:S(2)}) collective-permute-start(f32[8,128,128]{2,1,0:T(8,128)S(1)} %pad_maximum_fusion.5.rest_1_), channel_id=1, source_target_pairs={{0,16},{1,17},{2,18},{3,19},{4,20},{5,21},{6,22},{7,23},{8,24},{9,... | collective-permute-start | bytes 1572872 | tf_op jit(solution)/shard_map/ppermute | solution.py:52
  31.0 12.2 %collective-permute-start.12 = (f32[8,128,128]{2,1,0:T(8,128)S(1)}, f32[8,128,128]{2,1,0:T(8,128)S(1)}, u32[]{:S(2)}, u32[]{:S(2)}) collective-permute-start(f32[8,128,128]{2,1,0:T(8,128)S(1)} %collective-permute-done.4.rest_2_), channel_id=1, source_target_pairs={{0,3},{1,0},{2,1},{3,2},{4,7},{5,4},{6,5},{7,6},{8,11},{9,8},{10,9... | collective-permute-start | bytes 1572872 | tf_op jit(solution)/shard_map/ppermute | solution.py:52
  34.2 10.4 %collective-permute-start.13 = (f32[8,128,128]{2,1,0:T(8,128)S(1)}, f32[8,128,128]{2,1,0:T(8,128)S(1)}, u32[]{:S(2)}, u32[]{:S(2)}) collective-permute-start(f32[8,128,128]{2,1,0:T(8,128)S(1)} %collective-permute-done.11.rest_5_), channel_id=1, source_target_pairs={{0,1},{1,2},{2,3},{3,0},{4,5},{5,6},{6,7},{7,4},{8,9},{9,10},{10,1... | collective-permute-start | bytes 1572872 | tf_op jit(solution)/shard_map/ppermute | solution.py:52
  43.2 10.4 %collective-permute-start.8 = (f32[8,128,128]{2,1,0:T(8,128)S(1)}, f32[8,128,128]{2,1,0:T(8,128)S(1)}, u32[]{:S(2)}, u32[]{:S(2)}) collective-permute-start(f32[8,128,128]{2,1,0:T(8,128)S(1)} %collective-permute-done.7.rest_1_), channel_id=1, source_target_pairs={{0,1},{1,2},{2,3},{3,0},{4,5},{5,6},{6,7},{7,4},{8,9},{9,10},{10,1... | collective-permute-start | bytes 1572872 | tf_op jit(solution)/shard_map/ppermute | solution.py:52
  44.6 14.6 %collective-permute-start.17 = (f32[8,128,128]{2,1,0:T(8,128)S(1)}, f32[8,128,128]{2,1,0:T(8,128)S(1)}, u32[]{:S(2)}, u32[]{:S(2)}) collective-permute-start(f32[8,128,128]{2,1,0:T(8,128)S(1)} %constant_dynamic-update-slice_fusion.rest_0_), channel_id=1, source_target_pairs={{0,1},{1,2},{2,3},{3,0},{4,5},{5,6},{6,7},{7,4},{8,9},{9,10},{10,1... | collective-permute-start | bytes 1572872 | tf_op jit(solution)/shard_map/ppermute | solution.py:52
  45.6 13.6 %collective-permute-start.16 = (f32[8,128,128]{2,1,0:T(8,128)S(1)}, f32[8,128,128]{2,1,0:T(8,128)S(1)}, u32[]{:S(2)}, u32[]{:S(2)}) collective-permute-start(f32[8,128,128]{2,1,0:T(8,128)S(1)} %collective-permute-done.7.rest_1_), channel_id=1, source_target_pairs={{0,3},{1,0},{2,1},{3,2},{4,7},{5,4},{6,5},{7,6},{8,11},{9,8},{10,9... | collective-permute-start | bytes 1572872 | tf_op jit(solution)/shard_map/ppermute | solution.py:52
  53.8 11.0 %collective-permute-start.15 = (f32[8,128,128]{2,1,0:T(8,128)S(1)}, f32[8,128,128]{2,1,0:T(8,128)S(1)}, u32[]{:S(2)}, u32[]{:S(2)}) collective-permute-start(f32[8,128,128]{2,1,0:T(8,128)S(1)} %collective-permute-done.8.rest_5_), channel_id=1, source_target_pairs={{0,1},{1,2},{2,3},{3,0},{4,5},{5,6},{6,7},{7,4},{8,9},{9,10},{10,1... | collective-permute-start | bytes 1572872 | tf_op jit(solution)/shard_map/ppermute | solution.py:52
  69.6 12.3 %collective-permute-start.19 = (f32[4,128,128]{2,1,0:T(8,128)S(1)}, f32[4,128,128]{2,1,0:T(8,128)S(1)}, u32[]{:S(2)}, u32[]{:S(2)}) collective-permute-start(f32[4,128,128]{2,1,0:T(8,128)S(1)} %add.301), channel_id=1, source_target_pairs={{0,64},{1,65},{2,66},{3,67},{4,68},{5,69},{6,70},{7,71},{8,72},{9,... | collective-permute-start | bytes 786440 | tf_op jit(solution)/shard_map/ppermute | solution.py:52
  88.1 16.8 %collective-permute-start.24 = (f32[17,128,128]{2,1,0:T(8,128)S(1)}, f32[17,128,128]{2,1,0:T(8,128)S(1)}, u32[]{:S(2)}, u32[]{:S(2)}) collective-permute-start(f32[17,128,128]{2,1,0:T(8,128)S(1)} %get-tuple-element.81), channel_id=1, source_target_pairs={{0,1},{1,2},{2,3},{3,0},{4,5},{5,6},{6,7},{7,4},{8,9},{9,10},{10,1... | collective-permute-start | bytes 3342344 | tf_op jit(solution)/shard_map/ppermute | solution.py:52
  88.8 16.5 %collective-permute-start.26 = (f32[17,128,128]{2,1,0:T(8,128)S(1)}, f32[17,128,128]{2,1,0:T(8,128)S(1)}, u32[]{:S(2)}, u32[]{:S(2)}) collective-permute-start(f32[17,128,128]{2,1,0:T(8,128)S(1)} %get-tuple-element.83), channel_id=1, source_target_pairs={{0,3},{1,0},{2,1},{3,2},{4,7},{5,4},{6,5},{7,6},{8,11},{9,8},{10,9... | collective-permute-start | bytes 3342344 | tf_op jit(solution)/shard_map/ppermute | solution.py:52
  105.2 16.8 %collective-permute-start.28 = (f32[17,128,128]{2,1,0:T(8,128)S(1)}, f32[17,128,128]{2,1,0:T(8,128)S(1)}, u32[]{:S(2)}, u32[]{:S(2)}) collective-permute-start(f32[17,128,128]{2,1,0:T(8,128)S(1)} %get-tuple-element.107), channel_id=1, source_target_pairs={{0,1},{1,2},{2,3},{3,0},{4,5},{5,6},{6,7},{7,4},{8,9},{9,10},{10,1... | collective-permute-start | bytes 3342344 | tf_op jit(solution)/shard_map/ppermute | solution.py:52
  105.5 17.0 %collective-permute-start.29 = (f32[16,128,128]{2,1,0:T(8,128)S(1)}, f32[16,128,128]{2,1,0:T(8,128)S(1)}, u32[]{:S(2)}, u32[]{:S(2)}) collective-permute-start(f32[16,128,128]{2,1,0:T(8,128)S(1)} %get-tuple-element.105), channel_id=1, source_target_pairs={{0,3},{1,0},{2,1},{3,2},{4,7},{5,4},{6,5},{7,6},{8,11},{9,8},{10,9... | collective-permute-start | bytes 3145736 | tf_op jit(solution)/shard_map/ppermute | solution.py:52
  108.8 27.2 %collective-permute-start.25 = (f32[16,128,128]{2,1,0:T(8,128)S(1)}, f32[16,128,128]{2,1,0:T(8,128)S(1)}, u32[]{:S(2)}, u32[]{:S(2)}) collective-permute-start(f32[16,128,128]{2,1,0:T(8,128)S(1)} %get-tuple-element.102), channel_id=1, source_target_pairs={{0,1},{1,2},{2,3},{3,0},{4,5},{5,6},{6,7},{7,4},{8,9},{9,10},{10,1... | collective-permute-start | bytes 3145736 | tf_op jit(solution)/shard_map/ppermute | solution.py:52
  108.8 27.2 %collective-permute-start.27 = (f32[16,128,128]{2,1,0:T(8,128)S(1)}, f32[16,128,128]{2,1,0:T(8,128)S(1)}, u32[]{:S(2)}, u32[]{:S(2)}) collective-permute-start(f32[16,128,128]{2,1,0:T(8,128)S(1)} %get-tuple-element.104), channel_id=1, source_target_pairs={{0,3},{1,0},{2,1},{3,2},{4,7},{5,4},{6,5},{7,6},{8,11},{9,8},{10,9... | collective-permute-start | bytes 3145736 | tf_op jit(solution)/shard_map/ppermute | solution.py:52
  122.9 18.2 %collective-permute-start.31 = (f32[9,128,128]{2,1,0:T(8,128)S(1)}, f32[9,128,128]{2,1,0:T(8,128)S(1)}, u32[]{:S(2)}, u32[]{:S(2)}) collective-permute-start(f32[9,128,128]{2,1,0:T(8,128)S(1)} %pad_maximum_fusion), channel_id=1, source_target_pairs={{0,16},{1,17},{2,18},{3,19},{4,20},{5,21},{6,22},{7,23},{8,24},{9,... | collective-permute-start | bytes 1769480 | tf_op jit(solution)/shard_map/ppermute | solution.py:52
  127.1 10.8 %collective-permute-start.30 = (f32[4,128,128]{2,1,0:T(8,128)S(1)}, f32[4,128,128]{2,1,0:T(8,128)S(1)}, u32[]{:S(2)}, u32[]{:S(2)}) collective-permute-start(f32[4,128,128]{2,1,0:T(8,128)S(1)} %get-tuple-element.111), channel_id=1, source_target_pairs={{0,8},{1,9},{2,10},{3,11},{4,12},{5,13},{6,14},{7,15},{8,0},{9,1},... | collective-permute-start | bytes 786440 | tf_op jit(solution)/shard_map/ppermute | solution.py:52
  141.3 12.6 %collective-permute-start.33 = (f32[5,128,128]{2,1,0:T(8,128)S(1)}, f32[5,128,128]{2,1,0:T(8,128)S(1)}, u32[]{:S(2)}, u32[]{:S(2)}) collective-permute-start(f32[5,128,128]{2,1,0:T(8,128)S(1)} %get-tuple-element.114), channel_id=1, source_target_pairs={{0,4},{1,5},{2,6},{3,7},{4,8},{5,9},{6,10},{7,11},{8,12},{9,13},{1... | collective-permute-start | bytes 983048 | tf_op jit(solution)/shard_map/ppermute | solution.py:52
  141.4 12.5 %collective-permute-start.34 = (f32[5,128,128]{2,1,0:T(8,128)S(1)}, f32[5,128,128]{2,1,0:T(8,128)S(1)}, u32[]{:S(2)}, u32[]{:S(2)}) collective-permute-start(f32[5,128,128]{2,1,0:T(8,128)S(1)} %get-tuple-element.115), channel_id=1, source_target_pairs={{0,8},{1,9},{2,10},{3,11},{4,12},{5,13},{6,14},{7,15},{8,0},{9,1},... | collective-permute-start | bytes 983048 | tf_op jit(solution)/shard_map/ppermute | solution.py:52
  (19 other events, 138.0 us)
